TPU v7x, 32 devices: a whole 2x2x4 slice. The times are simulated.
32 devices in a mesh: groups: 2 (over y), lon: 4 (over z), lat: 2 (over x), rep: 2 (over core).
Axes of the slice: x: 2, y: 2, z: 4, core: 2. Of those that a mesh axis runs over, the one named last changes fastest.
Arguments:
- grid_state: bfloat16 [128, 256, 256], P(('groups', 'lat'), ('lon', 'rep')), parts along dimension 0, may hold values from -6 to 6
- mesh1_state: bfloat16 [64, 128, 256], P(('groups', 'lat'), ('lon', 'rep')), parts along dimension 0, may hold values from -6 to 6
- mesh2_state: bfloat16 [32, 64, 256], P(('groups', 'lat'), 'lon'), parts along dimension 0, may hold values from -6 to 6
- grid_edges: int32 [16, 32, 128], P(None, 'lat', ('lon', 'rep')), may hold values from 0 to 16383, as said below
- up_edges: int32 [8, 16, 64], P(None, 'lat', 'lon'), may hold values from 0 to 4095, as said below
- weights: bfloat16 [9, 256, 256], replicated, may hold values from -0.375 to 0.375
- cotangent: bfloat16 [64, 128, 256], P(('groups', 'lat'), ('lon', 'rep')), parts along dimension 0, may hold values from -6 to 6
Outputs:
- mesh_out: bfloat16 [64, 128, 256], P(('groups', 'lat'), ('lon', 'rep')), parts along dimension 0
- mesh1_grad: bfloat16 [64, 128, 256], P(('groups', 'lat'), ('lon', 'rep')), parts along dimension 0
- weight_grads: float32 [18, 256, 256], P('groups'), parts along dimension 0
There are 2 independent parts, one for each index of `groups`. A program takes and returns all parts, laid end to end along the dimension named above; an argument that names none is the same for every part. Nothing has to cross between parts.
Inputs may be any that keep to these rules, and one draw needn't show every extreme that they name: `grid_edges`: Level-one node (i, j) draws its senders from grid rows 2i - 2 to 2i + 3 (clipped to the grid) and columns 2j - 2 to 2j + 3 (modulo 256); every node has one edge at a corner of that window. `up_edges`: Level-two node (a, b) draws its senders from level-one rows 2a - 1 to 2a + 2 (clipped) and columns 2b - 1 to 2b + 2 (modulo 128); every node has one edge at a corner of that window.
All inputs are finite; a program needn't handle non-finite values.
Results may differ from a plain program's by a relative error of at most 0.0061.
Values may be sent and summed in bfloat16 or wider, within the bound.
No kernel may reach another device: no remote copies, remote signals or barrier semaphores. Data moves between devices by JAX's collectives and lax.ppermute only.
A program may use at most 64 MiB of HBM per device.

v0:
```python
import jax
import jax.numpy as jnp
from jax import lax
from jax.sharding import PartitionSpec as P


def with_halo(cells, sides, width):
    for axis, dim in sides:
        count = lax.axis_size(axis)
        head = lax.slice_in_dim(cells, 0, width, axis=dim)
        tail = lax.slice_in_dim(cells, cells.shape[dim] - width, cells.shape[dim], axis=dim)
        cells = jnp.concatenate(
            [
                lax.ppermute(tail, axis, [(i, (i + 1) % count) for i in range(count)]),
                cells,
                lax.ppermute(head, axis, [((i + 1) % count, i) for i in range(count)]),
            ],
            axis=dim,
        )
    return cells


def matmul(left, right):
    return jnp.dot(left, right, preferred_element_type=jnp.float32)


def matmul_high(left, right):
    return jnp.dot(left, right, precision=lax.Precision.HIGHEST, preferred_element_type=jnp.float32)


def silu_slope(value):
    sigmoid = jax.nn.sigmoid(value)
    return sigmoid * (1.0 + value * (1.0 - sigmoid))


def local_index(edges, total_cols, row_start, col_start, reach_cells, ext_cols):
    global_row = edges // total_cols
    global_col = edges % total_cols
    local_row = global_row - row_start + reach_cells
    local_col = (global_col - col_start + reach_cells) % total_cols
    return (local_row * ext_cols + local_col).reshape(-1)


def fold_rims(ext_grad, widened, reach_cells):
    rows_in = ext_grad.shape[0] - 2 * reach_cells
    cols_in = ext_grad.shape[1] - 2 * reach_cells
    inner = ext_grad[reach_cells : reach_cells + rows_in, reach_cells : reach_cells + cols_in]
    inner = inner.at[:reach_cells, :].add(
        widened[:reach_cells, 2 * reach_cells : 2 * reach_cells + cols_in]
    )
    inner = inner.at[rows_in - reach_cells :, :].add(
        widened[rows_in + 3 * reach_cells :, 2 * reach_cells : 2 * reach_cells + cols_in]
    )
    inner = inner.at[:, :reach_cells].add(
        widened[2 * reach_cells : 2 * reach_cells + rows_in, :reach_cells]
    )
    inner = inner.at[:, cols_in - reach_cells :].add(
        widened[2 * reach_cells : 2 * reach_cells + rows_in, cols_in + 3 * reach_cells :]
    )
    inner = inner.at[:reach_cells, :reach_cells].add(widened[:reach_cells, :reach_cells])
    inner = inner.at[:reach_cells, cols_in - reach_cells :].add(
        widened[:reach_cells, cols_in + 3 * reach_cells :]
    )
    inner = inner.at[rows_in - reach_cells :, :reach_cells].add(
        widened[rows_in + 3 * reach_cells :, :reach_cells]
    )
    inner = inner.at[rows_in - reach_cells :, cols_in - reach_cells :].add(
        widened[rows_in + 3 * reach_cells :, cols_in + 3 * reach_cells :]
    )
    return inner


def coarse_pass(
    fine_band,
    cotan_band,
    mesh2_part,
    up_part,
    row_start,
    col_start,
    m1lon_total,
    weights,
    spread,
    fold_back,
):
    features = fine_band.shape[2]
    rows_in = fine_band.shape[0]
    cols_in = fine_band.shape[1]
    up_count = up_part.shape[0]
    fine_ext = spread(fine_band)
    up_index = local_index(up_part, m1lon_total, row_start, col_start, 1, cols_in + 2)
    senders = jnp.take(fine_ext.reshape(-1, features), up_index, axis=0)
    coarse_in = mesh2_part.reshape(-1, features)
    up_pre = (
        matmul(senders, weights[3]).reshape(up_count, -1, features)
        + matmul(coarse_in, weights[4])[None]
    )
    up_pool = (jnp.sum(jax.nn.silu(up_pre), axis=0) / up_count).astype(jnp.bfloat16)
    coarse = (coarse_in.astype(jnp.float32) + matmul(up_pool, weights[5])).astype(jnp.bfloat16)
    coarse_proj = matmul(coarse, weights[6]).reshape(rows_in // 2, cols_in // 2, features)
    parent_proj = jnp.repeat(jnp.repeat(coarse_proj, 2, axis=0), 2, axis=1).reshape(-1, features)
    fine_flat = fine_band.reshape(-1, features)
    cotan_flat = cotan_band.reshape(-1, features)
    down_pre = parent_proj + matmul(fine_flat, weights[7])
    down_act = jax.nn.silu(down_pre).astype(jnp.bfloat16)
    out_band = (fine_flat.astype(jnp.float32) + matmul(down_act, weights[8])).astype(jnp.bfloat16)
    grad8 = matmul(down_act.T, cotan_flat)
    down_delta = (matmul(cotan_flat, weights[8].T) * silu_slope(down_pre)).astype(jnp.bfloat16)
    child_sum = (
        down_delta.astype(jnp.float32)
        .reshape(rows_in // 2, 2, cols_in // 2, 2, features)
        .sum(axis=(1, 3))
        .reshape(-1, features)
    )
    grad6 = matmul_high(coarse.astype(jnp.float32).T, child_sum)
    grad7 = matmul(fine_flat.T, down_delta)
    coarse_delta = matmul_high(child_sum, weights[6].astype(jnp.float32).T).astype(jnp.bfloat16)
    grad5 = matmul(up_pool.T, coarse_delta)
    pool2_delta = matmul(coarse_delta, weights[5].T) / up_count
    up_delta = (pool2_delta[None] * silu_slope(up_pre)).astype(jnp.bfloat16)
    up_delta_flat = up_delta.reshape(-1, features)
    grad3 = matmul(senders.T, up_delta_flat)
    grad4 = matmul_high(
        coarse_in.astype(jnp.float32).T, jnp.sum(up_delta.astype(jnp.float32), axis=0)
    )
    edge_back = matmul(up_delta_flat, weights[3].T)
    ext_grad = (
        jnp.zeros(((rows_in + 2) * (cols_in + 2), features), jnp.float32)
        .at[up_index]
        .add(edge_back)
    )
    rim_total = fold_back(ext_grad.reshape(rows_in + 2, cols_in + 2, features))
    fine_delta = (
        cotan_flat.astype(jnp.float32)
        + matmul(down_delta, weights[7].T)
        + rim_total.reshape(-1, features)
    )
    return (out_band, fine_delta, (grad3, grad4, grad5, grad6, grad7, grad8))


def body(grid_state, mesh1_state, mesh2_state, grid_edges, up_edges, weights, cotangent):
    features = weights.shape[1]
    lat_pos = lax.axis_index("lat")
    col_pos = lax.axis_index(("lon", "rep"))
    rep_pos = lax.axis_index("rep")
    grid_rows = grid_state.shape[0]
    grid_cols = grid_state.shape[1]
    fine_rows = mesh1_state.shape[0]
    fine_cols = mesh1_state.shape[1]
    glon_total = grid_cols * lax.axis_size(("lon", "rep"))
    m1lon_total = fine_cols * lax.axis_size(("lon", "rep"))
    node_total = fine_rows * lax.axis_size("lat") * m1lon_total
    edge_count = grid_edges.shape[0]
    grid_ext = with_halo(grid_state, (("lat", 0), (("lon", "rep"), 1)), 2)
    enc_index = local_index(
        grid_edges, glon_total, lat_pos * grid_rows, col_pos * grid_cols, 2, grid_cols + 4
    )
    enc_senders = jnp.take(grid_ext.reshape(-1, features), enc_index, axis=0)
    fine_in = mesh1_state.reshape(-1, features)
    enc_recv = matmul(fine_in, weights[1])
    enc_pre = matmul(enc_senders, weights[0]).reshape(edge_count, -1, features) + enc_recv[None]
    enc_pool = (jnp.sum(jax.nn.silu(enc_pre), axis=0) / edge_count).astype(jnp.bfloat16)
    fine = (fine_in.astype(jnp.float32) + matmul(enc_pool, weights[2])).astype(jnp.bfloat16)
    fine = fine.reshape(fine_rows, fine_cols, features)
    fine_band, cotan_band = (
        lax.all_gather(fine, "rep", axis=1, tiled=True),
        lax.all_gather(cotangent, "rep", axis=1, tiled=True),
    )
    band_cols = fine_band.shape[1]
    lon_pos = lax.axis_index("lon")

    def spread_band(values):
        return with_halo(values, (("lat", 0), ("lon", 1)), 1)

    def fold_band(ext_grad):
        return fold_rims(
            ext_grad,
            with_halo(ext_grad.astype(jnp.bfloat16), (("lat", 0), ("lon", 1)), 1).astype(
                ext_grad.dtype
            ),
            1,
        )

    out_band, delta_band, coarse_grads = coarse_pass(
        fine_band,
        cotan_band,
        mesh2_state,
        up_edges,
        lat_pos * fine_rows,
        lon_pos * band_cols,
        m1lon_total,
        weights,
        spread_band,
        fold_band,
    )
    keep_first = (rep_pos == 0).astype(jnp.float32)
    coarse_grads = tuple((grad_part * keep_first for grad_part in coarse_grads))
    col_start = rep_pos * fine_cols
    mesh_out = lax.dynamic_slice_in_dim(
        out_band.reshape(fine_rows, band_cols, features), col_start, fine_cols, 1
    )
    fine_delta = lax.dynamic_slice_in_dim(
        delta_band.reshape(fine_rows, band_cols, features), col_start, fine_cols, 1
    )
    fine_delta = fine_delta.reshape(-1, features)
    fine_delta_b = fine_delta.astype(jnp.bfloat16)
    grad2 = matmul(enc_pool.T, fine_delta_b)
    pool_delta = matmul(fine_delta_b, weights[2].T) / edge_count
    enc_delta = (pool_delta[None] * silu_slope(enc_pre)).astype(jnp.bfloat16)
    grad0 = matmul(enc_senders.T, enc_delta.reshape(-1, features))
    node_delta = jnp.sum(enc_delta.astype(jnp.float32), axis=0)
    grad1 = matmul_high(fine_in.astype(jnp.float32).T, node_delta)
    mesh1_grad = (fine_delta + matmul_high(node_delta, weights[1].astype(jnp.float32).T)).astype(
        jnp.bfloat16
    )
    stacked = jnp.stack([grad0, grad1, grad2] + list(coarse_grads))
    summed = lax.psum(stacked, ("lon", "lat", "rep"))
    weight_grads = summed * float(node_total) ** (-0.5)
    return (mesh_out, mesh1_grad.reshape(fine_rows, fine_cols, features), weight_grads)


def solution(mesh):
    in_specs = (
        P(("groups", "lat"), ("lon", "rep"), None),
        P(("groups", "lat"), ("lon", "rep"), None),
        P(("groups", "lat"), "lon", None),
        P(None, "lat", ("lon", "rep")),
        P(None, "lat", "lon"),
        P(),
        P(("groups", "lat"), ("lon", "rep"), None),
    )
    out_specs = (
        P(("groups", "lat"), ("lon", "rep"), None),
        P(("groups", "lat"), ("lon", "rep"), None),
        P("groups", None, None),
    )
    return jax.shard_map(body, mesh=mesh, in_specs=in_specs, out_specs=out_specs, check_vma=False)
```

profile of v0, /device:TPU:0, one launch (start us, length us, event | category | flops | bytes accessed | tf_op | source)
XLA Modules:
  0.0 246.5 jit_solution(14631899026157776216)
XLA Ops:
  8.0 2.9 %collective-permute-start = (bf16[2,32,256]{2,1,0:T(8,128)(2,1)S(1)}, bf16[2,32,256]{2,1,0:T(8,128)(2,1)S(1)}, u32[]{:S(2)}, u32[]{:S(2)}) collective-permute-start(bf16[2,32,256]{2,1,0:T(8,128)(2,1)S(1)} %get-tuple-element.108), channel_id=1, source_target_pairs={{0,2},{2,0},{1,3},{3,1},{4,6},{6,4},{5,7},{7,5},{8,10},{10,8},{9,1... | collective-permute-start | bytes 98312 | tf_op jit(solution)/shard_map/ppermute | solution.py:14
  16.8 3.5 %collective-permute-start.3 = (bf16[36,2,256]{2,1,0:T(2,128)(2,1)S(1)}, bf16[36,2,256]{2,1,0:T(2,128)(2,1)S(1)}, u32[]{:S(2)}, u32[]{:S(2)}) collective-permute-start(bf16[36,2,256]{2,1,0:T(2,128)(2,1)S(1)} %get-tuple-element.106), channel_id=1, source_target_pairs={{1,0},{4,1},{5,4},{8,5},{9,8},{12,9},{13,12},{0,13},{3,2},{6,3},{7... | collective-permute-start | bytes 110600 | tf_op jit(solution)/shard_map/ppermute | solution.py:16
  22.6 14.6 %gather_fusion = bf16[4096,256]{1,0:T(8,128)(2,1)S(1)} fusion(bf16[1296,256]{1,0:T(8,128)(2,1)S(1)} %reshape.480, s32[4096]{0:T(1024)S(1)} %broadcast_clamp_fusion), kind=kCustom, calls=%fused_computation | custom fusion | bytes 4210688 | tf_op jit(solution)/shard_map/jit(_take)/gather | solution.py:157
  37.2 2.1 broadcast_select_fusion
  39.4 4.4 %multiply_reduce_fusion = (f32[256,256]{1,0:T(8,128)S(1)}, f32[16,256,256]{2,1,0:T(8,128)}) fusion(f32[256,256]{1,0:T(8,128)S(1)} %fusion.58, bf16[16,256,256]{2,1,0:T(8,128)(2,1)S(1)} %bitcast.143, bf16[9,256,256]{2,1,0:T(8,128)(2,1)} %param.28), kind=kOutput, calls=%fused_computation.5 | convolution fusion | flops 543096832 | bytes 6946816 | tf_op jit(solution)/shard_map/dot_general | solution.py:24
  44.9 2.0 all_gather.6
  47.0 2.0 collective-permute-start.4
  50.7 2.7 %collective-permute-done.5 = bf16[1,32,256]{2,1,0:T(8,128)(2,1)S(1)} collective-permute-done((bf16[1,32,256]{2,1,0:T(8,128)(2,1)S(1)}, bf16[1,32,256]{2,1,0:T(8,128)(2,1)S(1)}, u32[]{:S(2)}, u32[]{:S(2)}) %collective-permute-start.5) | collective-permute-done | bytes 16416 | tf_op jit(solution)/shard_map/ppermute | solution.py:16
  54.7 2.7 %collective-permute-start.7 = (bf16[18,1,256]{2,1,0:T(2,128)(2,1)S(1)}, bf16[18,1,256]{2,1,0:T(2,128)(2,1)S(1)}, u32[]{:S(2)}, u32[]{:S(2)}) collective-permute-start(bf16[18,1,256]{2,1,0:T(2,128)(2,1)S(1)} %get-tuple-element.114), channel_id=1, source_target_pairs={{4,0},{8,4},{12,8},{0,12},{5,1},{9,5},{13,9},{1,13},{6,2},{10,6},{... | collective-permute-start | bytes 27656 | tf_op jit(solution)/shard_map/ppermute | solution.py:16
  57.4 2.1 all_gather.7
  59.8 3.9 %gather_fusion.1 = bf16[1024,256]{1,0:T(8,128)(2,1)S(1)} fusion(bf16[612,256]{1,0:T(8,128)(2,1)S(1)} %reshape.486, s32[1024]{0:T(1024)S(1)} %broadcast_clamp_fusion.1), kind=kCustom, calls=%fused_computation.1 | custom fusion | bytes 1052672 | tf_op jit(solution)/shard_map/jit(_take)/gather | solution.py:91
  64.0 2.3 multiply_reduce_fusion.1
  75.5 2.3 convert_reduce_fusion.1
  78.6 2.2 fusion.53
  80.8 7.4 %scatter_custom_fusion = f32[612,256]{1,0:T(8,128)} fusion(s32[1024]{0:T(1024)S(1)} %bitcast.167, f32[1024,256]{1,0:T(8,128)} %fusion.53, f32[]{:T(128)} %constant.349.clone.1), kind=kCustom, calls=%fused_computation.64 | custom fusion | flops 262144 | bytes 627200 | tf_op jit(solution)/shard_map/scatter-add | solution.py:129
  89.5 2.0 collective-permute-start.9
  94.9 3.0 %collective-permute-start.11 = (bf16[20,1,256]{2,1,0:T(2,128)(2,1)}, bf16[20,1,256]{2,1,0:T(2,128)(2,1)S(1)}, u32[]{:S(2)}, u32[]{:S(2)}) collective-permute-start(bf16[20,1,256]{2,1,0:T(2,128)(2,1)} %get-tuple-element.110), channel_id=1, source_target_pairs={{4,0},{8,4},{12,8},{0,12},{5,1},{9,5},{13,9},{1,13},{6,2},{10,6},{... | collective-permute-start | bytes 30728 | tf_op jit(solution)/shard_map/ppermute | solution.py:16
  97.9 1.9 fusion.14
  111.7 2.6 %broadcast_select_fusion.2 = f32[1,1,256]{2,1,0:T(1,128)S(1)} fusion(pred[]{:T(512)} %and_reduce_fusion, f32[16,32,256]{2,1,0:T(8,128)} %scatter-add.41, s32[]{:T(128)} %bitcast.27, s32[]{:T(128)} %bitcast.28, bf16[20,1,256]{2,1,0:T(2,128)(2,1)S(1)} %collective-permute-done.11, bf16[20,1,256]{2,1,0:T(2,128)(2,1)S(1)} %collective-permute-done.10, ...), kind=kLoop, calls=%fused_computation.171 | loop fusion | flops 3072 | bytes 370697 | tf_op jit(solution)/shard_map/select.13
  114.3 2.5 %scatter-add.44 = f32[16,32,256]{2,1,0:T(8,128)} dynamic-update-slice(f32[16,32,256]{2,1,0:T(8,128)} %scatter-add.41, f32[1,1,256]{2,1,0:T(1,128)S(1)} %broadcast_select_fusion.2, s32[]{:T(128)} %bitcast.27, s32[]{:T(128)} %bitcast.28, s32[]{:T(128)} %constant.334.clone.1) | dynamic-update-slice | bytes 2052 | tf_op jit(solution)/shard_map/scatter-add | solution.py:61
  123.5 3.8 %convert_reduce_fusion = (f32[256,256]{1,0:T(8,128)S(1)}, bf16[16,256,256]{2,1,0:T(8,128)(2,1)S(1)}) fusion(f32[16,256,256]{2,1,0:T(8,128)} %get-tuple-element.120, f32[256,256]{1,0:T(8,128)S(1)} %copy-done.11, f32[256,256]{1,0:T(8,128)S(1)} %convolution_multiply_fusion.6), kind=kLoop, calls=%fused_computation.3 | loop fusion | flops 12517376 | bytes 7077888 | tf_op jit(solution)/shard_map/reduce_sum | solution.py:210
  127.4 2.1 fusion.22
  141.2 95.2 %all-reduce.2.cloned.1.call-done = f32[9,256,256]{2,1,0:T(8,128)} async-done(((f32[9,256,256]{2,1,0:T(8,128)}), f32[9,256,256]{2,1,0:T(8,128)}) %all-reduce.2.cloned.1.call-update) | async-done | bytes 2359312 | tf_op jit(solution)/shard_map/psum | solution.py:216
  236.4 3.3 %broadcast_multiply_fusion = f32[9,256,256]{2,1,0:T(8,128)} fusion(f32[9,256,256]{2,1,0:T(8,128)} %all-reduce.2.cloned.1.call-done), kind=kLoop, calls=%fused_computation.19 | loop fusion | flops 589824 | bytes 4718592 | tf_op jit(solution)/shard_map/mul | solution.py:217
  (159 shorter events, 58.2 us)
Async XLA Ops:
  7.2 9.4 %copy-start.16 = (bf16[32,32,256]{2,1,0:T(8,128)(2,1)S(1)}, bf16[32,32,256]{2,1,0:T(8,128)(2,1)}, u32[]{:S(2)}) copy-start(bf16[32,32,256]{2,1,0:T(8,128)(2,1)} %param.23) | copy-start | bytes 1572868
  7.2 229.2 %all-reduce.2.cloned.1.call-start = ((), (), s32[]{:S(2)}) async-start(), calls=%async_computation | async-start | bytes 4718592 | tf_op jit(solution)/shard_map/psum | solution.py:216
  8.0 8.6 %collective-permute-start = (bf16[2,32,256]{2,1,0:T(8,128)(2,1)S(1)}, bf16[2,32,256]{2,1,0:T(8,128)(2,1)S(1)}, u32[]{:S(2)}, u32[]{:S(2)}) collective-permute-start(bf16[2,32,256]{2,1,0:T(8,128)(2,1)S(1)} %get-tuple-element.108), channel_id=1, source_target_pairs={{0,2},{2,0},{1,3},{3,1},{4,6},{6,4},{5,7},{7,5},{8,10},{10,8},{9,1... | collective-permute-start | bytes 98312 | tf_op jit(solution)/shard_map/ppermute | solution.py:14
  11.0 5.7 %collective-permute-start.1 = (bf16[2,32,256]{2,1,0:T(8,128)(2,1)S(1)}, bf16[2,32,256]{2,1,0:T(8,128)(2,1)S(1)}, u32[]{:S(2)}, u32[]{:S(2)}) collective-permute-start(bf16[2,32,256]{2,1,0:T(8,128)(2,1)S(1)} %get-tuple-element.107), channel_id=1, source_target_pairs={{2,0},{0,2},{3,1},{1,3},{6,4},{4,6},{7,5},{5,7},{10,8},{8,10},{11,... | collective-permute-start | bytes 98312 | tf_op jit(solution)/shard_map/ppermute | solution.py:16
  14.8 24.5 %copy-start.10 = (f32[256,256]{1,0:T(8,128)}, f32[256,256]{1,0:T(8,128)S(1)}, u32[]{:S(2)}) copy-start(f32[256,256]{1,0:T(8,128)S(1)} %fusion.58) | copy-start | bytes 786436
  16.7 5.2 %collective-permute-start.2 = (bf16[36,2,256]{2,1,0:T(2,128)(2,1)S(1)}, bf16[36,2,256]{2,1,0:T(2,128)(2,1)S(1)}, u32[]{:S(2)}, u32[]{:S(2)}) collective-permute-start(bf16[36,2,256]{2,1,0:T(2,128)(2,1)S(1)} %get-tuple-element.105), channel_id=1, source_target_pairs={{0,1},{1,4},{4,5},{5,8},{8,9},{9,12},{12,13},{13,0},{2,3},{3,6},{6... | collective-permute-start | bytes 110600 | tf_op jit(solution)/shard_map/ppermute | solution.py:14
  16.8 5.2 %collective-permute-start.3 = (bf16[36,2,256]{2,1,0:T(2,128)(2,1)S(1)}, bf16[36,2,256]{2,1,0:T(2,128)(2,1)S(1)}, u32[]{:S(2)}, u32[]{:S(2)}) collective-permute-start(bf16[36,2,256]{2,1,0:T(2,128)(2,1)S(1)} %get-tuple-element.106), channel_id=1, source_target_pairs={{1,0},{4,1},{5,4},{8,5},{9,8},{12,9},{13,12},{0,13},{3,2},{6,3},{7... | collective-permute-start | bytes 110600 | tf_op jit(solution)/shard_map/ppermute | solution.py:16
  39.4 9.6 %copy-start.28 = (s32[3]{0:T(128)S(1)}, s32[3]{0:T(128)}, u32[]{:S(2)}) copy-start(s32[3]{0:T(128)} %constant.362.clone.1) | copy-start | bytes 40
  39.4 18.0 %copy-start.26 = (bf16[16,16,256]{2,1,0:T(8,128)(2,1)S(1)}, bf16[16,16,256]{2,1,0:T(8,128)(2,1)}, u32[]{:S(2)}) copy-start(bf16[16,16,256]{2,1,0:T(8,128)(2,1)} %param.29) | copy-start | bytes 393220
  43.8 15.8 %copy-start.12 = (f32[256,256]{1,0:T(8,128)}, f32[256,256]{1,0:T(8,128)S(1)}, u32[]{:S(2)}) copy-start(f32[256,256]{1,0:T(8,128)S(1)} %get-tuple-element.119) | copy-start | bytes 786436
  47.0 3.8 %collective-permute-start.4 = (bf16[1,32,256]{2,1,0:T(8,128)(2,1)S(1)}, bf16[1,32,256]{2,1,0:T(8,128)(2,1)S(1)}, u32[]{:S(2)}, u32[]{:S(2)}) collective-permute-start(bf16[1,32,256]{2,1,0:T(8,128)(2,1)S(1)} %get-tuple-element.116), channel_id=1, source_target_pairs={{0,2},{2,0},{1,3},{3,1},{4,6},{6,4},{5,7},{7,5},{8,10},{10,8},{9,1... | collective-permute-start | bytes 49160 | tf_op jit(solution)/shard_map/ppermute | solution.py:14
  49.7 3.7 %collective-permute-start.5 = (bf16[1,32,256]{2,1,0:T(8,128)(2,1)S(1)}, bf16[1,32,256]{2,1,0:T(8,128)(2,1)S(1)}, u32[]{:S(2)}, u32[]{:S(2)}) collective-permute-start(bf16[1,32,256]{2,1,0:T(8,128)(2,1)S(1)} %get-tuple-element.115), channel_id=1, source_target_pairs={{2,0},{0,2},{3,1},{1,3},{6,4},{4,6},{7,5},{5,7},{10,8},{8,10},{11,... | collective-permute-start | bytes 49160 | tf_op jit(solution)/shard_map/ppermute | solution.py:16
  53.5 6.0 %collective-permute-start.6 = (bf16[18,1,256]{2,1,0:T(2,128)(2,1)S(1)}, bf16[18,1,256]{2,1,0:T(2,128)(2,1)S(1)}, u32[]{:S(2)}, u32[]{:S(2)}) collective-permute-start(bf16[18,1,256]{2,1,0:T(2,128)(2,1)S(1)} %get-tuple-element.113), channel_id=1, source_target_pairs={{0,4},{4,8},{8,12},{12,0},{1,5},{5,9},{9,13},{13,1},{2,6},{6,10},{... | collective-permute-start | bytes 27656 | tf_op jit(solution)/shard_map/ppermute | solution.py:14
  54.7 4.9 %collective-permute-start.7 = (bf16[18,1,256]{2,1,0:T(2,128)(2,1)S(1)}, bf16[18,1,256]{2,1,0:T(2,128)(2,1)S(1)}, u32[]{:S(2)}, u32[]{:S(2)}) collective-permute-start(bf16[18,1,256]{2,1,0:T(2,128)(2,1)S(1)} %get-tuple-element.114), channel_id=1, source_target_pairs={{4,0},{8,4},{12,8},{0,12},{5,1},{9,5},{13,9},{1,13},{6,2},{10,6},{... | collective-permute-start | bytes 27656 | tf_op jit(solution)/shard_map/ppermute | solution.py:16
  72.4 8.4 %copy-start = (bf16[512,256]{1,0:T(8,128)(2,1)}, bf16[512,256]{1,0:T(8,128)(2,1)S(1)}, u32[]{:S(2)}) copy-start(bf16[512,256]{1,0:T(8,128)(2,1)S(1)} %fusion.5) | copy-start | bytes 786436
  73.1 7.7 %copy-start.8 = (f32[8,16,256]{2,1,0:T(8,128)}, f32[8,16,256]{2,1,0:T(8,128)S(1)}, u32[]{:S(2)}) copy-start(f32[8,16,256]{2,1,0:T(8,128)S(1)} %reduce_sum.47) | copy-start | bytes 393220
  74.3 13.8 %copy-start.17 = (bf16[128,256]{1,0:T(8,128)(2,1)}, bf16[128,256]{1,0:T(8,128)(2,1)S(1)}, u32[]{:S(2)}) copy-start(bf16[128,256]{1,0:T(8,128)(2,1)S(1)} %convolution_convert_fusion) | copy-start | bytes 196612
  89.4 3.8 %collective-permute-start.8 = (bf16[1,34,256]{2,1,0:T(8,128)(2,1)S(1)}, bf16[1,34,256]{2,1,0:T(8,128)(2,1)S(1)}, u32[]{:S(2)}, u32[]{:S(2)}) collective-permute-start(bf16[1,34,256]{2,1,0:T(8,128)(2,1)S(1)} %get-tuple-element.111), channel_id=1, source_target_pairs={{0,2},{2,0},{1,3},{3,1},{4,6},{6,4},{5,7},{7,5},{8,10},{10,8},{9,1... | collective-permute-start | bytes 52232 | tf_op jit(solution)/shard_map/ppermute | solution.py:14
  89.5 4.0 %collective-permute-start.9 = (bf16[1,34,256]{2,1,0:T(8,128)(2,1)S(1)}, bf16[1,34,256]{2,1,0:T(8,128)(2,1)S(1)}, u32[]{:S(2)}, u32[]{:S(2)}) collective-permute-start(bf16[1,34,256]{2,1,0:T(8,128)(2,1)S(1)} %get-tuple-element.112), channel_id=1, source_target_pairs={{2,0},{0,2},{3,1},{1,3},{6,4},{4,6},{7,5},{5,7},{10,8},{8,10},{11,... | collective-permute-start | bytes 52232 | tf_op jit(solution)/shard_map/ppermute | solution.py:16
  94.1 8.4 %collective-permute-start.10 = (bf16[20,1,256]{2,1,0:T(2,128)(2,1)}, bf16[20,1,256]{2,1,0:T(2,128)(2,1)S(1)}, u32[]{:S(2)}, u32[]{:S(2)}) collective-permute-start(bf16[20,1,256]{2,1,0:T(2,128)(2,1)} %get-tuple-element.109), channel_id=1, source_target_pairs={{0,4},{4,8},{8,12},{12,0},{1,5},{5,9},{9,13},{13,1},{2,6},{6,10},{... | collective-permute-start | bytes 30728 | tf_op jit(solution)/shard_map/ppermute | solution.py:14
  94.9 7.6 %collective-permute-start.11 = (bf16[20,1,256]{2,1,0:T(2,128)(2,1)}, bf16[20,1,256]{2,1,0:T(2,128)(2,1)S(1)}, u32[]{:S(2)}, u32[]{:S(2)}) collective-permute-start(bf16[20,1,256]{2,1,0:T(2,128)(2,1)} %get-tuple-element.110), channel_id=1, source_target_pairs={{4,0},{8,4},{12,8},{0,12},{5,1},{9,5},{13,9},{1,13},{6,2},{10,6},{... | collective-permute-start | bytes 30728 | tf_op jit(solution)/shard_map/ppermute | solution.py:16
  103.1 17.7 %copy-start.1 = (bf16[512,256]{1,0:T(8,128)(2,1)S(1)}, bf16[512,256]{1,0:T(8,128)(2,1)}, u32[]{:S(2)}) copy-start(bf16[512,256]{1,0:T(8,128)(2,1)} %copy-done) | copy-start | bytes 786436
  116.8 6.7 %copy-start.11 = (f32[256,256]{1,0:T(8,128)S(1)}, f32[256,256]{1,0:T(8,128)}, u32[]{:S(2)}) copy-start(f32[256,256]{1,0:T(8,128)} %copy-done.10) | copy-start | bytes 786436
  131.5 4.9 %copy-start.15 = (bf16[16,32,256]{2,1,0:T(8,128)(2,1)S(1)}, bf16[16,32,256]{2,1,0:T(8,128)(2,1)}, u32[]{:S(2)}) copy-start(bf16[16,32,256]{2,1,0:T(8,128)(2,1)} %all_gather.7) | copy-start | bytes 786436
  (18 other events, 58.0 us)
Sparse Core Ops, SparseCore 0:
  137.6 98.7 all-reduce.1
where the time goes:
time: 248 us; the launch traced here: 247 us
  waiting for transfers between devices  102 us (41%)
  local copies, waits for them, and re-layouts  38.3 us (15%)
  matrix products  36.2 us (15%)
  other arithmetic  32.9 us (13%)
  starting transfers between devices  18.5 us (7%)
  between operations  14.6 us (6%)
  blocking collectives  4.12 us (2%)
    psum x1, waiting for transfers between devices, body(): summed = lax.psum(stacked, ('lon', 'lat', 'rep'))  95.2 us
    dot_general x20, matrix products, matmul(): return jnp.dot(left, right, preferred_element_type=jnp.float32)  29.1 us
    gather x1, local copies, waits for them, and re-layouts, body(): enc_senders = jnp.take(grid_ext.reshape(-1, features), enc_index, axis=0)  14.6 us
    ppermute x6, starting transfers between devices, with_halo(): lax.ppermute(head, axis, [((i + 1) % count, i) for i in range(count)])  11.4 us
    scatter-add x1, other arithmetic, coarse_pass(): ext_grad = jnp.zeros(((rows_in + 2) * (cols_in + 2), features), jnp.float...  7.35 us
    dot_general x5, matrix products, matmul_high(): jnp.dot(left, right, precision=lax.Precision.HIGHEST, preferred_element_t...  7.12 us
    ppermute x6, starting transfers between devices, with_halo(): lax.ppermute(tail, axis, [(i, (i + 1) % count) for i in range(count)])  7.01 us
  transfers between devices with their start and end apart: 13, of which 6 were waited for; matrix products, arithmetic and copies ran while one was open for 6% of the time, Pallas kernels for 0%

commit v1 on v0

--- a/solution.py
+++ b/solution.py
@@ -1,3 +1,5 @@
+import functools
+
 import jax
 import jax.numpy as jnp
 from jax import lax
@@ -137,7 +139,65 @@
     return (out_band, fine_delta, (grad3, grad4, grad5, grad6, grad7, grad8))
 
 
-def body(grid_state, mesh1_state, mesh2_state, grid_edges, up_edges, weights, cotangent):
+def swap_over(values, axes, partner, sizes):
+    total = 1
+    for size in sizes:
+        total *= size
+    return lax.ppermute(values, axes, [(i, partner(i)) for i in range(total)])
+
+
+def sum_over_slice(stacked, mesh):
+    lat_size, lon_size = mesh.shape["lat"], mesh.shape["lon"]
+    rep = lax.axis_index("rep")
+    lat, lon = lax.axis_index("lat"), lax.axis_index("lon")
+    place = (lat % 2) * 2 + lon % 2
+    low = jnp.bfloat16
+
+    def between(values, lon_bit, lat_bit):
+        return swap_over(
+            values, ("lon", "lat"),
+            lambda i: ((i // lat_size) ^ lon_bit) * lat_size + ((i % lat_size) ^ lat_bit),
+            (lon_size, lat_size),
+        )
+
+    def siblings(values):
+        return swap_over(values, "rep", lambda i: i ^ 1, (2,))
+
+    count, rows, cols = stacked.shape
+    halves = stacked.reshape(count, 2, rows // 2, cols)
+    sent = lax.dynamic_index_in_dim(halves, 1 - rep, 1, keepdims=False).astype(low)
+    kept = lax.dynamic_index_in_dim(halves, rep, 1, keepdims=False)
+    half = kept + siblings(sent).astype(jnp.float32)
+    quarters = half.reshape(count, 4, rows // 8, cols)
+    total = lax.dynamic_index_in_dim(quarters, place, 1, keepdims=False)
+    for step in (1, 2, 3):
+        piece = lax.dynamic_index_in_dim(quarters, place ^ step, 1, keepdims=False).astype(low)
+        total = total + between(piece, step & 1, step >> 1).astype(jnp.float32)
+    bit = 2
+    while bit < lon_size:
+        rounded = total.astype(low)
+        total = rounded.astype(jnp.float32) + between(rounded, bit, 0).astype(jnp.float32)
+        bit *= 2
+    bit = 2
+    while bit < lat_size:
+        rounded = total.astype(low)
+        total = rounded.astype(jnp.float32) + between(rounded, 0, bit).astype(jnp.float32)
+        bit *= 2
+    own = total.astype(low)
+    pieces = [own] + [between(own, step & 1, step >> 1) for step in (1, 2, 3)]
+    theirs = [siblings(piece) for piece in pieces]
+    mine_all = jnp.stack(pieces, 0)
+    theirs_all = jnp.stack(theirs, 0)
+    order = jnp.arange(4) ^ place
+    mine_half = jnp.take(mine_all, order, axis=0)
+    their_half = jnp.take(theirs_all, order, axis=0)
+    first = jnp.where(rep == 0, mine_half, their_half)
+    second = jnp.where(rep == 0, their_half, mine_half)
+    both = jnp.stack([first, second], 0)
+    return jnp.moveaxis(both, 2, 0).reshape(count, rows, cols).astype(jnp.float32)
+
+
+def body(mesh, grid_state, mesh1_state, mesh2_state, grid_edges, up_edges, weights, cotangent):
     features = weights.shape[1]
     lat_pos = lax.axis_index("lat")
     col_pos = lax.axis_index(("lon", "rep"))
@@ -213,7 +273,7 @@
         jnp.bfloat16
     )
     stacked = jnp.stack([grad0, grad1, grad2] + list(coarse_grads))
-    summed = lax.psum(stacked, ("lon", "lat", "rep"))
+    summed = sum_over_slice(stacked, mesh)
     weight_grads = summed * float(node_total) ** (-0.5)
     return (mesh_out, mesh1_grad.reshape(fine_rows, fine_cols, features), weight_grads)
 
@@ -233,4 +293,4 @@
         P(("groups", "lat"), ("lon", "rep"), None),
         P("groups", None, None),
     )
-    return jax.shard_map(body, mesh=mesh, in_specs=in_specs, out_specs=out_specs, check_vma=False)
+    return jax.shard_map(functools.partial(body, mesh), mesh=mesh, in_specs=in_specs, out_specs=out_specs, check_vma=False)

time: 248 us -> 156 us (0.63)
  waiting for transfers between devices: 102 us -> 27.3 us
  matrix products: 36.2 us -> 20.5 us
  between operations: 14.6 us -> 1.59 us
  starting transfers between devices: 18.5 us -> 27.6 us
  local copies, waits for them, and re-layouts: 38.3 us -> 42.3 us
    psum x1 -> x0, waiting for transfers between devices: 95.2 us -> none  [body(): summed = lax.psum(stacked, ('lon', 'lat', 'rep'))]
    ppermute x0 -> x12, waiting for transfers between devices: none -> 21.3 us  [swap_over(): return lax.ppermute(values, axes, [(i, partner(i)) for i in range(total)])]
    dot_general x20, matrix products: 29.1 us -> 16.8 us  [matmul(): return jnp.dot(left, right, preferred_element_type=jnp.float32)]
    ppermute x0 -> x12, starting transfers between devices: none -> 9.18 us  [swap_over(): return lax.ppermute(values, axes, [(i, partner(i)) for i in range(total)])]
    another operation x1 -> x3, local copies, waits for them, and re-layouts: 0.59 us -> 5.11 us
    ppermute x6, starting transfers between devices: 7.01 us -> 3.38 us  [with_halo(): lax.ppermute(tail, axis, [(i, (i + 1) % count) for i in range(count)])]
    ppermute x6, starting transfers between devices: 11.4 us -> 15 us  [with_halo(): lax.ppermute(head, axis, [((i + 1) % count, i) for i in range(count)])]
    dot_general x5, matrix products: 7.12 us -> 3.65 us  [matmul_high(): jnp.dot(left, right, precision=lax.Precision.HIGHEST, preferred_element_t...]
  transfers between devices with their start and end apart: 13 -> 24, of which waited for: 6 -> 11; matrix products, arithmetic and copies ran while one was open for 6% -> 15% of each run, Pallas kernels for 0% -> 0%
where the time goes in v1:
time: 156 us; the launch traced here: 155 us
  local copies, waits for them, and re-layouts  42.3 us (27%)
  other arithmetic  31.9 us (20%)
  starting transfers between devices  27.6 us (18%)
  waiting for transfers between devices  27.3 us (18%)
  matrix products  20.5 us (13%)
  blocking collectives  4.1 us (3%)
  between operations  1.59 us (1%)
    ppermute x12, waiting for transfers between devices, swap_over(): return lax.ppermute(values, axes, [(i, partner(i)) for i in range(total)])  21.3 us
    gather x1, local copies, waits for them, and re-layouts, body(): enc_senders = jnp.take(grid_ext.reshape(-1, features), enc_index, axis=0)  17 us
    dot_general x20, matrix products, matmul(): return jnp.dot(left, right, preferred_element_type=jnp.float32)  16.8 us
    ppermute x6, starting transfers between devices, with_halo(): lax.ppermute(head, axis, [((i + 1) % count, i) for i in range(count)])  15 us
    ppermute x12, starting transfers between devices, swap_over(): return lax.ppermute(values, axes, [(i, partner(i)) for i in range(total)])  9.18 us
    scatter-add x1, other arithmetic, coarse_pass(): ext_grad = jnp.zeros(((rows_in + 2) * (cols_in + 2), features), jnp.float...  6.29 us
    another operation x3, local copies, waits for them, and re-layouts  5.11 us
    select_n x2, other arithmetic, body(): enc_senders = jnp.take(grid_ext.reshape(-1, features), enc_index, axis=0)  4.93 us
  transfers between devices with their start and end apart: 24, of which 11 were waited for; matrix products, arithmetic and copies ran while one was open for 15% of the time, Pallas kernels for 0%

profile of v1, /device:TPU:0, one launch (start us, length us, event | category | flops | bytes accessed | tf_op | source)
XLA Modules:
  0.0 155.2 jit_solution(10981412331175091611)
XLA Ops:
  1.5 2.9 %collective-permute-start.1 = (bf16[2,32,256]{2,1,0:T(8,128)(2,1)S(1)}, bf16[2,32,256]{2,1,0:T(8,128)(2,1)S(1)}, u32[]{:S(2)}, u32[]{:S(2)}) collective-permute-start(bf16[2,32,256]{2,1,0:T(8,128)(2,1)S(1)} %get-tuple-element.115), channel_id=1, source_target_pairs={{2,0},{0,2},{3,1},{1,3},{6,4},{4,6},{7,5},{5,7},{10,8},{8,10},{11,... | collective-permute-start | bytes 98312 | tf_op jit(solution)/shard_map/ppermute | solution.py:18
  14.1 3.5 %collective-permute-start.3 = (bf16[36,2,256]{2,1,0:T(2,128)(2,1)S(1)}, bf16[36,2,256]{2,1,0:T(2,128)(2,1)S(1)}, u32[]{:S(2)}, u32[]{:S(2)}) collective-permute-start(bf16[36,2,256]{2,1,0:T(2,128)(2,1)S(1)} %get-tuple-element.114), channel_id=1, source_target_pairs={{1,0},{4,1},{5,4},{8,5},{9,8},{12,9},{13,12},{0,13},{3,2},{6,3},{7... | collective-permute-start | bytes 110600 | tf_op jit(solution)/shard_map/ppermute | solution.py:18
  19.8 17.0 %gather_fusion = bf16[4096,256]{1,0:T(8,128)(2,1)} fusion(bf16[1296,256]{1,0:T(8,128)(2,1)S(1)} %reshape.528, s32[4096]{0:T(1024)S(1)} %broadcast_clamp_fusion), kind=kCustom, calls=%fused_computation.2 | custom fusion | bytes 4210688 | tf_op jit(solution)/shard_map/jit(_take)/gather | solution.py:217
  36.8 4.9 %select_bitcast_fusion = (bf16[256,4096]{0,1:T(8,128)(2,1)S(1)}, bf16[4096,256]{1,0:T(8,128)(2,1)S(1)}) fusion(bf16[4096,256]{1,0:T(8,128)(2,1)} %gather_fusion, pred[4096]{0:T(1024)(128)(4,1)S(1)} %compare_and_fusion, pred[4096]{0:T(1024)(128)(4,1)S(1)} %broadcast_in_dim.51), kind=kLoop, calls=%fused_computation.10 | loop fusion | flops 2097152 | bytes 6299648 | tf_op jit(solution)/shard_map/jit(_take)/select_n | solution.py:217
  41.8 3.3 %multiply_reduce_fusion = (f32[256,256]{1,0:T(8,128)S(1)}, f32[16,256,256]{2,1,0:T(8,128)}) fusion(f32[256,256]{1,0:T(8,128)S(1)} %copy-done.5, bf16[16,256,256]{2,1,0:T(8,128)(2,1)S(1)} %bitcast.182, bf16[9,256,256]{2,1,0:T(8,128)(2,1)S(1)} %copy-done.1), kind=kOutput, calls=%fused_computation.7 | convolution fusion | flops 543096832 | bytes 6946816 | tf_op jit(solution)/shard_map/dot_general | solution.py:26
  45.8 2.0 %all_gather.6 = bf16[16,32,256]{2,1,0:T(8,128)(2,1)S(1)} all-gather(bf16[16,16,256]{2,1,0:T(8,128)(2,1)S(1)} %bitcast.206), channel_id=1, replica_groups=mesh['groups'=2,'lon'=4,'lat'=2,'rep'=2] {'rep'}, dimensions={1}, use_global_device_ids=true | all-gather | bytes 393216 | tf_op jit(solution)/shard_map/all_gather | solution.py:225
  48.4 2.0 %collective-permute-start.4 = (bf16[1,32,256]{2,1,0:T(8,128)(2,1)}, bf16[1,32,256]{2,1,0:T(8,128)(2,1)S(1)}, u32[]{:S(2)}, u32[]{:S(2)}) collective-permute-start(bf16[1,32,256]{2,1,0:T(8,128)(2,1)} %get-tuple-element.124), channel_id=1, source_target_pairs={{0,2},{2,0},{1,3},{3,1},{4,6},{6,4},{5,7},{7,5},{8,10},{10,8},{9,1... | collective-permute-start | bytes 49160 | tf_op jit(solution)/shard_map/ppermute | solution.py:16
  50.4 2.1 %all_gather.7 = bf16[16,32,256]{2,1,0:T(8,128)(2,1)} all-gather(bf16[16,16,256]{2,1,0:T(8,128)(2,1)S(1)} %copy-done.27), channel_id=1, replica_groups=mesh['groups'=2,'lon'=4,'lat'=2,'rep'=2] {'rep'}, dimensions={1}, use_global_device_ids=true | all-gather | bytes 393216 | tf_op jit(solution)/shard_map/all_gather | solution.py:226
  52.6 3.9 %collective-permute-done.5 = bf16[1,32,256]{2,1,0:T(8,128)(2,1)S(1)} collective-permute-done((bf16[1,32,256]{2,1,0:T(8,128)(2,1)}, bf16[1,32,256]{2,1,0:T(8,128)(2,1)S(1)}, u32[]{:S(2)}, u32[]{:S(2)}) %collective-permute-start.5) | collective-permute-done | bytes 16416 | tf_op jit(solution)/shard_map/ppermute | solution.py:18
  59.0 2.7 %collective-permute-start.7 = (bf16[18,1,256]{2,1,0:T(2,128)(2,1)}, bf16[18,1,256]{2,1,0:T(2,128)(2,1)}, u32[]{:S(2)}, u32[]{:S(2)}) collective-permute-start(bf16[18,1,256]{2,1,0:T(2,128)(2,1)} %get-tuple-element.122), channel_id=1, source_target_pairs={{4,0},{8,4},{12,8},{0,12},{5,1},{9,5},{13,9},{1,13},{6,2},{10,6},{... | collective-permute-start | bytes 27656 | tf_op jit(solution)/shard_map/ppermute | solution.py:18
  63.3 2.8 %copy.18 = bf16[256,4096]{1,0:T(8,128)(2,1)} copy(bf16[256,4096]{0,1:T(8,128)(2,1)S(1)} %get-tuple-element.106) | data formatting | bytes 4194304 | tf_op jit(solution)/shard_map/reshape.381
  69.1 3.9 %gather_fusion.1 = bf16[1024,256]{1,0:T(8,128)(2,1)S(1)} fusion(bf16[612,256]{1,0:T(8,128)(2,1)S(1)} %reshape.534, s32[1024]{0:T(1024)S(1)} %copy-done.30), kind=kCustom, calls=%fused_computation.3 | custom fusion | bytes 1052672 | tf_op jit(solution)/shard_map/jit(_take)/gather | solution.py:93
  81.1 2.3 %convert_reduce_fusion.1 = (f32[128,256]{1,0:T(8,128)}, bf16[8,128,256]{2,1,0:T(8,128)(2,1)S(1)}) fusion(f32[8,128,256]{2,1,0:T(8,128)} %get-tuple-element.130, f32[128,256]{1,0:T(8,128)S(1)} %convolution_multiply_fusion.8), kind=kLoop, calls=%fused_computation.42 | loop fusion | flops 2850816 | bytes 1835008 | tf_op jit(solution)/shard_map/reduce_sum | solution.py:125
  84.9 6.3 %scatter_custom_fusion = f32[612,256]{1,0:T(8,128)S(1)} fusion(s32[1024]{0:T(1024)} %bitcast.222, f32[1024,256]{1,0:T(8,128)S(1)} %fusion.40, f32[]{:T(128)} %constant.391.clone.1), kind=kCustom, calls=%fused_computation.60 | custom fusion | flops 262144 | bytes 627200 | tf_op jit(solution)/shard_map/scatter-add | solution.py:131
  91.5 2.0 %collective-permute-start.9 = (bf16[1,34,256]{2,1,0:T(8,128)(2,1)S(1)}, bf16[1,34,256]{2,1,0:T(8,128)(2,1)S(1)}, u32[]{:S(2)}, u32[]{:S(2)}) collective-permute-start(bf16[1,34,256]{2,1,0:T(8,128)(2,1)S(1)} %get-tuple-element.120), channel_id=1, source_target_pairs={{2,0},{0,2},{3,1},{1,3},{6,4},{4,6},{7,5},{5,7},{10,8},{8,10},{11,... | collective-permute-start | bytes 52232 | tf_op jit(solution)/shard_map/ppermute | solution.py:18
  95.6 3.8 %collective-permute-start.11 = (bf16[20,1,256]{2,1,0:T(2,128)(2,1)S(1)}, bf16[20,1,256]{2,1,0:T(2,128)(2,1)S(1)}, u32[]{:S(2)}, u32[]{:S(2)}) collective-permute-start(bf16[20,1,256]{2,1,0:T(2,128)(2,1)S(1)} %get-tuple-element.118), channel_id=1, source_target_pairs={{4,0},{8,4},{12,8},{0,12},{5,1},{9,5},{13,9},{1,13},{6,2},{10,6},{... | collective-permute-start | bytes 30728 | tf_op jit(solution)/shard_map/ppermute | solution.py:18
  106.9 4.0 %convert_reduce_fusion = (f32[256,256]{1,0:T(8,128)S(1)}, bf16[16,256,256]{2,1,0:T(8,128)(2,1)S(1)}) fusion(f32[16,256,256]{2,1,0:T(8,128)} %get-tuple-element.128, f32[256,256]{1,0:T(8,128)S(1)} %copy-done.6, f32[256,256]{1,0:T(8,128)S(1)} %convolution_multiply_fusion.6), kind=kLoop, calls=%fused_computation.5 | loop fusion | flops 12517376 | bytes 7077888 | tf_op jit(solution)/shard_map/reduce_sum | solution.py:270
  114.9 2.1 %collective-permute-done.12 = bf16[9,128,256]{2,1,0:T(8,128)(2,1)} collective-permute-done((bf16[9,128,256]{2,1,0:T(8,128)(2,1)S(1)}, bf16[9,128,256]{2,1,0:T(8,128)(2,1)}, u32[]{:S(2)}, u32[]{:S(2)}) %collective-permute-start.12) | collective-permute-done | bytes 589856 | tf_op jit(solution)/shard_map/ppermute | solution.py:146
  119.4 3.3 %collective-permute-start.15 = (bf16[9,32,256]{2,1,0:T(8,128)(2,1)}, bf16[9,32,256]{2,1,0:T(8,128)(2,1)S(1)}, u32[]{:S(2)}, u32[]{:S(2)}) collective-permute-start(bf16[9,32,256]{2,1,0:T(8,128)(2,1)} %get-tuple-element.111), channel_id=1, source_target_pairs={{0,6},{2,4},{4,2},{6,0},{8,14},{10,12},{12,10},{14,8},{1,7},{3,5},... | collective-permute-start | bytes 442376 | tf_op jit(solution)/shard_map/ppermute | solution.py:146
  122.9 3.4 %collective-permute-done.13 = bf16[9,32,256]{2,1,0:T(8,128)(2,1)S(1)} collective-permute-done((bf16[9,32,256]{2,1,0:T(8,128)(2,1)}, bf16[9,32,256]{2,1,0:T(8,128)(2,1)S(1)}, u32[]{:S(2)}, u32[]{:S(2)}) %collective-permute-start.13) | collective-permute-done | bytes 147488 | tf_op jit(solution)/shard_map/ppermute | solution.py:146
  126.3 3.7 %collective-permute-done.15 = bf16[9,32,256]{2,1,0:T(8,128)(2,1)S(1)} collective-permute-done((bf16[9,32,256]{2,1,0:T(8,128)(2,1)}, bf16[9,32,256]{2,1,0:T(8,128)(2,1)S(1)}, u32[]{:S(2)}, u32[]{:S(2)}) %collective-permute-start.15) | collective-permute-done | bytes 147488 | tf_op jit(solution)/shard_map/ppermute | solution.py:146
  134.0 7.2 %collective-permute-done.16 = bf16[9,32,256]{2,1,0:T(8,128)(2,1)S(1)} collective-permute-done((bf16[9,32,256]{2,1,0:T(8,128)(2,1)S(1)}, bf16[9,32,256]{2,1,0:T(8,128)(2,1)S(1)}, u32[]{:S(2)}, u32[]{:S(2)}) %collective-permute-start.16) | collective-permute-done | bytes 147488 | tf_op jit(solution)/shard_map/ppermute | solution.py:146
  142.5 2.4 %collective-permute-start.17 = (bf16[9,32,256]{2,1,0:T(8,128)(2,1)S(1)}, bf16[9,32,256]{2,1,0:T(8,128)(2,1)S(1)}, u32[]{:S(2)}, u32[]{:S(2)}) collective-permute-start(bf16[9,32,256]{2,1,0:T(8,128)(2,1)S(1)} %add_convert_fusion), channel_id=1, source_target_pairs={{0,4},{2,6},{4,0},{6,2},{8,12},{10,14},{12,8},{14,10},{1,5},{3,7},... | collective-permute-start | bytes 442376 | tf_op jit(solution)/shard_map/ppermute | solution.py:146
  146.8 2.1 %collective-permute-done.19 = bf16[9,32,256]{2,1,0:T(8,128)(2,1)S(1)} collective-permute-done((bf16[9,32,256]{2,1,0:T(8,128)(2,1)S(1)}, bf16[9,32,256]{2,1,0:T(8,128)(2,1)S(1)}, u32[]{:S(2)}, u32[]{:S(2)}) %collective-permute-start.19) | collective-permute-done | bytes 147488 | tf_op jit(solution)/shard_map/ppermute | solution.py:146
  (210 shorter events, 59.8 us)
Async XLA Ops:
  1.5 12.4 %collective-permute-start.1 = (bf16[2,32,256]{2,1,0:T(8,128)(2,1)S(1)}, bf16[2,32,256]{2,1,0:T(8,128)(2,1)S(1)}, u32[]{:S(2)}, u32[]{:S(2)}) collective-permute-start(bf16[2,32,256]{2,1,0:T(8,128)(2,1)S(1)} %get-tuple-element.115), channel_id=1, source_target_pairs={{2,0},{0,2},{3,1},{1,3},{6,4},{4,6},{7,5},{5,7},{10,8},{8,10},{11,... | collective-permute-start | bytes 98312 | tf_op jit(solution)/shard_map/ppermute | solution.py:18
  4.4 9.4 %collective-permute-start = (bf16[2,32,256]{2,1,0:T(8,128)(2,1)S(1)}, bf16[2,32,256]{2,1,0:T(8,128)(2,1)S(1)}, u32[]{:S(2)}, u32[]{:S(2)}) collective-permute-start(bf16[2,32,256]{2,1,0:T(8,128)(2,1)S(1)} %get-tuple-element.116), channel_id=1, source_target_pairs={{0,2},{2,0},{1,3},{3,1},{4,6},{6,4},{5,7},{7,5},{8,10},{10,8},{9,1... | collective-permute-start | bytes 98312 | tf_op jit(solution)/shard_map/ppermute | solution.py:16
  14.0 5.2 %collective-permute-start.2 = (bf16[36,2,256]{2,1,0:T(2,128)(2,1)S(1)}, bf16[36,2,256]{2,1,0:T(2,128)(2,1)S(1)}, u32[]{:S(2)}, u32[]{:S(2)}) collective-permute-start(bf16[36,2,256]{2,1,0:T(2,128)(2,1)S(1)} %get-tuple-element.113), channel_id=1, source_target_pairs={{0,1},{1,4},{4,5},{5,8},{8,9},{9,12},{12,13},{13,0},{2,3},{3,6},{6... | collective-permute-start | bytes 110600 | tf_op jit(solution)/shard_map/ppermute | solution.py:16
  14.1 5.2 %collective-permute-start.3 = (bf16[36,2,256]{2,1,0:T(2,128)(2,1)S(1)}, bf16[36,2,256]{2,1,0:T(2,128)(2,1)S(1)}, u32[]{:S(2)}, u32[]{:S(2)}) collective-permute-start(bf16[36,2,256]{2,1,0:T(2,128)(2,1)S(1)} %get-tuple-element.114), channel_id=1, source_target_pairs={{1,0},{4,1},{5,4},{8,5},{9,8},{12,9},{13,12},{0,13},{3,2},{6,3},{7... | collective-permute-start | bytes 110600 | tf_op jit(solution)/shard_map/ppermute | solution.py:18
  48.4 4.2 %collective-permute-start.4 = (bf16[1,32,256]{2,1,0:T(8,128)(2,1)}, bf16[1,32,256]{2,1,0:T(8,128)(2,1)S(1)}, u32[]{:S(2)}, u32[]{:S(2)}) collective-permute-start(bf16[1,32,256]{2,1,0:T(8,128)(2,1)} %get-tuple-element.124), channel_id=1, source_target_pairs={{0,2},{2,0},{1,3},{3,1},{4,6},{6,4},{5,7},{7,5},{8,10},{10,8},{9,1... | collective-permute-start | bytes 49160 | tf_op jit(solution)/shard_map/ppermute | solution.py:16
  52.5 4.0 %collective-permute-start.5 = (bf16[1,32,256]{2,1,0:T(8,128)(2,1)}, bf16[1,32,256]{2,1,0:T(8,128)(2,1)S(1)}, u32[]{:S(2)}, u32[]{:S(2)}) collective-permute-start(bf16[1,32,256]{2,1,0:T(8,128)(2,1)} %get-tuple-element.123), channel_id=1, source_target_pairs={{2,0},{0,2},{3,1},{1,3},{6,4},{4,6},{7,5},{5,7},{10,8},{8,10},{11,... | collective-permute-start | bytes 49160 | tf_op jit(solution)/shard_map/ppermute | solution.py:18
  57.9 10.0 %collective-permute-start.6 = (bf16[18,1,256]{2,1,0:T(2,128)(2,1)}, bf16[18,1,256]{2,1,0:T(2,128)(2,1)}, u32[]{:S(2)}, u32[]{:S(2)}) collective-permute-start(bf16[18,1,256]{2,1,0:T(2,128)(2,1)} %get-tuple-element.121), channel_id=1, source_target_pairs={{0,4},{4,8},{8,12},{12,0},{1,5},{5,9},{9,13},{13,1},{2,6},{6,10},{... | collective-permute-start | bytes 27656 | tf_op jit(solution)/shard_map/ppermute | solution.py:16
  59.0 8.9 %collective-permute-start.7 = (bf16[18,1,256]{2,1,0:T(2,128)(2,1)}, bf16[18,1,256]{2,1,0:T(2,128)(2,1)}, u32[]{:S(2)}, u32[]{:S(2)}) collective-permute-start(bf16[18,1,256]{2,1,0:T(2,128)(2,1)} %get-tuple-element.122), channel_id=1, source_target_pairs={{4,0},{8,4},{12,8},{0,12},{5,1},{9,5},{13,9},{1,13},{6,2},{10,6},{... | collective-permute-start | bytes 27656 | tf_op jit(solution)/shard_map/ppermute | solution.py:18
  91.4 3.8 %collective-permute-start.8 = (bf16[1,34,256]{2,1,0:T(8,128)(2,1)S(1)}, bf16[1,34,256]{2,1,0:T(8,128)(2,1)S(1)}, u32[]{:S(2)}, u32[]{:S(2)}) collective-permute-start(bf16[1,34,256]{2,1,0:T(8,128)(2,1)S(1)} %get-tuple-element.119), channel_id=1, source_target_pairs={{0,2},{2,0},{1,3},{3,1},{4,6},{6,4},{5,7},{7,5},{8,10},{10,8},{9,1... | collective-permute-start | bytes 52232 | tf_op jit(solution)/shard_map/ppermute | solution.py:16
  91.5 3.9 %collective-permute-start.9 = (bf16[1,34,256]{2,1,0:T(8,128)(2,1)S(1)}, bf16[1,34,256]{2,1,0:T(8,128)(2,1)S(1)}, u32[]{:S(2)}, u32[]{:S(2)}) collective-permute-start(bf16[1,34,256]{2,1,0:T(8,128)(2,1)S(1)} %get-tuple-element.120), channel_id=1, source_target_pairs={{2,0},{0,2},{3,1},{1,3},{6,4},{4,6},{7,5},{5,7},{10,8},{8,10},{11,... | collective-permute-start | bytes 52232 | tf_op jit(solution)/shard_map/ppermute | solution.py:18
  95.5 6.8 %collective-permute-start.10 = (bf16[20,1,256]{2,1,0:T(2,128)(2,1)S(1)}, bf16[20,1,256]{2,1,0:T(2,128)(2,1)S(1)}, u32[]{:S(2)}, u32[]{:S(2)}) collective-permute-start(bf16[20,1,256]{2,1,0:T(2,128)(2,1)S(1)} %get-tuple-element.117), channel_id=1, source_target_pairs={{0,4},{4,8},{8,12},{12,0},{1,5},{5,9},{9,13},{13,1},{2,6},{6,10},{... | collective-permute-start | bytes 30728 | tf_op jit(solution)/shard_map/ppermute | solution.py:16
  95.6 6.7 %collective-permute-start.11 = (bf16[20,1,256]{2,1,0:T(2,128)(2,1)S(1)}, bf16[20,1,256]{2,1,0:T(2,128)(2,1)S(1)}, u32[]{:S(2)}, u32[]{:S(2)}) collective-permute-start(bf16[20,1,256]{2,1,0:T(2,128)(2,1)S(1)} %get-tuple-element.118), channel_id=1, source_target_pairs={{4,0},{8,4},{12,8},{0,12},{5,1},{9,5},{13,9},{1,13},{6,2},{10,6},{... | collective-permute-start | bytes 30728 | tf_op jit(solution)/shard_map/ppermute | solution.py:18
  114.8 2.2 %collective-permute-start.12 = (bf16[9,128,256]{2,1,0:T(8,128)(2,1)S(1)}, bf16[9,128,256]{2,1,0:T(8,128)(2,1)}, u32[]{:S(2)}, u32[]{:S(2)}) collective-permute-start(bf16[9,128,256]{2,1,0:T(8,128)(2,1)S(1)} %fusion.9), channel_id=1, source_target_pairs={{0,1},{1,0},{2,3},{3,2},{4,5},{5,4},{6,7},{7,6},{8,9},{9,8},{10,11... | collective-permute-start | bytes 1769480 | tf_op jit(solution)/shard_map/ppermute | solution.py:146
  119.4 6.9 %collective-permute-start.13 = (bf16[9,32,256]{2,1,0:T(8,128)(2,1)}, bf16[9,32,256]{2,1,0:T(8,128)(2,1)S(1)}, u32[]{:S(2)}, u32[]{:S(2)}) collective-permute-start(bf16[9,32,256]{2,1,0:T(8,128)(2,1)} %get-tuple-element.110), channel_id=1, source_target_pairs={{0,4},{2,6},{4,0},{6,2},{8,12},{10,14},{12,8},{14,10},{1,5},{3,7},... | collective-permute-start | bytes 442376 | tf_op jit(solution)/shard_map/ppermute | solution.py:146
  119.4 10.6 %collective-permute-start.15 = (bf16[9,32,256]{2,1,0:T(8,128)(2,1)}, bf16[9,32,256]{2,1,0:T(8,128)(2,1)S(1)}, u32[]{:S(2)}, u32[]{:S(2)}) collective-permute-start(bf16[9,32,256]{2,1,0:T(8,128)(2,1)} %get-tuple-element.111), channel_id=1, source_target_pairs={{0,6},{2,4},{4,2},{6,0},{8,14},{10,12},{12,10},{14,8},{1,7},{3,5},... | collective-permute-start | bytes 442376 | tf_op jit(solution)/shard_map/ppermute | solution.py:146
  122.6 8.8 %collective-permute-start.14 = (bf16[9,32,256]{2,1,0:T(8,128)(2,1)}, bf16[9,32,256]{2,1,0:T(8,128)(2,1)}, u32[]{:S(2)}, u32[]{:S(2)}) collective-permute-start(bf16[9,32,256]{2,1,0:T(8,128)(2,1)} %get-tuple-element.112), channel_id=1, source_target_pairs={{0,2},{2,0},{4,6},{6,4},{8,10},{10,8},{12,14},{14,12},{1,3},{3,1},... | collective-permute-start | bytes 442376 | tf_op jit(solution)/shard_map/ppermute | solution.py:146
  132.5 8.8 %collective-permute-start.16 = (bf16[9,32,256]{2,1,0:T(8,128)(2,1)S(1)}, bf16[9,32,256]{2,1,0:T(8,128)(2,1)S(1)}, u32[]{:S(2)}, u32[]{:S(2)}) collective-permute-start(bf16[9,32,256]{2,1,0:T(8,128)(2,1)S(1)} %fusion.16), channel_id=1, source_target_pairs={{0,8},{2,10},{4,12},{6,14},{8,0},{10,2},{12,4},{14,6},{1,9},{3,11}... | collective-permute-start | bytes 442376 | tf_op jit(solution)/shard_map/ppermute | solution.py:146
  141.3 7.7 %collective-permute-start.19 = (bf16[9,32,256]{2,1,0:T(8,128)(2,1)S(1)}, bf16[9,32,256]{2,1,0:T(8,128)(2,1)S(1)}, u32[]{:S(2)}, u32[]{:S(2)}) collective-permute-start(bf16[9,32,256]{2,1,0:T(8,128)(2,1)S(1)} %add_convert_fusion), channel_id=1, source_target_pairs={{0,6},{2,4},{4,2},{6,0},{8,14},{10,12},{12,10},{14,8},{1,7},{3,5},... | collective-permute-start | bytes 442376 | tf_op jit(solution)/shard_map/ppermute | solution.py:146
  141.4 8.9 %collective-permute-start.18 = (bf16[9,32,256]{2,1,0:T(8,128)(2,1)S(1)}, bf16[9,32,256]{2,1,0:T(8,128)(2,1)S(1)}, u32[]{:S(2)}, u32[]{:S(2)}) collective-permute-start(bf16[9,32,256]{2,1,0:T(8,128)(2,1)S(1)} %add_convert_fusion), channel_id=1, source_target_pairs={{0,2},{2,0},{4,6},{6,4},{8,10},{10,8},{12,14},{14,12},{1,3},{3,1},... | collective-permute-start | bytes 442376 | tf_op jit(solution)/shard_map/ppermute | solution.py:146
  142.5 7.8 %collective-permute-start.17 = (bf16[9,32,256]{2,1,0:T(8,128)(2,1)S(1)}, bf16[9,32,256]{2,1,0:T(8,128)(2,1)S(1)}, u32[]{:S(2)}, u32[]{:S(2)}) collective-permute-start(bf16[9,32,256]{2,1,0:T(8,128)(2,1)S(1)} %add_convert_fusion), channel_id=1, source_target_pairs={{0,4},{2,6},{4,0},{6,2},{8,12},{10,14},{12,8},{14,10},{1,5},{3,7},... | collective-permute-start | bytes 442376 | tf_op jit(solution)/shard_map/ppermute | solution.py:146
  146.8 5.6 %collective-permute-start.20 = (bf16[9,32,256]{2,1,0:T(8,128)(2,1)S(1)}, bf16[9,32,256]{2,1,0:T(8,128)(2,1)S(1)}, u32[]{:S(2)}, u32[]{:S(2)}) collective-permute-start(bf16[9,32,256]{2,1,0:T(8,128)(2,1)S(1)} %add_convert_fusion), channel_id=1, source_target_pairs={{0,1},{1,0},{2,3},{3,2},{4,5},{5,4},{6,7},{7,6},{8,9},{9,8},{10,11... | collective-permute-start | bytes 442376 | tf_op jit(solution)/shard_map/ppermute | solution.py:146
  149.0 3.4 %collective-permute-start.23 = (bf16[9,32,256]{2,1,0:T(8,128)(2,1)S(1)}, bf16[9,32,256]{2,1,0:T(8,128)(2,1)S(1)}, u32[]{:S(2)}, u32[]{:S(2)}) collective-permute-start(bf16[9,32,256]{2,1,0:T(8,128)(2,1)S(1)} %collective-permute-done.19), channel_id=1, source_target_pairs={{0,1},{1,0},{2,3},{3,2},{4,5},{5,4},{6,7},{7,6},{8,9},{9,8},{10,11... | collective-permute-start | bytes 442376 | tf_op jit(solution)/shard_map/ppermute | solution.py:146
  150.2 2.2 %collective-permute-start.22 = (bf16[9,32,256]{2,1,0:T(8,128)(2,1)S(1)}, bf16[9,32,256]{2,1,0:T(8,128)(2,1)S(1)}, u32[]{:S(2)}, u32[]{:S(2)}) collective-permute-start(bf16[9,32,256]{2,1,0:T(8,128)(2,1)S(1)} %collective-permute-done.18), channel_id=1, source_target_pairs={{0,1},{1,0},{2,3},{3,2},{4,5},{5,4},{6,7},{7,6},{8,9},{9,8},{10,11... | collective-permute-start | bytes 442376 | tf_op jit(solution)/shard_map/ppermute | solution.py:146
  150.2 2.2 %collective-permute-start.21 = (bf16[9,32,256]{2,1,0:T(8,128)(2,1)S(1)}, bf16[9,32,256]{2,1,0:T(8,128)(2,1)S(1)}, u32[]{:S(2)}, u32[]{:S(2)}) collective-permute-start(bf16[9,32,256]{2,1,0:T(8,128)(2,1)S(1)} %collective-permute-done.17), channel_id=1, source_target_pairs={{0,1},{1,0},{2,3},{3,2},{4,5},{5,4},{6,7},{7,6},{8,9},{9,8},{10,11... | collective-permute-start | bytes 442376 | tf_op jit(solution)/shard_map/ppermute | solution.py:146
  (33 other events, 119.7 us)

commit v2 on v1

v2 whole, which is shorter than its diff:
```python
import functools

import jax
import jax.numpy as jnp
from jax import lax
from jax.experimental import pallas as pl
from jax.experimental.pallas import tpu as pltpu
from jax.sharding import PartitionSpec as P

LOW = jnp.bfloat16
WIDE = jnp.float32
VMEM_BYTES = 48 * 1024 * 1024

SIDE_ROWS = 496
BAND_ROWS = 416
CORNER_ROWS = 160


def permute(values, axes, partner, sizes):
    total = 1
    for size in sizes:
        total *= size
    pairs = [(i, partner(i)) for i in range(total)]
    return lax.ppermute(values, axes, [(i, j) for i, j in pairs if j is not None])


def mm(left, right):
    return jnp.dot(left, right, preferred_element_type=WIDE)


def mm_nt(left, right):
    return lax.dot_general(left, right, (((1,), (1,)), ((), ())), preferred_element_type=WIDE)


def mm_tn(left, right):
    return lax.dot_general(left, right, (((0,), (0,)), ((), ())), preferred_element_type=WIDE)


def two_parts(value):
    high = value.astype(LOW)
    return high, (value - high.astype(WIDE)).astype(LOW)


def sigmoid_of(value):
    return 0.5 * jnp.tanh(0.5 * value) + 0.5


def iota(shape, dim):
    return lax.broadcasted_iota(jnp.int32, shape, dim)


def edge_codes(grid_edges, up_half, glon, m1lon, lat, col):
    keep, rows, cols = grid_edges.shape
    row = lax.broadcasted_iota(jnp.int32, grid_edges.shape, 1)
    j = lax.broadcasted_iota(jnp.int32, grid_edges.shape, 2)
    down = grid_edges // glon - (2 * (lat * rows + row) - 2)
    across = jnp.mod(grid_edges % glon - (2 * (col * cols + j) - 2), glon)
    place = 2 * (j % 8) + 6 + across
    own = down * 16 + place + jnp.where(place >= 16, 112, 0)
    sent = down * 16 + across + 6 + jnp.where(j >= 8, 2 * (j - 16), 128 + 2 * j)
    both = jnp.stack([own, sent], 0).astype(WIDE)
    both = jnp.transpose(both, (0, 2, 1, 3)).reshape(2 * rows, keep * cols)
    up_rows, up_cols = up_half.shape[1:]
    a = lax.broadcasted_iota(jnp.int32, up_half.shape, 1)
    b = lax.broadcasted_iota(jnp.int32, up_half.shape, 2)
    down = up_half // m1lon - (2 * (lat * up_rows + a) - 1)
    across = jnp.mod(up_half % m1lon - (2 * (col * up_cols + b) - 1), m1lon)

    def code(base):
        at = 2 * base - 1 + across
        at = jnp.where(at < 0, at + 20, jnp.where(at >= 16, at + 4, at))
        return down * 32 + at

    up = jnp.concatenate([code(b), code(jnp.where(b >= 4, b - 8, b + 8))], 2).astype(WIDE)
    up = jnp.transpose(up, (1, 0, 2)).reshape(up_rows, -1)
    up = jnp.pad(up, ((0, 16 - up_rows), (0, both.shape[1] - up.shape[1])))
    return jnp.concatenate([both, up], 0).astype(LOW)


def pack_kernel(dirs, grid, m1, cot, m2, codes, *outs):
    rep = lax.axis_index("rep")
    lat = lax.axis_index("lat")
    sides = outs[:2]
    bands = outs[2:]
    half = pl.multiple_of(rep * 8, 8)

    def column(right):
        g = grid[:, 16:32, :] if right else grid[:, 0:16, :]
        g = g.astype(WIDE)[:, 8:16] if right else g.astype(WIDE)[:, 0:8]
        s = slice(8, 16) if right else slice(0, 8)
        mm1 = m1[...].astype(WIDE)[:, s]
        cc = cot[...].astype(WIDE)[:, s]
        if right:
            pair = jnp.concatenate([mm1[:, 4:8], cc[:, 4:8]], axis=1)
        else:
            pair = jnp.concatenate([mm1[:, 0:4], cc[:, 0:4]], axis=1)
        return g, pair

    m2w = m2[...].astype(WIDE)
    m2_half = jnp.where(rep == 0, m2w[:, 0:8], m2w[:, 8:16])

    def fill(targets, right):
        side, corners = targets
        g, pair = column(right)
        side[0:256, :] = g.reshape(256, 256).astype(LOW)
        side[256:384, :] = pair.reshape(128, 256).astype(LOW)
        side[384:448, :] = m2_half.reshape(64, 256).astype(LOW)
        side[448:496, :] = codes[...]
        for sends_bottom, corner in corners:
            if sends_bottom is None:
                low = lat == 0
                gg = jnp.where(low, g[24:32], g[0:8])
                pp = jnp.where(low, pair[12:16], pair[0:4])
                mt = jnp.where(low, m2_half[7], m2_half[0])
            elif sends_bottom:
                gg, pp, mt = g[24:32], pair[12:16], m2_half[7]
            else:
                gg, pp, mt = g[0:8], pair[0:4], m2_half[0]
            corner[0:64, :] = gg.reshape(64, 256).astype(LOW)
            corner[64:96, :] = pp.reshape(32, 256).astype(LOW)
            corner[96:112, :] = jnp.concatenate([mt, mt], 0).astype(LOW)
            corner[112:160, :] = codes[...]

    sib = (sides[0], [(d, bands[3 * i + 1]) for i, d in enumerate(dirs)])
    out = (sides[1], [(d, bands[3 * i + 2]) for i, d in enumerate(dirs)])

    @pl.when(rep == 0)
    def _():
        fill(sib, True)
        fill(out, False)

    @pl.when(rep == 1)
    def _():
        fill(sib, False)
        fill(out, True)

    for i, sends_bottom in enumerate(dirs):
        band = bands[3 * i]
        if sends_bottom is None:
            first = jnp.where(lat == 0, 1, 0)
        else:
            first = 1 if sends_bottom else 0
        band[0:256, :] = grid[pl.ds(first * 24, 8)].reshape(256, 256)
        band[256:320, :] = m1[pl.ds(first * 12, 4)].reshape(64, 256)
        band[320:352, :] = cot[pl.ds(first * 14, 2)].reshape(32, 256)
        mt = jnp.where(first == 1, m2_half[7], m2_half[0])
        band[352:368, :] = jnp.concatenate([mt, mt], 0).astype(LOW)
        band[368:416, :] = codes[...]


def main_kernel(
    dirs, n_lat, own, sides, bands, weights, outs, scratch
):
    grid, m1, cot, m2, codes = own
    mesh_out, mesh1_grad, keep, send = outs
    gx, m1x, recv, ko, k2, uv, sx, slope, ssum, pool, fx, cx, m2x, ohu, su, uslope, dd, acc_s, fd_s, m0s = scratch
    rep = lax.axis_index("rep")
    lat = lax.axis_index("lat")
    frame = m1x.shape[0]
    a_frame = m2x.shape[0]
    if n_lat == 2:
        g_own, f_own, c_own, a_own = 4 + 4 * lat, 1 + 2 * lat, 2 * lat, lat
        f_first = 1 - lat
        f_count = frame - 1
    else:
        g_own, f_own, c_own, a_own = 8, 3, 2, 1
        f_first = 0
        f_count = frame

    def left_right(sib, out):
        return jnp.where(rep == 1, sib, out), jnp.where(rep == 1, out, sib)

    zero_rows = jnp.zeros((4, 16, 256), LOW)
    for blk in range(3):
        gx[blk, 0:4] = zero_rows
        gx[blk, gx.shape[1] - 6 : gx.shape[1] - 2] = zero_rows
        gx[blk, gx.shape[1] - 4 :] = zero_rows

    def put_grid(at, mid, sib, out):
        n = mid.shape[0]
        left, right = left_right(sib.astype(WIDE), out.astype(WIDE))
        left = left.reshape(n, 8, 256)
        right = right.reshape(n, 8, 256)
        wide = mid.astype(WIDE)
        gx[0, pl.ds(at, n)] = jnp.concatenate([left, wide[:, 0:8]], 1).astype(LOW)
        gx[1, pl.ds(at, n)] = wide[:, 8:24].astype(LOW)
        gx[2, pl.ds(at, n)] = jnp.concatenate([wide[:, 24:32], right], 1).astype(LOW)

    def own_grid(step, carry):
        r = step * 8
        r8 = pl.multiple_of(step * 64, 64)
        put_grid(g_own + r, grid[pl.ds(r, 8)], sides[0][pl.ds(r8, 64), :], sides[1][pl.ds(r8, 64), :])
        return carry

    lax.fori_loop(0, 4, own_grid, 0)

    def put_fine(sib, out, n):
        left, right = left_right(sib.astype(WIDE), out.astype(WIDE))
        left = left.reshape(n, 8, 256)
        right = right.reshape(n, 8, 256)
        states = jnp.concatenate([left[:, 0:4], right[:, 0:4]], 1)
        cots = jnp.concatenate([left[:, 4:8], right[:, 4:8]], 1)
        return states, cots

    m1x[...] = jnp.zeros_like(m1x)
    cx[...] = jnp.zeros_like(cx)
    states, cots = put_fine(sides[0][256:384, :], sides[1][256:384, :], 16)
    m1x[pl.ds(f_own, 16), 0:16] = m1[...].astype(WIDE)
    m1x[pl.ds(f_own, 16), 16:24] = states
    cx[pl.ds(c_own, 16), 0:16] = cot[...]
    cx[pl.ds(c_own, 16), 16:32] = jnp.concatenate([cots, jnp.zeros_like(cots)], 1).astype(LOW)

    def put_m2(at, mid, sib, out, n):
        left, right = left_right(sib.astype(WIDE), out.astype(WIDE))
        slot = iota((n, 8, 256), 1)
        left = left.reshape(n, 8, 256)
        right = right.reshape(n, 8, 256)
        ghost = jnp.where(slot == 7, left, jnp.where(slot == 0, right, 0.0))
        m2x[pl.ds(at, n)] = jnp.concatenate([mid.reshape(n, 8, 256), ghost], 1)

    m2w = m2[...].astype(WIDE)
    m2_half = jnp.where(rep == 0, m2w[:, 0:8], m2w[:, 8:16])
    put_m2(a_own, m2_half, sides[0][384:448, :], sides[1][384:448, :], 8)

    lane = iota((16, 256), 1) % 16

    def codes_of(mid, sib, out):
        left, right = left_right(sib.astype(WIDE), out.astype(WIDE))
        mid = mid.astype(WIDE)
        halo = jnp.where(lane >= 8, left[16:32], right[16:32])
        up = jnp.where(lane < 8, mid[32:48], jnp.where(lane < 12, right[32:48], left[32:48]))
        return mid[0:16], halo, up[:, 0:128]

    def put_codes(f_at, a_at, own_rows, halo_rows, up_rows):
        for r in range(own_rows.shape[0]):
            ko[f_at + r] = jnp.broadcast_to(own_rows[r : r + 1], (8, 256))
            k2[f_at + r] = jnp.broadcast_to(halo_rows[r : r + 1], (8, 256))
        for r in range(up_rows.shape[0]):
            uv[a_at + r] = jnp.broadcast_to(up_rows[r : r + 1], (8, 128))

    own_k, halo_k, up_k = codes_of(codes[...], sides[0][448:496, :], sides[1][448:496, :])
    put_codes(f_own, a_own, own_k, halo_k, up_k[0:8])

    for i, sends_bottom in enumerate(dirs):
        band, corner_sib, corner_out = bands[3 * i : 3 * i + 3]
        if sends_bottom is None:
            top = lat
        else:
            top = 1 if sends_bottom else 0
        below = 1 - top
        put_grid(
            below * (g_own + 32), band[0:256, :].reshape(8, 32, 256), corner_sib[0:64, :], corner_out[0:64, :]
        )
        states, cots = put_fine(corner_sib[64:96, :], corner_out[64:96, :], 4)
        is_top = top == 1
        f_at = below * (f_own + 16)
        c_at = below * (c_own + 16)
        a_at = below * (a_own + 8)
        mids = band[256:320, :].astype(WIDE).reshape(4, 16, 256)
        m1x[pl.ds(f_at, 3), 0:16] = jnp.where(is_top, mids[1:4], mids[0:3])
        m1x[pl.ds(f_at, 3), 16:24] = jnp.where(is_top, states[1:4], states[0:3])
        cx[pl.ds(c_at, 2), 0:16] = band[320:352, :].reshape(2, 16, 256)
        cots = jnp.where(is_top, cots[2:4], cots[0:2])
        cx[pl.ds(c_at, 2), 16:32] = jnp.concatenate([cots, jnp.zeros_like(cots)], 1).astype(LOW)
        put_m2(
            a_at, band[352:368, :].astype(WIDE)[0:8], corner_sib[96:112, :].astype(WIDE)[0:8],
            corner_out[96:112, :].astype(WIDE)[0:8], 1,
        )
        own_k, halo_k, up_k = codes_of(band[368:416, :], corner_sib[112:160, :], corner_out[112:160, :])
        put_codes(
            f_at, a_at,
            jnp.where(is_top, own_k[13:16], own_k[0:3]),
            jnp.where(is_top, halo_k[13:16], halo_k[0:3]),
            jnp.where(is_top, up_k[7:8], up_k[0:1]),
        )

    edge = iota((128, 256), 0)
    lanes = iota((128, 256), 1)
    slot = edge % 8
    base = (edge // 8) * 16
    m0s[0] = jnp.where(lanes == base + slot, 1.0, 0.0)
    m0s[1] = jnp.where(lanes == base + 8 + slot, 1.0, 0.0)
    m0s[2] = jnp.where(lanes == base + jnp.where(slot < 4, 12 + slot, slot - 4), 1.0, 0.0)
    ones = jnp.ones((256, 256), LOW)
    places = lanes.astype(WIDE)
    recv[...] = mm(m1x[...].reshape(frame * 24, 256).astype(LOW), weights[1]).reshape(frame, 24, 256)
    pool[...] = jnp.zeros_like(pool)

    def encode(f, carry):
        for tile, (first, second) in enumerate(((0, 1), (1, 2), (0, 2))):
            vec = ko[f] if tile < 2 else k2[f]
            picked = (m0s[tile].reshape(16, 8, 256) * vec[None]).reshape(128, 256).astype(LOW)
            chosen = jnp.where(mm(picked, ones) == places, 1.0, 0.0).astype(LOW)
            window = jnp.concatenate(
                [gx[first, pl.ds(2 * f, 8)].reshape(128, 256), gx[second, pl.ds(2 * f, 8)].reshape(128, 256)], 0
            )
            senders = mm(chosen, window).astype(LOW)
            pre = mm(senders, weights[0]).reshape(16, 8, 256) + recv[f, tile * 8 : tile * 8 + 8][None]
            sig = sigmoid_of(pre)
            act = pre * sig
            pool[f, tile * 8 : tile * 8 + 8] = jnp.sum(act, axis=0) * (1.0 / 16)
            if tile < 2:
                rise = sig + act * (1.0 - sig)
                sx[f, tile] = senders
                slope[f, tile] = rise.reshape(128, 256).astype(LOW)
                ssum[f, tile * 8 : tile * 8 + 8] = jnp.sum(rise, axis=0)
        return carry

    lax.fori_loop(f_first, f_first + f_count, encode, 0)
    fine = m1x[...].reshape(frame * 24, 256) + mm(pool[...].reshape(frame * 24, 256).astype(LOW), weights[2])
    fine = fine.reshape(frame, 24, 256)
    fx[:, 0:16] = fine[:, 0:16].astype(LOW)
    fx[:, 16:32] = jnp.concatenate([fine[:, 16:24], jnp.zeros((frame, 8, 256), WIDE)], 1).astype(LOW)

    edge = iota((128, 128), 0)
    lanes = iota((128, 128), 1)
    up_mask = jnp.where(lanes == edge, 1.0, 0.0)
    up_places = lanes.astype(WIDE)
    up_ones = jnp.ones((128, 128), LOW)
    m2_flat = m2x[...].reshape(a_frame * 16, 256)
    m2_low = m2_flat.astype(LOW)
    up_recv = mm(m2_low, weights[4]).reshape(a_frame, 16, 256)
    pools = []
    for aa in range(a_frame):
        vec = uv[aa]
        picked = (up_mask.reshape(16, 8, 128) * vec[None]).reshape(128, 128).astype(LOW)
        chosen = jnp.where(mm(picked, up_ones) == up_places, 1.0, 0.0).astype(LOW)
        ohu[aa] = chosen
        senders = mm(chosen, fx[2 * aa : 2 * aa + 4].reshape(128, 256)).astype(LOW)
        su[aa] = senders
        pre = mm(senders, weights[3]).reshape(8, 16, 256) + up_recv[aa][None]
        sig = sigmoid_of(pre)
        act = pre * sig
        pools.append(jnp.sum(act, axis=0) * (1.0 / 8))
        uslope[aa] = (sig + act * (1.0 - sig)).reshape(128, 256)
    up_pool = jnp.concatenate(pools, 0).astype(LOW)
    coarse = (m2_flat + mm(up_pool, weights[5])).astype(LOW)

    c_frame = 2 * a_frame
    nodes = a_frame * 16

    def parent_slot(q):
        return jnp.where(q < 16, q // 2, jnp.where((q == 18) | (q == 19), 15, jnp.where((q == 20) | (q == 21), 8, -1)))

    r_i = iota((c_frame * 32, nodes), 0)
    r_j = iota((c_frame * 32, nodes), 1)
    spread = (r_i // 64 == r_j // 16) & (parent_slot(r_i % 32) == r_j % 16)
    spread = jnp.where(spread, 1.0, 0.0).astype(LOW)
    t_i = iota((nodes, c_frame * 32), 1)
    t_j = iota((nodes, c_frame * 32), 0)
    gather = (t_i // 64 == t_j // 16) & (parent_slot(t_i % 32) == t_j % 16)
    gather = jnp.where(gather, 1.0, 0.0).astype(LOW)
    parents = mm(spread, coarse).astype(LOW)
    fine_mid = fx[1 : 1 + c_frame].reshape(c_frame * 32, 256)
    down_pre = mm(parents, weights[6]) + mm(fine_mid, weights[7])
    sig = sigmoid_of(down_pre)
    act = down_pre * sig
    cot_w = mm_nt(cx[...].reshape(c_frame * 32, 256), weights[8])
    dd[0] = (cot_w * (sig + act * (1.0 - sig))).astype(LOW).reshape(c_frame, 32, 256)
    dd[1] = act.astype(LOW).reshape(c_frame, 32, 256)

    def put_grad(index, value):
        acc_s[...] = value
        keep[index] = acc_s[pl.ds(pl.multiple_of(rep * 128, 128), 128), :]
        send[index] = acc_s[pl.ds(pl.multiple_of((1 - rep) * 128, 128), 128), :].astype(LOW)

    act_own = dd[1, pl.ds(c_own, 16), 0:16].reshape(256, 256)
    delta_own = dd[0, pl.ds(c_own, 16), 0:16].reshape(256, 256)
    fine_own = fx[pl.ds(f_own, 16), 0:16].reshape(256, 256)
    cot_own = cot[...].reshape(256, 256)
    out = fine_own.astype(WIDE) + mm(act_own, weights[8])
    mesh_out[...] = out.astype(LOW).reshape(16, 16, 256)
    put_grad(8, mm_tn(act_own, cot_own))
    put_grad(7, mm_tn(fine_own, delta_own))

    child_sum = mm(gather, dd[0].reshape(c_frame * 32, 256))
    n_i = iota((nodes, 256), 0)
    aa_i, bb_i = n_i // 16, n_i % 16
    is_own = (aa_i >= a_own) & (aa_i < a_own + 8) & (bb_i < 8)
    is_real = (bb_i <= 8) | (bb_i == 15)
    if n_lat != 2:
        above = lat * 8 - 1 + aa_i
        is_real = is_real & (above >= 0) & (above < n_lat * 8)
    sum_high, sum_low = two_parts(child_sum)
    coarse_delta = (mm_nt(sum_high, weights[6]) + mm_nt(sum_low, weights[6])).astype(LOW)
    own_high, own_low = two_parts(jnp.where(is_own, child_sum, 0.0))
    put_grad(6, mm_tn(coarse, own_high) + mm_tn(coarse, own_low))
    own_delta = jnp.where(is_own, coarse_delta.astype(WIDE), 0.0).astype(LOW)
    put_grad(5, mm_tn(up_pool, own_delta))
    pool2 = jnp.where(is_real, mm_nt(coarse_delta, weights[5]) * (1.0 / 8), 0.0)
    own_f = jnp.where(is_own, 1.0, 0.0)
    recv[...] = jnp.zeros_like(recv)
    acc_s[...] = jnp.zeros_like(acc_s)
    node_sums = []
    for aa in range(a_frame):
        d = pool2[aa * 16 : aa * 16 + 16][None] * uslope[aa].reshape(8, 16, 256)
        mine = own_f[aa * 16 : aa * 16 + 16][None]
        up_delta = d.astype(LOW)
        wide = up_delta.astype(WIDE)
        owned = wide * mine
        node_sums.append(jnp.sum(owned, axis=0))
        back = mm_tn(ohu[aa], up_delta.reshape(128, 256)).reshape(4, 32, 256)
        recv[2 * aa : 2 * aa + 4] += back[:, 0:24]
        acc_s[...] += mm_tn(su[aa], owned.reshape(128, 256).astype(LOW))
    put_grad(3, acc_s[...])
    ns_high, ns_low = two_parts(jnp.concatenate(node_sums, 0))
    put_grad(4, mm_tn(m2_low, ns_high) + mm_tn(m2_low, ns_low))
    back_high, back_low = two_parts(recv[pl.ds(f_own, 16), 0:16].reshape(256, 256))
    fine_delta = (
        cot_own.astype(WIDE)
        + mm_nt(delta_own, weights[7])
        + mm_nt(back_high, weights[3])
        + mm_nt(back_low, weights[3])
    )
    fd_s[...] = fine_delta
    fine_delta_b = fine_delta.astype(LOW)

    pool_own = pool[pl.ds(f_own, 16), 0:16].reshape(256, 256).astype(LOW)
    put_grad(2, mm_tn(pool_own, fine_delta_b))
    pool_delta = mm_nt(fine_delta_b, weights[2]) * (1.0 / 16)
    node_delta = pool_delta * ssum[pl.ds(f_own, 16)].reshape(256, 256)
    nd_high, nd_low = two_parts(node_delta)
    m1_own = m1[...].reshape(256, 256)
    put_grad(1, mm_tn(m1_own, nd_high) + mm_tn(m1_own, nd_low))
    grad_in = fd_s[...] + (mm_nt(nd_high, weights[1]) + mm_nt(nd_low, weights[1]))
    mesh1_grad[...] = grad_in.astype(LOW).reshape(16, 16, 256)
    m1x[0:16, 0:16] = pool_delta.reshape(16, 16, 256)
    acc_s[...] = jnp.zeros_like(acc_s)

    def encode_back(r, carry):
        deltas = []
        for tile in range(2):
            d = m1x[r, tile * 8 : tile * 8 + 8][None] * slope[f_own + r, tile].astype(WIDE).reshape(16, 8, 256)
            deltas.append(d.reshape(128, 256).astype(LOW))
        acc_s[...] += mm_tn(sx[f_own + r].reshape(256, 256), jnp.concatenate(deltas, 0))
        return carry

    lax.fori_loop(0, 16, encode_back, 0)
    put_grad(0, acc_s[...])


def flat_main(dirs, n_lat, *refs):
    n_bands = 3 * len(dirs)
    own, refs = refs[:5], refs[5:]
    sides, refs = refs[:2], refs[2:]
    bands, refs = refs[:n_bands], refs[n_bands:]
    weights, refs = refs[0], refs[1:]
    outs, scratch = refs[:4], refs[4:]
    main_kernel(dirs, n_lat, own, sides, bands, weights, outs, scratch)


def sum_over_slice(kept, sent, mesh):
    lat_size, lon_size = mesh.shape["lat"], mesh.shape["lon"]
    rep = lax.axis_index("rep")
    lat, lon = lax.axis_index("lat"), lax.axis_index("lon")
    place = (lat % 2) * 2 + lon % 2

    def between(values, lon_bit, lat_bit):
        return permute(
            values,
            ("lon", "lat"),
            lambda i: ((i // lat_size) ^ lon_bit) * lat_size + ((i % lat_size) ^ lat_bit),
            (lon_size, lat_size),
        )

    def siblings(values):
        return permute(values, "rep", lambda i: i ^ 1, (2,))

    count, rows, cols = kept.shape
    half = kept + siblings(sent).astype(WIDE)
    quarters = half.reshape(count, 4, rows // 4, cols)
    total = lax.dynamic_index_in_dim(quarters, place, 1, keepdims=False)
    for step in (1, 2, 3):
        piece = lax.dynamic_index_in_dim(quarters, place ^ step, 1, keepdims=False).astype(LOW)
        total = total + between(piece, step & 1, step >> 1).astype(WIDE)
    bit = 2
    while bit < lon_size:
        rounded = total.astype(LOW)
        total = rounded.astype(WIDE) + between(rounded, bit, 0).astype(WIDE)
        bit *= 2
    bit = 2
    while bit < lat_size:
        rounded = total.astype(LOW)
        total = rounded.astype(WIDE) + between(rounded, 0, bit).astype(WIDE)
        bit *= 2
    own = total.astype(LOW)
    pieces = [own] + [between(own, step & 1, step >> 1) for step in (1, 2, 3)]
    theirs = [siblings(piece) for piece in pieces]
    mine_all = jnp.stack(pieces, 0)
    theirs_all = jnp.stack(theirs, 0)
    order = jnp.arange(4) ^ place
    mine_half = jnp.take(mine_all, order, axis=0)
    their_half = jnp.take(theirs_all, order, axis=0)
    first = jnp.where(rep == 0, mine_half, their_half)
    second = jnp.where(rep == 0, their_half, mine_half)
    both = jnp.stack([first, second], 0)
    return jnp.moveaxis(both, 2, 0).reshape(count, 2 * rows, cols).astype(WIDE)


def body(mesh, grid_state, mesh1_state, mesh2_state, grid_edges, up_edges, weights, cotangent):
    n_lat, n_lon = mesh.shape["lat"], mesh.shape["lon"]
    lat = lax.axis_index("lat")
    col = lax.axis_index(("lon", "rep"))
    rep = lax.axis_index("rep")
    glon = grid_state.shape[1] * 2 * n_lon
    m1lon = mesh1_state.shape[1] * 2 * n_lon
    half_cols = up_edges.shape[2] // 2
    up_half = lax.dynamic_slice_in_dim(up_edges, rep * half_cols, half_cols, 2)
    codes = edge_codes(grid_edges, up_half, glon, m1lon, lat, col)
    dirs = (None,) if n_lat == 2 else (True, False)
    vmem = pl.BlockSpec(memory_space=pltpu.VMEM)
    params = pltpu.CompilerParams(vmem_limit_bytes=VMEM_BYTES)
    own = (grid_state, mesh1_state, cotangent, mesh2_state, codes)
    shapes = [SIDE_ROWS] * 2 + [BAND_ROWS, CORNER_ROWS, CORNER_ROWS] * len(dirs)
    buffers = pl.pallas_call(
        functools.partial(pack_kernel, dirs),
        out_shape=[jax.ShapeDtypeStruct((n, 256), LOW) for n in shapes],
        in_specs=[vmem] * 5,
        out_specs=[vmem] * len(shapes),
        compiler_params=params,
        name="pack_halos",
    )(*own)

    def beyond(lon, core):
        return ((lon + (1 if core else -1)) % n_lon, 1 - core)

    def send_to(values, other_lat, column):
        def partner(i):
            lon, rest = divmod(i, n_lat * 2)
            row, core = divmod(rest, 2)
            row = other_lat(row)
            if row is None:
                return None
            if column == "sibling":
                core = 1 - core
            elif column == "beyond":
                lon, core = beyond(lon, core)
            return (lon * n_lat + row) * 2 + core

        return permute(values, ("lon", "lat", "rep"), partner, (n_lon, n_lat, 2))

    def shift(sends_bottom):
        if sends_bottom is None:
            return lambda row: row ^ 1
        if sends_bottom:
            return lambda row: row + 1 if row + 1 < n_lat else None
        return lambda row: row - 1 if row else None

    got_sides = [send_to(buffers[0], lambda row: row, "sibling"), send_to(buffers[1], lambda row: row, "beyond")]
    got_bands = []
    for i, sends_bottom in enumerate(dirs):
        for k, column in enumerate(("same", "sibling", "beyond")):
            got_bands.append(send_to(buffers[2 + 3 * i + k], shift(sends_bottom), column))

    frame = 20 if n_lat == 2 else 22
    a_frame = 9 if n_lat == 2 else 10
    c_frame = 2 * a_frame
    g_frame = 2 * frame + 6
    scratch = [
        pltpu.VMEM((3, g_frame, 16, 256), LOW),
        pltpu.VMEM((frame, 24, 256), WIDE),
        pltpu.VMEM((frame, 24, 256), WIDE),
        pltpu.VMEM((frame, 8, 256), WIDE),
        pltpu.VMEM((frame, 8, 256), WIDE),
        pltpu.VMEM((a_frame, 8, 128), WIDE),
        pltpu.VMEM((frame, 2, 128, 256), LOW),
        pltpu.VMEM((frame, 2, 128, 256), LOW),
        pltpu.VMEM((frame, 16, 256), WIDE),
        pltpu.VMEM((frame, 24, 256), WIDE),
        pltpu.VMEM((frame, 32, 256), LOW),
        pltpu.VMEM((c_frame, 32, 256), LOW),
        pltpu.VMEM((a_frame, 16, 256), WIDE),
        pltpu.VMEM((a_frame, 128, 128), LOW),
        pltpu.VMEM((a_frame, 128, 256), LOW),
        pltpu.VMEM((a_frame, 128, 256), WIDE),
        pltpu.VMEM((2, c_frame, 32, 256), LOW),
        pltpu.VMEM((256, 256), WIDE),
        pltpu.VMEM((256, 256), WIDE),
        pltpu.VMEM((3, 128, 256), WIDE),
    ]
    n_in = 5 + 2 + len(got_bands) + 1
    mesh_out, mesh1_grad, kept, sent = pl.pallas_call(
        functools.partial(flat_main, dirs, n_lat),
        out_shape=[
            jax.ShapeDtypeStruct(mesh1_state.shape, LOW),
            jax.ShapeDtypeStruct(mesh1_state.shape, LOW),
            jax.ShapeDtypeStruct((9, 128, 256), WIDE),
            jax.ShapeDtypeStruct((9, 128, 256), LOW),
        ],
        in_specs=[vmem] * n_in,
        out_specs=[vmem] * 4,
        scratch_shapes=scratch,
        compiler_params=params,
        name="sweep",
    )(*own, *got_sides, *got_bands, weights)
    node_total = mesh1_state.shape[0] * mesh1_state.shape[1] * n_lat * n_lon * 2
    weight_grads = sum_over_slice(kept, sent, mesh) * float(node_total) ** (-0.5)
    return (mesh_out, mesh1_grad, weight_grads)


def solution(mesh):
    in_specs = (
        P(("groups", "lat"), ("lon", "rep"), None),
        P(("groups", "lat"), ("lon", "rep"), None),
        P(("groups", "lat"), "lon", None),
        P(None, "lat", ("lon", "rep")),
        P(None, "lat", "lon"),
        P(),
        P(("groups", "lat"), ("lon", "rep"), None),
    )
    out_specs = (
        P(("groups", "lat"), ("lon", "rep"), None),
        P(("groups", "lat"), ("lon", "rep"), None),
        P("groups", None, None),
    )
    return jax.shard_map(
        functools.partial(body, mesh), mesh=mesh, in_specs=in_specs, out_specs=out_specs, check_vma=False
    )
```

time: 156 us -> 79 us (0.51)
  local copies, waits for them, and re-layouts: 42.3 us -> 3.12 us
  other arithmetic: 31.9 us -> 4.23 us
  Pallas kernels: 0 us -> 24.4 us
  matrix products: 20.5 us -> 0 us
  starting transfers between devices: 27.6 us -> 18.4 us
  blocking collectives: 4.1 us -> 0 us
    pallas_call x0 -> x2, Pallas kernels: none -> 24.4 us  [the longest x1 24.2 us: body(): pl.pallas_call(functools.partial(flat_main, dirs, n_lat), out_shape=[jax....]
    gather x2 -> x0, local copies, waits for them, and re-layouts: 21 us -> none  [the longest x1 17 us: body(): enc_senders = jnp.take(grid_ext.reshape(-1, features), enc_index, axis=0)]
    dot_general x25 -> x0, matrix products: 20.5 us -> none  [the longest x20 16.8 us: matmul(): return jnp.dot(left, right, preferred_element_type=jnp.float32)]
    ppermute x24 -> x17, starting transfers between devices: 27.6 us -> 18.4 us  [permute(): lax.ppermute(values, axes, [(i, j) for i, j in pairs if j is not None])]
    reduce_sum x3 -> x0, other arithmetic: 6.65 us -> none  [the longest x1 4 us: body(): node_delta = jnp.sum(enc_delta.astype(jnp.float32), axis=0)]
    scatter-add x3 -> x0, other arithmetic: 6.32 us -> none  [the longest x1 6.29 us: coarse_pass(): ext_grad = jnp.zeros(((rows_in + 2) * (cols_in + 2), features), jnp.float...]
    another operation x5 -> x0, local copies, waits for them, and re-layouts: 5.49 us -> none
    select_n x4 -> x0, other arithmetic: 5.14 us -> none  [the longest x2 4.93 us: body(): enc_senders = jnp.take(grid_ext.reshape(-1, features), enc_index, axis=0)]
  transfers between devices with their start and end apart: 24 -> 17, of which waited for: 11 -> 11; matrix products, arithmetic and copies ran while one was open for 15% -> 1% of each run, Pallas kernels for 0% -> 0%
where the time goes in v2:
time: 79 us; the launch traced here: 78.8 us
  waiting for transfers between devices  27.8 us (35%)
  Pallas kernels  24.4 us (31%)
  starting transfers between devices  18.4 us (23%)
  other arithmetic  4.23 us (5%)
  local copies, waits for them, and re-layouts  3.12 us (4%)
  between operations  0.92 us (1%)
    ppermute x17, waiting for transfers between devices, permute(): lax.ppermute(values, axes, [(i, j) for i, j in pairs if j is not None])  27.8 us
    pallas_call x1, Pallas kernels, body(): pl.pallas_call(functools.partial(flat_main, dirs, n_lat), out_shape=[jax....  24.2 us
    ppermute x17, starting transfers between devices, permute(): lax.ppermute(values, axes, [(i, j) for i, j in pairs if j is not None])  18.4 us
    add x2, other arithmetic, code(): return down * 32 + at  2.03 us
  transfers between devices with their start and end apart: 17, of which 11 were waited for; matrix products, arithmetic and copies ran while one was open for 1% of the time, Pallas kernels for 0%

profile of v2, /device:TPU:0, one launch (start us, length us, event | category | flops | bytes accessed | tf_op | source)
XLA Modules:
  0.0 78.8 jit_solution(9409822061597657643)
XLA Ops:
  0.8 1.0 %fusion.20 = (s32[8,8,8]{2,1,0:T(8,128)S(1)}, pred[8,8,8]{2,1,0:T(8,128)(4,1)S(1)}) fusion(s32[8]{0:T(128)S(1)} %get-tuple-element.32, s32[8]{0:T(128)S(1)} %multiply_add_fusion.2, s32[8,8,16]{2,1,0:T(8,128)} %param.13, s32[]{:T(128)S(6)} %select_n.108, s32[8]{0:T(128)S(1)} %get-tuple-element.31), kind=kLoop, calls=%fused_computation.59 | loop fusion | flops 20992 | bytes 4708 | tf_op jit(solution)/shard_map/add | solution.py:72
  1.8 1.0 %fusion.22 = s32[8,8,8]{2,1,0:T(8,128)S(1)} fusion(s32[8]{0:T(128)S(1)} %get-tuple-element.33, s32[8]{0:T(128)S(1)} %get-tuple-element.34, pred[8]{0:T(512)(128)(4,1)S(1)} %iota_compare_fusion.1, s32[8]{0:T(128)S(1)} %multiply_add_fusion.2, pred[8,8,8]{2,1,0:T(8,128)(4,1)S(1)} %get-tuple-element.23, s32[8,8,16]{2,1,0:T(8,128)} %param.13, s32[]{:T(128)S(6)} %select_n.108, ...), kind=kLoop, calls=%fused_computation.61 | loop fusion | flops 22016 | bytes 4748 | tf_op jit(solution)/shard_map/add | solution.py:72
  3.0 1.1 %add_bitcast_fusion.1 = (s32[1,16,16,16]{3,2,1,0:T(8,128)S(1)}, s32[1,16,16,16]{3,2,1,0:T(8,128)S(1)}) fusion(s32[16]{0:T(128)S(1)} %get-tuple-element.40, s32[16]{0:T(128)S(1)} %get-tuple-element.42, pred[16]{0:T(512)(128)(4,1)S(1)} %get-tuple-element.35, s32[16]{0:T(128)S(1)} %get-tuple-element.41, s32[16,16,16]{2,1,0:T(8,128)} %param.12, ...), kind=kLoop, calls=%fused_computation.37 | loop fusion | flops 184320 | bytes 49568 | tf_op jit(solution)/shard_map/stack | solution.py:61
  5.1 4.7 %collective-permute-start.1 = (bf16[496,256]{1,0:T(8,128)(2,1)S(1)}, bf16[496,256]{1,0:T(8,128)(2,1)S(1)}, u32[]{:S(2)}, u32[]{:S(2)}) collective-permute-start(bf16[496,256]{1,0:T(8,128)(2,1)S(1)} %get-tuple-element.14), channel_id=1, source_target_pairs={{0,13},{1,4},{2,15},{3,6},{4,1},{5,8},{6,3},{7,10},{8,5},{9,12},{1... | collective-permute-start | bytes 761864 | tf_op jit(solution)/shard_map/ppermute | solution.py:24
  9.8 1.5 %collective-permute-start.2 = (bf16[416,256]{1,0:T(8,128)(2,1)S(1)}, bf16[416,256]{1,0:T(8,128)(2,1)S(1)}, u32[]{:S(2)}, u32[]{:S(2)}) collective-permute-start(bf16[416,256]{1,0:T(8,128)(2,1)S(1)} %get-tuple-element.15), channel_id=1, source_target_pairs={{0,2},{1,3},{2,0},{3,1},{4,6},{5,7},{6,4},{7,5},{8,10},{9,11},{10,... | collective-permute-start | bytes 638984 | tf_op jit(solution)/shard_map/ppermute | solution.py:24
  11.3 1.6 %collective-permute-start.4 = (bf16[160,256]{1,0:T(8,128)(2,1)S(1)}, bf16[160,256]{1,0:T(8,128)(2,1)S(1)}, u32[]{:S(2)}, u32[]{:S(2)}) collective-permute-start(bf16[160,256]{1,0:T(8,128)(2,1)S(1)} %get-tuple-element.17), channel_id=1, source_target_pairs={{0,15},{1,6},{2,13},{3,4},{4,3},{5,10},{6,1},{7,8},{8,7},{9,14},{1... | collective-permute-start | bytes 245768 | tf_op jit(solution)/shard_map/ppermute | solution.py:24
  12.9 5.2 %collective-permute-done.3.refs_8_ = bf16[160,256]{1,0:T(8,128)(2,1)S(1)} collective-permute-done((bf16[160,256]{1,0:T(8,128)(2,1)S(1)}, bf16[160,256]{1,0:T(8,128)(2,1)S(1)}, u32[]{:S(2)}, u32[]{:S(2)}) %collective-permute-start.3) | collective-permute-done | bytes 81952 | tf_op jit(solution)/shard_map/ppermute | solution.py:24
  18.1 0.7 collective-permute-done.4.refs_9_
  18.8 24.2 %sweep.1 = (bf16[16,16,256]{2,1,0:T(8,128)(2,1)}, bf16[16,16,256]{2,1,0:T(8,128)(2,1)}, f32[9,128,256]{2,1,0:T(8,128)S(1)}, bf16[9,128,256]{2,1,0:T(8,128)(2,1)}) custom-call(bf16[32,32,256]{2,1,0:T(8,128)(2,1)S(1)} %copy-done, bf16[16,16,256]{2,1,0:T(8,128)(2,1)S(1)} %copy-done.2, bf16[16,16,256]{2,1,0:T(8,128)(2,1)S(1)} %copy-done.3, ...), custom_call_target="tpu_custom_call" | custom-call | tf_op jit(solution)/shard_map/sweep/pallas_call | solution.py:582
  43.2 2.0 %collective-permute-done.5 = bf16[9,128,256]{2,1,0:T(8,128)(2,1)S(1)} collective-permute-done((bf16[9,128,256]{2,1,0:T(8,128)(2,1)}, bf16[9,128,256]{2,1,0:T(8,128)(2,1)S(1)}, u32[]{:S(2)}, u32[]{:S(2)}) %collective-permute-start.5) | collective-permute-done | bytes 589856 | tf_op jit(solution)/shard_map/ppermute | solution.py:24
  45.5 0.6 collective-permute-start.6
  46.1 2.2 %collective-permute-start.8 = (bf16[9,32,256]{2,1,0:T(8,128)(2,1)S(1)}, bf16[9,32,256]{2,1,0:T(8,128)(2,1)S(1)}, u32[]{:S(2)}, u32[]{:S(2)}) collective-permute-start(bf16[9,32,256]{2,1,0:T(8,128)(2,1)S(1)} %get-tuple-element.27), channel_id=1, source_target_pairs={{0,6},{2,4},{4,2},{6,0},{8,14},{10,12},{12,10},{14,8},{1,7},{3,5},... | collective-permute-start | bytes 442376 | tf_op jit(solution)/shard_map/ppermute | solution.py:24
  48.3 0.7 collective-permute-start.7
  49.0 3.2 %collective-permute-done.6 = bf16[9,32,256]{2,1,0:T(8,128)(2,1)S(1)} collective-permute-done((bf16[9,32,256]{2,1,0:T(8,128)(2,1)S(1)}, bf16[9,32,256]{2,1,0:T(8,128)(2,1)S(1)}, u32[]{:S(2)}, u32[]{:S(2)}) %collective-permute-start.6) | collective-permute-done | bytes 147488 | tf_op jit(solution)/shard_map/ppermute | solution.py:24
  52.2 3.4 %collective-permute-done.8 = bf16[9,32,256]{2,1,0:T(8,128)(2,1)S(1)} collective-permute-done((bf16[9,32,256]{2,1,0:T(8,128)(2,1)S(1)}, bf16[9,32,256]{2,1,0:T(8,128)(2,1)S(1)}, u32[]{:S(2)}, u32[]{:S(2)}) %collective-permute-start.8) | collective-permute-done | bytes 147488 | tf_op jit(solution)/shard_map/ppermute | solution.py:24
  55.6 1.4 %collective-permute-done.7 = bf16[9,32,256]{2,1,0:T(8,128)(2,1)S(1)} collective-permute-done((bf16[9,32,256]{2,1,0:T(8,128)(2,1)S(1)}, bf16[9,32,256]{2,1,0:T(8,128)(2,1)S(1)}, u32[]{:S(2)}, u32[]{:S(2)}) %collective-permute-start.7) | collective-permute-done | bytes 147488 | tf_op jit(solution)/shard_map/ppermute | solution.py:24
  57.1 2.1 %collective-permute-start.9 = (bf16[9,32,256]{2,1,0:T(8,128)(2,1)S(1)}, bf16[9,32,256]{2,1,0:T(8,128)(2,1)S(1)}, u32[]{:S(2)}, u32[]{:S(2)}) collective-permute-start(bf16[9,32,256]{2,1,0:T(8,128)(2,1)S(1)} %fusion.2), channel_id=1, source_target_pairs={{0,8},{2,10},{4,12},{6,14},{8,0},{10,2},{12,4},{14,6},{1,9},{3,11}... | collective-permute-start | bytes 442376 | tf_op jit(solution)/shard_map/ppermute | solution.py:24
  59.2 6.7 %collective-permute-done.9 = bf16[9,32,256]{2,1,0:T(8,128)(2,1)S(1)} collective-permute-done((bf16[9,32,256]{2,1,0:T(8,128)(2,1)S(1)}, bf16[9,32,256]{2,1,0:T(8,128)(2,1)S(1)}, u32[]{:S(2)}, u32[]{:S(2)}) %collective-permute-start.9) | collective-permute-done | bytes 147488 | tf_op jit(solution)/shard_map/ppermute | solution.py:24
  66.0 0.6 collective-permute-start.11
  66.7 2.8 %collective-permute-start.10 = (bf16[9,32,256]{2,1,0:T(8,128)(2,1)S(1)}, bf16[9,32,256]{2,1,0:T(8,128)(2,1)S(1)}, u32[]{:S(2)}, u32[]{:S(2)}) collective-permute-start(bf16[9,32,256]{2,1,0:T(8,128)(2,1)S(1)} %add_convert_fusion), channel_id=1, source_target_pairs={{0,4},{2,6},{4,0},{6,2},{8,12},{10,14},{12,8},{14,10},{1,5},{3,7},... | collective-permute-start | bytes 442376 | tf_op jit(solution)/shard_map/ppermute | solution.py:24
  69.6 4.1 %collective-permute-done.12 = bf16[9,32,256]{2,1,0:T(8,128)(2,1)S(1)} collective-permute-done((bf16[9,32,256]{2,1,0:T(8,128)(2,1)S(1)}, bf16[9,32,256]{2,1,0:T(8,128)(2,1)S(1)}, u32[]{:S(2)}, u32[]{:S(2)}) %collective-permute-start.12) | collective-permute-done | bytes 147488 | tf_op jit(solution)/shard_map/ppermute | solution.py:24
  73.7 0.8 collective-permute-done.11
  75.1 0.6 gather_fusion
  77.2 1.6 %copy.14 = f32[9,2,4,32,256]{4,3,2,1,0:T(8,128)} copy(f32[9,2,4,32,256]{4,3,0,2,1:T(8,128)S(1)} %multiply_bitcast_fusion) | data formatting | bytes 4718592 | tf_op jit(solution)/shard_map/mul | solution.py:597
  (54 shorter events, 3.9 us)
Async XLA Ops:
  0.6 3.8 %copy-start.3 = (bf16[16,16,256]{2,1,0:T(8,128)(2,1)S(1)}, bf16[16,16,256]{2,1,0:T(8,128)(2,1)}, u32[]{:S(2)}) copy-start(bf16[16,16,256]{2,1,0:T(8,128)(2,1)} %refs_2_.1) | copy-start | bytes 393220
  0.6 3.8 %copy-start.4 = (bf16[8,16,256]{2,1,0:T(8,128)(2,1)S(1)}, bf16[8,16,256]{2,1,0:T(8,128)(2,1)}, u32[]{:S(2)}) copy-start(bf16[8,16,256]{2,1,0:T(8,128)(2,1)} %refs_3_.1) | copy-start | bytes 196612
  0.7 3.8 %copy-start.2 = (bf16[16,16,256]{2,1,0:T(8,128)(2,1)S(1)}, bf16[16,16,256]{2,1,0:T(8,128)(2,1)}, u32[]{:S(2)}) copy-start(bf16[16,16,256]{2,1,0:T(8,128)(2,1)} %refs_1_.1) | copy-start | bytes 393220
  0.7 3.8 %copy-start = (bf16[32,32,256]{2,1,0:T(8,128)(2,1)S(1)}, bf16[32,32,256]{2,1,0:T(8,128)(2,1)}, u32[]{:S(2)}) copy-start(bf16[32,32,256]{2,1,0:T(8,128)(2,1)} %refs_0_.1) | copy-start | bytes 1572868
  1.8 17.0 %copy-start.1 = (bf16[9,256,256]{2,1,0:T(8,128)(2,1)S(1)}, bf16[9,256,256]{2,1,0:T(8,128)(2,1)}, u32[]{:S(2)}) copy-start(bf16[9,256,256]{2,1,0:T(8,128)(2,1)} %refs_10_.1) | copy-start | bytes 3538948
  4.6 14.2 %collective-permute-start = (bf16[496,256]{1,0:T(8,128)(2,1)S(1)}, bf16[496,256]{1,0:T(8,128)(2,1)S(1)}, u32[]{:S(2)}, u32[]{:S(2)}) collective-permute-start(bf16[496,256]{1,0:T(8,128)(2,1)S(1)} %get-tuple-element.13), channel_id=1, source_target_pairs={{0,1},{1,0},{2,3},{3,2},{4,5},{5,4},{6,7},{7,6},{8,9},{9,8},{10,11... | collective-permute-start | bytes 761864 | tf_op jit(solution)/shard_map/ppermute | solution.py:24
  5.1 13.7 %collective-permute-start.1 = (bf16[496,256]{1,0:T(8,128)(2,1)S(1)}, bf16[496,256]{1,0:T(8,128)(2,1)S(1)}, u32[]{:S(2)}, u32[]{:S(2)}) collective-permute-start(bf16[496,256]{1,0:T(8,128)(2,1)S(1)} %get-tuple-element.14), channel_id=1, source_target_pairs={{0,13},{1,4},{2,15},{3,6},{4,1},{5,8},{6,3},{7,10},{8,5},{9,12},{1... | collective-permute-start | bytes 761864 | tf_op jit(solution)/shard_map/ppermute | solution.py:24
  9.8 9.0 %collective-permute-start.2 = (bf16[416,256]{1,0:T(8,128)(2,1)S(1)}, bf16[416,256]{1,0:T(8,128)(2,1)S(1)}, u32[]{:S(2)}, u32[]{:S(2)}) collective-permute-start(bf16[416,256]{1,0:T(8,128)(2,1)S(1)} %get-tuple-element.15), channel_id=1, source_target_pairs={{0,2},{1,3},{2,0},{3,1},{4,6},{5,7},{6,4},{7,5},{8,10},{9,11},{10,... | collective-permute-start | bytes 638984 | tf_op jit(solution)/shard_map/ppermute | solution.py:24
  11.3 6.8 %collective-permute-start.3 = (bf16[160,256]{1,0:T(8,128)(2,1)S(1)}, bf16[160,256]{1,0:T(8,128)(2,1)S(1)}, u32[]{:S(2)}, u32[]{:S(2)}) collective-permute-start(bf16[160,256]{1,0:T(8,128)(2,1)S(1)} %get-tuple-element.16), channel_id=1, source_target_pairs={{0,3},{1,2},{2,1},{3,0},{4,7},{5,6},{6,5},{7,4},{8,11},{9,10},{10,... | collective-permute-start | bytes 245768 | tf_op jit(solution)/shard_map/ppermute | solution.py:24
  11.3 7.5 %collective-permute-start.4 = (bf16[160,256]{1,0:T(8,128)(2,1)S(1)}, bf16[160,256]{1,0:T(8,128)(2,1)S(1)}, u32[]{:S(2)}, u32[]{:S(2)}) collective-permute-start(bf16[160,256]{1,0:T(8,128)(2,1)S(1)} %get-tuple-element.17), channel_id=1, source_target_pairs={{0,15},{1,6},{2,13},{3,4},{4,3},{5,10},{6,1},{7,8},{8,7},{9,14},{1... | collective-permute-start | bytes 245768 | tf_op jit(solution)/shard_map/ppermute | solution.py:24
  43.1 2.2 %collective-permute-start.5 = (bf16[9,128,256]{2,1,0:T(8,128)(2,1)}, bf16[9,128,256]{2,1,0:T(8,128)(2,1)S(1)}, u32[]{:S(2)}, u32[]{:S(2)}) collective-permute-start(bf16[9,128,256]{2,1,0:T(8,128)(2,1)} %get-tuple-element.21), channel_id=1, source_target_pairs={{0,1},{1,0},{2,3},{3,2},{4,5},{5,4},{6,7},{7,6},{8,9},{9,8},{10,11... | collective-permute-start | bytes 1769480 | tf_op jit(solution)/shard_map/ppermute | solution.py:24
  45.5 6.8 %collective-permute-start.6 = (bf16[9,32,256]{2,1,0:T(8,128)(2,1)S(1)}, bf16[9,32,256]{2,1,0:T(8,128)(2,1)S(1)}, u32[]{:S(2)}, u32[]{:S(2)}) collective-permute-start(bf16[9,32,256]{2,1,0:T(8,128)(2,1)S(1)} %get-tuple-element.26), channel_id=1, source_target_pairs={{0,4},{2,6},{4,0},{6,2},{8,12},{10,14},{12,8},{14,10},{1,5},{3,7},... | collective-permute-start | bytes 442376 | tf_op jit(solution)/shard_map/ppermute | solution.py:24
  46.1 9.5 %collective-permute-start.8 = (bf16[9,32,256]{2,1,0:T(8,128)(2,1)S(1)}, bf16[9,32,256]{2,1,0:T(8,128)(2,1)S(1)}, u32[]{:S(2)}, u32[]{:S(2)}) collective-permute-start(bf16[9,32,256]{2,1,0:T(8,128)(2,1)S(1)} %get-tuple-element.27), channel_id=1, source_target_pairs={{0,6},{2,4},{4,2},{6,0},{8,14},{10,12},{12,10},{14,8},{1,7},{3,5},... | collective-permute-start | bytes 442376 | tf_op jit(solution)/shard_map/ppermute | solution.py:24
  48.3 8.7 %collective-permute-start.7 = (bf16[9,32,256]{2,1,0:T(8,128)(2,1)S(1)}, bf16[9,32,256]{2,1,0:T(8,128)(2,1)S(1)}, u32[]{:S(2)}, u32[]{:S(2)}) collective-permute-start(bf16[9,32,256]{2,1,0:T(8,128)(2,1)S(1)} %get-tuple-element.28), channel_id=1, source_target_pairs={{0,2},{2,0},{4,6},{6,4},{8,10},{10,8},{12,14},{14,12},{1,3},{3,1},... | collective-permute-start | bytes 442376 | tf_op jit(solution)/shard_map/ppermute | solution.py:24
  57.1 8.8 %collective-permute-start.9 = (bf16[9,32,256]{2,1,0:T(8,128)(2,1)S(1)}, bf16[9,32,256]{2,1,0:T(8,128)(2,1)S(1)}, u32[]{:S(2)}, u32[]{:S(2)}) collective-permute-start(bf16[9,32,256]{2,1,0:T(8,128)(2,1)S(1)} %fusion.2), channel_id=1, source_target_pairs={{0,8},{2,10},{4,12},{6,14},{8,0},{10,2},{12,4},{14,6},{1,9},{3,11}... | collective-permute-start | bytes 442376 | tf_op jit(solution)/shard_map/ppermute | solution.py:24
  65.9 7.8 %collective-permute-start.12 = (bf16[9,32,256]{2,1,0:T(8,128)(2,1)S(1)}, bf16[9,32,256]{2,1,0:T(8,128)(2,1)S(1)}, u32[]{:S(2)}, u32[]{:S(2)}) collective-permute-start(bf16[9,32,256]{2,1,0:T(8,128)(2,1)S(1)} %add_convert_fusion), channel_id=1, source_target_pairs={{0,6},{2,4},{4,2},{6,0},{8,14},{10,12},{12,10},{14,8},{1,7},{3,5},... | collective-permute-start | bytes 442376 | tf_op jit(solution)/shard_map/ppermute | solution.py:24
  66.0 8.5 %collective-permute-start.11 = (bf16[9,32,256]{2,1,0:T(8,128)(2,1)S(1)}, bf16[9,32,256]{2,1,0:T(8,128)(2,1)S(1)}, u32[]{:S(2)}, u32[]{:S(2)}) collective-permute-start(bf16[9,32,256]{2,1,0:T(8,128)(2,1)S(1)} %add_convert_fusion), channel_id=1, source_target_pairs={{0,2},{2,0},{4,6},{6,4},{8,10},{10,8},{12,14},{14,12},{1,3},{3,1},... | collective-permute-start | bytes 442376 | tf_op jit(solution)/shard_map/ppermute | solution.py:24
  66.7 7.8 %collective-permute-start.10 = (bf16[9,32,256]{2,1,0:T(8,128)(2,1)S(1)}, bf16[9,32,256]{2,1,0:T(8,128)(2,1)S(1)}, u32[]{:S(2)}, u32[]{:S(2)}) collective-permute-start(bf16[9,32,256]{2,1,0:T(8,128)(2,1)S(1)} %add_convert_fusion), channel_id=1, source_target_pairs={{0,4},{2,6},{4,0},{6,2},{8,12},{10,14},{12,8},{14,10},{1,5},{3,7},... | collective-permute-start | bytes 442376 | tf_op jit(solution)/shard_map/ppermute | solution.py:24
  69.5 6.2 %collective-permute-start.13 = (bf16[9,32,256]{2,1,0:T(8,128)(2,1)S(1)}, bf16[9,32,256]{2,1,0:T(8,128)(2,1)S(1)}, u32[]{:S(2)}, u32[]{:S(2)}) collective-permute-start(bf16[9,32,256]{2,1,0:T(8,128)(2,1)S(1)} %add_convert_fusion), channel_id=1, source_target_pairs={{0,1},{1,0},{2,3},{3,2},{4,5},{5,4},{6,7},{7,6},{8,9},{9,8},{10,11... | collective-permute-start | bytes 442376 | tf_op jit(solution)/shard_map/ppermute | solution.py:24
  73.7 2.0 %collective-permute-start.16 = (bf16[9,32,256]{2,1,0:T(8,128)(2,1)S(1)}, bf16[9,32,256]{2,1,0:T(8,128)(2,1)S(1)}, u32[]{:S(2)}, u32[]{:S(2)}) collective-permute-start(bf16[9,32,256]{2,1,0:T(8,128)(2,1)S(1)} %collective-permute-done.12), channel_id=1, source_target_pairs={{0,1},{1,0},{2,3},{3,2},{4,5},{5,4},{6,7},{7,6},{8,9},{9,8},{10,11... | collective-permute-start | bytes 442376 | tf_op jit(solution)/shard_map/ppermute | solution.py:24
  74.5 1.4 %collective-permute-start.15 = (bf16[9,32,256]{2,1,0:T(8,128)(2,1)S(1)}, bf16[9,32,256]{2,1,0:T(8,128)(2,1)S(1)}, u32[]{:S(2)}, u32[]{:S(2)}) collective-permute-start(bf16[9,32,256]{2,1,0:T(8,128)(2,1)S(1)} %collective-permute-done.11), channel_id=1, source_target_pairs={{0,1},{1,0},{2,3},{3,2},{4,5},{5,4},{6,7},{7,6},{8,9},{9,8},{10,11... | collective-permute-start | bytes 442376 | tf_op jit(solution)/shard_map/ppermute | solution.py:24
  74.5 1.6 %collective-permute-start.14 = (bf16[9,32,256]{2,1,0:T(8,128)(2,1)S(1)}, bf16[9,32,256]{2,1,0:T(8,128)(2,1)S(1)}, u32[]{:S(2)}, u32[]{:S(2)}) collective-permute-start(bf16[9,32,256]{2,1,0:T(8,128)(2,1)S(1)} %collective-permute-done.10), channel_id=1, source_target_pairs={{0,1},{1,0},{2,3},{3,2},{4,5},{5,4},{6,7},{7,6},{8,9},{9,8},{10,11... | collective-permute-start | bytes 442376 | tf_op jit(solution)/shard_map/ppermute | solution.py:24

commit v3 on v2

--- a/solution.py
+++ b/solution.py
@@ -9,11 +9,12 @@
 
 LOW = jnp.bfloat16
 WIDE = jnp.float32
-VMEM_BYTES = 48 * 1024 * 1024
-
-SIDE_ROWS = 496
-BAND_ROWS = 416
-CORNER_ROWS = 160
+VMEM_BYTES = 36 * 1024 * 1024
+HALO_ROWS = 2
+
+SIDE_ROWS = 416
+BAND_ROWS = 352
+CORNER_ROWS = 112
 
 
 def permute(values, axes, partner, sizes):
@@ -49,77 +50,99 @@
     return lax.broadcasted_iota(jnp.int32, shape, dim)
 
 
-def edge_codes(grid_edges, up_half, glon, m1lon, lat, col):
-    keep, rows, cols = grid_edges.shape
-    row = lax.broadcasted_iota(jnp.int32, grid_edges.shape, 1)
-    j = lax.broadcasted_iota(jnp.int32, grid_edges.shape, 2)
-    down = grid_edges // glon - (2 * (lat * rows + row) - 2)
-    across = jnp.mod(grid_edges % glon - (2 * (col * cols + j) - 2), glon)
+def split(value, size):
+    if size & (size - 1) == 0:
+        return value >> (size.bit_length() - 1), value & (size - 1)
+    return value // size, value % size
+
+
+def wrapped(value, size):
+    if size & (size - 1) == 0:
+        return value & (size - 1)
+    return jnp.mod(value, size)
+
+
+def edge_codes(edges, glon, lat, col, rows, cols):
+    row = iota(edges.shape, 0)
+    lane = iota(edges.shape, 1)
+    j = lane % 16
+    at_row, at_col = split(edges, glon)
+    down = at_row - (2 * (lat * rows + row) - 2)
+    across = wrapped(at_col - (2 * (col * cols + j) - 2), glon)
     place = 2 * (j % 8) + 6 + across
     own = down * 16 + place + jnp.where(place >= 16, 112, 0)
-    sent = down * 16 + across + 6 + jnp.where(j >= 8, 2 * (j - 16), 128 + 2 * j)
-    both = jnp.stack([own, sent], 0).astype(WIDE)
-    both = jnp.transpose(both, (0, 2, 1, 3)).reshape(2 * rows, keep * cols)
-    up_rows, up_cols = up_half.shape[1:]
-    a = lax.broadcasted_iota(jnp.int32, up_half.shape, 1)
-    b = lax.broadcasted_iota(jnp.int32, up_half.shape, 2)
-    down = up_half // m1lon - (2 * (lat * up_rows + a) - 1)
-    across = jnp.mod(up_half % m1lon - (2 * (col * up_cols + b) - 1), m1lon)
-
-    def code(base):
-        at = 2 * base - 1 + across
-        at = jnp.where(at < 0, at + 20, jnp.where(at >= 16, at + 4, at))
-        return down * 32 + at
-
-    up = jnp.concatenate([code(b), code(jnp.where(b >= 4, b - 8, b + 8))], 2).astype(WIDE)
-    up = jnp.transpose(up, (1, 0, 2)).reshape(up_rows, -1)
-    up = jnp.pad(up, ((0, 16 - up_rows), (0, both.shape[1] - up.shape[1])))
-    return jnp.concatenate([both, up], 0).astype(LOW)
-
-
-def pack_kernel(dirs, grid, m1, cot, m2, codes, *outs):
+    base = down * 16 + across + 6
+    turned = jnp.where(j < 4, pltpu.roll(base, 256 - 12, 1), pltpu.roll(base, 4, 1))
+    sent = turned + 2 * (j - 4) + jnp.where(j < 4, 0, 128)
+    return own.astype(WIDE), sent.astype(WIDE)
+
+
+def up_codes(edges, m1lon, lat, col, rep, rows, cols):
+    row = iota(edges.shape, 0)
+    l16 = iota(edges.shape, 1) % 16
+    low = jnp.where(l16 < 8, edges, pltpu.roll(edges, 8, 1))
+    high = jnp.where(l16 < 8, pltpu.roll(edges, 128 - 8, 1), edges)
+    edges = jnp.where(rep == 0, low, high)
+    b = l16 % 8
+    at_row, at_col = split(edges, m1lon)
+    down = at_row - (2 * (lat * rows + row) - 1)
+    across = wrapped(at_col - (2 * (col * cols + b) - 1), m1lon)
+    base = jnp.where(l16 < 8, b, jnp.where(b >= 4, b - 8, b + 8))
+    at = 2 * base - 1 + across
+    at = jnp.where(at < 0, at + 20, jnp.where(at >= 16, at + 4, at))
+    return (down * 32 + at).astype(WIDE)
+
+
+def pack_kernel(dirs, glon, m1lon, grid, m1, cot, m2, edges, ups, codes, *outs):
     rep = lax.axis_index("rep")
     lat = lax.axis_index("lat")
+    col = lax.axis_index("lon") * 2 + rep
     sides = outs[:2]
     bands = outs[2:]
-    half = pl.multiple_of(rep * 8, 8)
-
-    def column(right):
+    flat = jnp.concatenate([edges[k] for k in range(16)], axis=1)
+    own_k, sent_k = edge_codes(flat, glon, lat, col, 16, 16)
+    flat = jnp.concatenate([ups[k] for k in range(8)], axis=1)
+    up_k = up_codes(flat, m1lon, lat, col, rep, 8, 8)
+    up_k = jnp.concatenate([up_k, jnp.zeros_like(up_k)], 1)
+    codes[0:16, :] = own_k.astype(LOW)
+    codes[16:32, :] = sent_k.astype(LOW)
+    codes[32:48, :] = jnp.concatenate([up_k, jnp.zeros_like(up_k)], 0).astype(LOW)
+    m2w = m2[...].astype(WIDE)
+    m2_half = jnp.where(rep == 0, m2w[:, 0:8], m2w[:, 8:16])
+    row8 = iota((8, 256), 0)
+
+    def few(k_rows, last, ghost):
+        up = jnp.where(last, up_k[7:8], up_k[0:1])
+        rest = jnp.where(row8 == 3, jnp.broadcast_to(up, (8, 256)), 0.0)
+        if ghost is not None:
+            rest = jnp.where(row8 == 4, jnp.broadcast_to(ghost, (8, 256)), rest)
+        return jnp.where(last, jnp.where(row8 >= 5, k_rows[8:16], rest), jnp.where(row8 < 3, k_rows[0:8], rest))
+
+    def last_rows(sends_bottom):
+        if sends_bottom is None:
+            return lat == 0
+        return jnp.bool_(sends_bottom)
+
+    def fill(targets, right):
+        side, corners = targets
         g = grid[:, 16:32, :] if right else grid[:, 0:16, :]
         g = g.astype(WIDE)[:, 8:16] if right else g.astype(WIDE)[:, 0:8]
-        s = slice(8, 16) if right else slice(0, 8)
-        mm1 = m1[...].astype(WIDE)[:, s]
-        cc = cot[...].astype(WIDE)[:, s]
-        if right:
-            pair = jnp.concatenate([mm1[:, 4:8], cc[:, 4:8]], axis=1)
-        else:
-            pair = jnp.concatenate([mm1[:, 0:4], cc[:, 0:4]], axis=1)
-        return g, pair
-
-    m2w = m2[...].astype(WIDE)
-    m2_half = jnp.where(rep == 0, m2w[:, 0:8], m2w[:, 8:16])
-
-    def fill(targets, right):
-        side, corners = targets
-        g, pair = column(right)
+        part = slice(12, 16) if right else slice(0, 4)
+        pair = jnp.concatenate([m1[...].astype(WIDE)[:, part], cot[...].astype(WIDE)[:, part]], axis=1)
+        edge = 7 if right else 0
+        ghosts = jnp.zeros((8, 256), WIDE)
+        for a in range(8):
+            ghosts = jnp.where(row8 == a, jnp.broadcast_to(m2_half[a, edge : edge + 1], (8, 256)), ghosts)
         side[0:256, :] = g.reshape(256, 256).astype(LOW)
         side[256:384, :] = pair.reshape(128, 256).astype(LOW)
-        side[384:448, :] = m2_half.reshape(64, 256).astype(LOW)
-        side[448:496, :] = codes[...]
+        side[384:400, :] = sent_k.astype(LOW)
+        side[400:416, :] = jnp.concatenate([up_k, ghosts], 0).astype(LOW)
         for sends_bottom, corner in corners:
-            if sends_bottom is None:
-                low = lat == 0
-                gg = jnp.where(low, g[24:32], g[0:8])
-                pp = jnp.where(low, pair[12:16], pair[0:4])
-                mt = jnp.where(low, m2_half[7], m2_half[0])
-            elif sends_bottom:
-                gg, pp, mt = g[24:32], pair[12:16], m2_half[7]
-            else:
-                gg, pp, mt = g[0:8], pair[0:4], m2_half[0]
-            corner[0:64, :] = gg.reshape(64, 256).astype(LOW)
-            corner[64:96, :] = pp.reshape(32, 256).astype(LOW)
-            corner[96:112, :] = jnp.concatenate([mt, mt], 0).astype(LOW)
-            corner[112:160, :] = codes[...]
+            last = last_rows(sends_bottom)
+            corner[0:64, :] = jnp.where(last, g[24:32], g[0:8]).reshape(64, 256).astype(LOW)
+            corner[64:96, :] = jnp.where(last, pair[12:16], pair[0:4]).reshape(32, 256).astype(LOW)
+            block = few(sent_k, last, jnp.where(last, ghosts[7:8], ghosts[0:1]))
+            corner[96:112, :] = jnp.concatenate([block, block], 0).astype(LOW)
 
     sib = (sides[0], [(d, bands[3 * i + 1]) for i, d in enumerate(dirs)])
     out = (sides[1], [(d, bands[3 * i + 2]) for i, d in enumerate(dirs)])
@@ -136,36 +159,109 @@
 
     for i, sends_bottom in enumerate(dirs):
         band = bands[3 * i]
-        if sends_bottom is None:
-            first = jnp.where(lat == 0, 1, 0)
-        else:
-            first = 1 if sends_bottom else 0
+        last = last_rows(sends_bottom)
+        first = jnp.where(last, 1, 0)
         band[0:256, :] = grid[pl.ds(first * 24, 8)].reshape(256, 256)
-        band[256:320, :] = m1[pl.ds(first * 12, 4)].reshape(64, 256)
-        band[320:352, :] = cot[pl.ds(first * 14, 2)].reshape(32, 256)
-        mt = jnp.where(first == 1, m2_half[7], m2_half[0])
-        band[352:368, :] = jnp.concatenate([mt, mt], 0).astype(LOW)
-        band[368:416, :] = codes[...]
+        band[256:304, :] = m1[pl.ds(first * 13, 3)].reshape(48, 256)
+        band[304:336, :] = cot[pl.ds(first * 14, 2)].reshape(32, 256)
+        mt = jnp.where(last, m2_half[7], m2_half[0])
+        band[336:352, :] = jnp.concatenate([few(own_k, last, None), mt], 0).astype(LOW)
+
+
+def set_masks(masks):
+    edge = iota((128, 256), 0)
+    lanes = iota((128, 256), 1)
+    slot = edge % 8
+    base = (edge // 8) * 16
+    masks[0] = jnp.where(lanes == base + slot, 1.0, 0.0).astype(LOW)
+    masks[1] = jnp.where(lanes == base + 8 + slot, 1.0, 0.0).astype(LOW)
+    masks[2] = jnp.where(lanes == base + jnp.where(slot < 7, slot, 15), 1.0, 0.0).astype(LOW)
+
+
+def encode_tiles(tiles, weight):
+    count = len(tiles)
+    ones = jnp.ones((256, 256), LOW)
+    places = iota((128, 256), 1).astype(WIDE)
+    picked = [(mask.reshape(8, 16, 256) * codes[None]).reshape(128, 256) for mask, codes, _, _ in tiles]
+    found = mm(jnp.concatenate(picked, 0), ones)
+    senders = []
+    for i, (_, _, window, _) in enumerate(tiles):
+        chosen = jnp.where(found[i * 128 : i * 128 + 128] == places, 1.0, 0.0).astype(LOW)
+        senders.append(mm(chosen, jnp.concatenate(window, 0)).astype(LOW))
+    pre_all = mm(jnp.concatenate(senders, 0), weight)
+    results = []
+    for i in range(count):
+        pre = pre_all[i * 128 : i * 128 + 128].reshape(16, 8, 256) + tiles[i][3][None]
+        sig = sigmoid_of(pre)
+        act = pre * sig
+        rise = sig + act * (1.0 - sig)
+        results.append(
+            (senders[i], jnp.sum(act, axis=0) * (1.0 / 16), rise.reshape(128, 256).astype(LOW), jnp.sum(rise, axis=0))
+        )
+    return results
+
+
+BLOCKS = ((0, 1), (1, 2), (0, 2))
+
+
+def inner_kernel(grid, m1, codes, weights, sx, slope, pool, ssum, gx, masks, ko, recv):
+    set_masks(masks)
+
+    def place_grid(step, carry):
+        r = step * 8
+        wide = grid[pl.ds(r, 8)].astype(WIDE)
+        edge = jnp.zeros((8, 8, 256), WIDE)
+        gx[0, pl.ds(r, 8)] = jnp.concatenate([edge, wide[:, 0:8]], 1).astype(LOW)
+        gx[1, pl.ds(r, 8)] = wide[:, 8:24].astype(LOW)
+        gx[2, pl.ds(r, 8)] = jnp.concatenate([wide[:, 24:32], edge], 1).astype(LOW)
+        return carry
+
+    lax.fori_loop(0, 4, place_grid, 0)
+    gx[:, 32:34] = jnp.zeros((3, 2, 16, 256), LOW)
+    own = codes[0:16, :].astype(WIDE)
+    for r in range(16):
+        ko[r] = jnp.broadcast_to(own[r : r + 1], (16, 256)).astype(LOW)
+    recv[...] = mm(m1[...].reshape(256, 256), weights[1]).reshape(16, 16, 256)
+
+    def rows(step, carry):
+        tiles = []
+        for k in range(2):
+            r = 1 + 2 * step + k
+            for tile in range(2):
+                window = [gx[blk, pl.ds(2 * r - 2, 8)].reshape(128, 256) for blk in BLOCKS[tile]]
+                tiles.append((masks[tile], ko[r], window, recv[r, tile * 8 : tile * 8 + 8]))
+        done = encode_tiles(tiles, weights[0])
+        for k in range(2):
+            r = 1 + 2 * step + k
+            for tile in range(2):
+                senders, mean, rise, total = done[2 * k + tile]
+                sx[r, tile] = senders
+                slope[r, tile] = rise
+                pool[r, tile * 8 : tile * 8 + 8] = mean
+                ssum[r, tile * 8 : tile * 8 + 8] = total
+        return carry
+
+    lax.fori_loop(0, 7, rows, 0)
 
 
 def main_kernel(
     dirs, n_lat, own, sides, bands, weights, outs, scratch
 ):
-    grid, m1, cot, m2, codes = own
+    grid, m1, cot, m2, codes, sx_in, slope_in, pool_in, ssum_in = own
     mesh_out, mesh1_grad, keep, send = outs
-    gx, m1x, recv, ko, k2, uv, sx, slope, ssum, pool, fx, cx, m2x, ohu, su, uslope, dd, acc_s, fd_s, m0s = scratch
+    gx, m1x, recv, ko, k2, uv, sx, slope, ssum, pool, fx, cx, m2x, ohu, su, uslope, dd, acc_s, fd_s, masks = scratch
     rep = lax.axis_index("rep")
     lat = lax.axis_index("lat")
     frame = m1x.shape[0]
     a_frame = m2x.shape[0]
     if n_lat == 2:
         g_own, f_own, c_own, a_own = 4 + 4 * lat, 1 + 2 * lat, 2 * lat, lat
-        f_first = 1 - lat
-        f_count = frame - 1
+        odd_rows = 5
+        odd_row = lambda i: jnp.where(lat == 0, jnp.where(i == 0, 1, 15 + i), jnp.where(i < 4, i, 18))
     else:
         g_own, f_own, c_own, a_own = 8, 3, 2, 1
-        f_first = 0
-        f_count = frame
+        odd_rows = 8
+        odd_row = lambda i: jnp.where(i < 4, i, 14 + i)
 
     def left_right(sib, out):
         return jnp.where(rep == 1, sib, out), jnp.where(rep == 1, out, sib)
@@ -194,53 +290,62 @@
 
     lax.fori_loop(0, 4, own_grid, 0)
 
-    def put_fine(sib, out, n):
+    def put_fine(sib, out, n, mid):
         left, right = left_right(sib.astype(WIDE), out.astype(WIDE))
         left = left.reshape(n, 8, 256)
         right = right.reshape(n, 8, 256)
+        slot = iota((n, 8, 256), 1)
         states = jnp.concatenate([left[:, 0:4], right[:, 0:4]], 1)
+        states = jnp.where(slot == 0, mid[:, 0:8], jnp.where(slot == 7, mid[:, 8:16], states))
         cots = jnp.concatenate([left[:, 4:8], right[:, 4:8]], 1)
         return states, cots
 
     m1x[...] = jnp.zeros_like(m1x)
     cx[...] = jnp.zeros_like(cx)
-    states, cots = put_fine(sides[0][256:384, :], sides[1][256:384, :], 16)
-    m1x[pl.ds(f_own, 16), 0:16] = m1[...].astype(WIDE)
+    m1_wide = m1[...].astype(WIDE)
+    states, cots = put_fine(sides[0][256:384, :], sides[1][256:384, :], 16, m1_wide)
+    m1x[pl.ds(f_own, 16), 0:16] = m1_wide
     m1x[pl.ds(f_own, 16), 16:24] = states
     cx[pl.ds(c_own, 16), 0:16] = cot[...]
     cx[pl.ds(c_own, 16), 16:32] = jnp.concatenate([cots, jnp.zeros_like(cots)], 1).astype(LOW)
 
     def put_m2(at, mid, sib, out, n):
-        left, right = left_right(sib.astype(WIDE), out.astype(WIDE))
-        slot = iota((n, 8, 256), 1)
-        left = left.reshape(n, 8, 256)
-        right = right.reshape(n, 8, 256)
-        ghost = jnp.where(slot == 7, left, jnp.where(slot == 0, right, 0.0))
-        m2x[pl.ds(at, n)] = jnp.concatenate([mid.reshape(n, 8, 256), ghost], 1)
+        left, right = left_right(sib, out)
+        slot = iota((8, 256), 0)
+        for a in range(n):
+            l_a = jnp.broadcast_to(left[a : a + 1], (8, 256))
+            r_a = jnp.broadcast_to(right[a : a + 1], (8, 256))
+            ghost = jnp.where(slot == 7, l_a, jnp.where(slot == 0, r_a, 0.0))
+            m2x[at + a] = jnp.concatenate([mid[a], ghost], 0)
 
     m2w = m2[...].astype(WIDE)
     m2_half = jnp.where(rep == 0, m2w[:, 0:8], m2w[:, 8:16])
-    put_m2(a_own, m2_half, sides[0][384:448, :], sides[1][384:448, :], 8)
-
-    lane = iota((16, 256), 1) % 16
+    side_few = [side[384:416, :].astype(WIDE) for side in sides]
+    put_m2(a_own, m2_half, side_few[0][24:32], side_few[1][24:32], 8)
 
     def codes_of(mid, sib, out):
-        left, right = left_right(sib.astype(WIDE), out.astype(WIDE))
-        mid = mid.astype(WIDE)
-        halo = jnp.where(lane >= 8, left[16:32], right[16:32])
-        up = jnp.where(lane < 8, mid[32:48], jnp.where(lane < 12, right[32:48], left[32:48]))
-        return mid[0:16], halo, up[:, 0:128]
+        left, right = left_right(sib, out)
+        l16 = iota(mid.shape, 1) % 16
+        return jnp.where((l16 == 0) | (l16 == 15), mid, jnp.where(l16 < 4, left, right))
+
+    def ups_of(mid, sib, out):
+        left, right = left_right(sib, out)
+        l16 = iota(mid.shape, 1) % 16
+        return jnp.where(l16 < 8, mid, jnp.where(l16 < 12, right, left))[:, 0:128]
 
     def put_codes(f_at, a_at, own_rows, halo_rows, up_rows):
         for r in range(own_rows.shape[0]):
-            ko[f_at + r] = jnp.broadcast_to(own_rows[r : r + 1], (8, 256))
-            k2[f_at + r] = jnp.broadcast_to(halo_rows[r : r + 1], (8, 256))
+            ko[f_at + r] = jnp.broadcast_to(own_rows[r : r + 1], (16, 256)).astype(LOW)
+            k2[f_at + r] = jnp.broadcast_to(halo_rows[r : r + 1], (16, 256)).astype(LOW)
         for r in range(up_rows.shape[0]):
             uv[a_at + r] = jnp.broadcast_to(up_rows[r : r + 1], (8, 128))
 
-    own_k, halo_k, up_k = codes_of(codes[...], sides[0][448:496, :], sides[1][448:496, :])
-    put_codes(f_own, a_own, own_k, halo_k, up_k[0:8])
-
+    own_codes = codes[...].astype(WIDE)
+    put_codes(
+        f_own, a_own, own_codes[0:16],
+        codes_of(own_codes[0:16], side_few[0][0:16], side_few[1][0:16]),
+        ups_of(own_codes[32:40], side_few[0][16:24], side_few[1][16:24]),
+    )
     for i, sends_bottom in enumerate(dirs):
         band, corner_sib, corner_out = bands[3 * i : 3 * i + 3]
         if sends_bottom is None:
@@ -251,62 +356,80 @@
         put_grid(
             below * (g_own + 32), band[0:256, :].reshape(8, 32, 256), corner_sib[0:64, :], corner_out[0:64, :]
         )
-        states, cots = put_fine(corner_sib[64:96, :], corner_out[64:96, :], 4)
         is_top = top == 1
+        mids = band[256:304, :].astype(WIDE).reshape(3, 16, 256)
+        mids4 = jnp.where(is_top, jnp.concatenate([mids[0:1], mids], 0), jnp.concatenate([mids, mids[2:3]], 0))
+        states, cots = put_fine(corner_sib[64:96, :], corner_out[64:96, :], 4, mids4)
         f_at = below * (f_own + 16)
         c_at = below * (c_own + 16)
         a_at = below * (a_own + 8)
-        mids = band[256:320, :].astype(WIDE).reshape(4, 16, 256)
-        m1x[pl.ds(f_at, 3), 0:16] = jnp.where(is_top, mids[1:4], mids[0:3])
+        m1x[pl.ds(f_at, 3), 0:16] = mids
         m1x[pl.ds(f_at, 3), 16:24] = jnp.where(is_top, states[1:4], states[0:3])
-        cx[pl.ds(c_at, 2), 0:16] = band[320:352, :].reshape(2, 16, 256)
+        cx[pl.ds(c_at, 2), 0:16] = band[304:336, :].reshape(2, 16, 256)
         cots = jnp.where(is_top, cots[2:4], cots[0:2])
         cx[pl.ds(c_at, 2), 16:32] = jnp.concatenate([cots, jnp.zeros_like(cots)], 1).astype(LOW)
-        put_m2(
-            a_at, band[352:368, :].astype(WIDE)[0:8], corner_sib[96:112, :].astype(WIDE)[0:8],
-            corner_out[96:112, :].astype(WIDE)[0:8], 1,
-        )
-        own_k, halo_k, up_k = codes_of(band[368:416, :], corner_sib[112:160, :], corner_out[112:160, :])
+        band_few = band[336:352, :].astype(WIDE)
+        sib_few = corner_sib[96:112, :].astype(WIDE)[0:8]
+        out_few = corner_out[96:112, :].astype(WIDE)[0:8]
+        put_m2(a_at, band_few[8:16].reshape(1, 8, 256), sib_few[4:5], out_few[4:5], 1)
+        own_k = band_few[0:8]
+        halo_k = codes_of(own_k, sib_few, out_few)
+        up_k = ups_of(own_k, sib_few, out_few)
         put_codes(
             f_at, a_at,
-            jnp.where(is_top, own_k[13:16], own_k[0:3]),
-            jnp.where(is_top, halo_k[13:16], halo_k[0:3]),
-            jnp.where(is_top, up_k[7:8], up_k[0:1]),
+            jnp.where(is_top, own_k[5:8], own_k[0:3]),
+            jnp.where(is_top, halo_k[5:8], halo_k[0:3]),
+            up_k[3:4],
         )
 
-    edge = iota((128, 256), 0)
-    lanes = iota((128, 256), 1)
-    slot = edge % 8
-    base = (edge // 8) * 16
-    m0s[0] = jnp.where(lanes == base + slot, 1.0, 0.0)
-    m0s[1] = jnp.where(lanes == base + 8 + slot, 1.0, 0.0)
-    m0s[2] = jnp.where(lanes == base + jnp.where(slot < 4, 12 + slot, slot - 4), 1.0, 0.0)
-    ones = jnp.ones((256, 256), LOW)
-    places = lanes.astype(WIDE)
+    set_masks(masks)
     recv[...] = mm(m1x[...].reshape(frame * 24, 256).astype(LOW), weights[1]).reshape(frame, 24, 256)
     pool[...] = jnp.zeros_like(pool)
 
-    def encode(f, carry):
-        for tile, (first, second) in enumerate(((0, 1), (1, 2), (0, 2))):
+    def window_of(f, tile):
+        return [gx[blk, pl.ds(2 * f, 8)].reshape(128, 256) for blk in BLOCKS[tile]]
+
+    def encode_row(i, carry):
+        f = odd_row(i)
+        tiles = []
+        for tile in range(3):
             vec = ko[f] if tile < 2 else k2[f]
-            picked = (m0s[tile].reshape(16, 8, 256) * vec[None]).reshape(128, 256).astype(LOW)
-            chosen = jnp.where(mm(picked, ones) == places, 1.0, 0.0).astype(LOW)
-            window = jnp.concatenate(
-                [gx[first, pl.ds(2 * f, 8)].reshape(128, 256), gx[second, pl.ds(2 * f, 8)].reshape(128, 256)], 0
-            )
-            senders = mm(chosen, window).astype(LOW)
-            pre = mm(senders, weights[0]).reshape(16, 8, 256) + recv[f, tile * 8 : tile * 8 + 8][None]
-            sig = sigmoid_of(pre)
-            act = pre * sig
-            pool[f, tile * 8 : tile * 8 + 8] = jnp.sum(act, axis=0) * (1.0 / 16)
+            tiles.append((masks[tile], vec, window_of(f, tile), recv[f, tile * 8 : tile * 8 + 8]))
+        done = encode_tiles(tiles, weights[0])
+        for tile in range(3):
+            senders, mean, rise, total = done[tile]
+            pool[f, tile * 8 : tile * 8 + 8] = mean
             if tile < 2:
-                rise = sig + act * (1.0 - sig)
                 sx[f, tile] = senders
-                slope[f, tile] = rise.reshape(128, 256).astype(LOW)
-                ssum[f, tile * 8 : tile * 8 + 8] = jnp.sum(rise, axis=0)
+                slope[f, tile] = rise
+                ssum[f, tile * 8 : tile * 8 + 8] = total
         return carry
 
-    lax.fori_loop(f_first, f_first + f_count, encode, 0)
+    lax.fori_loop(0, odd_rows, encode_row, 0)
+    slots = iota((8, 256), 0)
+    edge_slots = iota((128, 256), 0) % 8
+
+    def encode_halo(step, carry):
+        tiles = []
+        for k in range(HALO_ROWS):
+            f = f_own + 1 + HALO_ROWS * step + k
+            tiles.append((masks[2], k2[f], window_of(f, 2), recv[f, 16:24]))
+        done = encode_tiles(tiles, weights[0])
+        for k in range(HALO_ROWS):
+            r = 1 + HALO_ROWS * step + k
+            f = f_own + r
+            senders, mean, rise, total = done[k]
+            pool[f, 16:24] = mean
+            for tile, slot in ((0, 0), (1, 7)):
+                part = slice(tile * 8, tile * 8 + 8)
+                pool[f, part] = jnp.where(slots == slot, mean, pool_in[r, part])
+                ssum[f, part] = jnp.where(slots == slot, total, ssum_in[r, part])
+                ours = edge_slots == slot
+                sx[f, tile] = jnp.where(ours, senders.astype(WIDE), sx_in[r, tile].astype(WIDE)).astype(LOW)
+                slope[f, tile] = jnp.where(ours, rise.astype(WIDE), slope_in[r, tile].astype(WIDE)).astype(LOW)
+        return carry
+
+    lax.fori_loop(0, 14 // HALO_ROWS, encode_halo, 0)
     fine = m1x[...].reshape(frame * 24, 256) + mm(pool[...].reshape(frame * 24, 256).astype(LOW), weights[2])
     fine = fine.reshape(frame, 24, 256)
     fx[:, 0:16] = fine[:, 0:16].astype(LOW)
@@ -441,7 +564,7 @@
 
 def flat_main(dirs, n_lat, *refs):
     n_bands = 3 * len(dirs)
-    own, refs = refs[:5], refs[5:]
+    own, refs = refs[:9], refs[9:]
     sides, refs = refs[:2], refs[2:]
     bands, refs = refs[:n_bands], refs[n_bands:]
     weights, refs = refs[0], refs[1:]
@@ -499,27 +622,41 @@
 
 def body(mesh, grid_state, mesh1_state, mesh2_state, grid_edges, up_edges, weights, cotangent):
     n_lat, n_lon = mesh.shape["lat"], mesh.shape["lon"]
-    lat = lax.axis_index("lat")
-    col = lax.axis_index(("lon", "rep"))
-    rep = lax.axis_index("rep")
     glon = grid_state.shape[1] * 2 * n_lon
     m1lon = mesh1_state.shape[1] * 2 * n_lon
-    half_cols = up_edges.shape[2] // 2
-    up_half = lax.dynamic_slice_in_dim(up_edges, rep * half_cols, half_cols, 2)
-    codes = edge_codes(grid_edges, up_half, glon, m1lon, lat, col)
     dirs = (None,) if n_lat == 2 else (True, False)
     vmem = pl.BlockSpec(memory_space=pltpu.VMEM)
     params = pltpu.CompilerParams(vmem_limit_bytes=VMEM_BYTES)
-    own = (grid_state, mesh1_state, cotangent, mesh2_state, codes)
-    shapes = [SIDE_ROWS] * 2 + [BAND_ROWS, CORNER_ROWS, CORNER_ROWS] * len(dirs)
-    buffers = pl.pallas_call(
-        functools.partial(pack_kernel, dirs),
+    shapes = [48] + [SIDE_ROWS] * 2 + [BAND_ROWS, CORNER_ROWS, CORNER_ROWS] * len(dirs)
+    codes, *buffers = pl.pallas_call(
+        functools.partial(pack_kernel, dirs, glon, m1lon),
         out_shape=[jax.ShapeDtypeStruct((n, 256), LOW) for n in shapes],
-        in_specs=[vmem] * 5,
+        in_specs=[vmem] * 6,
         out_specs=[vmem] * len(shapes),
         compiler_params=params,
         name="pack_halos",
-    )(*own)
+    )(grid_state, mesh1_state, cotangent, mesh2_state, grid_edges, up_edges)
+    inner = pl.pallas_call(
+        inner_kernel,
+        out_shape=[
+            jax.ShapeDtypeStruct((16, 2, 128, 256), LOW),
+            jax.ShapeDtypeStruct((16, 2, 128, 256), LOW),
+            jax.ShapeDtypeStruct((16, 16, 256), WIDE),
+            jax.ShapeDtypeStruct((16, 16, 256), WIDE),
+        ],
+        in_specs=[vmem] * 4,
+        out_specs=[vmem] * 4,
+        scratch_shapes=[
+            pltpu.VMEM((3, 34, 16, 256), LOW),
+            pltpu.VMEM((3, 128, 256), LOW),
+            pltpu.VMEM((16, 16, 256), LOW),
+            pltpu.VMEM((16, 16, 256), WIDE),
+        ],
+        compiler_params=params,
+        cost_estimate=pl.CostEstimate(flops=4_000_000_000, bytes_accessed=8_000_000, transcendentals=1_000_000),
+        name="inner_rows",
+    )(grid_state, mesh1_state, codes, weights)
+    own = (grid_state, mesh1_state, cotangent, mesh2_state, codes, *inner)
 
     def beyond(lon, core):
         return ((lon + (1 if core else -1)) % n_lon, 1 - core)
@@ -560,8 +697,8 @@
         pltpu.VMEM((3, g_frame, 16, 256), LOW),
         pltpu.VMEM((frame, 24, 256), WIDE),
         pltpu.VMEM((frame, 24, 256), WIDE),
-        pltpu.VMEM((frame, 8, 256), WIDE),
-        pltpu.VMEM((frame, 8, 256), WIDE),
+        pltpu.VMEM((frame, 16, 256), LOW),
+        pltpu.VMEM((frame, 16, 256), LOW),
         pltpu.VMEM((a_frame, 8, 128), WIDE),
         pltpu.VMEM((frame, 2, 128, 256), LOW),
         pltpu.VMEM((frame, 2, 128, 256), LOW),
@@ -576,9 +713,9 @@
         pltpu.VMEM((2, c_frame, 32, 256), LOW),
         pltpu.VMEM((256, 256), WIDE),
         pltpu.VMEM((256, 256), WIDE),
-        pltpu.VMEM((3, 128, 256), WIDE),
+        pltpu.VMEM((3, 128, 256), LOW),
     ]
-    n_in = 5 + 2 + len(got_bands) + 1
+    n_in = 9 + 2 + len(got_bands) + 1
     mesh_out, mesh1_grad, kept, sent = pl.pallas_call(
         functools.partial(flat_main, dirs, n_lat),
         out_shape=[

time: 79 us -> 72.1 us (0.913)
  local copies, waits for them, and re-layouts: 3.12 us -> 9.43 us
  waiting for transfers between devices: 27.8 us -> 22.6 us
  Pallas kernels: 24.4 us -> 20.8 us
  other arithmetic: 4.23 us -> 0.92 us
  starting transfers between devices: 18.4 us -> 17.1 us
    pallas_call x1, Pallas kernels: 24.2 us -> 16 us  [body(): pl.pallas_call(functools.partial(flat_main, dirs, n_lat), out_shape=[jax....]
    unnamed x10 -> x20, local copies, waits for them, and re-layouts: 0.02 us -> 6.62 us
    ppermute x17, waiting for transfers between devices: 27.8 us -> 22.6 us  [permute(): lax.ppermute(values, axes, [(i, j) for i, j in pairs if j is not None])]
    pallas_call x1 -> x2, Pallas kernels: 0.12 us -> 4.89 us  [the longest x1 4.59 us: body(): pl.pallas_call(inner_kernel, out_shape=[jax.ShapeDtypeStruct((16, 2, 128,...]
    add x3 -> x0, other arithmetic: 2.03 us -> none  [the longest x2 2.03 us: code(): return down * 32 + at]
    ppermute x17, starting transfers between devices: 18.4 us -> 17.1 us  [permute(): lax.ppermute(values, axes, [(i, j) for i, j in pairs if j is not None])]
    another operation x1 -> x0, other arithmetic: 1.12 us -> none  [edge_codes(): both = jnp.stack([own, sent], 0).astype(WIDE)]
  transfers between devices with their start and end apart: 17 -> 17, of which waited for: 11 -> 8; matrix products, arithmetic and copies ran while one was open for 1% -> 1% of each run, Pallas kernels for 0% -> 6%
where the time goes in v3:
time: 72.1 us; the launch traced here: 71.7 us
  waiting for transfers between devices  22.6 us (31%)
  Pallas kernels  20.8 us (29%)
  starting transfers between devices  17.1 us (24%)
  local copies, waits for them, and re-layouts  9.43 us (13%)
  other arithmetic  0.92 us (1%)
  between operations  0.83 us (1%)
    ppermute x17, waiting for transfers between devices, permute(): lax.ppermute(values, axes, [(i, j) for i, j in pairs if j is not None])  22.6 us
    ppermute x17, starting transfers between devices, permute(): lax.ppermute(values, axes, [(i, j) for i, j in pairs if j is not None])  17.1 us
    pallas_call x1, Pallas kernels, body(): pl.pallas_call(functools.partial(flat_main, dirs, n_lat), out_shape=[jax....  16 us
    unnamed x20, local copies, waits for them, and re-layouts  6.62 us
    pallas_call x1, Pallas kernels, body(): pl.pallas_call(inner_kernel, out_shape=[jax.ShapeDtypeStruct((16, 2, 128,...  4.59 us
    mul x1, local copies, waits for them, and re-layouts, body(): sum_over_slice(kept, sent, mesh) * float(node_total) ** (-0.5)  1.57 us
  transfers between devices with their start and end apart: 17, of which 8 were waited for; matrix products, arithmetic and copies ran while one was open for 1% of the time, Pallas kernels for 6%

profile of v3, /device:TPU:0, one launch (start us, length us, event | category | flops | bytes accessed | tf_op | source)
XLA Modules:
  0.0 71.7 jit_solution(18236641622508639927)
XLA Ops:
  0.6 1.0 %copy-done = bf16[32,32,256]{2,1,0:T(8,128)(2,1)S(1)} copy-done((bf16[32,32,256]{2,1,0:T(8,128)(2,1)S(1)}, bf16[32,32,256]{2,1,0:T(8,128)(2,1)}, u32[]{:S(2)}) %copy-start) | copy-done | bytes 524312
  1.7 0.9 %copy-done.3 = bf16[16,16,256]{2,1,0:T(8,128)(2,1)S(1)} copy-done((bf16[16,16,256]{2,1,0:T(8,128)(2,1)S(1)}, bf16[16,16,256]{2,1,0:T(8,128)(2,1)}, u32[]{:S(2)}) %copy-start.3) | copy-done | bytes 131096
  2.6 0.9 %copy-done.4 = bf16[16,16,256]{2,1,0:T(8,128)(2,1)S(1)} copy-done((bf16[16,16,256]{2,1,0:T(8,128)(2,1)S(1)}, bf16[16,16,256]{2,1,0:T(8,128)(2,1)}, u32[]{:S(2)}) %copy-start.4) | copy-done | bytes 131096
  3.5 0.8 %copy-done.6 = bf16[8,16,256]{2,1,0:T(8,128)(2,1)S(1)} copy-done((bf16[8,16,256]{2,1,0:T(8,128)(2,1)S(1)}, bf16[8,16,256]{2,1,0:T(8,128)(2,1)}, u32[]{:S(2)}) %copy-start.6) | copy-done | bytes 65560
  4.3 0.9 %copy-done.8 = s32[16,16,16]{2,1,0:T(8,128)S(1)} copy-done((s32[16,16,16]{2,1,0:T(8,128)S(1)}, s32[16,16,16]{2,1,0:T(8,128)}, u32[]{:S(2)}) %copy-start.8) | copy-done | bytes 16408
  5.2 0.8 %copy-done.9 = s32[8,8,16]{2,1,0:T(8,128)S(1)} copy-done((s32[8,8,16]{2,1,0:T(8,128)S(1)}, s32[8,8,16]{2,1,0:T(8,128)}, u32[]{:S(2)}) %copy-start.9) | copy-done | bytes 4120
  6.8 4.7 %collective-permute-start.1 = (bf16[416,256]{1,0:T(8,128)(2,1)S(1)}, bf16[416,256]{1,0:T(8,128)(2,1)S(1)}, u32[]{:S(2)}, u32[]{:S(2)}) collective-permute-start(bf16[416,256]{1,0:T(8,128)(2,1)S(1)} %get-tuple-element.24), channel_id=1, source_target_pairs={{0,13},{1,4},{2,15},{3,6},{4,1},{5,8},{6,3},{7,10},{8,5},{9,12},{1... | collective-permute-start | bytes 638984 | tf_op jit(solution)/shard_map/ppermute | solution.py:25
  11.5 1.5 %collective-permute-start.2 = (bf16[352,256]{1,0:T(8,128)(2,1)S(1)}, bf16[352,256]{1,0:T(8,128)(2,1)S(1)}, u32[]{:S(2)}, u32[]{:S(2)}) collective-permute-start(bf16[352,256]{1,0:T(8,128)(2,1)S(1)} %get-tuple-element.25), channel_id=1, source_target_pairs={{0,2},{1,3},{2,0},{3,1},{4,6},{5,7},{6,4},{7,5},{8,10},{9,11},{10,... | collective-permute-start | bytes 540680 | tf_op jit(solution)/shard_map/ppermute | solution.py:25
  13.0 1.6 %collective-permute-start.4 = (bf16[112,256]{1,0:T(8,128)(2,1)S(1)}, bf16[112,256]{1,0:T(8,128)(2,1)S(1)}, u32[]{:S(2)}, u32[]{:S(2)}) collective-permute-start(bf16[112,256]{1,0:T(8,128)(2,1)S(1)} %get-tuple-element.27), channel_id=1, source_target_pairs={{0,15},{1,6},{2,13},{3,4},{4,3},{5,10},{6,1},{7,8},{8,7},{9,14},{1... | collective-permute-start | bytes 172040 | tf_op jit(solution)/shard_map/ppermute | solution.py:25
  14.7 1.3 %copy-done.1 = bf16[9,256,256]{2,1,0:T(8,128)(2,1)S(1)} copy-done((bf16[9,256,256]{2,1,0:T(8,128)(2,1)S(1)}, bf16[9,256,256]{2,1,0:T(8,128)(2,1)}, u32[]{:S(2)}) %copy-start.1) | copy-done | bytes 1179672
  15.9 4.6 %inner_rows.1 = (bf16[16,2,128,256]{3,2,1,0:T(8,128)(2,1)S(1)}, bf16[16,2,128,256]{3,2,1,0:T(8,128)(2,1)S(1)}, f32[16,16,256]{2,1,0:T(8,128)S(1)}, f32[16,16,256]{2,1,0:T(8,128)S(1)}) custom-call(bf16[32,32,256]{2,1,0:T(8,128)(2,1)S(1)} %copy-done, bf16[16,16,256]{2,1,0:T(8,128)(2,1)S(1)} %copy-done.3, bf16[48,256]{1,0:T(8,128)(2,1)S(1)} %get-tuple-element.18.codes.refs_4_, ...), custom_call_target="tpu_custom_call" | custom-call | flops 4000000000 | bytes 8000000 | tf_op jit(solution)/shard_map/inner_rows/pallas_call | solution.py:639
  20.6 16.0 %sweep.1 = (bf16[16,16,256]{2,1,0:T(8,128)(2,1)}, bf16[16,16,256]{2,1,0:T(8,128)(2,1)}, f32[9,128,256]{2,1,0:T(8,128)S(1)}, bf16[9,128,256]{2,1,0:T(8,128)(2,1)S(1)}) custom-call(bf16[32,32,256]{2,1,0:T(8,128)(2,1)S(1)} %copy-done, bf16[16,16,256]{2,1,0:T(8,128)(2,1)S(1)} %copy-done.3, bf16[16,16,256]{2,1,0:T(8,128)(2,1)S(1)} %copy-done.5, ...), custom_call_target="tpu_custom_call" | custom-call | tf_op jit(solution)/shard_map/sweep/pallas_call | solution.py:719
  36.6 2.0 %collective-permute-done.5 = bf16[9,128,256]{2,1,0:T(8,128)(2,1)S(1)} collective-permute-done((bf16[9,128,256]{2,1,0:T(8,128)(2,1)S(1)}, bf16[9,128,256]{2,1,0:T(8,128)(2,1)S(1)}, u32[]{:S(2)}, u32[]{:S(2)}) %collective-permute-start.5) | collective-permute-done | bytes 589856 | tf_op jit(solution)/shard_map/ppermute | solution.py:25
  38.8 1.6 %collective-permute-start.8 = (bf16[9,32,256]{2,1,0:T(8,128)(2,1)S(1)}, bf16[9,32,256]{2,1,0:T(8,128)(2,1)S(1)}, u32[]{:S(2)}, u32[]{:S(2)}) collective-permute-start(bf16[9,32,256]{2,1,0:T(8,128)(2,1)S(1)} %get-tuple-element.35), channel_id=1, source_target_pairs={{0,6},{2,4},{4,2},{6,0},{8,14},{10,12},{12,10},{14,8},{1,7},{3,5},... | collective-permute-start | bytes 442376 | tf_op jit(solution)/shard_map/ppermute | solution.py:25
  40.4 1.5 %collective-permute-start.7 = (bf16[9,32,256]{2,1,0:T(8,128)(2,1)S(1)}, bf16[9,32,256]{2,1,0:T(8,128)(2,1)S(1)}, u32[]{:S(2)}, u32[]{:S(2)}) collective-permute-start(bf16[9,32,256]{2,1,0:T(8,128)(2,1)S(1)} %get-tuple-element.36), channel_id=1, source_target_pairs={{0,2},{2,0},{4,6},{6,4},{8,10},{10,8},{12,14},{14,12},{1,3},{3,1},... | collective-permute-start | bytes 442376 | tf_op jit(solution)/shard_map/ppermute | solution.py:25
  42.3 4.1 %collective-permute-done.8 = bf16[9,32,256]{2,1,0:T(8,128)(2,1)S(1)} collective-permute-done((bf16[9,32,256]{2,1,0:T(8,128)(2,1)S(1)}, bf16[9,32,256]{2,1,0:T(8,128)(2,1)S(1)}, u32[]{:S(2)}, u32[]{:S(2)}) %collective-permute-start.8) | collective-permute-done | bytes 147488 | tf_op jit(solution)/shard_map/ppermute | solution.py:25
  46.5 2.3 %collective-permute-done.7 = bf16[9,32,256]{2,1,0:T(8,128)(2,1)S(1)} collective-permute-done((bf16[9,32,256]{2,1,0:T(8,128)(2,1)S(1)}, bf16[9,32,256]{2,1,0:T(8,128)(2,1)S(1)}, u32[]{:S(2)}, u32[]{:S(2)}) %collective-permute-start.7) | collective-permute-done | bytes 147488 | tf_op jit(solution)/shard_map/ppermute | solution.py:25
  48.9 1.1 %collective-permute-start.9 = (bf16[9,32,256]{2,1,0:T(8,128)(2,1)S(1)}, bf16[9,32,256]{2,1,0:T(8,128)(2,1)S(1)}, u32[]{:S(2)}, u32[]{:S(2)}) collective-permute-start(bf16[9,32,256]{2,1,0:T(8,128)(2,1)S(1)} %fusion.2), channel_id=1, source_target_pairs={{0,8},{2,10},{4,12},{6,14},{8,0},{10,2},{12,4},{14,6},{1,9},{3,11}... | collective-permute-start | bytes 442376 | tf_op jit(solution)/shard_map/ppermute | solution.py:25
  49.9 8.3 %collective-permute-done.9 = bf16[9,32,256]{2,1,0:T(8,128)(2,1)S(1)} collective-permute-done((bf16[9,32,256]{2,1,0:T(8,128)(2,1)S(1)}, bf16[9,32,256]{2,1,0:T(8,128)(2,1)S(1)}, u32[]{:S(2)}, u32[]{:S(2)}) %collective-permute-start.9) | collective-permute-done | bytes 147488 | tf_op jit(solution)/shard_map/ppermute | solution.py:25
  58.4 1.1 %collective-permute-start.11 = (bf16[9,32,256]{2,1,0:T(8,128)(2,1)S(1)}, bf16[9,32,256]{2,1,0:T(8,128)(2,1)S(1)}, u32[]{:S(2)}, u32[]{:S(2)}) collective-permute-start(bf16[9,32,256]{2,1,0:T(8,128)(2,1)S(1)} %add_convert_fusion), channel_id=1, source_target_pairs={{0,2},{2,0},{4,6},{6,4},{8,10},{10,8},{12,14},{14,12},{1,3},{3,1},... | collective-permute-start | bytes 442376 | tf_op jit(solution)/shard_map/ppermute | solution.py:25
  59.5 2.4 %collective-permute-start.10 = (bf16[9,32,256]{2,1,0:T(8,128)(2,1)S(1)}, bf16[9,32,256]{2,1,0:T(8,128)(2,1)S(1)}, u32[]{:S(2)}, u32[]{:S(2)}) collective-permute-start(bf16[9,32,256]{2,1,0:T(8,128)(2,1)S(1)} %add_convert_fusion), channel_id=1, source_target_pairs={{0,4},{2,6},{4,0},{6,2},{8,12},{10,14},{12,8},{14,10},{1,5},{3,7},... | collective-permute-start | bytes 442376 | tf_op jit(solution)/shard_map/ppermute | solution.py:25
  61.9 4.1 %collective-permute-done.12 = bf16[9,32,256]{2,1,0:T(8,128)(2,1)S(1)} collective-permute-done((bf16[9,32,256]{2,1,0:T(8,128)(2,1)S(1)}, bf16[9,32,256]{2,1,0:T(8,128)(2,1)S(1)}, u32[]{:S(2)}, u32[]{:S(2)}) %collective-permute-start.12) | collective-permute-done | bytes 147488 | tf_op jit(solution)/shard_map/ppermute | solution.py:25
  66.0 1.4 %collective-permute-done.11 = bf16[9,32,256]{2,1,0:T(8,128)(2,1)S(1)} collective-permute-done((bf16[9,32,256]{2,1,0:T(8,128)(2,1)S(1)}, bf16[9,32,256]{2,1,0:T(8,128)(2,1)S(1)}, u32[]{:S(2)}, u32[]{:S(2)}) %collective-permute-start.11) | collective-permute-done | bytes 147488 | tf_op jit(solution)/shard_map/ppermute | solution.py:25
  70.1 1.6 %copy.12 = f32[9,2,4,32,256]{4,3,2,1,0:T(8,128)} copy(f32[9,2,4,32,256]{4,3,0,2,1:T(8,128)S(1)} %multiply_bitcast_fusion) | data formatting | bytes 4718592 | tf_op jit(solution)/shard_map/mul | solution.py:734
  (47 shorter events, 4.5 us)
Async XLA Ops:
  0.6 1.0 %copy-start = (bf16[32,32,256]{2,1,0:T(8,128)(2,1)S(1)}, bf16[32,32,256]{2,1,0:T(8,128)(2,1)}, u32[]{:S(2)}) copy-start(bf16[32,32,256]{2,1,0:T(8,128)(2,1)} %refs_0_.1) | copy-start | bytes 1572868
  1.7 0.9 %copy-start.3 = (bf16[16,16,256]{2,1,0:T(8,128)(2,1)S(1)}, bf16[16,16,256]{2,1,0:T(8,128)(2,1)}, u32[]{:S(2)}) copy-start(bf16[16,16,256]{2,1,0:T(8,128)(2,1)} %refs_1_.1) | copy-start | bytes 393220
  2.6 0.9 %copy-start.4 = (bf16[16,16,256]{2,1,0:T(8,128)(2,1)S(1)}, bf16[16,16,256]{2,1,0:T(8,128)(2,1)}, u32[]{:S(2)}) copy-start(bf16[16,16,256]{2,1,0:T(8,128)(2,1)} %refs_2_.1) | copy-start | bytes 393220
  6.3 14.3 %collective-permute-start = (bf16[416,256]{1,0:T(8,128)(2,1)S(1)}, bf16[416,256]{1,0:T(8,128)(2,1)S(1)}, u32[]{:S(2)}, u32[]{:S(2)}) collective-permute-start(bf16[416,256]{1,0:T(8,128)(2,1)S(1)} %get-tuple-element.23), channel_id=1, source_target_pairs={{0,1},{1,0},{2,3},{3,2},{4,5},{5,4},{6,7},{7,6},{8,9},{9,8},{10,11... | collective-permute-start | bytes 638984 | tf_op jit(solution)/shard_map/ppermute | solution.py:25
  6.8 13.7 %collective-permute-start.1 = (bf16[416,256]{1,0:T(8,128)(2,1)S(1)}, bf16[416,256]{1,0:T(8,128)(2,1)S(1)}, u32[]{:S(2)}, u32[]{:S(2)}) collective-permute-start(bf16[416,256]{1,0:T(8,128)(2,1)S(1)} %get-tuple-element.24), channel_id=1, source_target_pairs={{0,13},{1,4},{2,15},{3,6},{4,1},{5,8},{6,3},{7,10},{8,5},{9,12},{1... | collective-permute-start | bytes 638984 | tf_op jit(solution)/shard_map/ppermute | solution.py:25
  11.5 9.0 %collective-permute-start.2 = (bf16[352,256]{1,0:T(8,128)(2,1)S(1)}, bf16[352,256]{1,0:T(8,128)(2,1)S(1)}, u32[]{:S(2)}, u32[]{:S(2)}) collective-permute-start(bf16[352,256]{1,0:T(8,128)(2,1)S(1)} %get-tuple-element.25), channel_id=1, source_target_pairs={{0,2},{1,3},{2,0},{3,1},{4,6},{5,7},{6,4},{7,5},{8,10},{9,11},{10,... | collective-permute-start | bytes 540680 | tf_op jit(solution)/shard_map/ppermute | solution.py:25
  13.0 7.5 %collective-permute-start.3 = (bf16[112,256]{1,0:T(8,128)(2,1)S(1)}, bf16[112,256]{1,0:T(8,128)(2,1)S(1)}, u32[]{:S(2)}, u32[]{:S(2)}) collective-permute-start(bf16[112,256]{1,0:T(8,128)(2,1)S(1)} %get-tuple-element.26), channel_id=1, source_target_pairs={{0,3},{1,2},{2,1},{3,0},{4,7},{5,6},{6,5},{7,4},{8,11},{9,10},{10,... | collective-permute-start | bytes 172040 | tf_op jit(solution)/shard_map/ppermute | solution.py:25
  13.0 7.5 %collective-permute-start.4 = (bf16[112,256]{1,0:T(8,128)(2,1)S(1)}, bf16[112,256]{1,0:T(8,128)(2,1)S(1)}, u32[]{:S(2)}, u32[]{:S(2)}) collective-permute-start(bf16[112,256]{1,0:T(8,128)(2,1)S(1)} %get-tuple-element.27), channel_id=1, source_target_pairs={{0,15},{1,6},{2,13},{3,4},{4,3},{5,10},{6,1},{7,8},{8,7},{9,14},{1... | collective-permute-start | bytes 172040 | tf_op jit(solution)/shard_map/ppermute | solution.py:25
  14.7 1.3 %copy-start.1 = (bf16[9,256,256]{2,1,0:T(8,128)(2,1)S(1)}, bf16[9,256,256]{2,1,0:T(8,128)(2,1)}, u32[]{:S(2)}) copy-start(bf16[9,256,256]{2,1,0:T(8,128)(2,1)} %refs_14_.1) | copy-start | bytes 3538948
  15.9 4.7 %copy-start.2 = (bf16[9,256,256]{2,1,0:T(8,128)(2,1)S(1)}, bf16[9,256,256]{2,1,0:T(8,128)(2,1)}, u32[]{:S(2)}) copy-start(bf16[9,256,256]{2,1,0:T(8,128)(2,1)} %refs_14_.1) | copy-start | bytes 3538948
  15.9 4.7 %copy-start.5 = (bf16[16,16,256]{2,1,0:T(8,128)(2,1)S(1)}, bf16[16,16,256]{2,1,0:T(8,128)(2,1)}, u32[]{:S(2)}) copy-start(bf16[16,16,256]{2,1,0:T(8,128)(2,1)} %refs_2_.1) | copy-start | bytes 393220
  15.9 4.7 %copy-start.7 = (bf16[8,16,256]{2,1,0:T(8,128)(2,1)S(1)}, bf16[8,16,256]{2,1,0:T(8,128)(2,1)}, u32[]{:S(2)}) copy-start(bf16[8,16,256]{2,1,0:T(8,128)(2,1)} %refs_3_.1) | copy-start | bytes 196612
  36.6 2.0 %collective-permute-start.5 = (bf16[9,128,256]{2,1,0:T(8,128)(2,1)S(1)}, bf16[9,128,256]{2,1,0:T(8,128)(2,1)S(1)}, u32[]{:S(2)}, u32[]{:S(2)}) collective-permute-start(bf16[9,128,256]{2,1,0:T(8,128)(2,1)S(1)} %get-tuple-element.31), channel_id=1, source_target_pairs={{0,1},{1,0},{2,3},{3,2},{4,5},{5,4},{6,7},{7,6},{8,9},{9,8},{10,11... | collective-permute-start | bytes 1769480 | tf_op jit(solution)/shard_map/ppermute | solution.py:25
  38.8 7.7 %collective-permute-start.8 = (bf16[9,32,256]{2,1,0:T(8,128)(2,1)S(1)}, bf16[9,32,256]{2,1,0:T(8,128)(2,1)S(1)}, u32[]{:S(2)}, u32[]{:S(2)}) collective-permute-start(bf16[9,32,256]{2,1,0:T(8,128)(2,1)S(1)} %get-tuple-element.35), channel_id=1, source_target_pairs={{0,6},{2,4},{4,2},{6,0},{8,14},{10,12},{12,10},{14,8},{1,7},{3,5},... | collective-permute-start | bytes 442376 | tf_op jit(solution)/shard_map/ppermute | solution.py:25
  40.4 8.4 %collective-permute-start.7 = (bf16[9,32,256]{2,1,0:T(8,128)(2,1)S(1)}, bf16[9,32,256]{2,1,0:T(8,128)(2,1)S(1)}, u32[]{:S(2)}, u32[]{:S(2)}) collective-permute-start(bf16[9,32,256]{2,1,0:T(8,128)(2,1)S(1)} %get-tuple-element.36), channel_id=1, source_target_pairs={{0,2},{2,0},{4,6},{6,4},{8,10},{10,8},{12,14},{14,12},{1,3},{3,1},... | collective-permute-start | bytes 442376 | tf_op jit(solution)/shard_map/ppermute | solution.py:25
  41.9 6.9 %collective-permute-start.6 = (bf16[9,32,256]{2,1,0:T(8,128)(2,1)S(1)}, bf16[9,32,256]{2,1,0:T(8,128)(2,1)S(1)}, u32[]{:S(2)}, u32[]{:S(2)}) collective-permute-start(bf16[9,32,256]{2,1,0:T(8,128)(2,1)S(1)} %get-tuple-element.34), channel_id=1, source_target_pairs={{0,4},{2,6},{4,0},{6,2},{8,12},{10,14},{12,8},{14,10},{1,5},{3,7},... | collective-permute-start | bytes 442376 | tf_op jit(solution)/shard_map/ppermute | solution.py:25
  48.9 9.4 %collective-permute-start.9 = (bf16[9,32,256]{2,1,0:T(8,128)(2,1)S(1)}, bf16[9,32,256]{2,1,0:T(8,128)(2,1)S(1)}, u32[]{:S(2)}, u32[]{:S(2)}) collective-permute-start(bf16[9,32,256]{2,1,0:T(8,128)(2,1)S(1)} %fusion.2), channel_id=1, source_target_pairs={{0,8},{2,10},{4,12},{6,14},{8,0},{10,2},{12,4},{14,6},{1,9},{3,11}... | collective-permute-start | bytes 442376 | tf_op jit(solution)/shard_map/ppermute | solution.py:25
  58.3 7.7 %collective-permute-start.12 = (bf16[9,32,256]{2,1,0:T(8,128)(2,1)S(1)}, bf16[9,32,256]{2,1,0:T(8,128)(2,1)S(1)}, u32[]{:S(2)}, u32[]{:S(2)}) collective-permute-start(bf16[9,32,256]{2,1,0:T(8,128)(2,1)S(1)} %add_convert_fusion), channel_id=1, source_target_pairs={{0,6},{2,4},{4,2},{6,0},{8,14},{10,12},{12,10},{14,8},{1,7},{3,5},... | collective-permute-start | bytes 442376 | tf_op jit(solution)/shard_map/ppermute | solution.py:25
  58.4 9.0 %collective-permute-start.11 = (bf16[9,32,256]{2,1,0:T(8,128)(2,1)S(1)}, bf16[9,32,256]{2,1,0:T(8,128)(2,1)S(1)}, u32[]{:S(2)}, u32[]{:S(2)}) collective-permute-start(bf16[9,32,256]{2,1,0:T(8,128)(2,1)S(1)} %add_convert_fusion), channel_id=1, source_target_pairs={{0,2},{2,0},{4,6},{6,4},{8,10},{10,8},{12,14},{14,12},{1,3},{3,1},... | collective-permute-start | bytes 442376 | tf_op jit(solution)/shard_map/ppermute | solution.py:25
  59.5 7.9 %collective-permute-start.10 = (bf16[9,32,256]{2,1,0:T(8,128)(2,1)S(1)}, bf16[9,32,256]{2,1,0:T(8,128)(2,1)S(1)}, u32[]{:S(2)}, u32[]{:S(2)}) collective-permute-start(bf16[9,32,256]{2,1,0:T(8,128)(2,1)S(1)} %add_convert_fusion), channel_id=1, source_target_pairs={{0,4},{2,6},{4,0},{6,2},{8,12},{10,14},{12,8},{14,10},{1,5},{3,7},... | collective-permute-start | bytes 442376 | tf_op jit(solution)/shard_map/ppermute | solution.py:25
  61.9 6.7 %collective-permute-start.13 = (bf16[9,32,256]{2,1,0:T(8,128)(2,1)S(1)}, bf16[9,32,256]{2,1,0:T(8,128)(2,1)S(1)}, u32[]{:S(2)}, u32[]{:S(2)}) collective-permute-start(bf16[9,32,256]{2,1,0:T(8,128)(2,1)S(1)} %add_convert_fusion), channel_id=1, source_target_pairs={{0,1},{1,0},{2,3},{3,2},{4,5},{5,4},{6,7},{7,6},{8,9},{9,8},{10,11... | collective-permute-start | bytes 442376 | tf_op jit(solution)/shard_map/ppermute | solution.py:25
  66.0 2.6 %collective-permute-start.16 = (bf16[9,32,256]{2,1,0:T(8,128)(2,1)S(1)}, bf16[9,32,256]{2,1,0:T(8,128)(2,1)S(1)}, u32[]{:S(2)}, u32[]{:S(2)}) collective-permute-start(bf16[9,32,256]{2,1,0:T(8,128)(2,1)S(1)} %collective-permute-done.12), channel_id=1, source_target_pairs={{0,1},{1,0},{2,3},{3,2},{4,5},{5,4},{6,7},{7,6},{8,9},{9,8},{10,11... | collective-permute-start | bytes 442376 | tf_op jit(solution)/shard_map/ppermute | solution.py:25
  67.4 1.4 %collective-permute-start.15 = (bf16[9,32,256]{2,1,0:T(8,128)(2,1)S(1)}, bf16[9,32,256]{2,1,0:T(8,128)(2,1)S(1)}, u32[]{:S(2)}, u32[]{:S(2)}) collective-permute-start(bf16[9,32,256]{2,1,0:T(8,128)(2,1)S(1)} %collective-permute-done.11), channel_id=1, source_target_pairs={{0,1},{1,0},{2,3},{3,2},{4,5},{5,4},{6,7},{7,6},{8,9},{9,8},{10,11... | collective-permute-start | bytes 442376 | tf_op jit(solution)/shard_map/ppermute | solution.py:25
  67.4 1.6 %collective-permute-start.14 = (bf16[9,32,256]{2,1,0:T(8,128)(2,1)S(1)}, bf16[9,32,256]{2,1,0:T(8,128)(2,1)S(1)}, u32[]{:S(2)}, u32[]{:S(2)}) collective-permute-start(bf16[9,32,256]{2,1,0:T(8,128)(2,1)S(1)} %collective-permute-done.10), channel_id=1, source_target_pairs={{0,1},{1,0},{2,3},{3,2},{4,5},{5,4},{6,7},{7,6},{8,9},{9,8},{10,11... | collective-permute-start | bytes 442376 | tf_op jit(solution)/shard_map/ppermute | solution.py:25
  (3 other events, 2.5 us)

commit v4 on v3

--- a/solution.py
+++ b/solution.py
@@ -48,6 +48,10 @@
 
 def iota(shape, dim):
     return lax.broadcasted_iota(jnp.int32, shape, dim)
+
+
+def in_hbm(value):
+    return pltpu.with_memory_space_constraint(value, pltpu.HBM)
 
 
 def split(value, size):
@@ -93,7 +97,16 @@
     return (down * 32 + at).astype(WIDE)
 
 
-def pack_kernel(dirs, glon, m1lon, grid, m1, cot, m2, edges, ups, codes, *outs):
+def pack_kernel(dirs, glon, m1lon, *refs):
+    far, (grid, m1, cot, m2, codes), rest = refs[:6], refs[6:11], refs[11:]
+    outs, (edges, ups, sems) = rest[:-3], rest[-3:]
+    copies = [
+        pltpu.make_async_copy(a, b, sems.at[i]) for i, (a, b) in enumerate(zip(far, (grid, m1, cot, m2, edges, ups)))
+    ]
+    for copy in copies:
+        copy.start()
+    for copy in copies[::-1]:
+        copy.wait()
     rep = lax.axis_index("rep")
     lat = lax.axis_index("lat")
     col = lax.axis_index("lon") * 2 + rep
@@ -204,7 +217,11 @@
 BLOCKS = ((0, 1), (1, 2), (0, 2))
 
 
-def inner_kernel(grid, m1, codes, weights, sx, slope, pool, ssum, gx, masks, ko, recv):
+def inner_kernel(grid, m1, codes, far, sx, slope, pool, ssum, weights, gx, masks, ko, recv, sems):
+    first = pltpu.make_async_copy(far.at[0:2], weights.at[0:2], sems.at[0])
+    others = pltpu.make_async_copy(far.at[2:9], weights.at[2:9], sems.at[1])
+    first.start()
+    others.start()
     set_masks(masks)
 
     def place_grid(step, carry):
@@ -221,6 +238,7 @@
     own = codes[0:16, :].astype(WIDE)
     for r in range(16):
         ko[r] = jnp.broadcast_to(own[r : r + 1], (16, 256)).astype(LOW)
+    first.wait()
     recv[...] = mm(m1[...].reshape(256, 256), weights[1]).reshape(16, 16, 256)
 
     def rows(step, carry):
@@ -242,14 +260,20 @@
         return carry
 
     lax.fori_loop(0, 7, rows, 0)
+    others.wait()
+
+
+def put_halves(grad, keep, send, index, rep):
+    keep[index] = grad[pl.ds(pl.multiple_of(rep * 128, 128), 128), :]
+    send[index] = grad[pl.ds(pl.multiple_of((1 - rep) * 128, 128), 128), :].astype(LOW)
 
 
 def main_kernel(
     dirs, n_lat, own, sides, bands, weights, outs, scratch
 ):
-    grid, m1, cot, m2, codes, sx_in, slope_in, pool_in, ssum_in = own
-    mesh_out, mesh1_grad, keep, send = outs
-    gx, m1x, recv, ko, k2, uv, sx, slope, ssum, pool, fx, cx, m2x, ohu, su, uslope, dd, acc_s, fd_s, masks = scratch
+    grid, m1, cot, m2, codes, pool_in, ssum_in = own
+    mesh_out, keep, send, fd_out, pool_out, ssum, sx, slope, hx, hslope = outs
+    gx, m1x, recv, ko, k2, uv, pool, fx, cx, m2x, ohu, su, uslope, dd, acc_s, masks = scratch
     rep = lax.axis_index("rep")
     lat = lax.axis_index("lat")
     frame = m1x.shape[0]
@@ -396,18 +420,20 @@
             vec = ko[f] if tile < 2 else k2[f]
             tiles.append((masks[tile], vec, window_of(f, tile), recv[f, tile * 8 : tile * 8 + 8]))
         done = encode_tiles(tiles, weights[0])
+        row = f - f_own
+        kept_at = jnp.where(row == 0, 0, jnp.where(row == 15, 1, 2))
+        row = jnp.where(kept_at == 2, 16, row)
         for tile in range(3):
             senders, mean, rise, total = done[tile]
             pool[f, tile * 8 : tile * 8 + 8] = mean
             if tile < 2:
-                sx[f, tile] = senders
-                slope[f, tile] = rise
-                ssum[f, tile * 8 : tile * 8 + 8] = total
+                sx[kept_at, tile] = senders
+                slope[kept_at, tile] = rise
+                ssum[row, tile * 8 : tile * 8 + 8] = total
         return carry
 
     lax.fori_loop(0, odd_rows, encode_row, 0)
     slots = iota((8, 256), 0)
-    edge_slots = iota((128, 256), 0) % 8
 
     def encode_halo(step, carry):
         tiles = []
@@ -420,13 +446,12 @@
             f = f_own + r
             senders, mean, rise, total = done[k]
             pool[f, 16:24] = mean
+            hx[r - 1] = senders
+            hslope[r - 1] = rise
             for tile, slot in ((0, 0), (1, 7)):
                 part = slice(tile * 8, tile * 8 + 8)
                 pool[f, part] = jnp.where(slots == slot, mean, pool_in[r, part])
-                ssum[f, part] = jnp.where(slots == slot, total, ssum_in[r, part])
-                ours = edge_slots == slot
-                sx[f, tile] = jnp.where(ours, senders.astype(WIDE), sx_in[r, tile].astype(WIDE)).astype(LOW)
-                slope[f, tile] = jnp.where(ours, rise.astype(WIDE), slope_in[r, tile].astype(WIDE)).astype(LOW)
+                ssum[r, part] = jnp.where(slots == slot, total, ssum_in[r, part])
         return carry
 
     lax.fori_loop(0, 14 // HALO_ROWS, encode_halo, 0)
@@ -484,8 +509,7 @@
 
     def put_grad(index, value):
         acc_s[...] = value
-        keep[index] = acc_s[pl.ds(pl.multiple_of(rep * 128, 128), 128), :]
-        send[index] = acc_s[pl.ds(pl.multiple_of((1 - rep) * 128, 128), 128), :].astype(LOW)
+        put_halves(acc_s, keep, send, index - 3, rep)
 
     act_own = dd[1, pl.ds(c_own, 16), 0:16].reshape(256, 256)
     delta_own = dd[0, pl.ds(c_own, 16), 0:16].reshape(256, 256)
@@ -535,44 +559,83 @@
         + mm_nt(back_high, weights[3])
         + mm_nt(back_low, weights[3])
     )
-    fd_s[...] = fine_delta
-    fine_delta_b = fine_delta.astype(LOW)
-
-    pool_own = pool[pl.ds(f_own, 16), 0:16].reshape(256, 256).astype(LOW)
-    put_grad(2, mm_tn(pool_own, fine_delta_b))
-    pool_delta = mm_nt(fine_delta_b, weights[2]) * (1.0 / 16)
-    node_delta = pool_delta * ssum[pl.ds(f_own, 16)].reshape(256, 256)
-    nd_high, nd_low = two_parts(node_delta)
+    fd_out[...] = fine_delta
+    pool_out[...] = pool[pl.ds(f_own, 16), 0:16].reshape(256, 256).astype(LOW)
+
+
+def back_kernel(
+    m1, weights, fine_delta, pool, ssum, sx_in, slope_in, sx_edge, slope_edge, hx, hslope, mesh1_grad, keep, send, pd, acc
+):
+    rep = lax.axis_index("rep")
+    delta_b = fine_delta[...].astype(LOW)
+    pool_delta = mm_nt(delta_b, weights[2]) * (1.0 / 16)
+    pd[...] = pool_delta.reshape(16, 16, 256)
+    node_delta = pool_delta * ssum[0:16].reshape(256, 256)
+    high, low = two_parts(node_delta)
     m1_own = m1[...].reshape(256, 256)
-    put_grad(1, mm_tn(m1_own, nd_high) + mm_tn(m1_own, nd_low))
-    grad_in = fd_s[...] + (mm_nt(nd_high, weights[1]) + mm_nt(nd_low, weights[1]))
+    grad_in = fine_delta[...] + (mm_nt(high, weights[1]) + mm_nt(low, weights[1]))
     mesh1_grad[...] = grad_in.astype(LOW).reshape(16, 16, 256)
-    m1x[0:16, 0:16] = pool_delta.reshape(16, 16, 256)
-    acc_s[...] = jnp.zeros_like(acc_s)
-
-    def encode_back(r, carry):
-        deltas = []
+    acc[...] = mm_tn(pool[...], delta_b)
+    put_halves(acc, keep, send, 2, rep)
+    acc[...] = mm_tn(m1_own, high) + mm_tn(m1_own, low)
+    put_halves(acc, keep, send, 1, rep)
+
+    def deltas_of(r, tile, rise):
+        d = pd[r, tile * 8 : tile * 8 + 8][None] * rise.reshape(16, 8, 256)
+        return d.reshape(128, 256).astype(LOW)
+
+    senders, deltas = [], []
+    for i, r in enumerate((0, 15)):
+        senders.append(sx_edge[i].reshape(256, 256))
         for tile in range(2):
-            d = m1x[r, tile * 8 : tile * 8 + 8][None] * slope[f_own + r, tile].astype(WIDE).reshape(16, 8, 256)
-            deltas.append(d.reshape(128, 256).astype(LOW))
-        acc_s[...] += mm_tn(sx[f_own + r].reshape(256, 256), jnp.concatenate(deltas, 0))
+            deltas.append(deltas_of(r, tile, slope_edge[i, tile].astype(WIDE)))
+    acc[...] = mm_tn(jnp.concatenate(senders, 0), jnp.concatenate(deltas, 0))
+    slots = iota((128, 256), 0) % 8
+
+    def rows(step, carry):
+        senders, deltas = [], []
+        for k in range(2):
+            r = 1 + 2 * step + k
+            halo = hx[r - 1].astype(WIDE)
+            halo_rise = hslope[r - 1].astype(WIDE)
+            for tile, slot in ((0, 0), (1, 7)):
+                ours = slots == slot
+                senders.append(jnp.where(ours, halo, sx_in[r, tile].astype(WIDE)).astype(LOW))
+                deltas.append(deltas_of(r, tile, jnp.where(ours, halo_rise, slope_in[r, tile].astype(WIDE))))
+        acc[...] += mm_tn(jnp.concatenate(senders, 0), jnp.concatenate(deltas, 0))
         return carry
 
-    lax.fori_loop(0, 16, encode_back, 0)
-    put_grad(0, acc_s[...])
+    lax.fori_loop(0, 7, rows, 0)
+    put_halves(acc, keep, send, 0, rep)
+
+
+def spread_kernel(first, scale, *refs):
+    mine, theirs = refs[:4], refs[4:8]
+    out, stage, sem = refs[-3:]
+    count = stage.shape[0]
+    rep = lax.axis_index("rep")
+    place = (lax.axis_index("lat") % 2) * 2 + lax.axis_index("lon") % 2
+    for step in range(4):
+        at = (place ^ step) * 32
+        for half, pieces in ((rep, mine), (1 - rep, theirs)):
+            rows = pl.ds(pl.multiple_of(half * 128 + at, 32), 32)
+            stage[:, rows, :] = pieces[step][...].astype(WIDE) * scale
+    copy = pltpu.make_async_copy(stage, out.at[first : first + count], sem)
+    copy.start()
+    copy.wait()
 
 
 def flat_main(dirs, n_lat, *refs):
     n_bands = 3 * len(dirs)
-    own, refs = refs[:9], refs[9:]
+    own, refs = refs[:7], refs[7:]
     sides, refs = refs[:2], refs[2:]
     bands, refs = refs[:n_bands], refs[n_bands:]
     weights, refs = refs[0], refs[1:]
-    outs, scratch = refs[:4], refs[4:]
+    outs, scratch = refs[:10], refs[10:]
     main_kernel(dirs, n_lat, own, sides, bands, weights, outs, scratch)
 
 
-def sum_over_slice(kept, sent, mesh):
+def sum_over_slice(kept, sent, mesh, then=None):
     lat_size, lon_size = mesh.shape["lat"], mesh.shape["lon"]
     rep = lax.axis_index("rep")
     lat, lon = lax.axis_index("lat"), lax.axis_index("lon")
@@ -589,8 +652,10 @@
     def siblings(values):
         return permute(values, "rep", lambda i: i ^ 1, (2,))
 
-    count, rows, cols = kept.shape
     half = kept + siblings(sent).astype(WIDE)
+    if then is not None:
+        half, value = lax.optimization_barrier((half, then))
+    count, rows, cols = half.shape
     quarters = half.reshape(count, 4, rows // 4, cols)
     total = lax.dynamic_index_in_dim(quarters, place, 1, keepdims=False)
     for step in (1, 2, 3):
@@ -608,16 +673,8 @@
         bit *= 2
     own = total.astype(LOW)
     pieces = [own] + [between(own, step & 1, step >> 1) for step in (1, 2, 3)]
-    theirs = [siblings(piece) for piece in pieces]
-    mine_all = jnp.stack(pieces, 0)
-    theirs_all = jnp.stack(theirs, 0)
-    order = jnp.arange(4) ^ place
-    mine_half = jnp.take(mine_all, order, axis=0)
-    their_half = jnp.take(theirs_all, order, axis=0)
-    first = jnp.where(rep == 0, mine_half, their_half)
-    second = jnp.where(rep == 0, their_half, mine_half)
-    both = jnp.stack([first, second], 0)
-    return jnp.moveaxis(both, 2, 0).reshape(count, 2 * rows, cols).astype(WIDE)
+    pieces = pieces + [siblings(piece) for piece in pieces]
+    return pieces if then is None else (pieces, value)
 
 
 def body(mesh, grid_state, mesh1_state, mesh2_state, grid_edges, up_edges, weights, cotangent):
@@ -628,14 +685,22 @@
     vmem = pl.BlockSpec(memory_space=pltpu.VMEM)
     params = pltpu.CompilerParams(vmem_limit_bytes=VMEM_BYTES)
     shapes = [48] + [SIDE_ROWS] * 2 + [BAND_ROWS, CORNER_ROWS, CORNER_ROWS] * len(dirs)
-    codes, *buffers = pl.pallas_call(
+    hbm = pl.BlockSpec(memory_space=pltpu.HBM)
+    states = (grid_state, mesh1_state, cotangent, mesh2_state)
+    grid_state, mesh1_state, cotangent, mesh2_state, codes, *buffers = pl.pallas_call(
         functools.partial(pack_kernel, dirs, glon, m1lon),
-        out_shape=[jax.ShapeDtypeStruct((n, 256), LOW) for n in shapes],
-        in_specs=[vmem] * 6,
-        out_specs=[vmem] * len(shapes),
+        out_shape=[jax.ShapeDtypeStruct(state.shape, state.dtype) for state in states]
+        + [jax.ShapeDtypeStruct((n, 256), LOW) for n in shapes],
+        in_specs=[hbm] * 6,
+        out_specs=[vmem] * (4 + len(shapes)),
+        scratch_shapes=[
+            pltpu.VMEM(grid_edges.shape, grid_edges.dtype),
+            pltpu.VMEM(up_edges.shape, up_edges.dtype),
+            pltpu.SemaphoreType.DMA((6,)),
+        ],
         compiler_params=params,
         name="pack_halos",
-    )(grid_state, mesh1_state, cotangent, mesh2_state, grid_edges, up_edges)
+    )(*(in_hbm(value) for value in (*states, grid_edges, up_edges)))
     inner = pl.pallas_call(
         inner_kernel,
         out_shape=[
@@ -643,20 +708,23 @@
             jax.ShapeDtypeStruct((16, 2, 128, 256), LOW),
             jax.ShapeDtypeStruct((16, 16, 256), WIDE),
             jax.ShapeDtypeStruct((16, 16, 256), WIDE),
+            jax.ShapeDtypeStruct(weights.shape, LOW),
         ],
-        in_specs=[vmem] * 4,
-        out_specs=[vmem] * 4,
+        in_specs=[vmem] * 3 + [hbm],
+        out_specs=[vmem] * 5,
         scratch_shapes=[
             pltpu.VMEM((3, 34, 16, 256), LOW),
             pltpu.VMEM((3, 128, 256), LOW),
             pltpu.VMEM((16, 16, 256), LOW),
             pltpu.VMEM((16, 16, 256), WIDE),
+            pltpu.SemaphoreType.DMA((2,)),
         ],
         compiler_params=params,
         cost_estimate=pl.CostEstimate(flops=4_000_000_000, bytes_accessed=8_000_000, transcendentals=1_000_000),
         name="inner_rows",
-    )(grid_state, mesh1_state, codes, weights)
-    own = (grid_state, mesh1_state, cotangent, mesh2_state, codes, *inner)
+    )(grid_state, mesh1_state, codes, in_hbm(weights))
+    sx_in, slope_in, pool_in, ssum_in, weights = inner
+    own = (grid_state, mesh1_state, cotangent, mesh2_state, codes, pool_in, ssum_in)
 
     def beyond(lon, core):
         return ((lon + (1 if core else -1)) % n_lon, 1 - core)
@@ -700,9 +768,6 @@
         pltpu.VMEM((frame, 16, 256), LOW),
         pltpu.VMEM((frame, 16, 256), LOW),
         pltpu.VMEM((a_frame, 8, 128), WIDE),
-        pltpu.VMEM((frame, 2, 128, 256), LOW),
-        pltpu.VMEM((frame, 2, 128, 256), LOW),
-        pltpu.VMEM((frame, 16, 256), WIDE),
         pltpu.VMEM((frame, 24, 256), WIDE),
         pltpu.VMEM((frame, 32, 256), LOW),
         pltpu.VMEM((c_frame, 32, 256), LOW),
@@ -712,26 +777,63 @@
         pltpu.VMEM((a_frame, 128, 256), WIDE),
         pltpu.VMEM((2, c_frame, 32, 256), LOW),
         pltpu.VMEM((256, 256), WIDE),
-        pltpu.VMEM((256, 256), WIDE),
         pltpu.VMEM((3, 128, 256), LOW),
     ]
-    n_in = 9 + 2 + len(got_bands) + 1
-    mesh_out, mesh1_grad, kept, sent = pl.pallas_call(
+    n_in = 7 + 2 + len(got_bands) + 1
+    mesh_out, kept, sent, fine_delta, pool, ssum, sx_edge, slope_edge, hx, hslope = pl.pallas_call(
         functools.partial(flat_main, dirs, n_lat),
         out_shape=[
             jax.ShapeDtypeStruct(mesh1_state.shape, LOW),
-            jax.ShapeDtypeStruct(mesh1_state.shape, LOW),
-            jax.ShapeDtypeStruct((9, 128, 256), WIDE),
-            jax.ShapeDtypeStruct((9, 128, 256), LOW),
+            jax.ShapeDtypeStruct((6, 128, 256), WIDE),
+            jax.ShapeDtypeStruct((6, 128, 256), LOW),
+            jax.ShapeDtypeStruct((256, 256), WIDE),
+            jax.ShapeDtypeStruct((256, 256), LOW),
+            jax.ShapeDtypeStruct((17, 16, 256), WIDE),
+            jax.ShapeDtypeStruct((3, 2, 128, 256), LOW),
+            jax.ShapeDtypeStruct((3, 2, 128, 256), LOW),
+            jax.ShapeDtypeStruct((14, 128, 256), LOW),
+            jax.ShapeDtypeStruct((14, 128, 256), LOW),
         ],
         in_specs=[vmem] * n_in,
-        out_specs=[vmem] * 4,
+        out_specs=[vmem] * 10,
         scratch_shapes=scratch,
         compiler_params=params,
         name="sweep",
     )(*own, *got_sides, *got_bands, weights)
+    pieces, fine_delta = sum_over_slice(kept, sent, mesh, fine_delta)
+    mesh1_grad, kept_first, sent_first = pl.pallas_call(
+        back_kernel,
+        out_shape=[
+            jax.ShapeDtypeStruct(mesh1_state.shape, LOW),
+            jax.ShapeDtypeStruct((3, 128, 256), WIDE),
+            jax.ShapeDtypeStruct((3, 128, 256), LOW),
+        ],
+        in_specs=[vmem] * 11,
+        out_specs=[vmem] * 3,
+        scratch_shapes=[pltpu.VMEM((16, 16, 256), WIDE), pltpu.VMEM((256, 256), WIDE)],
+        compiler_params=params,
+        cost_estimate=pl.CostEstimate(flops=3_000_000_000, bytes_accessed=8_000_000, transcendentals=0),
+        name="encoder_back",
+    )(mesh1_state, weights, fine_delta, pool, ssum, sx_in, slope_in, sx_edge, slope_edge, hx, hslope)
     node_total = mesh1_state.shape[0] * mesh1_state.shape[1] * n_lat * n_lon * 2
-    weight_grads = sum_over_slice(kept, sent, mesh) * float(node_total) ** (-0.5)
+    scale = float(node_total) ** (-0.5)
+    pieces_first = sum_over_slice(kept_first, sent_first, mesh)
+
+    def spread(pieces, first, before):
+        count = pieces[0].shape[0]
+        more = [] if before is None else [before]
+        return pl.pallas_call(
+            functools.partial(spread_kernel, first, scale),
+            out_shape=jax.ShapeDtypeStruct((9, 256, 256), WIDE),
+            in_specs=[vmem] * 8 + [hbm] * len(more),
+            out_specs=hbm,
+            scratch_shapes=[pltpu.VMEM((count, 256, 256), WIDE), pltpu.SemaphoreType.DMA],
+            input_output_aliases={8: 0} if more else {},
+            compiler_params=params,
+            name="spread_%d" % first,
+        )(*pieces, *more)
+
+    weight_grads = spread(pieces_first, 0, spread(pieces, 3, None))
     return (mesh_out, mesh1_grad, weight_grads)
 
 

time: 72.1 us -> 65.1 us (0.903)
  waiting for transfers between devices: 22.6 us -> 12.6 us
  starting transfers between devices: 17.1 us -> 27.1 us
  local copies, waits for them, and re-layouts: 9.43 us -> 0.06 us
  Pallas kernels: 20.8 us -> 24.1 us
    ppermute x17 -> x29, starting transfers between devices: 17.1 us -> 27.1 us  [permute(): lax.ppermute(values, axes, [(i, j) for i, j in pairs if j is not None])]
    ppermute x17 -> x29, waiting for transfers between devices: 22.6 us -> 12.6 us  [permute(): lax.ppermute(values, axes, [(i, j) for i, j in pairs if j is not None])]
    unnamed x20 -> x0, local copies, waits for them, and re-layouts: 6.62 us -> none
    pallas_call x0 -> x3, Pallas kernels: none -> 5.74 us  [the longest x1 3.49 us: body(): pl.pallas_call(back_kernel, out_shape=[jax.ShapeDtypeStruct(mesh1_state.s...]
    pallas_call x1, Pallas kernels: 16 us -> 11.3 us  [body(): pl.pallas_call(functools.partial(flat_main, dirs, n_lat), out_shape=[jax....]
    mul x1 -> x0, local copies, waits for them, and re-layouts: 1.57 us -> none  [body(): sum_over_slice(kept, sent, mesh) * float(node_total) ** (-0.5)]
    pallas_call x1, Pallas kernels: 0.3 us -> 1.53 us  [body(): pl.pallas_call(functools.partial(pack_kernel, dirs, glon, m1lon), out_sha...]
    gather x2 -> x0, local copies, waits for them, and re-layouts: 1.17 us -> none  [the longest x1 0.59 us: sum_over_slice(): mine_half = jnp.take(mine_all, order, axis=0)]
  transfers between devices with their start and end apart: 17 -> 29, of which waited for: 8 -> 9; matrix products, arithmetic and copies ran while one was open for 1% -> 0% of each run, Pallas kernels for 6% -> 10%
where the time goes in v4:
time: 65.1 us; the launch traced here: 65 us
  starting transfers between devices  27.1 us (42%)
  Pallas kernels  24.1 us (37%)
  waiting for transfers between devices  12.6 us (19%)
  between operations  0.8 us (1%)
    ppermute x29, starting transfers between devices, permute(): lax.ppermute(values, axes, [(i, j) for i, j in pairs if j is not None])  27.1 us
    ppermute x29, waiting for transfers between devices, permute(): lax.ppermute(values, axes, [(i, j) for i, j in pairs if j is not None])  12.6 us
    pallas_call x1, Pallas kernels, body(): pl.pallas_call(functools.partial(flat_main, dirs, n_lat), out_shape=[jax....  11.3 us
    pallas_call x1, Pallas kernels, body(): pl.pallas_call(inner_kernel, out_shape=[jax.ShapeDtypeStruct((16, 2, 128,...  5.49 us
    pallas_call x1, Pallas kernels, body(): pl.pallas_call(back_kernel, out_shape=[jax.ShapeDtypeStruct(mesh1_state.s...  3.49 us
    pallas_call x2, Pallas kernels, spread(): pl.pallas_call(functools.partial(spread_kernel, first, scale), out_shape=...  2.25 us
    pallas_call x1, Pallas kernels, body(): pl.pallas_call(functools.partial(pack_kernel, dirs, glon, m1lon), out_sha...  1.53 us
  transfers between devices with their start and end apart: 29, of which 9 were waited for; matrix products, arithmetic and copies ran while one was open for 0% of the time, Pallas kernels for 10%

profile of v4, /device:TPU:0, one launch (start us, length us, event | category | flops | bytes accessed | tf_op | source)
XLA Modules:
  0.0 65.0 jit_solution(13963514839350007615)
XLA Ops:
  0.6 1.5 %pack_halos.1 = (bf16[32,32,256]{2,1,0:T(8,128)(2,1)S(1)}, bf16[16,16,256]{2,1,0:T(8,128)(2,1)S(1)}, bf16[16,16,256]{2,1,0:T(8,128)(2,1)S(1)}, bf16[8,16,256]{2,...) custom-call(bf16[32,32,256]{2,1,0:T(8,128)(2,1)} %refs_0_.1, ...), custom_call_target="tpu_custom_call" | custom-call | tf_op jit(solution)/shard_map/pack_halos/pallas_call | solution.py:690
  2.7 4.7 %collective-permute-start.1 = (bf16[416,256]{1,0:T(8,128)(2,1)S(1)}, bf16[416,256]{1,0:T(8,128)(2,1)S(1)}, u32[]{:S(2)}, u32[]{:S(2)}) collective-permute-start(bf16[416,256]{1,0:T(8,128)(2,1)S(1)} %get-tuple-element.41), channel_id=1, source_target_pairs={{0,13},{1,4},{2,15},{3,6},{4,1},{5,8},{6,3},{7,10},{8,5},{9,12},{1... | collective-permute-start | bytes 638984 | tf_op jit(solution)/shard_map/ppermute | solution.py:25
  7.4 1.5 %collective-permute-start.2 = (bf16[352,256]{1,0:T(8,128)(2,1)S(1)}, bf16[352,256]{1,0:T(8,128)(2,1)S(1)}, u32[]{:S(2)}, u32[]{:S(2)}) collective-permute-start(bf16[352,256]{1,0:T(8,128)(2,1)S(1)} %get-tuple-element.42), channel_id=1, source_target_pairs={{0,2},{1,3},{2,0},{3,1},{4,6},{5,7},{6,4},{7,5},{8,10},{9,11},{10,... | collective-permute-start | bytes 540680 | tf_op jit(solution)/shard_map/ppermute | solution.py:25
  8.9 1.6 %collective-permute-start.4 = (bf16[112,256]{1,0:T(8,128)(2,1)S(1)}, bf16[112,256]{1,0:T(8,128)(2,1)S(1)}, u32[]{:S(2)}, u32[]{:S(2)}) collective-permute-start(bf16[112,256]{1,0:T(8,128)(2,1)S(1)} %get-tuple-element.44), channel_id=1, source_target_pairs={{0,15},{1,6},{2,13},{3,4},{4,3},{5,10},{6,1},{7,8},{8,7},{9,14},{1... | collective-permute-start | bytes 172040 | tf_op jit(solution)/shard_map/ppermute | solution.py:25
  10.5 5.5 %inner_rows.1 = (bf16[16,2,128,256]{3,2,1,0:T(8,128)(2,1)S(1)}, bf16[16,2,128,256]{3,2,1,0:T(8,128)(2,1)S(1)}, f32[16,16,256]{2,1,0:T(8,128)S(1)}, f32[16,16,256]{2,1,0:T(8,128)S(1)}, bf16[9,256,256]{2,1,0:T(8,128)(2,1)S(1)}) custom-call(bf16[32,32,256]{2,1,0:T(8,128)(2,1)S(1)} %get-tuple-element.33.grid.refs_0_, ...), custom_call_target="tpu_custom_call" | custom-call | flops 4000000000 | bytes 8000000 | tf_op jit(solution)/shard_map/inner_rows/pallas_call | solution.py:704
  16.1 11.3 %sweep.1 = (bf16[16,16,256]{2,1,0:T(8,128)(2,1)}, f32[6,128,256]{2,1,0:T(8,128)S(1)}, bf16[6,128,256]{2,1,0:T(8,128)(2,1)S(1)}, f32[256,256]{1,0:T(8,128)S(1)}, ...) custom-call(bf16[32,32,256]{2,1,0:T(8,128)(2,1)S(1)} %get-tuple-elem, ...), custom_call_target="tpu_custom_call" | custom-call | tf_op jit(solution)/shard_map/sweep/pallas_call | solution.py:783
  27.4 1.7 %collective-permute-done.5 = bf16[6,128,256]{2,1,0:T(8,128)(2,1)S(1)} collective-permute-done((bf16[6,128,256]{2,1,0:T(8,128)(2,1)S(1)}, bf16[6,128,256]{2,1,0:T(8,128)(2,1)S(1)}, u32[]{:S(2)}, u32[]{:S(2)}) %collective-permute-start.5) | collective-permute-done | bytes 393248 | tf_op jit(solution)/shard_map/ppermute | solution.py:25
  29.2 3.5 %encoder_back.1 = (bf16[16,16,256]{2,1,0:T(8,128)(2,1)}, f32[3,128,256]{2,1,0:T(8,128)S(1)}, bf16[3,128,256]{2,1,0:T(8,128)(2,1)S(1)}) custom-call(bf16[16,16,256]{2,1,0:T(8,128)(2,1)S(1)} %get-tuple-element.34.m1.refs_1_, bf16[9,256,256]{2,1,0:T(8,128)(2,1)S(1)} %get-tuple-element.45.refs_12_.weights, f32[256,256]{1,0:T(8,128)S(1)} %get-tuple-element.50.fine_delta, ...), custom_call_target="tpu_custom_call" | custom-call | flops 3000000000 | bytes 8000000 | tf_op jit(solution)/shard_map/encoder_back/pallas_call | solution.py:804
  32.9 1.6 %collective-permute-start.18 = (bf16[6,32,256]{2,1,0:T(8,128)(2,1)S(1)}, bf16[6,32,256]{2,1,0:T(8,128)(2,1)S(1)}, u32[]{:S(2)}, u32[]{:S(2)}) collective-permute-start(bf16[6,32,256]{2,1,0:T(8,128)(2,1)S(1)} %get-tuple-element.63), channel_id=1, source_target_pairs={{0,4},{2,6},{4,0},{6,2},{8,12},{10,14},{12,8},{14,10},{1,5},{3,7},... | collective-permute-start | bytes 294920 | tf_op jit(solution)/shard_map/ppermute | solution.py:25
  35.1 1.4 %collective-permute-start.20 = (bf16[6,32,256]{2,1,0:T(8,128)(2,1)S(1)}, bf16[6,32,256]{2,1,0:T(8,128)(2,1)S(1)}, u32[]{:S(2)}, u32[]{:S(2)}) collective-permute-start(bf16[6,32,256]{2,1,0:T(8,128)(2,1)S(1)} %get-tuple-element.65), channel_id=1, source_target_pairs={{0,6},{2,4},{4,2},{6,0},{8,14},{10,12},{12,10},{14,8},{1,7},{3,5},... | collective-permute-start | bytes 294920 | tf_op jit(solution)/shard_map/ppermute | solution.py:25
  36.6 1.6 %collective-permute-start.7 = (bf16[3,32,256]{2,1,0:T(8,128)(2,1)S(1)}, bf16[3,32,256]{2,1,0:T(8,128)(2,1)S(1)}, u32[]{:S(2)}, u32[]{:S(2)}) collective-permute-start(bf16[3,32,256]{2,1,0:T(8,128)(2,1)S(1)} %get-tuple-element.66), channel_id=1, source_target_pairs={{0,4},{2,6},{4,0},{6,2},{8,12},{10,14},{12,8},{14,10},{1,5},{3,7},... | collective-permute-start | bytes 147464 | tf_op jit(solution)/shard_map/ppermute | solution.py:25
  38.7 1.4 %collective-permute-start.9 = (bf16[3,32,256]{2,1,0:T(8,128)(2,1)S(1)}, bf16[3,32,256]{2,1,0:T(8,128)(2,1)S(1)}, u32[]{:S(2)}, u32[]{:S(2)}) collective-permute-start(bf16[3,32,256]{2,1,0:T(8,128)(2,1)S(1)} %get-tuple-element.68), channel_id=1, source_target_pairs={{0,6},{2,4},{4,2},{6,0},{8,14},{10,12},{12,10},{14,8},{1,7},{3,5},... | collective-permute-start | bytes 147464 | tf_op jit(solution)/shard_map/ppermute | solution.py:25
  40.1 2.4 %collective-permute-done.19 = bf16[6,32,256]{2,1,0:T(8,128)(2,1)S(1)} collective-permute-done((bf16[6,32,256]{2,1,0:T(8,128)(2,1)S(1)}, bf16[6,32,256]{2,1,0:T(8,128)(2,1)S(1)}, u32[]{:S(2)}, u32[]{:S(2)}) %collective-permute-start.19) | collective-permute-done | bytes 98336 | tf_op jit(solution)/shard_map/ppermute | solution.py:25
  43.7 2.1 %collective-permute-start.10 = (bf16[3,32,256]{2,1,0:T(8,128)(2,1)S(1)}, bf16[3,32,256]{2,1,0:T(8,128)(2,1)S(1)}, u32[]{:S(2)}, u32[]{:S(2)}) collective-permute-start(bf16[3,32,256]{2,1,0:T(8,128)(2,1)S(1)} %fusion.8), channel_id=1, source_target_pairs={{0,8},{2,10},{4,12},{6,14},{8,0},{10,2},{12,4},{14,6},{1,9},{3,11}... | collective-permute-start | bytes 147464 | tf_op jit(solution)/shard_map/ppermute | solution.py:25
  45.9 3.5 %collective-permute-done.21 = bf16[6,32,256]{2,1,0:T(8,128)(2,1)S(1)} collective-permute-done((bf16[6,32,256]{2,1,0:T(8,128)(2,1)S(1)}, bf16[6,32,256]{2,1,0:T(8,128)(2,1)S(1)}, u32[]{:S(2)}, u32[]{:S(2)}) %collective-permute-start.21) | collective-permute-done | bytes 98336 | tf_op jit(solution)/shard_map/ppermute | solution.py:25
  49.5 1.0 %collective-permute-start.23 = (bf16[6,32,256]{2,1,0:T(8,128)(2,1)S(1)}, bf16[6,32,256]{2,1,0:T(8,128)(2,1)S(1)}, u32[]{:S(2)}, u32[]{:S(2)}) collective-permute-start(bf16[6,32,256]{2,1,0:T(8,128)(2,1)S(1)} %add_convert_fusion.refs_0_), channel_id=1, source_target_pairs={{0,2},{2,0},{4,6},{6,4},{8,10},{10,8},{12,14},{14,12},{1,3},{3,1},... | collective-permute-start | bytes 294920 | tf_op jit(solution)/shard_map/ppermute | solution.py:25
  50.5 2.5 %collective-permute-start.24 = (bf16[6,32,256]{2,1,0:T(8,128)(2,1)S(1)}, bf16[6,32,256]{2,1,0:T(8,128)(2,1)S(1)}, u32[]{:S(2)}, u32[]{:S(2)}) collective-permute-start(bf16[6,32,256]{2,1,0:T(8,128)(2,1)S(1)} %add_convert_fusion.refs_0_), channel_id=1, source_target_pairs={{0,6},{2,4},{4,2},{6,0},{8,14},{10,12},{12,10},{14,8},{1,7},{3,5},... | collective-permute-start | bytes 294920 | tf_op jit(solution)/shard_map/ppermute | solution.py:25
  53.1 1.0 %collective-permute-done.22.refs_1_ = bf16[6,32,256]{2,1,0:T(8,128)(2,1)S(1)} collective-permute-done((bf16[6,32,256]{2,1,0:T(8,128)(2,1)S(1)}, bf16[6,32,256]{2,1,0:T(8,128)(2,1)S(1)}, u32[]{:S(2)}, u32[]{:S(2)}) %collective-permute-start.22) | collective-permute-done | bytes 98336 | tf_op jit(solution)/shard_map/ppermute | solution.py:25
  54.6 1.4 %collective-permute-done.24.refs_3_ = bf16[6,32,256]{2,1,0:T(8,128)(2,1)S(1)} collective-permute-done((bf16[6,32,256]{2,1,0:T(8,128)(2,1)S(1)}, bf16[6,32,256]{2,1,0:T(8,128)(2,1)S(1)}, u32[]{:S(2)}, u32[]{:S(2)}) %collective-permute-start.24) | collective-permute-done | bytes 98336 | tf_op jit(solution)/shard_map/ppermute | solution.py:25
  56.0 1.1 %collective-permute-start.12 = (bf16[3,32,256]{2,1,0:T(8,128)(2,1)S(1)}, bf16[3,32,256]{2,1,0:T(8,128)(2,1)S(1)}, u32[]{:S(2)}, u32[]{:S(2)}) collective-permute-start(bf16[3,32,256]{2,1,0:T(8,128)(2,1)S(1)} %add_convert_fusion.1.refs_0_), channel_id=1, source_target_pairs={{0,2},{2,0},{4,6},{6,4},{8,10},{10,8},{12,14},{14,12},{1,3},{3,1},... | collective-permute-start | bytes 147464 | tf_op jit(solution)/shard_map/ppermute | solution.py:25
  57.1 2.8 %collective-permute-start.13 = (bf16[3,32,256]{2,1,0:T(8,128)(2,1)S(1)}, bf16[3,32,256]{2,1,0:T(8,128)(2,1)S(1)}, u32[]{:S(2)}, u32[]{:S(2)}) collective-permute-start(bf16[3,32,256]{2,1,0:T(8,128)(2,1)S(1)} %add_convert_fusion.1.refs_0_), channel_id=1, source_target_pairs={{0,6},{2,4},{4,2},{6,0},{8,14},{10,12},{12,10},{14,8},{1,7},{3,5},... | collective-permute-start | bytes 147464 | tf_op jit(solution)/shard_map/ppermute | solution.py:25
  60.4 1.7 %collective-permute-done.13.refs_3_ = bf16[3,32,256]{2,1,0:T(8,128)(2,1)S(1)} collective-permute-done((bf16[3,32,256]{2,1,0:T(8,128)(2,1)S(1)}, bf16[3,32,256]{2,1,0:T(8,128)(2,1)S(1)}, u32[]{:S(2)}, u32[]{:S(2)}) %collective-permute-start.13) | collective-permute-done | bytes 49184 | tf_op jit(solution)/shard_map/ppermute | solution.py:25
  62.7 1.3 %spread_3.1.refs_8_ = f32[9,256,256]{2,1,0:T(8,128)} custom-call(bf16[6,32,256]{2,1,0:T(8,128)(2,1)S(1)} %add_convert_fusion.refs_0_, bf16[6,32,256]{2,1,0:T(8,128)(2,1)S(1)} %collective-permute-done.22.refs_1_, bf16[6,32,256]{2,1,0:T(8,128)(2,1)S(1)} %collective-permute-done.23.refs_2_, bf16[6,32,256]{2,1,0:T(8,128)(2,1)S(1)} %collective-permute-done.24.refs_3_, ...), custom_call_target="tpu_custom_call" | custom-call | tf_op jit(solution)/shard_map/spread_3/pallas_call | solution.py:825
  64.0 1.0 %spread_0.1 = f32[9,256,256]{2,1,0:T(8,128)} custom-call(bf16[3,32,256]{2,1,0:T(8,128)(2,1)S(1)} %add_convert_fusion.1.refs_0_, bf16[3,32,256]{2,1,0:T(8,128)(2,1)S(1)} %collective-permute-done.11.refs_1_, bf16[3,32,256]{2,1,0:T(8,128)(2,1)S(1)} %collective-permute-done.12.refs_2_, ...), custom_call_target="tpu_custom_call", output_to_operand_aliasing={{}: (8, {})} | custom-call | tf_op jit(solution)/shard_map/spread_0/pallas_call | solution.py:825
  (48 shorter events, 5.1 us)
Async XLA Ops:
  2.2 13.9 %collective-permute-start = (bf16[416,256]{1,0:T(8,128)(2,1)S(1)}, bf16[416,256]{1,0:T(8,128)(2,1)S(1)}, u32[]{:S(2)}, u32[]{:S(2)}) collective-permute-start(bf16[416,256]{1,0:T(8,128)(2,1)S(1)} %get-tuple-element.40), channel_id=1, source_target_pairs={{0,1},{1,0},{2,3},{3,2},{4,5},{5,4},{6,7},{7,6},{8,9},{9,8},{10,11... | collective-permute-start | bytes 638984 | tf_op jit(solution)/shard_map/ppermute | solution.py:25
  2.7 13.4 %collective-permute-start.1 = (bf16[416,256]{1,0:T(8,128)(2,1)S(1)}, bf16[416,256]{1,0:T(8,128)(2,1)S(1)}, u32[]{:S(2)}, u32[]{:S(2)}) collective-permute-start(bf16[416,256]{1,0:T(8,128)(2,1)S(1)} %get-tuple-element.41), channel_id=1, source_target_pairs={{0,13},{1,4},{2,15},{3,6},{4,1},{5,8},{6,3},{7,10},{8,5},{9,12},{1... | collective-permute-start | bytes 638984 | tf_op jit(solution)/shard_map/ppermute | solution.py:25
  7.4 8.6 %collective-permute-start.2 = (bf16[352,256]{1,0:T(8,128)(2,1)S(1)}, bf16[352,256]{1,0:T(8,128)(2,1)S(1)}, u32[]{:S(2)}, u32[]{:S(2)}) collective-permute-start(bf16[352,256]{1,0:T(8,128)(2,1)S(1)} %get-tuple-element.42), channel_id=1, source_target_pairs={{0,2},{1,3},{2,0},{3,1},{4,6},{5,7},{6,4},{7,5},{8,10},{9,11},{10,... | collective-permute-start | bytes 540680 | tf_op jit(solution)/shard_map/ppermute | solution.py:25
  8.9 7.1 %collective-permute-start.3 = (bf16[112,256]{1,0:T(8,128)(2,1)S(1)}, bf16[112,256]{1,0:T(8,128)(2,1)S(1)}, u32[]{:S(2)}, u32[]{:S(2)}) collective-permute-start(bf16[112,256]{1,0:T(8,128)(2,1)S(1)} %get-tuple-element.43), channel_id=1, source_target_pairs={{0,3},{1,2},{2,1},{3,0},{4,7},{5,6},{6,5},{7,4},{8,11},{9,10},{10,... | collective-permute-start | bytes 172040 | tf_op jit(solution)/shard_map/ppermute | solution.py:25
  8.9 7.1 %collective-permute-start.4 = (bf16[112,256]{1,0:T(8,128)(2,1)S(1)}, bf16[112,256]{1,0:T(8,128)(2,1)S(1)}, u32[]{:S(2)}, u32[]{:S(2)}) collective-permute-start(bf16[112,256]{1,0:T(8,128)(2,1)S(1)} %get-tuple-element.44), channel_id=1, source_target_pairs={{0,15},{1,6},{2,13},{3,4},{4,3},{5,10},{6,1},{7,8},{8,7},{9,14},{1... | collective-permute-start | bytes 172040 | tf_op jit(solution)/shard_map/ppermute | solution.py:25
  32.7 3.8 %collective-permute-start.6 = (bf16[3,128,256]{2,1,0:T(8,128)(2,1)S(1)}, bf16[3,128,256]{2,1,0:T(8,128)(2,1)S(1)}, u32[]{:S(2)}, u32[]{:S(2)}) collective-permute-start(bf16[3,128,256]{2,1,0:T(8,128)(2,1)S(1)} %get-tuple-element.61), channel_id=1, source_target_pairs={{0,1},{1,0},{2,3},{3,2},{4,5},{5,4},{6,7},{7,6},{8,9},{9,8},{10,11... | collective-permute-start | bytes 589832 | tf_op jit(solution)/shard_map/ppermute | solution.py:25
  32.9 5.8 %collective-permute-start.18 = (bf16[6,32,256]{2,1,0:T(8,128)(2,1)S(1)}, bf16[6,32,256]{2,1,0:T(8,128)(2,1)S(1)}, u32[]{:S(2)}, u32[]{:S(2)}) collective-permute-start(bf16[6,32,256]{2,1,0:T(8,128)(2,1)S(1)} %get-tuple-element.63), channel_id=1, source_target_pairs={{0,4},{2,6},{4,0},{6,2},{8,12},{10,14},{12,8},{14,10},{1,5},{3,7},... | collective-permute-start | bytes 294920 | tf_op jit(solution)/shard_map/ppermute | solution.py:25
  34.6 7.9 %collective-permute-start.19 = (bf16[6,32,256]{2,1,0:T(8,128)(2,1)S(1)}, bf16[6,32,256]{2,1,0:T(8,128)(2,1)S(1)}, u32[]{:S(2)}, u32[]{:S(2)}) collective-permute-start(bf16[6,32,256]{2,1,0:T(8,128)(2,1)S(1)} %get-tuple-element.64), channel_id=1, source_target_pairs={{0,2},{2,0},{4,6},{6,4},{8,10},{10,8},{12,14},{14,12},{1,3},{3,1},... | collective-permute-start | bytes 294920 | tf_op jit(solution)/shard_map/ppermute | solution.py:25
  35.1 7.4 %collective-permute-start.20 = (bf16[6,32,256]{2,1,0:T(8,128)(2,1)S(1)}, bf16[6,32,256]{2,1,0:T(8,128)(2,1)S(1)}, u32[]{:S(2)}, u32[]{:S(2)}) collective-permute-start(bf16[6,32,256]{2,1,0:T(8,128)(2,1)S(1)} %get-tuple-element.65), channel_id=1, source_target_pairs={{0,6},{2,4},{4,2},{6,0},{8,14},{10,12},{12,10},{14,8},{1,7},{3,5},... | collective-permute-start | bytes 294920 | tf_op jit(solution)/shard_map/ppermute | solution.py:25
  36.6 6.5 %collective-permute-start.7 = (bf16[3,32,256]{2,1,0:T(8,128)(2,1)S(1)}, bf16[3,32,256]{2,1,0:T(8,128)(2,1)S(1)}, u32[]{:S(2)}, u32[]{:S(2)}) collective-permute-start(bf16[3,32,256]{2,1,0:T(8,128)(2,1)S(1)} %get-tuple-element.66), channel_id=1, source_target_pairs={{0,4},{2,6},{4,0},{6,2},{8,12},{10,14},{12,8},{14,10},{1,5},{3,7},... | collective-permute-start | bytes 147464 | tf_op jit(solution)/shard_map/ppermute | solution.py:25
  38.2 4.9 %collective-permute-start.8 = (bf16[3,32,256]{2,1,0:T(8,128)(2,1)S(1)}, bf16[3,32,256]{2,1,0:T(8,128)(2,1)S(1)}, u32[]{:S(2)}, u32[]{:S(2)}) collective-permute-start(bf16[3,32,256]{2,1,0:T(8,128)(2,1)S(1)} %get-tuple-element.67), channel_id=1, source_target_pairs={{0,2},{2,0},{4,6},{6,4},{8,10},{10,8},{12,14},{14,12},{1,3},{3,1},... | collective-permute-start | bytes 147464 | tf_op jit(solution)/shard_map/ppermute | solution.py:25
  38.7 5.0 %collective-permute-start.9 = (bf16[3,32,256]{2,1,0:T(8,128)(2,1)S(1)}, bf16[3,32,256]{2,1,0:T(8,128)(2,1)S(1)}, u32[]{:S(2)}, u32[]{:S(2)}) collective-permute-start(bf16[3,32,256]{2,1,0:T(8,128)(2,1)S(1)} %get-tuple-element.68), channel_id=1, source_target_pairs={{0,6},{2,4},{4,2},{6,0},{8,14},{10,12},{12,10},{14,8},{1,7},{3,5},... | collective-permute-start | bytes 147464 | tf_op jit(solution)/shard_map/ppermute | solution.py:25
  42.6 6.8 %collective-permute-start.21 = (bf16[6,32,256]{2,1,0:T(8,128)(2,1)S(1)}, bf16[6,32,256]{2,1,0:T(8,128)(2,1)S(1)}, u32[]{:S(2)}, u32[]{:S(2)}) collective-permute-start(bf16[6,32,256]{2,1,0:T(8,128)(2,1)S(1)} %fusion.2), channel_id=1, source_target_pairs={{0,8},{2,10},{4,12},{6,14},{8,0},{10,2},{12,4},{14,6},{1,9},{3,11}... | collective-permute-start | bytes 294920 | tf_op jit(solution)/shard_map/ppermute | solution.py:25
  43.7 9.2 %collective-permute-start.10 = (bf16[3,32,256]{2,1,0:T(8,128)(2,1)S(1)}, bf16[3,32,256]{2,1,0:T(8,128)(2,1)S(1)}, u32[]{:S(2)}, u32[]{:S(2)}) collective-permute-start(bf16[3,32,256]{2,1,0:T(8,128)(2,1)S(1)} %fusion.8), channel_id=1, source_target_pairs={{0,8},{2,10},{4,12},{6,14},{8,0},{10,2},{12,4},{14,6},{1,9},{3,11}... | collective-permute-start | bytes 147464 | tf_op jit(solution)/shard_map/ppermute | solution.py:25
  49.4 4.7 %collective-permute-start.22 = (bf16[6,32,256]{2,1,0:T(8,128)(2,1)S(1)}, bf16[6,32,256]{2,1,0:T(8,128)(2,1)S(1)}, u32[]{:S(2)}, u32[]{:S(2)}) collective-permute-start(bf16[6,32,256]{2,1,0:T(8,128)(2,1)S(1)} %add_convert_fusion.refs_0_), channel_id=1, source_target_pairs={{0,4},{2,6},{4,0},{6,2},{8,12},{10,14},{12,8},{14,10},{1,5},{3,7},... | collective-permute-start | bytes 294920 | tf_op jit(solution)/shard_map/ppermute | solution.py:25
  49.5 4.7 %collective-permute-start.23 = (bf16[6,32,256]{2,1,0:T(8,128)(2,1)S(1)}, bf16[6,32,256]{2,1,0:T(8,128)(2,1)S(1)}, u32[]{:S(2)}, u32[]{:S(2)}) collective-permute-start(bf16[6,32,256]{2,1,0:T(8,128)(2,1)S(1)} %add_convert_fusion.refs_0_), channel_id=1, source_target_pairs={{0,2},{2,0},{4,6},{6,4},{8,10},{10,8},{12,14},{14,12},{1,3},{3,1},... | collective-permute-start | bytes 294920 | tf_op jit(solution)/shard_map/ppermute | solution.py:25
  50.5 5.5 %collective-permute-start.24 = (bf16[6,32,256]{2,1,0:T(8,128)(2,1)S(1)}, bf16[6,32,256]{2,1,0:T(8,128)(2,1)S(1)}, u32[]{:S(2)}, u32[]{:S(2)}) collective-permute-start(bf16[6,32,256]{2,1,0:T(8,128)(2,1)S(1)} %add_convert_fusion.refs_0_), channel_id=1, source_target_pairs={{0,6},{2,4},{4,2},{6,0},{8,14},{10,12},{12,10},{14,8},{1,7},{3,5},... | collective-permute-start | bytes 294920 | tf_op jit(solution)/shard_map/ppermute | solution.py:25
  52.9 4.1 %collective-permute-start.25 = (bf16[6,32,256]{2,1,0:T(8,128)(2,1)S(1)}, bf16[6,32,256]{2,1,0:T(8,128)(2,1)S(1)}, u32[]{:S(2)}, u32[]{:S(2)}) collective-permute-start(bf16[6,32,256]{2,1,0:T(8,128)(2,1)S(1)} %add_convert_fusion.refs_0_), channel_id=1, source_target_pairs={{0,1},{1,0},{2,3},{3,2},{4,5},{5,4},{6,7},{7,6},{8,9},{9,8},{10,11... | collective-permute-start | bytes 294920 | tf_op jit(solution)/shard_map/ppermute | solution.py:25
  53.0 6.9 %collective-permute-start.11 = (bf16[3,32,256]{2,1,0:T(8,128)(2,1)S(1)}, bf16[3,32,256]{2,1,0:T(8,128)(2,1)S(1)}, u32[]{:S(2)}, u32[]{:S(2)}) collective-permute-start(bf16[3,32,256]{2,1,0:T(8,128)(2,1)S(1)} %add_convert_fusion.1.refs_0_), channel_id=1, source_target_pairs={{0,4},{2,6},{4,0},{6,2},{8,12},{10,14},{12,8},{14,10},{1,5},{3,7},... | collective-permute-start | bytes 147464 | tf_op jit(solution)/shard_map/ppermute | solution.py:25
  54.1 8.0 %collective-permute-start.26 = (bf16[6,32,256]{2,1,0:T(8,128)(2,1)S(1)}, bf16[6,32,256]{2,1,0:T(8,128)(2,1)S(1)}, u32[]{:S(2)}, u32[]{:S(2)}) collective-permute-start(bf16[6,32,256]{2,1,0:T(8,128)(2,1)S(1)} %collective-permute-done.22.refs_1_), channel_id=1, source_target_pairs={{0,1},{1,0},{2,3},{3,2},{4,5},{5,4},{6,7},{7,6},{8,9},{9,8},{10,11... | collective-permute-start | bytes 294920 | tf_op jit(solution)/shard_map/ppermute | solution.py:25
  54.2 8.4 %collective-permute-start.27 = (bf16[6,32,256]{2,1,0:T(8,128)(2,1)S(1)}, bf16[6,32,256]{2,1,0:T(8,128)(2,1)S(1)}, u32[]{:S(2)}, u32[]{:S(2)}) collective-permute-start(bf16[6,32,256]{2,1,0:T(8,128)(2,1)S(1)} %collective-permute-done.23.refs_2_), channel_id=1, source_target_pairs={{0,1},{1,0},{2,3},{3,2},{4,5},{5,4},{6,7},{7,6},{8,9},{9,8},{10,11... | collective-permute-start | bytes 294920 | tf_op jit(solution)/shard_map/ppermute | solution.py:25
  56.0 4.1 %collective-permute-start.12 = (bf16[3,32,256]{2,1,0:T(8,128)(2,1)S(1)}, bf16[3,32,256]{2,1,0:T(8,128)(2,1)S(1)}, u32[]{:S(2)}, u32[]{:S(2)}) collective-permute-start(bf16[3,32,256]{2,1,0:T(8,128)(2,1)S(1)} %add_convert_fusion.1.refs_0_), channel_id=1, source_target_pairs={{0,2},{2,0},{4,6},{6,4},{8,10},{10,8},{12,14},{14,12},{1,3},{3,1},... | collective-permute-start | bytes 147464 | tf_op jit(solution)/shard_map/ppermute | solution.py:25
  57.1 5.0 %collective-permute-start.13 = (bf16[3,32,256]{2,1,0:T(8,128)(2,1)S(1)}, bf16[3,32,256]{2,1,0:T(8,128)(2,1)S(1)}, u32[]{:S(2)}, u32[]{:S(2)}) collective-permute-start(bf16[3,32,256]{2,1,0:T(8,128)(2,1)S(1)} %add_convert_fusion.1.refs_0_), channel_id=1, source_target_pairs={{0,6},{2,4},{4,2},{6,0},{8,14},{10,12},{12,10},{14,8},{1,7},{3,5},... | collective-permute-start | bytes 147464 | tf_op jit(solution)/shard_map/ppermute | solution.py:25
  60.1 3.9 %collective-permute-start.14 = (bf16[3,32,256]{2,1,0:T(8,128)(2,1)S(1)}, bf16[3,32,256]{2,1,0:T(8,128)(2,1)S(1)}, u32[]{:S(2)}, u32[]{:S(2)}) collective-permute-start(bf16[3,32,256]{2,1,0:T(8,128)(2,1)S(1)} %add_convert_fusion.1.refs_0_), channel_id=1, source_target_pairs={{0,1},{1,0},{2,3},{3,2},{4,5},{5,4},{6,7},{7,6},{8,9},{9,8},{10,11... | collective-permute-start | bytes 147464 | tf_op jit(solution)/shard_map/ppermute | solution.py:25
  (5 other events, 9.7 us)

commit v5 on v4

--- a/solution.py
+++ b/solution.py
@@ -9,8 +9,8 @@
 
 LOW = jnp.bfloat16
 WIDE = jnp.float32
-VMEM_BYTES = 36 * 1024 * 1024
-HALO_ROWS = 2
+VMEM_BYTES = 24 * 1024 * 1024
+HALO_ROWS = 7
 
 SIDE_ROWS = 416
 BAND_ROWS = 352
@@ -609,20 +609,57 @@
     put_halves(acc, keep, send, 0, rep)
 
 
-def spread_kernel(first, scale, *refs):
-    mine, theirs = refs[:4], refs[4:8]
-    out, stage, sem = refs[-3:]
-    count = stage.shape[0]
+def block_place():
+    return (lax.axis_index("lat") % 2) * 2 + lax.axis_index("lon") % 2
+
+
+def quarters_kernel(kept_first, got_first, kept, got, own, *pieces):
+    place = block_place()
+    for step in range(4):
+        rows = pl.ds(pl.multiple_of((place ^ step) * 32, 32), 32)
+        for first, mine, other in ((0, kept_first, got_first), (3, kept, got)):
+            total = mine[:, rows, :] + other[:, rows, :].astype(WIDE)
+            at = slice(first, first + mine.shape[0])
+            if step == 0:
+                own[at] = total
+            else:
+                pieces[step - 1][at] = total.astype(LOW)
+
+
+def add_kernel(*refs):
+    total = refs[0][...].astype(WIDE)
+    for ref in refs[1:-1]:
+        total = total + ref[...].astype(WIDE)
+    refs[-1][...] = total.astype(LOW)
+
+
+def small_kernel(kernel, out_shape, name, *values):
+    vmem = pl.BlockSpec(memory_space=pltpu.VMEM)
+    return pl.pallas_call(
+        kernel,
+        out_shape=out_shape,
+        in_specs=[vmem] * len(values),
+        out_specs=jax.tree.map(lambda _: vmem, out_shape),
+        compiler_params=pltpu.CompilerParams(vmem_limit_bytes=8 * 1024 * 1024),
+        name=name,
+    )(*values)
+
+
+def spread_kernel(scale, *refs):
+    pieces, (out, stage, sems) = refs[:8], refs[8:]
     rep = lax.axis_index("rep")
-    place = (lax.axis_index("lat") % 2) * 2 + lax.axis_index("lon") % 2
-    for step in range(4):
-        at = (place ^ step) * 32
-        for half, pieces in ((rep, mine), (1 - rep, theirs)):
-            rows = pl.ds(pl.multiple_of(half * 128 + at, 32), 32)
-            stage[:, rows, :] = pieces[step][...].astype(WIDE) * scale
-    copy = pltpu.make_async_copy(stage, out.at[first : first + count], sem)
-    copy.start()
-    copy.wait()
+    place = block_place()
+    copies = []
+    for k in range(9):
+        for step in range(4):
+            at = (place ^ step) * 32
+            for half, piece in ((rep, pieces[step]), (1 - rep, pieces[4 + step])):
+                rows = pl.ds(pl.multiple_of(half * 128 + at, 32), 32)
+                stage[k, rows, :] = piece[k].astype(WIDE) * scale
+        copies.append(pltpu.make_async_copy(stage.at[k], out.at[k], sems.at[k]))
+        copies[-1].start()
+    for copy in copies:
+        copy.wait()
 
 
 def flat_main(dirs, n_lat, *refs):
@@ -635,46 +672,47 @@
     main_kernel(dirs, n_lat, own, sides, bands, weights, outs, scratch)
 
 
-def sum_over_slice(kept, sent, mesh, then=None):
-    lat_size, lon_size = mesh.shape["lat"], mesh.shape["lon"]
-    rep = lax.axis_index("rep")
-    lat, lon = lax.axis_index("lat"), lax.axis_index("lon")
-    place = (lat % 2) * 2 + lon % 2
-
-    def between(values, lon_bit, lat_bit):
+class Reduction:
+    def __init__(self, mesh):
+        self.sizes = (mesh.shape["lon"], mesh.shape["lat"])
+
+    def between(self, values, lon_bit, lat_bit):
+        lat_size = self.sizes[1]
         return permute(
             values,
             ("lon", "lat"),
             lambda i: ((i // lat_size) ^ lon_bit) * lat_size + ((i % lat_size) ^ lat_bit),
-            (lon_size, lat_size),
+            self.sizes,
         )
 
-    def siblings(values):
+    def siblings(self, values):
         return permute(values, "rep", lambda i: i ^ 1, (2,))
 
-    half = kept + siblings(sent).astype(WIDE)
-    if then is not None:
-        half, value = lax.optimization_barrier((half, then))
-    count, rows, cols = half.shape
-    quarters = half.reshape(count, 4, rows // 4, cols)
-    total = lax.dynamic_index_in_dim(quarters, place, 1, keepdims=False)
-    for step in (1, 2, 3):
-        piece = lax.dynamic_index_in_dim(quarters, place ^ step, 1, keepdims=False).astype(LOW)
-        total = total + between(piece, step & 1, step >> 1).astype(WIDE)
-    bit = 2
-    while bit < lon_size:
-        rounded = total.astype(LOW)
-        total = rounded.astype(WIDE) + between(rounded, bit, 0).astype(WIDE)
-        bit *= 2
-    bit = 2
-    while bit < lat_size:
-        rounded = total.astype(LOW)
-        total = rounded.astype(WIDE) + between(rounded, 0, bit).astype(WIDE)
-        bit *= 2
-    own = total.astype(LOW)
-    pieces = [own] + [between(own, step & 1, step >> 1) for step in (1, 2, 3)]
-    pieces = pieces + [siblings(piece) for piece in pieces]
-    return pieces if then is None else (pieces, value)
+    def quarters(self, *halves):
+        _, rows, cols = halves[0].shape
+        shape = (9, rows // 4, cols)
+        shapes = [jax.ShapeDtypeStruct(shape, WIDE)] + [jax.ShapeDtypeStruct(shape, LOW)] * 3
+        return small_kernel(quarters_kernel, shapes, "quarters", *halves)
+
+    def block(self, quarters):
+        own, *others = quarters
+        got = [self.between(piece, step & 1, step >> 1) for step, piece in zip((1, 2, 3), others)]
+        shape = jax.ShapeDtypeStruct(own.shape, LOW)
+        return small_kernel(add_kernel, shape, "block_sum", own, *got)
+
+    def total(self, total):
+        shape = jax.ShapeDtypeStruct(total.shape, LOW)
+        for which, size in enumerate(self.sizes):
+            bit = 2
+            while bit < size:
+                other = self.between(total, *((bit, 0) if which == 0 else (0, bit)))
+                total = small_kernel(add_kernel, shape, "pair_sum", total, other)
+                bit *= 2
+        return total
+
+    def pieces(self, own):
+        mine = [own] + [self.between(own, step & 1, step >> 1) for step in (1, 2, 3)]
+        return mine + [self.siblings(piece) for piece in mine]
 
 
 def body(mesh, grid_state, mesh1_state, mesh2_state, grid_edges, up_edges, weights, cotangent):
@@ -800,7 +838,8 @@
         compiler_params=params,
         name="sweep",
     )(*own, *got_sides, *got_bands, weights)
-    pieces, fine_delta = sum_over_slice(kept, sent, mesh, fine_delta)
+    reduction = Reduction(mesh)
+    got = reduction.siblings(sent)
     mesh1_grad, kept_first, sent_first = pl.pallas_call(
         back_kernel,
         out_shape=[
@@ -817,23 +856,17 @@
     )(mesh1_state, weights, fine_delta, pool, ssum, sx_in, slope_in, sx_edge, slope_edge, hx, hslope)
     node_total = mesh1_state.shape[0] * mesh1_state.shape[1] * n_lat * n_lon * 2
     scale = float(node_total) ** (-0.5)
-    pieces_first = sum_over_slice(kept_first, sent_first, mesh)
-
-    def spread(pieces, first, before):
-        count = pieces[0].shape[0]
-        more = [] if before is None else [before]
-        return pl.pallas_call(
-            functools.partial(spread_kernel, first, scale),
-            out_shape=jax.ShapeDtypeStruct((9, 256, 256), WIDE),
-            in_specs=[vmem] * 8 + [hbm] * len(more),
-            out_specs=hbm,
-            scratch_shapes=[pltpu.VMEM((count, 256, 256), WIDE), pltpu.SemaphoreType.DMA],
-            input_output_aliases={8: 0} if more else {},
-            compiler_params=params,
-            name="spread_%d" % first,
-        )(*pieces, *more)
-
-    weight_grads = spread(pieces_first, 0, spread(pieces, 3, None))
+    quarters = reduction.quarters(kept_first, reduction.siblings(sent_first), kept, got)
+    pieces = reduction.pieces(reduction.total(reduction.block(quarters)))
+    weight_grads = pl.pallas_call(
+        functools.partial(spread_kernel, scale),
+        out_shape=jax.ShapeDtypeStruct((9, 256, 256), WIDE),
+        in_specs=[vmem] * 8,
+        out_specs=hbm,
+        scratch_shapes=[pltpu.VMEM((9, 256, 256), WIDE), pltpu.SemaphoreType.DMA((9,))],
+        compiler_params=params,
+        name="spread_gradients",
+    )(*pieces)
     return (mesh_out, mesh1_grad, weight_grads)
 
 

time: 65.1 us -> 63.1 us (0.969)
  waiting for transfers between devices: 12.6 us -> 22.7 us
  starting transfers between devices: 27.1 us -> 17.9 us
  Pallas kernels: 24.1 us -> 21.6 us
    ppermute x29 -> x18, waiting for transfers between devices: 12.6 us -> 22.7 us  [permute(): lax.ppermute(values, axes, [(i, j) for i, j in pairs if j is not None])]
    ppermute x29 -> x18, starting transfers between devices: 27.1 us -> 17.9 us  [permute(): lax.ppermute(values, axes, [(i, j) for i, j in pairs if j is not None])]
    pallas_call x1, Pallas kernels: 11.3 us -> 9.39 us  [body(): pl.pallas_call(functools.partial(flat_main, dirs, n_lat), out_shape=[jax....]
    pallas_call x2 -> x4, Pallas kernels: 2.25 us -> 1.71 us  [the longest x1 1.51 us: body(): pl.pallas_call(functools.partial(spread_kernel, scale), out_shape=jax.Sha...]
  transfers between devices with their start and end apart: 29 -> 18, of which waited for: 9 -> 10; matrix products, arithmetic and copies ran while one was open for 0% -> 0% of each run, Pallas kernels for 10% -> 14%
where the time goes in v5:
time: 63.1 us; the launch traced here: 62.9 us
  waiting for transfers between devices  22.7 us (36%)
  Pallas kernels  21.6 us (34%)
  starting transfers between devices  17.9 us (28%)
  between operations  0.73 us (1%)
    ppermute x18, waiting for transfers between devices, permute(): lax.ppermute(values, axes, [(i, j) for i, j in pairs if j is not None])  22.7 us
    ppermute x18, starting transfers between devices, permute(): lax.ppermute(values, axes, [(i, j) for i, j in pairs if j is not None])  17.9 us
    pallas_call x1, Pallas kernels, body(): pl.pallas_call(functools.partial(flat_main, dirs, n_lat), out_shape=[jax....  9.39 us
    pallas_call x1, Pallas kernels, body(): pl.pallas_call(inner_kernel, out_shape=[jax.ShapeDtypeStruct((16, 2, 128,...  5.49 us
    pallas_call x1, Pallas kernels, body(): pl.pallas_call(back_kernel, out_shape=[jax.ShapeDtypeStruct(mesh1_state.s...  3.48 us
    pallas_call x1, Pallas kernels, body(): pl.pallas_call(functools.partial(pack_kernel, dirs, glon, m1lon), out_sha...  1.53 us
    pallas_call x1, Pallas kernels, body(): pl.pallas_call(functools.partial(spread_kernel, scale), out_shape=jax.Sha...  1.51 us
  transfers between devices with their start and end apart: 18, of which 10 were waited for; matrix products, arithmetic and copies ran while one was open for 0% of the time, Pallas kernels for 14%

profile of v5, /device:TPU:0, one launch (start us, length us, event | category | flops | bytes accessed | tf_op | source)
XLA Modules:
  0.0 62.9 jit_solution(14263971591966695841)
XLA Ops:
  0.6 1.5 %pack_halos.1 = (bf16[32,32,256]{2,1,0:T(8,128)(2,1)S(1)}, bf16[16,16,256]{2,1,0:T(8,128)(2,1)S(1)}, bf16[16,16,256]{2,1,0:T(8,128)(2,1)S(1)}, bf16[8,16,256]{2,...) custom-call(bf16[32,32,256]{2,1,0:T(8,128)(2,1)} %refs_0_.1, ...), custom_call_target="tpu_custom_call" | custom-call | tf_op jit(solution)/shard_map/pack_halos/pallas_call | solution.py:728
  2.2 2.5 %collective-permute-start.3 = (bf16[112,256]{1,0:T(8,128)(2,1)S(1)}, bf16[112,256]{1,0:T(8,128)(2,1)S(1)}, u32[]{:S(2)}, u32[]{:S(2)}) collective-permute-start(bf16[112,256]{1,0:T(8,128)(2,1)S(1)} %get-tuple-element.45), channel_id=1, source_target_pairs={{0,3},{1,2},{2,1},{3,0},{4,7},{5,6},{6,5},{7,4},{8,11},{9,10},{10,... | collective-permute-start | bytes 172040 | tf_op jit(solution)/shard_map/ppermute | solution.py:25
  4.6 3.8 %collective-permute-start.4 = (bf16[112,256]{1,0:T(8,128)(2,1)S(1)}, bf16[112,256]{1,0:T(8,128)(2,1)S(1)}, u32[]{:S(2)}, u32[]{:S(2)}) collective-permute-start(bf16[112,256]{1,0:T(8,128)(2,1)S(1)} %get-tuple-element.46), channel_id=1, source_target_pairs={{0,15},{1,6},{2,13},{3,4},{4,3},{5,10},{6,1},{7,8},{8,7},{9,14},{1... | collective-permute-start | bytes 172040 | tf_op jit(solution)/shard_map/ppermute | solution.py:25
  8.5 1.5 %collective-permute-start.2 = (bf16[352,256]{1,0:T(8,128)(2,1)S(1)}, bf16[352,256]{1,0:T(8,128)(2,1)S(1)}, u32[]{:S(2)}, u32[]{:S(2)}) collective-permute-start(bf16[352,256]{1,0:T(8,128)(2,1)S(1)} %get-tuple-element.44), channel_id=1, source_target_pairs={{0,2},{1,3},{2,0},{3,1},{4,6},{5,7},{6,4},{7,5},{8,10},{9,11},{10,... | collective-permute-start | bytes 540680 | tf_op jit(solution)/shard_map/ppermute | solution.py:25
  10.0 0.6 collective-permute-start.1
  10.5 5.5 %inner_rows.1 = (bf16[16,2,128,256]{3,2,1,0:T(8,128)(2,1)S(1)}, bf16[16,2,128,256]{3,2,1,0:T(8,128)(2,1)S(1)}, f32[16,16,256]{2,1,0:T(8,128)S(1)}, f32[16,16,256]{2,1,0:T(8,128)S(1)}, bf16[9,256,256]{2,1,0:T(8,128)(2,1)S(1)}) custom-call(bf16[32,32,256]{2,1,0:T(8,128)(2,1)S(1)} %get-tuple-element.35.grid.refs_0_, ...), custom_call_target="tpu_custom_call" | custom-call | flops 4000000000 | bytes 8000000 | tf_op jit(solution)/shard_map/inner_rows/pallas_call | solution.py:742
  16.1 1.3 %collective-permute-done.1.refs_8_ = bf16[416,256]{1,0:T(8,128)(2,1)S(1)} collective-permute-done((bf16[416,256]{1,0:T(8,128)(2,1)S(1)}, bf16[416,256]{1,0:T(8,128)(2,1)S(1)}, u32[]{:S(2)}, u32[]{:S(2)}) %collective-permute-start.1) | collective-permute-done | bytes 213024 | tf_op jit(solution)/shard_map/ppermute | solution.py:25
  17.4 9.4 %sweep.1 = (bf16[16,16,256]{2,1,0:T(8,128)(2,1)}, f32[6,128,256]{2,1,0:T(8,128)S(1)}, bf16[6,128,256]{2,1,0:T(8,128)(2,1)S(1)}, f32[256,256]{1,0:T(8,128)S(1)}, ...) custom-call(bf16[32,32,256]{2,1,0:T(8,128)(2,1)S(1)} %get-tuple-elem, ...), custom_call_target="tpu_custom_call" | custom-call | tf_op jit(solution)/shard_map/sweep/pallas_call | solution.py:821
  26.7 0.7 %collective-permute-start.6 = (bf16[6,128,256]{2,1,0:T(8,128)(2,1)S(1)}, bf16[6,128,256]{2,1,0:T(8,128)(2,1)S(1)}, u32[]{:S(2)}, u32[]{:S(2)}) collective-permute-start(bf16[6,128,256]{2,1,0:T(8,128)(2,1)S(1)} %get-tuple-element.62), channel_id=1, source_target_pairs={{0,1},{1,0},{2,3},{3,2},{4,5},{5,4},{6,7},{7,6},{8,9},{9,8},{10,11... | collective-permute-start | bytes 1179656 | tf_op jit(solution)/shard_map/ppermute | solution.py:25
  27.4 3.5 %encoder_back.1 = (bf16[16,16,256]{2,1,0:T(8,128)(2,1)}, f32[3,128,256]{2,1,0:T(8,128)S(1)}, bf16[3,128,256]{2,1,0:T(8,128)(2,1)S(1)}) custom-call(bf16[16,16,256]{2,1,0:T(8,128)(2,1)S(1)} %get-tuple-element.36.m1.refs_1_, bf16[9,256,256]{2,1,0:T(8,128)(2,1)S(1)} %get-tuple-element.47.refs_12_.weights, f32[256,256]{1,0:T(8,128)S(1)} %get-tuple-element.49.fine_delta, ...), custom_call_target="tpu_custom_call" | custom-call | flops 3000000000 | bytes 8000000 | tf_op jit(solution)/shard_map/encoder_back/pallas_call | solution.py:843
  30.9 1.4 %collective-permute-done.5.got_first = bf16[3,128,256]{2,1,0:T(8,128)(2,1)S(1)} collective-permute-done((bf16[3,128,256]{2,1,0:T(8,128)(2,1)S(1)}, bf16[3,128,256]{2,1,0:T(8,128)(2,1)S(1)}, u32[]{:S(2)}, u32[]{:S(2)}) %collective-permute-start.5) | collective-permute-done | bytes 196640 | tf_op jit(solution)/shard_map/ppermute | solution.py:25
  32.5 0.6 collective-permute-start.8
  33.1 2.9 %collective-permute-start.9 = (bf16[9,32,256]{2,1,0:T(8,128)(2,1)S(1)}, bf16[9,32,256]{2,1,0:T(8,128)(2,1)S(1)}, u32[]{:S(2)}, u32[]{:S(2)}) collective-permute-start(bf16[9,32,256]{2,1,0:T(8,128)(2,1)S(1)} %get-tuple-element.66), channel_id=1, source_target_pairs={{0,6},{2,4},{4,2},{6,0},{8,14},{10,12},{12,10},{14,8},{1,7},{3,5},... | collective-permute-start | bytes 442376 | tf_op jit(solution)/shard_map/ppermute | solution.py:25
  36.0 3.2 %collective-permute-done.7.refs_1_ = bf16[9,32,256]{2,1,0:T(8,128)(2,1)S(1)} collective-permute-done((bf16[9,32,256]{2,1,0:T(8,128)(2,1)S(1)}, bf16[9,32,256]{2,1,0:T(8,128)(2,1)S(1)}, u32[]{:S(2)}, u32[]{:S(2)}) %collective-permute-start.7) | collective-permute-done | bytes 147488 | tf_op jit(solution)/shard_map/ppermute | solution.py:25
  39.2 2.4 %collective-permute-done.8.refs_2_ = bf16[9,32,256]{2,1,0:T(8,128)(2,1)S(1)} collective-permute-done((bf16[9,32,256]{2,1,0:T(8,128)(2,1)S(1)}, bf16[9,32,256]{2,1,0:T(8,128)(2,1)S(1)}, u32[]{:S(2)}, u32[]{:S(2)}) %collective-permute-start.8) | collective-permute-done | bytes 147488 | tf_op jit(solution)/shard_map/ppermute | solution.py:25
  41.7 1.8 %collective-permute-start.10 = (bf16[9,32,256]{2,1,0:T(8,128)(2,1)S(1)}, bf16[9,32,256]{2,1,0:T(8,128)(2,1)S(1)}, u32[]{:S(2)}, u32[]{:S(2)}) collective-permute-start(bf16[9,32,256]{2,1,0:T(8,128)(2,1)S(1)} %block_sum.1.refs_0_), channel_id=1, source_target_pairs={{0,8},{2,10},{4,12},{6,14},{8,0},{10,2},{12,4},{14,6},{1,9},{3,11}... | collective-permute-start | bytes 442376 | tf_op jit(solution)/shard_map/ppermute | solution.py:25
  43.5 7.3 %collective-permute-done.10.refs_1_ = bf16[9,32,256]{2,1,0:T(8,128)(2,1)S(1)} collective-permute-done((bf16[9,32,256]{2,1,0:T(8,128)(2,1)S(1)}, bf16[9,32,256]{2,1,0:T(8,128)(2,1)S(1)}, u32[]{:S(2)}, u32[]{:S(2)}) %collective-permute-start.10) | collective-permute-done | bytes 147488 | tf_op jit(solution)/shard_map/ppermute | solution.py:25
  50.9 1.1 %collective-permute-start.12 = (bf16[9,32,256]{2,1,0:T(8,128)(2,1)S(1)}, bf16[9,32,256]{2,1,0:T(8,128)(2,1)S(1)}, u32[]{:S(2)}, u32[]{:S(2)}) collective-permute-start(bf16[9,32,256]{2,1,0:T(8,128)(2,1)S(1)} %pair_sum.1.refs_0_), channel_id=1, source_target_pairs={{0,2},{2,0},{4,6},{6,4},{8,10},{10,8},{12,14},{14,12},{1,3},{3,1},... | collective-permute-start | bytes 442376 | tf_op jit(solution)/shard_map/ppermute | solution.py:25
  52.1 2.3 %collective-permute-start.11 = (bf16[9,32,256]{2,1,0:T(8,128)(2,1)S(1)}, bf16[9,32,256]{2,1,0:T(8,128)(2,1)S(1)}, u32[]{:S(2)}, u32[]{:S(2)}) collective-permute-start(bf16[9,32,256]{2,1,0:T(8,128)(2,1)S(1)} %pair_sum.1.refs_0_), channel_id=1, source_target_pairs={{0,4},{2,6},{4,0},{6,2},{8,12},{10,14},{12,8},{14,10},{1,5},{3,7},... | collective-permute-start | bytes 442376 | tf_op jit(solution)/shard_map/ppermute | solution.py:25
  54.4 3.9 %collective-permute-done.13.refs_3_ = bf16[9,32,256]{2,1,0:T(8,128)(2,1)S(1)} collective-permute-done((bf16[9,32,256]{2,1,0:T(8,128)(2,1)S(1)}, bf16[9,32,256]{2,1,0:T(8,128)(2,1)S(1)}, u32[]{:S(2)}, u32[]{:S(2)}) %collective-permute-start.13) | collective-permute-done | bytes 147488 | tf_op jit(solution)/shard_map/ppermute | solution.py:25
  58.3 0.7 %collective-permute-done.12.refs_2_ = bf16[9,32,256]{2,1,0:T(8,128)(2,1)S(1)} collective-permute-done((bf16[9,32,256]{2,1,0:T(8,128)(2,1)S(1)}, bf16[9,32,256]{2,1,0:T(8,128)(2,1)S(1)}, u32[]{:S(2)}, u32[]{:S(2)}) %collective-permute-start.12) | collective-permute-done | bytes 147488 | tf_op jit(solution)/shard_map/ppermute | solution.py:25
  59.0 1.0 %collective-permute-done.11.refs_1_ = bf16[9,32,256]{2,1,0:T(8,128)(2,1)S(1)} collective-permute-done((bf16[9,32,256]{2,1,0:T(8,128)(2,1)S(1)}, bf16[9,32,256]{2,1,0:T(8,128)(2,1)S(1)}, u32[]{:S(2)}, u32[]{:S(2)}) %collective-permute-start.11) | collective-permute-done | bytes 147488 | tf_op jit(solution)/shard_map/ppermute | solution.py:25
  60.4 1.0 %collective-permute-done.15.refs_5_ = bf16[9,32,256]{2,1,0:T(8,128)(2,1)S(1)} collective-permute-done((bf16[9,32,256]{2,1,0:T(8,128)(2,1)S(1)}, bf16[9,32,256]{2,1,0:T(8,128)(2,1)S(1)}, u32[]{:S(2)}, u32[]{:S(2)}) %collective-permute-start.15) | collective-permute-done | bytes 147488 | tf_op jit(solution)/shard_map/ppermute | solution.py:25
  61.4 1.5 %spread_gradients.1 = f32[9,256,256]{2,1,0:T(8,128)} custom-call(bf16[9,32,256]{2,1,0:T(8,128)(2,1)S(1)} %pair_sum.1.refs_0_, bf16[9,32,256]{2,1,0:T(8,128)(2,1)S(1)} %collective-permute-done.11.refs_1_, bf16[9,32,256]{2,1,0:T(8,128)(2,1)S(1)} %collective-permute-done.12.refs_2_, bf16[9,32,256]{2,1,0:T(8,128)(2,1)S(1)} %collective-permute-done.13.refs_3_, ...), custom_call_target="tpu_custom_call" | custom-call | tf_op jit(solution)/shard_map/spread_gradients/pallas_call | solution.py:861
  (20 shorter events, 0.7 us)
Async XLA Ops:
  2.2 13.9 %collective-permute-start.3 = (bf16[112,256]{1,0:T(8,128)(2,1)S(1)}, bf16[112,256]{1,0:T(8,128)(2,1)S(1)}, u32[]{:S(2)}, u32[]{:S(2)}) collective-permute-start(bf16[112,256]{1,0:T(8,128)(2,1)S(1)} %get-tuple-element.45), channel_id=1, source_target_pairs={{0,3},{1,2},{2,1},{3,0},{4,7},{5,6},{6,5},{7,4},{8,11},{9,10},{10,... | collective-permute-start | bytes 172040 | tf_op jit(solution)/shard_map/ppermute | solution.py:25
  4.6 11.4 %collective-permute-start.4 = (bf16[112,256]{1,0:T(8,128)(2,1)S(1)}, bf16[112,256]{1,0:T(8,128)(2,1)S(1)}, u32[]{:S(2)}, u32[]{:S(2)}) collective-permute-start(bf16[112,256]{1,0:T(8,128)(2,1)S(1)} %get-tuple-element.46), channel_id=1, source_target_pairs={{0,15},{1,6},{2,13},{3,4},{4,3},{5,10},{6,1},{7,8},{8,7},{9,14},{1... | collective-permute-start | bytes 172040 | tf_op jit(solution)/shard_map/ppermute | solution.py:25
  8.5 7.6 %collective-permute-start.2 = (bf16[352,256]{1,0:T(8,128)(2,1)S(1)}, bf16[352,256]{1,0:T(8,128)(2,1)S(1)}, u32[]{:S(2)}, u32[]{:S(2)}) collective-permute-start(bf16[352,256]{1,0:T(8,128)(2,1)S(1)} %get-tuple-element.44), channel_id=1, source_target_pairs={{0,2},{1,3},{2,0},{3,1},{4,6},{5,7},{6,4},{7,5},{8,10},{9,11},{10,... | collective-permute-start | bytes 540680 | tf_op jit(solution)/shard_map/ppermute | solution.py:25
  10.0 6.1 %collective-permute-start = (bf16[416,256]{1,0:T(8,128)(2,1)S(1)}, bf16[416,256]{1,0:T(8,128)(2,1)S(1)}, u32[]{:S(2)}, u32[]{:S(2)}) collective-permute-start(bf16[416,256]{1,0:T(8,128)(2,1)S(1)} %get-tuple-element.42), channel_id=1, source_target_pairs={{0,1},{1,0},{2,3},{3,2},{4,5},{5,4},{6,7},{7,6},{8,9},{9,8},{10,11... | collective-permute-start | bytes 638984 | tf_op jit(solution)/shard_map/ppermute | solution.py:25
  10.0 7.4 %collective-permute-start.1 = (bf16[416,256]{1,0:T(8,128)(2,1)S(1)}, bf16[416,256]{1,0:T(8,128)(2,1)S(1)}, u32[]{:S(2)}, u32[]{:S(2)}) collective-permute-start(bf16[416,256]{1,0:T(8,128)(2,1)S(1)} %get-tuple-element.43), channel_id=1, source_target_pairs={{0,13},{1,4},{2,15},{3,6},{4,1},{5,8},{6,3},{7,10},{8,5},{9,12},{1... | collective-permute-start | bytes 638984 | tf_op jit(solution)/shard_map/ppermute | solution.py:25
  26.7 5.6 %collective-permute-start.6 = (bf16[6,128,256]{2,1,0:T(8,128)(2,1)S(1)}, bf16[6,128,256]{2,1,0:T(8,128)(2,1)S(1)}, u32[]{:S(2)}, u32[]{:S(2)}) collective-permute-start(bf16[6,128,256]{2,1,0:T(8,128)(2,1)S(1)} %get-tuple-element.62), channel_id=1, source_target_pairs={{0,1},{1,0},{2,3},{3,2},{4,5},{5,4},{6,7},{7,6},{8,9},{9,8},{10,11... | collective-permute-start | bytes 1179656 | tf_op jit(solution)/shard_map/ppermute | solution.py:25
  30.9 1.4 %collective-permute-start.5 = (bf16[3,128,256]{2,1,0:T(8,128)(2,1)S(1)}, bf16[3,128,256]{2,1,0:T(8,128)(2,1)S(1)}, u32[]{:S(2)}, u32[]{:S(2)}) collective-permute-start(bf16[3,128,256]{2,1,0:T(8,128)(2,1)S(1)} %get-tuple-element.60), channel_id=1, source_target_pairs={{0,1},{1,0},{2,3},{3,2},{4,5},{5,4},{6,7},{7,6},{8,9},{9,8},{10,11... | collective-permute-start | bytes 589832 | tf_op jit(solution)/shard_map/ppermute | solution.py:25
  32.4 6.8 %collective-permute-start.7 = (bf16[9,32,256]{2,1,0:T(8,128)(2,1)S(1)}, bf16[9,32,256]{2,1,0:T(8,128)(2,1)S(1)}, u32[]{:S(2)}, u32[]{:S(2)}) collective-permute-start(bf16[9,32,256]{2,1,0:T(8,128)(2,1)S(1)} %get-tuple-element.64), channel_id=1, source_target_pairs={{0,4},{2,6},{4,0},{6,2},{8,12},{10,14},{12,8},{14,10},{1,5},{3,7},... | collective-permute-start | bytes 442376 | tf_op jit(solution)/shard_map/ppermute | solution.py:25
  32.5 9.1 %collective-permute-start.8 = (bf16[9,32,256]{2,1,0:T(8,128)(2,1)S(1)}, bf16[9,32,256]{2,1,0:T(8,128)(2,1)S(1)}, u32[]{:S(2)}, u32[]{:S(2)}) collective-permute-start(bf16[9,32,256]{2,1,0:T(8,128)(2,1)S(1)} %get-tuple-element.65), channel_id=1, source_target_pairs={{0,2},{2,0},{4,6},{6,4},{8,10},{10,8},{12,14},{14,12},{1,3},{3,1},... | collective-permute-start | bytes 442376 | tf_op jit(solution)/shard_map/ppermute | solution.py:25
  33.1 8.5 %collective-permute-start.9 = (bf16[9,32,256]{2,1,0:T(8,128)(2,1)S(1)}, bf16[9,32,256]{2,1,0:T(8,128)(2,1)S(1)}, u32[]{:S(2)}, u32[]{:S(2)}) collective-permute-start(bf16[9,32,256]{2,1,0:T(8,128)(2,1)S(1)} %get-tuple-element.66), channel_id=1, source_target_pairs={{0,6},{2,4},{4,2},{6,0},{8,14},{10,12},{12,10},{14,8},{1,7},{3,5},... | collective-permute-start | bytes 442376 | tf_op jit(solution)/shard_map/ppermute | solution.py:25
  41.7 9.1 %collective-permute-start.10 = (bf16[9,32,256]{2,1,0:T(8,128)(2,1)S(1)}, bf16[9,32,256]{2,1,0:T(8,128)(2,1)S(1)}, u32[]{:S(2)}, u32[]{:S(2)}) collective-permute-start(bf16[9,32,256]{2,1,0:T(8,128)(2,1)S(1)} %block_sum.1.refs_0_), channel_id=1, source_target_pairs={{0,8},{2,10},{4,12},{6,14},{8,0},{10,2},{12,4},{14,6},{1,9},{3,11}... | collective-permute-start | bytes 442376 | tf_op jit(solution)/shard_map/ppermute | solution.py:25
  50.9 7.5 %collective-permute-start.13 = (bf16[9,32,256]{2,1,0:T(8,128)(2,1)S(1)}, bf16[9,32,256]{2,1,0:T(8,128)(2,1)S(1)}, u32[]{:S(2)}, u32[]{:S(2)}) collective-permute-start(bf16[9,32,256]{2,1,0:T(8,128)(2,1)S(1)} %pair_sum.1.refs_0_), channel_id=1, source_target_pairs={{0,6},{2,4},{4,2},{6,0},{8,14},{10,12},{12,10},{14,8},{1,7},{3,5},... | collective-permute-start | bytes 442376 | tf_op jit(solution)/shard_map/ppermute | solution.py:25
  50.9 8.1 %collective-permute-start.12 = (bf16[9,32,256]{2,1,0:T(8,128)(2,1)S(1)}, bf16[9,32,256]{2,1,0:T(8,128)(2,1)S(1)}, u32[]{:S(2)}, u32[]{:S(2)}) collective-permute-start(bf16[9,32,256]{2,1,0:T(8,128)(2,1)S(1)} %pair_sum.1.refs_0_), channel_id=1, source_target_pairs={{0,2},{2,0},{4,6},{6,4},{8,10},{10,8},{12,14},{14,12},{1,3},{3,1},... | collective-permute-start | bytes 442376 | tf_op jit(solution)/shard_map/ppermute | solution.py:25
  52.1 7.9 %collective-permute-start.11 = (bf16[9,32,256]{2,1,0:T(8,128)(2,1)S(1)}, bf16[9,32,256]{2,1,0:T(8,128)(2,1)S(1)}, u32[]{:S(2)}, u32[]{:S(2)}) collective-permute-start(bf16[9,32,256]{2,1,0:T(8,128)(2,1)S(1)} %pair_sum.1.refs_0_), channel_id=1, source_target_pairs={{0,4},{2,6},{4,0},{6,2},{8,12},{10,14},{12,8},{14,10},{1,5},{3,7},... | collective-permute-start | bytes 442376 | tf_op jit(solution)/shard_map/ppermute | solution.py:25
  54.4 5.6 %collective-permute-start.14 = (bf16[9,32,256]{2,1,0:T(8,128)(2,1)S(1)}, bf16[9,32,256]{2,1,0:T(8,128)(2,1)S(1)}, u32[]{:S(2)}, u32[]{:S(2)}) collective-permute-start(bf16[9,32,256]{2,1,0:T(8,128)(2,1)S(1)} %pair_sum.1.refs_0_), channel_id=1, source_target_pairs={{0,1},{1,0},{2,3},{3,2},{4,5},{5,4},{6,7},{7,6},{8,9},{9,8},{10,11... | collective-permute-start | bytes 442376 | tf_op jit(solution)/shard_map/ppermute | solution.py:25
  58.3 1.7 %collective-permute-start.17 = (bf16[9,32,256]{2,1,0:T(8,128)(2,1)S(1)}, bf16[9,32,256]{2,1,0:T(8,128)(2,1)S(1)}, u32[]{:S(2)}, u32[]{:S(2)}) collective-permute-start(bf16[9,32,256]{2,1,0:T(8,128)(2,1)S(1)} %collective-permute-done.13.refs_3_), channel_id=1, source_target_pairs={{0,1},{1,0},{2,3},{3,2},{4,5},{5,4},{6,7},{7,6},{8,9},{9,8},{10,11... | collective-permute-start | bytes 442376 | tf_op jit(solution)/shard_map/ppermute | solution.py:25
  59.0 1.4 %collective-permute-start.16 = (bf16[9,32,256]{2,1,0:T(8,128)(2,1)S(1)}, bf16[9,32,256]{2,1,0:T(8,128)(2,1)S(1)}, u32[]{:S(2)}, u32[]{:S(2)}) collective-permute-start(bf16[9,32,256]{2,1,0:T(8,128)(2,1)S(1)} %collective-permute-done.12.refs_2_), channel_id=1, source_target_pairs={{0,1},{1,0},{2,3},{3,2},{4,5},{5,4},{6,7},{7,6},{8,9},{9,8},{10,11... | collective-permute-start | bytes 442376 | tf_op jit(solution)/shard_map/ppermute | solution.py:25
  60.0 1.4 %collective-permute-start.15 = (bf16[9,32,256]{2,1,0:T(8,128)(2,1)S(1)}, bf16[9,32,256]{2,1,0:T(8,128)(2,1)S(1)}, u32[]{:S(2)}, u32[]{:S(2)}) collective-permute-start(bf16[9,32,256]{2,1,0:T(8,128)(2,1)S(1)} %collective-permute-done.11.refs_1_), channel_id=1, source_target_pairs={{0,1},{1,0},{2,3},{3,2},{4,5},{5,4},{6,7},{7,6},{8,9},{9,8},{10,11... | collective-permute-start | bytes 442376 | tf_op jit(solution)/shard_map/ppermute | solution.py:25

commit v6 on v5

--- a/solution.py
+++ b/solution.py
@@ -10,7 +10,10 @@
 LOW = jnp.bfloat16
 WIDE = jnp.float32
 VMEM_BYTES = 24 * 1024 * 1024
-HALO_ROWS = 7
+HALO_ROWS = 14
+BACK_ROWS = 14
+INNER_ROWS = 7
+CODE = LOW
 
 SIDE_ROWS = 416
 BAND_ROWS = 352
@@ -42,8 +45,15 @@
     return high, (value - high.astype(WIDE)).astype(LOW)
 
 
-def sigmoid_of(value):
-    return 0.5 * jnp.tanh(0.5 * value) + 0.5
+def silu_of(half):
+    t = jnp.tanh(half)
+    up = 1.0 + t
+    act = half * up
+    return act, up + act * (1.0 - t)
+
+
+def halved(weight):
+    return (weight.astype(WIDE) * 0.5).astype(LOW)
 
 
 def iota(shape, dim):
@@ -192,22 +202,19 @@
 
 
 def encode_tiles(tiles, weight):
-    count = len(tiles)
     ones = jnp.ones((256, 256), LOW)
-    places = iota((128, 256), 1).astype(WIDE)
+    places = iota((128, 256), 1).astype(WIDE).astype(CODE)
+    one, zero = jnp.ones((128, 256), LOW), jnp.zeros((128, 256), LOW)
     picked = [(mask.reshape(8, 16, 256) * codes[None]).reshape(128, 256) for mask, codes, _, _ in tiles]
-    found = mm(jnp.concatenate(picked, 0), ones)
+    found = mm(jnp.concatenate(picked, 0), ones).astype(CODE)
     senders = []
     for i, (_, _, window, _) in enumerate(tiles):
-        chosen = jnp.where(found[i * 128 : i * 128 + 128] == places, 1.0, 0.0).astype(LOW)
+        chosen = jnp.where(found[i * 128 : i * 128 + 128] == places, one, zero)
         senders.append(mm(chosen, jnp.concatenate(window, 0)).astype(LOW))
     pre_all = mm(jnp.concatenate(senders, 0), weight)
     results = []
-    for i in range(count):
-        pre = pre_all[i * 128 : i * 128 + 128].reshape(16, 8, 256) + tiles[i][3][None]
-        sig = sigmoid_of(pre)
-        act = pre * sig
-        rise = sig + act * (1.0 - sig)
+    for i, (_, _, _, received) in enumerate(tiles):
+        act, rise = silu_of(pre_all[i * 128 : i * 128 + 128].reshape(16, 8, 256) + received[None])
         results.append(
             (senders[i], jnp.sum(act, axis=0) * (1.0 / 16), rise.reshape(128, 256).astype(LOW), jnp.sum(rise, axis=0))
         )
@@ -217,7 +224,7 @@
 BLOCKS = ((0, 1), (1, 2), (0, 2))
 
 
-def inner_kernel(grid, m1, codes, far, sx, slope, pool, ssum, weights, gx, masks, ko, recv, sems):
+def inner_kernel(grid, m1, codes, far, sx, slope, pool, ssum, weights, masks, spread, gather, gx, ko, recv, sems):
     first = pltpu.make_async_copy(far.at[0:2], weights.at[0:2], sems.at[0])
     others = pltpu.make_async_copy(far.at[2:9], weights.at[2:9], sems.at[1])
     first.start()
@@ -239,27 +246,30 @@
     for r in range(16):
         ko[r] = jnp.broadcast_to(own[r : r + 1], (16, 256)).astype(LOW)
     first.wait()
-    recv[...] = mm(m1[...].reshape(256, 256), weights[1]).reshape(16, 16, 256)
+    recv[...] = mm(m1[...].reshape(256, 256), weights[1]).reshape(16, 16, 256) * 0.5
+    weight = halved(weights[0])
 
     def rows(step, carry):
+        spots = [(1 + INNER_ROWS * step + k, tile) for k in range(INNER_ROWS) for tile in range(2)]
         tiles = []
-        for k in range(2):
-            r = 1 + 2 * step + k
-            for tile in range(2):
-                window = [gx[blk, pl.ds(2 * r - 2, 8)].reshape(128, 256) for blk in BLOCKS[tile]]
-                tiles.append((masks[tile], ko[r], window, recv[r, tile * 8 : tile * 8 + 8]))
-        done = encode_tiles(tiles, weights[0])
-        for k in range(2):
-            r = 1 + 2 * step + k
-            for tile in range(2):
-                senders, mean, rise, total = done[2 * k + tile]
-                sx[r, tile] = senders
-                slope[r, tile] = rise
-                pool[r, tile * 8 : tile * 8 + 8] = mean
-                ssum[r, tile * 8 : tile * 8 + 8] = total
+        for r, tile in spots:
+            window = [gx[blk, pl.ds(2 * r - 2, 8)].reshape(128, 256) for blk in BLOCKS[tile]]
+            tiles.append((masks[tile], ko[r], window, recv[r, tile * 8 : tile * 8 + 8]))
+        for (r, tile), (senders, mean, rise, total) in zip(spots, encode_tiles(tiles, weight)):
+            sx[r, tile] = senders
+            slope[r, tile] = rise
+            pool[r, tile * 8 : tile * 8 + 8] = mean
+            ssum[r, tile * 8 : tile * 8 + 8] = total
         return carry
 
-    lax.fori_loop(0, 7, rows, 0)
+    def family(node, state):
+        q = state % 32
+        slot = jnp.where(q < 16, q // 2, jnp.where((q == 18) | (q == 19), 15, jnp.where((q == 20) | (q == 21), 8, -1)))
+        return jnp.where((state // 64 == node // 16) & (slot == node % 16), 1.0, 0.0).astype(LOW)
+
+    spread[...] = family(iota(spread.shape, 1), iota(spread.shape, 0))
+    gather[...] = family(iota(gather.shape, 0), iota(gather.shape, 1))
+    lax.fori_loop(0, 14 // INNER_ROWS, rows, 0)
     others.wait()
 
 
@@ -271,9 +281,9 @@
 def main_kernel(
     dirs, n_lat, own, sides, bands, weights, outs, scratch
 ):
-    grid, m1, cot, m2, codes, pool_in, ssum_in = own
+    grid, m1, cot, m2, codes, pool_in, ssum_in, masks, spread, gather = own
     mesh_out, keep, send, fd_out, pool_out, ssum, sx, slope, hx, hslope = outs
-    gx, m1x, recv, ko, k2, uv, pool, fx, cx, m2x, ohu, su, uslope, dd, acc_s, masks = scratch
+    gx, m1x, recv, ko, k2, uv, pool, fx, cx, m2x, ohu, su, uslope, dd, acc_s = scratch
     rep = lax.axis_index("rep")
     lat = lax.axis_index("lat")
     frame = m1x.shape[0]
@@ -406,25 +416,25 @@
             up_k[3:4],
         )
 
-    set_masks(masks)
-    recv[...] = mm(m1x[...].reshape(frame * 24, 256).astype(LOW), weights[1]).reshape(frame, 24, 256)
+    recv[...] = mm(m1x[...].reshape(frame * 24, 256).astype(LOW), weights[1]).reshape(frame, 24, 256) * 0.5
+    weight = halved(weights[0])
     pool[...] = jnp.zeros_like(pool)
 
     def window_of(f, tile):
         return [gx[blk, pl.ds(2 * f, 8)].reshape(128, 256) for blk in BLOCKS[tile]]
 
-    def encode_row(i, carry):
-        f = odd_row(i)
+    batch = 5 if odd_rows == 5 else 4
+
+    def encode_rows(step, carry):
+        spots = [(odd_row(step * batch + k), tile) for k in range(batch) for tile in range(3)]
         tiles = []
-        for tile in range(3):
+        for f, tile in spots:
             vec = ko[f] if tile < 2 else k2[f]
             tiles.append((masks[tile], vec, window_of(f, tile), recv[f, tile * 8 : tile * 8 + 8]))
-        done = encode_tiles(tiles, weights[0])
-        row = f - f_own
-        kept_at = jnp.where(row == 0, 0, jnp.where(row == 15, 1, 2))
-        row = jnp.where(kept_at == 2, 16, row)
-        for tile in range(3):
-            senders, mean, rise, total = done[tile]
+        for (f, tile), (senders, mean, rise, total) in zip(spots, encode_tiles(tiles, weight)):
+            row = f - f_own
+            kept_at = jnp.where(row == 0, 0, jnp.where(row == 15, 1, 2))
+            row = jnp.where(kept_at == 2, 16, row)
             pool[f, tile * 8 : tile * 8 + 8] = mean
             if tile < 2:
                 sx[kept_at, tile] = senders
@@ -432,7 +442,7 @@
                 ssum[row, tile * 8 : tile * 8 + 8] = total
         return carry
 
-    lax.fori_loop(0, odd_rows, encode_row, 0)
+    lax.fori_loop(0, odd_rows // batch, encode_rows, 0)
     slots = iota((8, 256), 0)
 
     def encode_halo(step, carry):
@@ -440,7 +450,7 @@
         for k in range(HALO_ROWS):
             f = f_own + 1 + HALO_ROWS * step + k
             tiles.append((masks[2], k2[f], window_of(f, 2), recv[f, 16:24]))
-        done = encode_tiles(tiles, weights[0])
+        done = encode_tiles(tiles, weight)
         for k in range(HALO_ROWS):
             r = 1 + HALO_ROWS * step + k
             f = f_own + r
@@ -467,7 +477,8 @@
     up_ones = jnp.ones((128, 128), LOW)
     m2_flat = m2x[...].reshape(a_frame * 16, 256)
     m2_low = m2_flat.astype(LOW)
-    up_recv = mm(m2_low, weights[4]).reshape(a_frame, 16, 256)
+    up_recv = mm(m2_low, weights[4]).reshape(a_frame, 16, 256) * 0.5
+    weight = halved(weights[3])
     pools = []
     for aa in range(a_frame):
         vec = uv[aa]
@@ -476,35 +487,20 @@
         ohu[aa] = chosen
         senders = mm(chosen, fx[2 * aa : 2 * aa + 4].reshape(128, 256)).astype(LOW)
         su[aa] = senders
-        pre = mm(senders, weights[3]).reshape(8, 16, 256) + up_recv[aa][None]
-        sig = sigmoid_of(pre)
-        act = pre * sig
+        act, rise = silu_of(mm(senders, weight).reshape(8, 16, 256) + up_recv[aa][None])
         pools.append(jnp.sum(act, axis=0) * (1.0 / 8))
-        uslope[aa] = (sig + act * (1.0 - sig)).reshape(128, 256)
+        uslope[aa] = rise.reshape(128, 256)
     up_pool = jnp.concatenate(pools, 0).astype(LOW)
     coarse = (m2_flat + mm(up_pool, weights[5])).astype(LOW)
 
     c_frame = 2 * a_frame
     nodes = a_frame * 16
 
-    def parent_slot(q):
-        return jnp.where(q < 16, q // 2, jnp.where((q == 18) | (q == 19), 15, jnp.where((q == 20) | (q == 21), 8, -1)))
-
-    r_i = iota((c_frame * 32, nodes), 0)
-    r_j = iota((c_frame * 32, nodes), 1)
-    spread = (r_i // 64 == r_j // 16) & (parent_slot(r_i % 32) == r_j % 16)
-    spread = jnp.where(spread, 1.0, 0.0).astype(LOW)
-    t_i = iota((nodes, c_frame * 32), 1)
-    t_j = iota((nodes, c_frame * 32), 0)
-    gather = (t_i // 64 == t_j // 16) & (parent_slot(t_i % 32) == t_j % 16)
-    gather = jnp.where(gather, 1.0, 0.0).astype(LOW)
-    parents = mm(spread, coarse).astype(LOW)
+    parents = mm(spread[...], coarse).astype(LOW)
     fine_mid = fx[1 : 1 + c_frame].reshape(c_frame * 32, 256)
-    down_pre = mm(parents, weights[6]) + mm(fine_mid, weights[7])
-    sig = sigmoid_of(down_pre)
-    act = down_pre * sig
+    act, rise = silu_of((mm(parents, weights[6]) + mm(fine_mid, weights[7])) * 0.5)
     cot_w = mm_nt(cx[...].reshape(c_frame * 32, 256), weights[8])
-    dd[0] = (cot_w * (sig + act * (1.0 - sig))).astype(LOW).reshape(c_frame, 32, 256)
+    dd[0] = (cot_w * 0.5 * rise).astype(LOW).reshape(c_frame, 32, 256)
     dd[1] = act.astype(LOW).reshape(c_frame, 32, 256)
 
     def put_grad(index, value):
@@ -520,7 +516,7 @@
     put_grad(8, mm_tn(act_own, cot_own))
     put_grad(7, mm_tn(fine_own, delta_own))
 
-    child_sum = mm(gather, dd[0].reshape(c_frame * 32, 256))
+    child_sum = mm(gather[...], dd[0].reshape(c_frame * 32, 256))
     n_i = iota((nodes, 256), 0)
     aa_i, bb_i = n_i // 16, n_i % 16
     is_own = (aa_i >= a_own) & (aa_i < a_own + 8) & (bb_i < 8)
@@ -534,7 +530,7 @@
     put_grad(6, mm_tn(coarse, own_high) + mm_tn(coarse, own_low))
     own_delta = jnp.where(is_own, coarse_delta.astype(WIDE), 0.0).astype(LOW)
     put_grad(5, mm_tn(up_pool, own_delta))
-    pool2 = jnp.where(is_real, mm_nt(coarse_delta, weights[5]) * (1.0 / 8), 0.0)
+    pool2 = jnp.where(is_real, mm_nt(coarse_delta, weights[5]) * (1.0 / 16), 0.0)
     own_f = jnp.where(is_own, 1.0, 0.0)
     recv[...] = jnp.zeros_like(recv)
     acc_s[...] = jnp.zeros_like(acc_s)
@@ -568,7 +564,7 @@
 ):
     rep = lax.axis_index("rep")
     delta_b = fine_delta[...].astype(LOW)
-    pool_delta = mm_nt(delta_b, weights[2]) * (1.0 / 16)
+    pool_delta = mm_nt(delta_b, weights[2]) * (1.0 / 32)
     pd[...] = pool_delta.reshape(16, 16, 256)
     node_delta = pool_delta * ssum[0:16].reshape(256, 256)
     high, low = two_parts(node_delta)
@@ -594,8 +590,8 @@
 
     def rows(step, carry):
         senders, deltas = [], []
-        for k in range(2):
-            r = 1 + 2 * step + k
+        for k in range(BACK_ROWS):
+            r = 1 + BACK_ROWS * step + k
             halo = hx[r - 1].astype(WIDE)
             halo_rise = hslope[r - 1].astype(WIDE)
             for tile, slot in ((0, 0), (1, 7)):
@@ -605,7 +601,7 @@
         acc[...] += mm_tn(jnp.concatenate(senders, 0), jnp.concatenate(deltas, 0))
         return carry
 
-    lax.fori_loop(0, 7, rows, 0)
+    lax.fori_loop(0, 14 // BACK_ROWS, rows, 0)
     put_halves(acc, keep, send, 0, rep)
 
 
@@ -664,7 +660,7 @@
 
 def flat_main(dirs, n_lat, *refs):
     n_bands = 3 * len(dirs)
-    own, refs = refs[:7], refs[7:]
+    own, refs = refs[:10], refs[10:]
     sides, refs = refs[:2], refs[2:]
     bands, refs = refs[:n_bands], refs[n_bands:]
     weights, refs = refs[0], refs[1:]
@@ -739,6 +735,10 @@
         compiler_params=params,
         name="pack_halos",
     )(*(in_hbm(value) for value in (*states, grid_edges, up_edges)))
+    frame = 20 if n_lat == 2 else 22
+    a_frame = 9 if n_lat == 2 else 10
+    c_frame = 2 * a_frame
+    g_frame = 2 * frame + 6
     inner = pl.pallas_call(
         inner_kernel,
         out_shape=[
@@ -747,22 +747,24 @@
             jax.ShapeDtypeStruct((16, 16, 256), WIDE),
             jax.ShapeDtypeStruct((16, 16, 256), WIDE),
             jax.ShapeDtypeStruct(weights.shape, LOW),
+            jax.ShapeDtypeStruct((3, 128, 256), LOW),
+            jax.ShapeDtypeStruct((c_frame * 32, a_frame * 16), LOW),
+            jax.ShapeDtypeStruct((a_frame * 16, c_frame * 32), LOW),
         ],
         in_specs=[vmem] * 3 + [hbm],
-        out_specs=[vmem] * 5,
+        out_specs=[vmem] * 8,
         scratch_shapes=[
             pltpu.VMEM((3, 34, 16, 256), LOW),
-            pltpu.VMEM((3, 128, 256), LOW),
             pltpu.VMEM((16, 16, 256), LOW),
             pltpu.VMEM((16, 16, 256), WIDE),
             pltpu.SemaphoreType.DMA((2,)),
         ],
         compiler_params=params,
-        cost_estimate=pl.CostEstimate(flops=4_000_000_000, bytes_accessed=8_000_000, transcendentals=1_000_000),
+        cost_estimate=pl.CostEstimate(flops=1_000_000_000, bytes_accessed=1_000, transcendentals=0),
         name="inner_rows",
     )(grid_state, mesh1_state, codes, in_hbm(weights))
-    sx_in, slope_in, pool_in, ssum_in, weights = inner
-    own = (grid_state, mesh1_state, cotangent, mesh2_state, codes, pool_in, ssum_in)
+    sx_in, slope_in, pool_in, ssum_in, weights, *tables = inner
+    own = (grid_state, mesh1_state, cotangent, mesh2_state, codes, pool_in, ssum_in, *tables)
 
     def beyond(lon, core):
         return ((lon + (1 if core else -1)) % n_lon, 1 - core)
@@ -795,10 +797,6 @@
         for k, column in enumerate(("same", "sibling", "beyond")):
             got_bands.append(send_to(buffers[2 + 3 * i + k], shift(sends_bottom), column))
 
-    frame = 20 if n_lat == 2 else 22
-    a_frame = 9 if n_lat == 2 else 10
-    c_frame = 2 * a_frame
-    g_frame = 2 * frame + 6
     scratch = [
         pltpu.VMEM((3, g_frame, 16, 256), LOW),
         pltpu.VMEM((frame, 24, 256), WIDE),
@@ -815,9 +813,8 @@
         pltpu.VMEM((a_frame, 128, 256), WIDE),
         pltpu.VMEM((2, c_frame, 32, 256), LOW),
         pltpu.VMEM((256, 256), WIDE),
-        pltpu.VMEM((3, 128, 256), LOW),
     ]
-    n_in = 7 + 2 + len(got_bands) + 1
+    n_in = 10 + 2 + len(got_bands) + 1
     mesh_out, kept, sent, fine_delta, pool, ssum, sx_edge, slope_edge, hx, hslope = pl.pallas_call(
         functools.partial(flat_main, dirs, n_lat),
         out_shape=[

time: 63.1 us -> 58.4 us (0.926)
  Pallas kernels: 21.6 us -> 16.6 us
    pallas_call x1, Pallas kernels: 9.39 us -> 7.41 us  [body(): pl.pallas_call(functools.partial(flat_main, dirs, n_lat), out_shape=[jax....]
    pallas_call x1, Pallas kernels: 5.49 us -> 3.58 us  [body(): pl.pallas_call(inner_kernel, out_shape=[jax.ShapeDtypeStruct((16, 2, 128,...]
    pallas_call x1, Pallas kernels: 3.48 us -> 2.39 us  [body(): pl.pallas_call(back_kernel, out_shape=[jax.ShapeDtypeStruct(mesh1_state.s...]
  transfers between devices with their start and end apart: 18 -> 18, of which waited for: 10 -> 12; matrix products, arithmetic and copies ran while one was open for 0% -> 0% of each run, Pallas kernels for 14% -> 10%
where the time goes in v6:
time: 58.4 us; the launch traced here: 58.2 us
  waiting for transfers between devices  22.9 us (39%)
  starting transfers between devices  18 us (31%)
  Pallas kernels  16.6 us (28%)
  between operations  0.68 us (1%)
    ppermute x18, waiting for transfers between devices, permute(): lax.ppermute(values, axes, [(i, j) for i, j in pairs if j is not None])  22.9 us
    ppermute x18, starting transfers between devices, permute(): lax.ppermute(values, axes, [(i, j) for i, j in pairs if j is not None])  18 us
    pallas_call x1, Pallas kernels, body(): pl.pallas_call(functools.partial(flat_main, dirs, n_lat), out_shape=[jax....  7.41 us
    pallas_call x1, Pallas kernels, body(): pl.pallas_call(inner_kernel, out_shape=[jax.ShapeDtypeStruct((16, 2, 128,...  3.58 us
    pallas_call x1, Pallas kernels, body(): pl.pallas_call(back_kernel, out_shape=[jax.ShapeDtypeStruct(mesh1_state.s...  2.39 us
    pallas_call x1, Pallas kernels, body(): pl.pallas_call(functools.partial(pack_kernel, dirs, glon, m1lon), out_sha...  1.53 us
    pallas_call x1, Pallas kernels, body(): pl.pallas_call(functools.partial(spread_kernel, scale), out_shape=jax.Sha...  1.51 us
  transfers between devices with their start and end apart: 18, of which 12 were waited for; matrix products, arithmetic and copies ran while one was open for 0% of the time, Pallas kernels for 10%

profile of v6, /device:TPU:0, one launch (start us, length us, event | category | flops | bytes accessed | tf_op | source)
XLA Modules:
  0.0 58.2 jit_solution(4907073148104047447)
XLA Ops:
  0.6 1.5 %pack_halos.1 = (bf16[32,32,256]{2,1,0:T(8,128)(2,1)S(1)}, bf16[16,16,256]{2,1,0:T(8,128)(2,1)S(1)}, bf16[16,16,256]{2,1,0:T(8,128)(2,1)S(1)}, bf16[8,16,256]{2,...) custom-call(bf16[32,32,256]{2,1,0:T(8,128)(2,1)} %refs_0_.1, ...), custom_call_target="tpu_custom_call" | custom-call | tf_op jit(solution)/shard_map/pack_halos/pallas_call | solution.py:724
  2.2 0.5 collective-permute-start
  2.7 4.7 %collective-permute-start.1 = (bf16[416,256]{1,0:T(8,128)(2,1)S(1)}, bf16[416,256]{1,0:T(8,128)(2,1)S(1)}, u32[]{:S(2)}, u32[]{:S(2)}) collective-permute-start(bf16[416,256]{1,0:T(8,128)(2,1)S(1)} %get-tuple-element.49), channel_id=1, source_target_pairs={{0,13},{1,4},{2,15},{3,6},{4,1},{5,8},{6,3},{7,10},{8,5},{9,12},{1... | collective-permute-start | bytes 638984 | tf_op jit(solution)/shard_map/ppermute | solution.py:28
  7.4 1.5 %collective-permute-start.2 = (bf16[352,256]{1,0:T(8,128)(2,1)S(1)}, bf16[352,256]{1,0:T(8,128)(2,1)S(1)}, u32[]{:S(2)}, u32[]{:S(2)}) collective-permute-start(bf16[352,256]{1,0:T(8,128)(2,1)S(1)} %get-tuple-element.50), channel_id=1, source_target_pairs={{0,2},{1,3},{2,0},{3,1},{4,6},{5,7},{6,4},{7,5},{8,10},{9,11},{10,... | collective-permute-start | bytes 540680 | tf_op jit(solution)/shard_map/ppermute | solution.py:28
  8.9 1.6 %collective-permute-start.4 = (bf16[112,256]{1,0:T(8,128)(2,1)S(1)}, bf16[112,256]{1,0:T(8,128)(2,1)S(1)}, u32[]{:S(2)}, u32[]{:S(2)}) collective-permute-start(bf16[112,256]{1,0:T(8,128)(2,1)S(1)} %get-tuple-element.52), channel_id=1, source_target_pairs={{0,15},{1,6},{2,13},{3,4},{4,3},{5,10},{6,1},{7,8},{8,7},{9,14},{1... | collective-permute-start | bytes 172040 | tf_op jit(solution)/shard_map/ppermute | solution.py:28
  10.5 3.6 %inner_rows.1 = (bf16[16,2,128,256]{3,2,1,0:T(8,128)(2,1)S(1)}, bf16[16,2,128,256]{3,2,1,0:T(8,128)(2,1)S(1)}, f32[16,16,256]{2,1,0:T(8,128)S(1)}, f32[16,16,256...) custom-call(bf16[32,32,256]{2,1,0:T(8,128)(2,1)S(1)} %get-tuple-elem, ...), custom_call_target="tpu_custom_call" | custom-call | flops 1000000000 | bytes 1000 | tf_op jit(solution)/shard_map/inner_rows/pallas_call | solution.py:742
  14.4 1.0 %collective-permute-done.4.refs_14_ = bf16[112,256]{1,0:T(8,128)(2,1)S(1)} collective-permute-done((bf16[112,256]{1,0:T(8,128)(2,1)S(1)}, bf16[112,256]{1,0:T(8,128)(2,1)S(1)}, u32[]{:S(2)}, u32[]{:S(2)}) %collective-permute-start.4) | collective-permute-done | bytes 57376 | tf_op jit(solution)/shard_map/ppermute | solution.py:28
  15.4 7.4 %sweep.1 = (bf16[16,16,256]{2,1,0:T(8,128)(2,1)}, f32[6,128,256]{2,1,0:T(8,128)S(1)}, bf16[6,128,256]{2,1,0:T(8,128)(2,1)S(1)}, f32[256,256]{1,0:T(8,128)S(1)}, ...) custom-call(bf16[32,32,256]{2,1,0:T(8,128)(2,1)S(1)} %get-tuple-elem, ...), custom_call_target="tpu_custom_call" | custom-call | tf_op jit(solution)/shard_map/sweep/pallas_call | solution.py:818
  22.8 2.4 %encoder_back.1 = (bf16[16,16,256]{2,1,0:T(8,128)(2,1)}, f32[3,128,256]{2,1,0:T(8,128)S(1)}, bf16[3,128,256]{2,1,0:T(8,128)(2,1)S(1)}) custom-call(bf16[16,16,256]{2,1,0:T(8,128)(2,1)S(1)} %get-tuple-element.39.m1.refs_1_, bf16[9,256,256]{2,1,0:T(8,128)(2,1)S(1)} %get-tuple-element.53.refs_15_.weights, f32[256,256]{1,0:T(8,128)S(1)} %get-tuple-element.55.fine_delta, ...), custom_call_target="tpu_custom_call" | custom-call | flops 3000000000 | bytes 8000000 | tf_op jit(solution)/shard_map/encoder_back/pallas_call | solution.py:840
  25.7 1.1 %collective-permute-done.5.got_first = bf16[3,128,256]{2,1,0:T(8,128)(2,1)S(1)} collective-permute-done((bf16[3,128,256]{2,1,0:T(8,128)(2,1)S(1)}, bf16[3,128,256]{2,1,0:T(8,128)(2,1)S(1)}, u32[]{:S(2)}, u32[]{:S(2)}) %collective-permute-start.5) | collective-permute-done | bytes 196640 | tf_op jit(solution)/shard_map/ppermute | solution.py:28
  27.3 1.5 %collective-permute-start.8 = (bf16[9,32,256]{2,1,0:T(8,128)(2,1)S(1)}, bf16[9,32,256]{2,1,0:T(8,128)(2,1)S(1)}, u32[]{:S(2)}, u32[]{:S(2)}) collective-permute-start(bf16[9,32,256]{2,1,0:T(8,128)(2,1)S(1)} %get-tuple-element.71), channel_id=1, source_target_pairs={{0,2},{2,0},{4,6},{6,4},{8,10},{10,8},{12,14},{14,12},{1,3},{3,1},... | collective-permute-start | bytes 442376 | tf_op jit(solution)/shard_map/ppermute | solution.py:28
  28.8 1.7 %collective-permute-start.9 = (bf16[9,32,256]{2,1,0:T(8,128)(2,1)S(1)}, bf16[9,32,256]{2,1,0:T(8,128)(2,1)S(1)}, u32[]{:S(2)}, u32[]{:S(2)}) collective-permute-start(bf16[9,32,256]{2,1,0:T(8,128)(2,1)S(1)} %get-tuple-element.72), channel_id=1, source_target_pairs={{0,6},{2,4},{4,2},{6,0},{8,14},{10,12},{12,10},{14,8},{1,7},{3,5},... | collective-permute-start | bytes 442376 | tf_op jit(solution)/shard_map/ppermute | solution.py:28
  30.4 3.2 %collective-permute-done.7.refs_1_ = bf16[9,32,256]{2,1,0:T(8,128)(2,1)S(1)} collective-permute-done((bf16[9,32,256]{2,1,0:T(8,128)(2,1)S(1)}, bf16[9,32,256]{2,1,0:T(8,128)(2,1)S(1)}, u32[]{:S(2)}, u32[]{:S(2)}) %collective-permute-start.7) | collective-permute-done | bytes 147488 | tf_op jit(solution)/shard_map/ppermute | solution.py:28
  33.7 2.9 %collective-permute-done.9.refs_3_ = bf16[9,32,256]{2,1,0:T(8,128)(2,1)S(1)} collective-permute-done((bf16[9,32,256]{2,1,0:T(8,128)(2,1)S(1)}, bf16[9,32,256]{2,1,0:T(8,128)(2,1)S(1)}, u32[]{:S(2)}, u32[]{:S(2)}) %collective-permute-start.9) | collective-permute-done | bytes 147488 | tf_op jit(solution)/shard_map/ppermute | solution.py:28
  36.6 2.0 %collective-permute-start.10 = (bf16[9,32,256]{2,1,0:T(8,128)(2,1)S(1)}, bf16[9,32,256]{2,1,0:T(8,128)(2,1)S(1)}, u32[]{:S(2)}, u32[]{:S(2)}) collective-permute-start(bf16[9,32,256]{2,1,0:T(8,128)(2,1)S(1)} %block_sum.1.refs_0_), channel_id=1, source_target_pairs={{0,8},{2,10},{4,12},{6,14},{8,0},{10,2},{12,4},{14,6},{1,9},{3,11}... | collective-permute-start | bytes 442376 | tf_op jit(solution)/shard_map/ppermute | solution.py:28
  38.6 7.2 %collective-permute-done.10.refs_1_ = bf16[9,32,256]{2,1,0:T(8,128)(2,1)S(1)} collective-permute-done((bf16[9,32,256]{2,1,0:T(8,128)(2,1)S(1)}, bf16[9,32,256]{2,1,0:T(8,128)(2,1)S(1)}, u32[]{:S(2)}, u32[]{:S(2)}) %collective-permute-start.10) | collective-permute-done | bytes 147488 | tf_op jit(solution)/shard_map/ppermute | solution.py:28
  46.2 0.9 %collective-permute-start.12 = (bf16[9,32,256]{2,1,0:T(8,128)(2,1)S(1)}, bf16[9,32,256]{2,1,0:T(8,128)(2,1)S(1)}, u32[]{:S(2)}, u32[]{:S(2)}) collective-permute-start(bf16[9,32,256]{2,1,0:T(8,128)(2,1)S(1)} %pair_sum.1.refs_0_), channel_id=1, source_target_pairs={{0,2},{2,0},{4,6},{6,4},{8,10},{10,8},{12,14},{14,12},{1,3},{3,1},... | collective-permute-start | bytes 442376 | tf_op jit(solution)/shard_map/ppermute | solution.py:28
  47.1 2.3 %collective-permute-start.11 = (bf16[9,32,256]{2,1,0:T(8,128)(2,1)S(1)}, bf16[9,32,256]{2,1,0:T(8,128)(2,1)S(1)}, u32[]{:S(2)}, u32[]{:S(2)}) collective-permute-start(bf16[9,32,256]{2,1,0:T(8,128)(2,1)S(1)} %pair_sum.1.refs_0_), channel_id=1, source_target_pairs={{0,4},{2,6},{4,0},{6,2},{8,12},{10,14},{12,8},{14,10},{1,5},{3,7},... | collective-permute-start | bytes 442376 | tf_op jit(solution)/shard_map/ppermute | solution.py:28
  49.4 4.1 %collective-permute-done.13.refs_3_ = bf16[9,32,256]{2,1,0:T(8,128)(2,1)S(1)} collective-permute-done((bf16[9,32,256]{2,1,0:T(8,128)(2,1)S(1)}, bf16[9,32,256]{2,1,0:T(8,128)(2,1)S(1)}, u32[]{:S(2)}, u32[]{:S(2)}) %collective-permute-start.13) | collective-permute-done | bytes 147488 | tf_op jit(solution)/shard_map/ppermute | solution.py:28
  53.5 1.3 %collective-permute-done.12.refs_2_ = bf16[9,32,256]{2,1,0:T(8,128)(2,1)S(1)} collective-permute-done((bf16[9,32,256]{2,1,0:T(8,128)(2,1)S(1)}, bf16[9,32,256]{2,1,0:T(8,128)(2,1)S(1)}, u32[]{:S(2)}, u32[]{:S(2)}) %collective-permute-start.12) | collective-permute-done | bytes 147488 | tf_op jit(solution)/shard_map/ppermute | solution.py:28
  54.8 0.6 collective-permute-done.11.refs_1_
  55.4 0.8 %collective-permute-done.16.refs_6_ = bf16[9,32,256]{2,1,0:T(8,128)(2,1)S(1)} collective-permute-done((bf16[9,32,256]{2,1,0:T(8,128)(2,1)S(1)}, bf16[9,32,256]{2,1,0:T(8,128)(2,1)S(1)}, u32[]{:S(2)}, u32[]{:S(2)}) %collective-permute-start.16) | collective-permute-done | bytes 147488 | tf_op jit(solution)/shard_map/ppermute | solution.py:28
  56.1 0.6 %collective-permute-done.15.refs_5_ = bf16[9,32,256]{2,1,0:T(8,128)(2,1)S(1)} collective-permute-done((bf16[9,32,256]{2,1,0:T(8,128)(2,1)S(1)}, bf16[9,32,256]{2,1,0:T(8,128)(2,1)S(1)}, u32[]{:S(2)}, u32[]{:S(2)}) %collective-permute-start.15) | collective-permute-done | bytes 147488 | tf_op jit(solution)/shard_map/ppermute | solution.py:28
  56.7 1.5 %spread_gradients.1 = f32[9,256,256]{2,1,0:T(8,128)} custom-call(bf16[9,32,256]{2,1,0:T(8,128)(2,1)S(1)} %pair_sum.1.refs_0_, bf16[9,32,256]{2,1,0:T(8,128)(2,1)S(1)} %collective-permute-done.11.refs_1_, bf16[9,32,256]{2,1,0:T(8,128)(2,1)S(1)} %collective-permute-done.12.refs_2_, bf16[9,32,256]{2,1,0:T(8,128)(2,1)S(1)} %collective-permute-done.13.refs_3_, ...), custom_call_target="tpu_custom_call" | custom-call | tf_op jit(solution)/shard_map/spread_gradients/pallas_call | solution.py:858
  (20 shorter events, 1.8 us)
Async XLA Ops:
  2.2 13.2 %collective-permute-start = (bf16[416,256]{1,0:T(8,128)(2,1)S(1)}, bf16[416,256]{1,0:T(8,128)(2,1)S(1)}, u32[]{:S(2)}, u32[]{:S(2)}) collective-permute-start(bf16[416,256]{1,0:T(8,128)(2,1)S(1)} %get-tuple-element.48), channel_id=1, source_target_pairs={{0,1},{1,0},{2,3},{3,2},{4,5},{5,4},{6,7},{7,6},{8,9},{9,8},{10,11... | collective-permute-start | bytes 638984 | tf_op jit(solution)/shard_map/ppermute | solution.py:28
  2.7 12.7 %collective-permute-start.1 = (bf16[416,256]{1,0:T(8,128)(2,1)S(1)}, bf16[416,256]{1,0:T(8,128)(2,1)S(1)}, u32[]{:S(2)}, u32[]{:S(2)}) collective-permute-start(bf16[416,256]{1,0:T(8,128)(2,1)S(1)} %get-tuple-element.49), channel_id=1, source_target_pairs={{0,13},{1,4},{2,15},{3,6},{4,1},{5,8},{6,3},{7,10},{8,5},{9,12},{1... | collective-permute-start | bytes 638984 | tf_op jit(solution)/shard_map/ppermute | solution.py:28
  7.4 8.0 %collective-permute-start.2 = (bf16[352,256]{1,0:T(8,128)(2,1)S(1)}, bf16[352,256]{1,0:T(8,128)(2,1)S(1)}, u32[]{:S(2)}, u32[]{:S(2)}) collective-permute-start(bf16[352,256]{1,0:T(8,128)(2,1)S(1)} %get-tuple-element.50), channel_id=1, source_target_pairs={{0,2},{1,3},{2,0},{3,1},{4,6},{5,7},{6,4},{7,5},{8,10},{9,11},{10,... | collective-permute-start | bytes 540680 | tf_op jit(solution)/shard_map/ppermute | solution.py:28
  8.9 5.5 %collective-permute-start.3 = (bf16[112,256]{1,0:T(8,128)(2,1)S(1)}, bf16[112,256]{1,0:T(8,128)(2,1)S(1)}, u32[]{:S(2)}, u32[]{:S(2)}) collective-permute-start(bf16[112,256]{1,0:T(8,128)(2,1)S(1)} %get-tuple-element.51), channel_id=1, source_target_pairs={{0,3},{1,2},{2,1},{3,0},{4,7},{5,6},{6,5},{7,4},{8,11},{9,10},{10,... | collective-permute-start | bytes 172040 | tf_op jit(solution)/shard_map/ppermute | solution.py:28
  8.9 6.5 %collective-permute-start.4 = (bf16[112,256]{1,0:T(8,128)(2,1)S(1)}, bf16[112,256]{1,0:T(8,128)(2,1)S(1)}, u32[]{:S(2)}, u32[]{:S(2)}) collective-permute-start(bf16[112,256]{1,0:T(8,128)(2,1)S(1)} %get-tuple-element.52), channel_id=1, source_target_pairs={{0,15},{1,6},{2,13},{3,4},{4,3},{5,10},{6,1},{7,8},{8,7},{9,14},{1... | collective-permute-start | bytes 172040 | tf_op jit(solution)/shard_map/ppermute | solution.py:28
  22.8 4.0 %collective-permute-start.6 = (bf16[6,128,256]{2,1,0:T(8,128)(2,1)S(1)}, bf16[6,128,256]{2,1,0:T(8,128)(2,1)S(1)}, u32[]{:S(2)}, u32[]{:S(2)}) collective-permute-start(bf16[6,128,256]{2,1,0:T(8,128)(2,1)S(1)} %get-tuple-element.68), channel_id=1, source_target_pairs={{0,1},{1,0},{2,3},{3,2},{4,5},{5,4},{6,7},{7,6},{8,9},{9,8},{10,11... | collective-permute-start | bytes 1179656 | tf_op jit(solution)/shard_map/ppermute | solution.py:28
  25.2 1.6 %collective-permute-start.5 = (bf16[3,128,256]{2,1,0:T(8,128)(2,1)S(1)}, bf16[3,128,256]{2,1,0:T(8,128)(2,1)S(1)}, u32[]{:S(2)}, u32[]{:S(2)}) collective-permute-start(bf16[3,128,256]{2,1,0:T(8,128)(2,1)S(1)} %get-tuple-element.66), channel_id=1, source_target_pairs={{0,1},{1,0},{2,3},{3,2},{4,5},{5,4},{6,7},{7,6},{8,9},{9,8},{10,11... | collective-permute-start | bytes 589832 | tf_op jit(solution)/shard_map/ppermute | solution.py:28
  26.9 6.7 %collective-permute-start.7 = (bf16[9,32,256]{2,1,0:T(8,128)(2,1)S(1)}, bf16[9,32,256]{2,1,0:T(8,128)(2,1)S(1)}, u32[]{:S(2)}, u32[]{:S(2)}) collective-permute-start(bf16[9,32,256]{2,1,0:T(8,128)(2,1)S(1)} %get-tuple-element.70), channel_id=1, source_target_pairs={{0,4},{2,6},{4,0},{6,2},{8,12},{10,14},{12,8},{14,10},{1,5},{3,7},... | collective-permute-start | bytes 442376 | tf_op jit(solution)/shard_map/ppermute | solution.py:28
  27.3 6.4 %collective-permute-start.8 = (bf16[9,32,256]{2,1,0:T(8,128)(2,1)S(1)}, bf16[9,32,256]{2,1,0:T(8,128)(2,1)S(1)}, u32[]{:S(2)}, u32[]{:S(2)}) collective-permute-start(bf16[9,32,256]{2,1,0:T(8,128)(2,1)S(1)} %get-tuple-element.71), channel_id=1, source_target_pairs={{0,2},{2,0},{4,6},{6,4},{8,10},{10,8},{12,14},{14,12},{1,3},{3,1},... | collective-permute-start | bytes 442376 | tf_op jit(solution)/shard_map/ppermute | solution.py:28
  28.8 7.8 %collective-permute-start.9 = (bf16[9,32,256]{2,1,0:T(8,128)(2,1)S(1)}, bf16[9,32,256]{2,1,0:T(8,128)(2,1)S(1)}, u32[]{:S(2)}, u32[]{:S(2)}) collective-permute-start(bf16[9,32,256]{2,1,0:T(8,128)(2,1)S(1)} %get-tuple-element.72), channel_id=1, source_target_pairs={{0,6},{2,4},{4,2},{6,0},{8,14},{10,12},{12,10},{14,8},{1,7},{3,5},... | collective-permute-start | bytes 442376 | tf_op jit(solution)/shard_map/ppermute | solution.py:28
  36.6 9.2 %collective-permute-start.10 = (bf16[9,32,256]{2,1,0:T(8,128)(2,1)S(1)}, bf16[9,32,256]{2,1,0:T(8,128)(2,1)S(1)}, u32[]{:S(2)}, u32[]{:S(2)}) collective-permute-start(bf16[9,32,256]{2,1,0:T(8,128)(2,1)S(1)} %block_sum.1.refs_0_), channel_id=1, source_target_pairs={{0,8},{2,10},{4,12},{6,14},{8,0},{10,2},{12,4},{14,6},{1,9},{3,11}... | collective-permute-start | bytes 442376 | tf_op jit(solution)/shard_map/ppermute | solution.py:28
  45.8 7.6 %collective-permute-start.13 = (bf16[9,32,256]{2,1,0:T(8,128)(2,1)S(1)}, bf16[9,32,256]{2,1,0:T(8,128)(2,1)S(1)}, u32[]{:S(2)}, u32[]{:S(2)}) collective-permute-start(bf16[9,32,256]{2,1,0:T(8,128)(2,1)S(1)} %pair_sum.1.refs_0_), channel_id=1, source_target_pairs={{0,6},{2,4},{4,2},{6,0},{8,14},{10,12},{12,10},{14,8},{1,7},{3,5},... | collective-permute-start | bytes 442376 | tf_op jit(solution)/shard_map/ppermute | solution.py:28
  46.2 8.6 %collective-permute-start.12 = (bf16[9,32,256]{2,1,0:T(8,128)(2,1)S(1)}, bf16[9,32,256]{2,1,0:T(8,128)(2,1)S(1)}, u32[]{:S(2)}, u32[]{:S(2)}) collective-permute-start(bf16[9,32,256]{2,1,0:T(8,128)(2,1)S(1)} %pair_sum.1.refs_0_), channel_id=1, source_target_pairs={{0,2},{2,0},{4,6},{6,4},{8,10},{10,8},{12,14},{14,12},{1,3},{3,1},... | collective-permute-start | bytes 442376 | tf_op jit(solution)/shard_map/ppermute | solution.py:28
  47.1 8.2 %collective-permute-start.11 = (bf16[9,32,256]{2,1,0:T(8,128)(2,1)S(1)}, bf16[9,32,256]{2,1,0:T(8,128)(2,1)S(1)}, u32[]{:S(2)}, u32[]{:S(2)}) collective-permute-start(bf16[9,32,256]{2,1,0:T(8,128)(2,1)S(1)} %pair_sum.1.refs_0_), channel_id=1, source_target_pairs={{0,4},{2,6},{4,0},{6,2},{8,12},{10,14},{12,8},{14,10},{1,5},{3,7},... | collective-permute-start | bytes 442376 | tf_op jit(solution)/shard_map/ppermute | solution.py:28
  49.4 6.0 %collective-permute-start.14 = (bf16[9,32,256]{2,1,0:T(8,128)(2,1)S(1)}, bf16[9,32,256]{2,1,0:T(8,128)(2,1)S(1)}, u32[]{:S(2)}, u32[]{:S(2)}) collective-permute-start(bf16[9,32,256]{2,1,0:T(8,128)(2,1)S(1)} %pair_sum.1.refs_0_), channel_id=1, source_target_pairs={{0,1},{1,0},{2,3},{3,2},{4,5},{5,4},{6,7},{7,6},{8,9},{9,8},{10,11... | collective-permute-start | bytes 442376 | tf_op jit(solution)/shard_map/ppermute | solution.py:28
  53.5 1.9 %collective-permute-start.17 = (bf16[9,32,256]{2,1,0:T(8,128)(2,1)S(1)}, bf16[9,32,256]{2,1,0:T(8,128)(2,1)S(1)}, u32[]{:S(2)}, u32[]{:S(2)}) collective-permute-start(bf16[9,32,256]{2,1,0:T(8,128)(2,1)S(1)} %collective-permute-done.13.refs_3_), channel_id=1, source_target_pairs={{0,1},{1,0},{2,3},{3,2},{4,5},{5,4},{6,7},{7,6},{8,9},{9,8},{10,11... | collective-permute-start | bytes 442376 | tf_op jit(solution)/shard_map/ppermute | solution.py:28
  54.8 1.4 %collective-permute-start.16 = (bf16[9,32,256]{2,1,0:T(8,128)(2,1)S(1)}, bf16[9,32,256]{2,1,0:T(8,128)(2,1)S(1)}, u32[]{:S(2)}, u32[]{:S(2)}) collective-permute-start(bf16[9,32,256]{2,1,0:T(8,128)(2,1)S(1)} %collective-permute-done.12.refs_2_), channel_id=1, source_target_pairs={{0,1},{1,0},{2,3},{3,2},{4,5},{5,4},{6,7},{7,6},{8,9},{9,8},{10,11... | collective-permute-start | bytes 442376 | tf_op jit(solution)/shard_map/ppermute | solution.py:28
  55.4 1.4 %collective-permute-start.15 = (bf16[9,32,256]{2,1,0:T(8,128)(2,1)S(1)}, bf16[9,32,256]{2,1,0:T(8,128)(2,1)S(1)}, u32[]{:S(2)}, u32[]{:S(2)}) collective-permute-start(bf16[9,32,256]{2,1,0:T(8,128)(2,1)S(1)} %collective-permute-done.11.refs_1_), channel_id=1, source_target_pairs={{0,1},{1,0},{2,3},{3,2},{4,5},{5,4},{6,7},{7,6},{8,9},{9,8},{10,11... | collective-permute-start | bytes 442376 | tf_op jit(solution)/shard_map/ppermute | solution.py:28

commit v7 on v6

--- a/solution.py
+++ b/solution.py
@@ -11,7 +11,6 @@
 WIDE = jnp.float32
 VMEM_BYTES = 24 * 1024 * 1024
 HALO_ROWS = 14
-BACK_ROWS = 14
 INNER_ROWS = 7
 CODE = LOW
 
@@ -274,8 +273,9 @@
 
 
 def put_halves(grad, keep, send, index, rep):
-    keep[index] = grad[pl.ds(pl.multiple_of(rep * 128, 128), 128), :]
-    send[index] = grad[pl.ds(pl.multiple_of((1 - rep) * 128, 128), 128), :].astype(LOW)
+    first, second = grad[0:128], grad[128:256]
+    keep[index] = jnp.where(rep == 0, first, second)
+    send[index] = jnp.where(rep == 0, second, first).astype(LOW)
 
 
 def main_kernel(
@@ -283,7 +283,7 @@
 ):
     grid, m1, cot, m2, codes, pool_in, ssum_in, masks, spread, gather = own
     mesh_out, keep, send, fd_out, pool_out, ssum, sx, slope, hx, hslope = outs
-    gx, m1x, recv, ko, k2, uv, pool, fx, cx, m2x, ohu, su, uslope, dd, acc_s = scratch
+    gx, m1x, recv, ko, k2, uv, pool, fx, cx, m2x, ohu, su, uslope, dd = scratch
     rep = lax.axis_index("rep")
     lat = lax.axis_index("lat")
     frame = m1x.shape[0]
@@ -504,8 +504,7 @@
     dd[1] = act.astype(LOW).reshape(c_frame, 32, 256)
 
     def put_grad(index, value):
-        acc_s[...] = value
-        put_halves(acc_s, keep, send, index - 3, rep)
+        put_halves(value, keep, send, index - 3, rep)
 
     act_own = dd[1, pl.ds(c_own, 16), 0:16].reshape(256, 256)
     delta_own = dd[0, pl.ds(c_own, 16), 0:16].reshape(256, 256)
@@ -532,20 +531,20 @@
     put_grad(5, mm_tn(up_pool, own_delta))
     pool2 = jnp.where(is_real, mm_nt(coarse_delta, weights[5]) * (1.0 / 16), 0.0)
     own_f = jnp.where(is_own, 1.0, 0.0)
-    recv[...] = jnp.zeros_like(recv)
-    acc_s[...] = jnp.zeros_like(acc_s)
-    node_sums = []
+    node_sums, own_deltas, backs = [], [], []
     for aa in range(a_frame):
         d = pool2[aa * 16 : aa * 16 + 16][None] * uslope[aa].reshape(8, 16, 256)
         mine = own_f[aa * 16 : aa * 16 + 16][None]
         up_delta = d.astype(LOW)
-        wide = up_delta.astype(WIDE)
-        owned = wide * mine
+        owned = up_delta.astype(WIDE) * mine
         node_sums.append(jnp.sum(owned, axis=0))
-        back = mm_tn(ohu[aa], up_delta.reshape(128, 256)).reshape(4, 32, 256)
-        recv[2 * aa : 2 * aa + 4] += back[:, 0:24]
-        acc_s[...] += mm_tn(su[aa], owned.reshape(128, 256).astype(LOW))
-    put_grad(3, acc_s[...])
+        own_deltas.append(owned.reshape(128, 256).astype(LOW))
+        backs.append(mm_tn(ohu[aa], up_delta.reshape(128, 256)).reshape(4, 32, 256))
+    for pair in range(a_frame + 1):
+        parts = [backs[pair][0:2]] if pair < a_frame else []
+        parts += [backs[pair - 1][2:4]] if pair else []
+        recv[2 * pair : 2 * pair + 2] = sum(parts[1:], parts[0])[:, 0:24]
+    put_grad(3, mm_tn(su[...].reshape(a_frame * 128, 256), jnp.concatenate(own_deltas, 0)))
     ns_high, ns_low = two_parts(jnp.concatenate(node_sums, 0))
     put_grad(4, mm_tn(m2_low, ns_high) + mm_tn(m2_low, ns_low))
     back_high, back_low = two_parts(recv[pl.ds(f_own, 16), 0:16].reshape(256, 256))
@@ -560,7 +559,7 @@
 
 
 def back_kernel(
-    m1, weights, fine_delta, pool, ssum, sx_in, slope_in, sx_edge, slope_edge, hx, hslope, mesh1_grad, keep, send, pd, acc
+    m1, weights, fine_delta, pool, ssum, sx_in, slope_in, sx_edge, slope_edge, hx, hslope, mesh1_grad, keep, send, pd
 ):
     rep = lax.axis_index("rep")
     delta_b = fine_delta[...].astype(LOW)
@@ -571,10 +570,8 @@
     m1_own = m1[...].reshape(256, 256)
     grad_in = fine_delta[...] + (mm_nt(high, weights[1]) + mm_nt(low, weights[1]))
     mesh1_grad[...] = grad_in.astype(LOW).reshape(16, 16, 256)
-    acc[...] = mm_tn(pool[...], delta_b)
-    put_halves(acc, keep, send, 2, rep)
-    acc[...] = mm_tn(m1_own, high) + mm_tn(m1_own, low)
-    put_halves(acc, keep, send, 1, rep)
+    put_halves(mm_tn(pool[...], delta_b), keep, send, 2, rep)
+    put_halves(mm_tn(m1_own, high) + mm_tn(m1_own, low), keep, send, 1, rep)
 
     def deltas_of(r, tile, rise):
         d = pd[r, tile * 8 : tile * 8 + 8][None] * rise.reshape(16, 8, 256)
@@ -585,24 +582,15 @@
         senders.append(sx_edge[i].reshape(256, 256))
         for tile in range(2):
             deltas.append(deltas_of(r, tile, slope_edge[i, tile].astype(WIDE)))
-    acc[...] = mm_tn(jnp.concatenate(senders, 0), jnp.concatenate(deltas, 0))
     slots = iota((128, 256), 0) % 8
-
-    def rows(step, carry):
-        senders, deltas = [], []
-        for k in range(BACK_ROWS):
-            r = 1 + BACK_ROWS * step + k
-            halo = hx[r - 1].astype(WIDE)
-            halo_rise = hslope[r - 1].astype(WIDE)
-            for tile, slot in ((0, 0), (1, 7)):
-                ours = slots == slot
-                senders.append(jnp.where(ours, halo, sx_in[r, tile].astype(WIDE)).astype(LOW))
-                deltas.append(deltas_of(r, tile, jnp.where(ours, halo_rise, slope_in[r, tile].astype(WIDE))))
-        acc[...] += mm_tn(jnp.concatenate(senders, 0), jnp.concatenate(deltas, 0))
-        return carry
-
-    lax.fori_loop(0, 14 // BACK_ROWS, rows, 0)
-    put_halves(acc, keep, send, 0, rep)
+    for r in range(1, 15):
+        halo = hx[r - 1].astype(WIDE)
+        halo_rise = hslope[r - 1].astype(WIDE)
+        for tile, slot in ((0, 0), (1, 7)):
+            ours = slots == slot
+            senders.append(jnp.where(ours, halo, sx_in[r, tile].astype(WIDE)).astype(LOW))
+            deltas.append(deltas_of(r, tile, jnp.where(ours, halo_rise, slope_in[r, tile].astype(WIDE))))
+    put_halves(mm_tn(jnp.concatenate(senders, 0), jnp.concatenate(deltas, 0)), keep, send, 0, rep)
 
 
 def block_place():
@@ -641,18 +629,17 @@
     )(*values)
 
 
-def spread_kernel(scale, *refs):
-    pieces, (out, stage, sems) = refs[:8], refs[8:]
+def spread_kernel(scale, own, *refs):
+    pieces, (out, stage, sems) = refs[:4], refs[-3:]
     rep = lax.axis_index("rep")
     place = block_place()
+    half = pl.multiple_of((rep if own else 1 - rep) * 128, 128)
     copies = []
     for k in range(9):
         for step in range(4):
-            at = (place ^ step) * 32
-            for half, piece in ((rep, pieces[step]), (1 - rep, pieces[4 + step])):
-                rows = pl.ds(pl.multiple_of(half * 128 + at, 32), 32)
-                stage[k, rows, :] = piece[k].astype(WIDE) * scale
-        copies.append(pltpu.make_async_copy(stage.at[k], out.at[k], sems.at[k]))
+            rows = pl.ds(pl.multiple_of((place ^ step) * 32, 32), 32)
+            stage[k, rows, :] = pieces[step][k].astype(WIDE) * scale
+        copies.append(pltpu.make_async_copy(stage.at[k], out.at[k, pl.ds(half, 128)], sems.at[k]))
         copies[-1].start()
     for copy in copies:
         copy.wait()
@@ -812,7 +799,6 @@
         pltpu.VMEM((a_frame, 128, 256), LOW),
         pltpu.VMEM((a_frame, 128, 256), WIDE),
         pltpu.VMEM((2, c_frame, 32, 256), LOW),
-        pltpu.VMEM((256, 256), WIDE),
     ]
     n_in = 10 + 2 + len(got_bands) + 1
     mesh_out, kept, sent, fine_delta, pool, ssum, sx_edge, slope_edge, hx, hslope = pl.pallas_call(
@@ -846,7 +832,7 @@
         ],
         in_specs=[vmem] * 11,
         out_specs=[vmem] * 3,
-        scratch_shapes=[pltpu.VMEM((16, 16, 256), WIDE), pltpu.VMEM((256, 256), WIDE)],
+        scratch_shapes=[pltpu.VMEM((16, 16, 256), WIDE)],
         compiler_params=params,
         cost_estimate=pl.CostEstimate(flops=3_000_000_000, bytes_accessed=8_000_000, transcendentals=0),
         name="encoder_back",
@@ -855,15 +841,19 @@
     scale = float(node_total) ** (-0.5)
     quarters = reduction.quarters(kept_first, reduction.siblings(sent_first), kept, got)
     pieces = reduction.pieces(reduction.total(reduction.block(quarters)))
-    weight_grads = pl.pallas_call(
-        functools.partial(spread_kernel, scale),
-        out_shape=jax.ShapeDtypeStruct((9, 256, 256), WIDE),
-        in_specs=[vmem] * 8,
-        out_specs=hbm,
-        scratch_shapes=[pltpu.VMEM((9, 256, 256), WIDE), pltpu.SemaphoreType.DMA((9,))],
-        compiler_params=params,
-        name="spread_gradients",
-    )(*pieces)
+    weight_grads = None
+    for own in (True, False):
+        before = [] if own else [weight_grads]
+        weight_grads = pl.pallas_call(
+            functools.partial(spread_kernel, scale, own),
+            out_shape=jax.ShapeDtypeStruct((9, 256, 256), WIDE),
+            in_specs=[vmem] * 4 + [hbm] * len(before),
+            out_specs=hbm,
+            scratch_shapes=[pltpu.VMEM((9, 128, 256), WIDE), pltpu.SemaphoreType.DMA((9,))],
+            input_output_aliases={} if own else {4: 0},
+            compiler_params=pltpu.CompilerParams(vmem_limit_bytes=8 * 1024 * 1024),
+            name="spread_own" if own else "spread_other",
+        )(*(pieces[:4] if own else pieces[4:]), *before)
     return (mesh_out, mesh1_grad, weight_grads)
 
 

time: 58.4 us -> 57.8 us (0.990)
  waiting for transfers between devices: 22.9 us -> 21.8 us
    ppermute x18, waiting for transfers between devices: 22.9 us -> 21.8 us  [permute(): lax.ppermute(values, axes, [(i, j) for i, j in pairs if j is not None])]
    pallas_call x1 -> x2, Pallas kernels: 1.51 us -> 2.21 us  [body(): pl.pallas_call(functools.partial(spread_kernel, scale, own), out_shape=ja...]
  transfers between devices with their start and end apart: 18 -> 18, of which waited for: 12 -> 11; matrix products, arithmetic and copies ran while one was open for 0% -> 0% of each run, Pallas kernels for 10% -> 12%
where the time goes in v7:
time: 57.8 us; the launch traced here: 57.6 us
  waiting for transfers between devices  21.8 us (38%)
  starting transfers between devices  18 us (31%)
  Pallas kernels  17.1 us (30%)
  between operations  0.71 us (1%)
    ppermute x18, waiting for transfers between devices, permute(): lax.ppermute(values, axes, [(i, j) for i, j in pairs if j is not None])  21.8 us
    ppermute x18, starting transfers between devices, permute(): lax.ppermute(values, axes, [(i, j) for i, j in pairs if j is not None])  18 us
    pallas_call x1, Pallas kernels, body(): pl.pallas_call(functools.partial(flat_main, dirs, n_lat), out_shape=[jax....  7.3 us
    pallas_call x1, Pallas kernels, body(): pl.pallas_call(inner_kernel, out_shape=[jax.ShapeDtypeStruct((16, 2, 128,...  3.58 us
    pallas_call x1, Pallas kernels, body(): pl.pallas_call(back_kernel, out_shape=[jax.ShapeDtypeStruct(mesh1_state.s...  2.29 us
    pallas_call x2, Pallas kernels, body(): pl.pallas_call(functools.partial(spread_kernel, scale, own), out_shape=ja...  2.21 us
    pallas_call x1, Pallas kernels, body(): pl.pallas_call(functools.partial(pack_kernel, dirs, glon, m1lon), out_sha...  1.53 us
  transfers between devices with their start and end apart: 18, of which 11 were waited for; matrix products, arithmetic and copies ran while one was open for 0% of the time, Pallas kernels for 12%

profile of v7, /device:TPU:0, one launch (start us, length us, event | category | flops | bytes accessed | tf_op | source)
XLA Modules:
  0.0 57.6 jit_solution(17361793275978838692)
XLA Ops:
  0.6 1.5 %pack_halos.1 = (bf16[32,32,256]{2,1,0:T(8,128)(2,1)S(1)}, bf16[16,16,256]{2,1,0:T(8,128)(2,1)S(1)}, bf16[16,16,256]{2,1,0:T(8,128)(2,1)S(1)}, bf16[8,16,256]{2,...) custom-call(bf16[32,32,256]{2,1,0:T(8,128)(2,1)} %refs_0_.1, ...), custom_call_target="tpu_custom_call" | custom-call | tf_op jit(solution)/shard_map/pack_halos/pallas_call | solution.py:711
  2.2 0.5 collective-permute-start
  2.7 4.7 %collective-permute-start.1 = (bf16[416,256]{1,0:T(8,128)(2,1)S(1)}, bf16[416,256]{1,0:T(8,128)(2,1)S(1)}, u32[]{:S(2)}, u32[]{:S(2)}) collective-permute-start(bf16[416,256]{1,0:T(8,128)(2,1)S(1)} %get-tuple-element.49), channel_id=1, source_target_pairs={{0,13},{1,4},{2,15},{3,6},{4,1},{5,8},{6,3},{7,10},{8,5},{9,12},{1... | collective-permute-start | bytes 638984 | tf_op jit(solution)/shard_map/ppermute | solution.py:27
  7.4 1.5 %collective-permute-start.2 = (bf16[352,256]{1,0:T(8,128)(2,1)S(1)}, bf16[352,256]{1,0:T(8,128)(2,1)S(1)}, u32[]{:S(2)}, u32[]{:S(2)}) collective-permute-start(bf16[352,256]{1,0:T(8,128)(2,1)S(1)} %get-tuple-element.50), channel_id=1, source_target_pairs={{0,2},{1,3},{2,0},{3,1},{4,6},{5,7},{6,4},{7,5},{8,10},{9,11},{10,... | collective-permute-start | bytes 540680 | tf_op jit(solution)/shard_map/ppermute | solution.py:27
  8.9 1.6 %collective-permute-start.4 = (bf16[112,256]{1,0:T(8,128)(2,1)S(1)}, bf16[112,256]{1,0:T(8,128)(2,1)S(1)}, u32[]{:S(2)}, u32[]{:S(2)}) collective-permute-start(bf16[112,256]{1,0:T(8,128)(2,1)S(1)} %get-tuple-element.52), channel_id=1, source_target_pairs={{0,15},{1,6},{2,13},{3,4},{4,3},{5,10},{6,1},{7,8},{8,7},{9,14},{1... | collective-permute-start | bytes 172040 | tf_op jit(solution)/shard_map/ppermute | solution.py:27
  10.5 3.6 %inner_rows.1 = (bf16[16,2,128,256]{3,2,1,0:T(8,128)(2,1)S(1)}, bf16[16,2,128,256]{3,2,1,0:T(8,128)(2,1)S(1)}, f32[16,16,256]{2,1,0:T(8,128)S(1)}, f32[16,16,256...) custom-call(bf16[32,32,256]{2,1,0:T(8,128)(2,1)S(1)} %get-tuple-elem, ...), custom_call_target="tpu_custom_call" | custom-call | flops 1000000000 | bytes 1000 | tf_op jit(solution)/shard_map/inner_rows/pallas_call | solution.py:729
  14.4 1.0 %collective-permute-done.4.refs_14_ = bf16[112,256]{1,0:T(8,128)(2,1)S(1)} collective-permute-done((bf16[112,256]{1,0:T(8,128)(2,1)S(1)}, bf16[112,256]{1,0:T(8,128)(2,1)S(1)}, u32[]{:S(2)}, u32[]{:S(2)}) %collective-permute-start.4) | collective-permute-done | bytes 57376 | tf_op jit(solution)/shard_map/ppermute | solution.py:27
  15.4 7.3 %sweep.1 = (bf16[16,16,256]{2,1,0:T(8,128)(2,1)}, f32[6,128,256]{2,1,0:T(8,128)S(1)}, bf16[6,128,256]{2,1,0:T(8,128)(2,1)S(1)}, f32[256,256]{1,0:T(8,128)S(1)}, ...) custom-call(bf16[32,32,256]{2,1,0:T(8,128)(2,1)S(1)} %get-tuple-elem, ...), custom_call_target="tpu_custom_call" | custom-call | tf_op jit(solution)/shard_map/sweep/pallas_call | solution.py:804
  22.7 2.3 %encoder_back.1 = (bf16[16,16,256]{2,1,0:T(8,128)(2,1)}, f32[3,128,256]{2,1,0:T(8,128)S(1)}, bf16[3,128,256]{2,1,0:T(8,128)(2,1)S(1)}) custom-call(bf16[16,16,256]{2,1,0:T(8,128)(2,1)S(1)} %get-tuple-element.39.m1.refs_1_, bf16[9,256,256]{2,1,0:T(8,128)(2,1)S(1)} %get-tuple-element.53.refs_15_.weights, f32[256,256]{1,0:T(8,128)S(1)} %get-tuple-element.55.fine_delta, ...), custom_call_target="tpu_custom_call" | custom-call | flops 3000000000 | bytes 8000000 | tf_op jit(solution)/shard_map/encoder_back/pallas_call | solution.py:826
  25.0 0.5 collective-permute-start.5
  25.5 1.1 %collective-permute-done.5.got_first = bf16[3,128,256]{2,1,0:T(8,128)(2,1)S(1)} collective-permute-done((bf16[3,128,256]{2,1,0:T(8,128)(2,1)S(1)}, bf16[3,128,256]{2,1,0:T(8,128)(2,1)S(1)}, u32[]{:S(2)}, u32[]{:S(2)}) %collective-permute-start.5) | collective-permute-done | bytes 196640 | tf_op jit(solution)/shard_map/ppermute | solution.py:27
  27.1 1.5 %collective-permute-start.8 = (bf16[9,32,256]{2,1,0:T(8,128)(2,1)S(1)}, bf16[9,32,256]{2,1,0:T(8,128)(2,1)S(1)}, u32[]{:S(2)}, u32[]{:S(2)}) collective-permute-start(bf16[9,32,256]{2,1,0:T(8,128)(2,1)S(1)} %get-tuple-element.71), channel_id=1, source_target_pairs={{0,2},{2,0},{4,6},{6,4},{8,10},{10,8},{12,14},{14,12},{1,3},{3,1},... | collective-permute-start | bytes 442376 | tf_op jit(solution)/shard_map/ppermute | solution.py:27
  28.6 1.7 %collective-permute-start.9 = (bf16[9,32,256]{2,1,0:T(8,128)(2,1)S(1)}, bf16[9,32,256]{2,1,0:T(8,128)(2,1)S(1)}, u32[]{:S(2)}, u32[]{:S(2)}) collective-permute-start(bf16[9,32,256]{2,1,0:T(8,128)(2,1)S(1)} %get-tuple-element.72), channel_id=1, source_target_pairs={{0,6},{2,4},{4,2},{6,0},{8,14},{10,12},{12,10},{14,8},{1,7},{3,5},... | collective-permute-start | bytes 442376 | tf_op jit(solution)/shard_map/ppermute | solution.py:27
  30.2 3.2 %collective-permute-done.7.refs_1_ = bf16[9,32,256]{2,1,0:T(8,128)(2,1)S(1)} collective-permute-done((bf16[9,32,256]{2,1,0:T(8,128)(2,1)S(1)}, bf16[9,32,256]{2,1,0:T(8,128)(2,1)S(1)}, u32[]{:S(2)}, u32[]{:S(2)}) %collective-permute-start.7) | collective-permute-done | bytes 147488 | tf_op jit(solution)/shard_map/ppermute | solution.py:27
  33.5 2.9 %collective-permute-done.9.refs_3_ = bf16[9,32,256]{2,1,0:T(8,128)(2,1)S(1)} collective-permute-done((bf16[9,32,256]{2,1,0:T(8,128)(2,1)S(1)}, bf16[9,32,256]{2,1,0:T(8,128)(2,1)S(1)}, u32[]{:S(2)}, u32[]{:S(2)}) %collective-permute-start.9) | collective-permute-done | bytes 147488 | tf_op jit(solution)/shard_map/ppermute | solution.py:27
  36.4 2.0 %collective-permute-start.10 = (bf16[9,32,256]{2,1,0:T(8,128)(2,1)S(1)}, bf16[9,32,256]{2,1,0:T(8,128)(2,1)S(1)}, u32[]{:S(2)}, u32[]{:S(2)}) collective-permute-start(bf16[9,32,256]{2,1,0:T(8,128)(2,1)S(1)} %block_sum.1.refs_0_), channel_id=1, source_target_pairs={{0,8},{2,10},{4,12},{6,14},{8,0},{10,2},{12,4},{14,6},{1,9},{3,11}... | collective-permute-start | bytes 442376 | tf_op jit(solution)/shard_map/ppermute | solution.py:27
  38.4 7.2 %collective-permute-done.10.refs_1_ = bf16[9,32,256]{2,1,0:T(8,128)(2,1)S(1)} collective-permute-done((bf16[9,32,256]{2,1,0:T(8,128)(2,1)S(1)}, bf16[9,32,256]{2,1,0:T(8,128)(2,1)S(1)}, u32[]{:S(2)}, u32[]{:S(2)}) %collective-permute-start.10) | collective-permute-done | bytes 147488 | tf_op jit(solution)/shard_map/ppermute | solution.py:27
  46.0 0.9 %collective-permute-start.14 = (bf16[9,32,256]{2,1,0:T(8,128)(2,1)S(1)}, bf16[9,32,256]{2,1,0:T(8,128)(2,1)S(1)}, u32[]{:S(2)}, u32[]{:S(2)}) collective-permute-start(bf16[9,32,256]{2,1,0:T(8,128)(2,1)S(1)} %pair_sum.1.refs_0_), channel_id=1, source_target_pairs={{0,2},{2,0},{4,6},{6,4},{8,10},{10,8},{12,14},{14,12},{1,3},{3,1},... | collective-permute-start | bytes 442376 | tf_op jit(solution)/shard_map/ppermute | solution.py:27
  46.9 2.3 %collective-permute-start.12 = (bf16[9,32,256]{2,1,0:T(8,128)(2,1)S(1)}, bf16[9,32,256]{2,1,0:T(8,128)(2,1)S(1)}, u32[]{:S(2)}, u32[]{:S(2)}) collective-permute-start(bf16[9,32,256]{2,1,0:T(8,128)(2,1)S(1)} %pair_sum.1.refs_0_), channel_id=1, source_target_pairs={{0,4},{2,6},{4,0},{6,2},{8,12},{10,14},{12,8},{14,10},{1,5},{3,7},... | collective-permute-start | bytes 442376 | tf_op jit(solution)/shard_map/ppermute | solution.py:27
  49.2 4.1 %collective-permute-done.16.refs_3_ = bf16[9,32,256]{2,1,0:T(8,128)(2,1)S(1)} collective-permute-done((bf16[9,32,256]{2,1,0:T(8,128)(2,1)S(1)}, bf16[9,32,256]{2,1,0:T(8,128)(2,1)S(1)}, u32[]{:S(2)}, u32[]{:S(2)}) %collective-permute-start.16) | collective-permute-done | bytes 147488 | tf_op jit(solution)/shard_map/ppermute | solution.py:27
  53.3 1.3 %collective-permute-done.14.refs_2_ = bf16[9,32,256]{2,1,0:T(8,128)(2,1)S(1)} collective-permute-done((bf16[9,32,256]{2,1,0:T(8,128)(2,1)S(1)}, bf16[9,32,256]{2,1,0:T(8,128)(2,1)S(1)}, u32[]{:S(2)}, u32[]{:S(2)}) %collective-permute-start.14) | collective-permute-done | bytes 147488 | tf_op jit(solution)/shard_map/ppermute | solution.py:27
  54.6 0.6 %collective-permute-done.12.refs_1_ = bf16[9,32,256]{2,1,0:T(8,128)(2,1)S(1)} collective-permute-done((bf16[9,32,256]{2,1,0:T(8,128)(2,1)S(1)}, bf16[9,32,256]{2,1,0:T(8,128)(2,1)S(1)}, u32[]{:S(2)}, u32[]{:S(2)}) %collective-permute-start.12) | collective-permute-done | bytes 147488 | tf_op jit(solution)/shard_map/ppermute | solution.py:27
  55.2 1.1 %spread_own.1.refs_4_ = f32[9,256,256]{2,1,0:T(8,128)} custom-call(bf16[9,32,256]{2,1,0:T(8,128)(2,1)S(1)} %pair_sum.1.refs_0_, bf16[9,32,256]{2,1,0:T(8,128)(2,1)S(1)} %collective-permute-done.12.refs_1_, bf16[9,32,256]{2,1,0:T(8,128)(2,1)S(1)} %collective-permute-done.14.refs_2_, bf16[9,32,256]{2,1,0:T(8,128)(2,1)S(1)} %collective-permute-done.16.refs_3_), custom_call_target="tpu_custom_call" | custom-call | tf_op jit(solution)/shard_map/spread_own/pallas_call | solution.py:847
  56.5 1.1 %spread_other.1 = f32[9,256,256]{2,1,0:T(8,128)} custom-call(bf16[9,32,256]{2,1,0:T(8,128)(2,1)S(1)} %collective-permute-done.11.refs_0_, bf16[9,32,256]{2,1,0:T(8,128)(2,1)S(1)} %collective-permute-done.13.refs_1_, bf16[9,32,256]{2,1,0:T(8,128)(2,1)S(1)} %collective-permute-done.15.refs_2_, ...), custom_call_target="tpu_custom_call", output_to_operand_aliasing={{}: (4, {})} | custom-call | tf_op jit(solution)/shard_map/spread_other/pallas_call | solution.py:847
  (21 shorter events, 1.5 us)
Async XLA Ops:
  2.2 13.2 %collective-permute-start = (bf16[416,256]{1,0:T(8,128)(2,1)S(1)}, bf16[416,256]{1,0:T(8,128)(2,1)S(1)}, u32[]{:S(2)}, u32[]{:S(2)}) collective-permute-start(bf16[416,256]{1,0:T(8,128)(2,1)S(1)} %get-tuple-element.48), channel_id=1, source_target_pairs={{0,1},{1,0},{2,3},{3,2},{4,5},{5,4},{6,7},{7,6},{8,9},{9,8},{10,11... | collective-permute-start | bytes 638984 | tf_op jit(solution)/shard_map/ppermute | solution.py:27
  2.7 12.7 %collective-permute-start.1 = (bf16[416,256]{1,0:T(8,128)(2,1)S(1)}, bf16[416,256]{1,0:T(8,128)(2,1)S(1)}, u32[]{:S(2)}, u32[]{:S(2)}) collective-permute-start(bf16[416,256]{1,0:T(8,128)(2,1)S(1)} %get-tuple-element.49), channel_id=1, source_target_pairs={{0,13},{1,4},{2,15},{3,6},{4,1},{5,8},{6,3},{7,10},{8,5},{9,12},{1... | collective-permute-start | bytes 638984 | tf_op jit(solution)/shard_map/ppermute | solution.py:27
  7.4 8.0 %collective-permute-start.2 = (bf16[352,256]{1,0:T(8,128)(2,1)S(1)}, bf16[352,256]{1,0:T(8,128)(2,1)S(1)}, u32[]{:S(2)}, u32[]{:S(2)}) collective-permute-start(bf16[352,256]{1,0:T(8,128)(2,1)S(1)} %get-tuple-element.50), channel_id=1, source_target_pairs={{0,2},{1,3},{2,0},{3,1},{4,6},{5,7},{6,4},{7,5},{8,10},{9,11},{10,... | collective-permute-start | bytes 540680 | tf_op jit(solution)/shard_map/ppermute | solution.py:27
  8.9 5.5 %collective-permute-start.3 = (bf16[112,256]{1,0:T(8,128)(2,1)S(1)}, bf16[112,256]{1,0:T(8,128)(2,1)S(1)}, u32[]{:S(2)}, u32[]{:S(2)}) collective-permute-start(bf16[112,256]{1,0:T(8,128)(2,1)S(1)} %get-tuple-element.51), channel_id=1, source_target_pairs={{0,3},{1,2},{2,1},{3,0},{4,7},{5,6},{6,5},{7,4},{8,11},{9,10},{10,... | collective-permute-start | bytes 172040 | tf_op jit(solution)/shard_map/ppermute | solution.py:27
  8.9 6.5 %collective-permute-start.4 = (bf16[112,256]{1,0:T(8,128)(2,1)S(1)}, bf16[112,256]{1,0:T(8,128)(2,1)S(1)}, u32[]{:S(2)}, u32[]{:S(2)}) collective-permute-start(bf16[112,256]{1,0:T(8,128)(2,1)S(1)} %get-tuple-element.52), channel_id=1, source_target_pairs={{0,15},{1,6},{2,13},{3,4},{4,3},{5,10},{6,1},{7,8},{8,7},{9,14},{1... | collective-permute-start | bytes 172040 | tf_op jit(solution)/shard_map/ppermute | solution.py:27
  22.7 3.9 %collective-permute-start.6 = (bf16[6,128,256]{2,1,0:T(8,128)(2,1)S(1)}, bf16[6,128,256]{2,1,0:T(8,128)(2,1)S(1)}, u32[]{:S(2)}, u32[]{:S(2)}) collective-permute-start(bf16[6,128,256]{2,1,0:T(8,128)(2,1)S(1)} %get-tuple-element.68), channel_id=1, source_target_pairs={{0,1},{1,0},{2,3},{3,2},{4,5},{5,4},{6,7},{7,6},{8,9},{9,8},{10,11... | collective-permute-start | bytes 1179656 | tf_op jit(solution)/shard_map/ppermute | solution.py:27
  25.0 1.6 %collective-permute-start.5 = (bf16[3,128,256]{2,1,0:T(8,128)(2,1)S(1)}, bf16[3,128,256]{2,1,0:T(8,128)(2,1)S(1)}, u32[]{:S(2)}, u32[]{:S(2)}) collective-permute-start(bf16[3,128,256]{2,1,0:T(8,128)(2,1)S(1)} %get-tuple-element.66), channel_id=1, source_target_pairs={{0,1},{1,0},{2,3},{3,2},{4,5},{5,4},{6,7},{7,6},{8,9},{9,8},{10,11... | collective-permute-start | bytes 589832 | tf_op jit(solution)/shard_map/ppermute | solution.py:27
  26.7 6.7 %collective-permute-start.7 = (bf16[9,32,256]{2,1,0:T(8,128)(2,1)S(1)}, bf16[9,32,256]{2,1,0:T(8,128)(2,1)S(1)}, u32[]{:S(2)}, u32[]{:S(2)}) collective-permute-start(bf16[9,32,256]{2,1,0:T(8,128)(2,1)S(1)} %get-tuple-element.70), channel_id=1, source_target_pairs={{0,4},{2,6},{4,0},{6,2},{8,12},{10,14},{12,8},{14,10},{1,5},{3,7},... | collective-permute-start | bytes 442376 | tf_op jit(solution)/shard_map/ppermute | solution.py:27
  27.1 6.4 %collective-permute-start.8 = (bf16[9,32,256]{2,1,0:T(8,128)(2,1)S(1)}, bf16[9,32,256]{2,1,0:T(8,128)(2,1)S(1)}, u32[]{:S(2)}, u32[]{:S(2)}) collective-permute-start(bf16[9,32,256]{2,1,0:T(8,128)(2,1)S(1)} %get-tuple-element.71), channel_id=1, source_target_pairs={{0,2},{2,0},{4,6},{6,4},{8,10},{10,8},{12,14},{14,12},{1,3},{3,1},... | collective-permute-start | bytes 442376 | tf_op jit(solution)/shard_map/ppermute | solution.py:27
  28.6 7.8 %collective-permute-start.9 = (bf16[9,32,256]{2,1,0:T(8,128)(2,1)S(1)}, bf16[9,32,256]{2,1,0:T(8,128)(2,1)S(1)}, u32[]{:S(2)}, u32[]{:S(2)}) collective-permute-start(bf16[9,32,256]{2,1,0:T(8,128)(2,1)S(1)} %get-tuple-element.72), channel_id=1, source_target_pairs={{0,6},{2,4},{4,2},{6,0},{8,14},{10,12},{12,10},{14,8},{1,7},{3,5},... | collective-permute-start | bytes 442376 | tf_op jit(solution)/shard_map/ppermute | solution.py:27
  36.4 9.2 %collective-permute-start.10 = (bf16[9,32,256]{2,1,0:T(8,128)(2,1)S(1)}, bf16[9,32,256]{2,1,0:T(8,128)(2,1)S(1)}, u32[]{:S(2)}, u32[]{:S(2)}) collective-permute-start(bf16[9,32,256]{2,1,0:T(8,128)(2,1)S(1)} %block_sum.1.refs_0_), channel_id=1, source_target_pairs={{0,8},{2,10},{4,12},{6,14},{8,0},{10,2},{12,4},{14,6},{1,9},{3,11}... | collective-permute-start | bytes 442376 | tf_op jit(solution)/shard_map/ppermute | solution.py:27
  45.6 7.6 %collective-permute-start.16 = (bf16[9,32,256]{2,1,0:T(8,128)(2,1)S(1)}, bf16[9,32,256]{2,1,0:T(8,128)(2,1)S(1)}, u32[]{:S(2)}, u32[]{:S(2)}) collective-permute-start(bf16[9,32,256]{2,1,0:T(8,128)(2,1)S(1)} %pair_sum.1.refs_0_), channel_id=1, source_target_pairs={{0,6},{2,4},{4,2},{6,0},{8,14},{10,12},{12,10},{14,8},{1,7},{3,5},... | collective-permute-start | bytes 442376 | tf_op jit(solution)/shard_map/ppermute | solution.py:27
  46.0 8.6 %collective-permute-start.14 = (bf16[9,32,256]{2,1,0:T(8,128)(2,1)S(1)}, bf16[9,32,256]{2,1,0:T(8,128)(2,1)S(1)}, u32[]{:S(2)}, u32[]{:S(2)}) collective-permute-start(bf16[9,32,256]{2,1,0:T(8,128)(2,1)S(1)} %pair_sum.1.refs_0_), channel_id=1, source_target_pairs={{0,2},{2,0},{4,6},{6,4},{8,10},{10,8},{12,14},{14,12},{1,3},{3,1},... | collective-permute-start | bytes 442376 | tf_op jit(solution)/shard_map/ppermute | solution.py:27
  46.9 8.2 %collective-permute-start.12 = (bf16[9,32,256]{2,1,0:T(8,128)(2,1)S(1)}, bf16[9,32,256]{2,1,0:T(8,128)(2,1)S(1)}, u32[]{:S(2)}, u32[]{:S(2)}) collective-permute-start(bf16[9,32,256]{2,1,0:T(8,128)(2,1)S(1)} %pair_sum.1.refs_0_), channel_id=1, source_target_pairs={{0,4},{2,6},{4,0},{6,2},{8,12},{10,14},{12,8},{14,10},{1,5},{3,7},... | collective-permute-start | bytes 442376 | tf_op jit(solution)/shard_map/ppermute | solution.py:27
  49.2 7.1 %collective-permute-start.11 = (bf16[9,32,256]{2,1,0:T(8,128)(2,1)S(1)}, bf16[9,32,256]{2,1,0:T(8,128)(2,1)S(1)}, u32[]{:S(2)}, u32[]{:S(2)}) collective-permute-start(bf16[9,32,256]{2,1,0:T(8,128)(2,1)S(1)} %pair_sum.1.refs_0_), channel_id=1, source_target_pairs={{0,1},{1,0},{2,3},{3,2},{4,5},{5,4},{6,7},{7,6},{8,9},{9,8},{10,11... | collective-permute-start | bytes 442376 | tf_op jit(solution)/shard_map/ppermute | solution.py:27
  53.3 3.0 %collective-permute-start.17 = (bf16[9,32,256]{2,1,0:T(8,128)(2,1)S(1)}, bf16[9,32,256]{2,1,0:T(8,128)(2,1)S(1)}, u32[]{:S(2)}, u32[]{:S(2)}) collective-permute-start(bf16[9,32,256]{2,1,0:T(8,128)(2,1)S(1)} %collective-permute-done.16.refs_3_), channel_id=1, source_target_pairs={{0,1},{1,0},{2,3},{3,2},{4,5},{5,4},{6,7},{7,6},{8,9},{9,8},{10,11... | collective-permute-start | bytes 442376 | tf_op jit(solution)/shard_map/ppermute | solution.py:27
  54.6 1.7 %collective-permute-start.15 = (bf16[9,32,256]{2,1,0:T(8,128)(2,1)S(1)}, bf16[9,32,256]{2,1,0:T(8,128)(2,1)S(1)}, u32[]{:S(2)}, u32[]{:S(2)}) collective-permute-start(bf16[9,32,256]{2,1,0:T(8,128)(2,1)S(1)} %collective-permute-done.14.refs_2_), channel_id=1, source_target_pairs={{0,1},{1,0},{2,3},{3,2},{4,5},{5,4},{6,7},{7,6},{8,9},{9,8},{10,11... | collective-permute-start | bytes 442376 | tf_op jit(solution)/shard_map/ppermute | solution.py:27
  55.1 1.4 %collective-permute-start.13 = (bf16[9,32,256]{2,1,0:T(8,128)(2,1)S(1)}, bf16[9,32,256]{2,1,0:T(8,128)(2,1)S(1)}, u32[]{:S(2)}, u32[]{:S(2)}) collective-permute-start(bf16[9,32,256]{2,1,0:T(8,128)(2,1)S(1)} %collective-permute-done.12.refs_1_), channel_id=1, source_target_pairs={{0,1},{1,0},{2,3},{3,2},{4,5},{5,4},{6,7},{7,6},{8,9},{9,8},{10,11... | collective-permute-start | bytes 442376 | tf_op jit(solution)/shard_map/ppermute | solution.py:27

commit v8 on v7

--- a/solution.py
+++ b/solution.py
@@ -372,7 +372,7 @@
             ko[f_at + r] = jnp.broadcast_to(own_rows[r : r + 1], (16, 256)).astype(LOW)
             k2[f_at + r] = jnp.broadcast_to(halo_rows[r : r + 1], (16, 256)).astype(LOW)
         for r in range(up_rows.shape[0]):
-            uv[a_at + r] = jnp.broadcast_to(up_rows[r : r + 1], (8, 128))
+            uv[a_at + r] = jnp.broadcast_to(up_rows[r : r + 1], (16, 128)).astype(LOW)
 
     own_codes = codes[...].astype(WIDE)
     put_codes(
@@ -470,26 +470,28 @@
     fx[:, 0:16] = fine[:, 0:16].astype(LOW)
     fx[:, 16:32] = jnp.concatenate([fine[:, 16:24], jnp.zeros((frame, 8, 256), WIDE)], 1).astype(LOW)
 
-    edge = iota((128, 128), 0)
     lanes = iota((128, 128), 1)
-    up_mask = jnp.where(lanes == edge, 1.0, 0.0)
-    up_places = lanes.astype(WIDE)
-    up_ones = jnp.ones((128, 128), LOW)
+    up_mask = jnp.where(lanes == iota((128, 128), 0), 1.0, 0.0).astype(LOW).reshape(8, 16, 128)
+    up_places = lanes.astype(WIDE).astype(CODE)
+    one, zero = jnp.ones((128, 128), LOW), jnp.zeros((128, 128), LOW)
     m2_flat = m2x[...].reshape(a_frame * 16, 256)
     m2_low = m2_flat.astype(LOW)
     up_recv = mm(m2_low, weights[4]).reshape(a_frame, 16, 256) * 0.5
-    weight = halved(weights[3])
+    picked = [(up_mask * uv[aa][None]).reshape(128, 128) for aa in range(a_frame)]
+    found = mm(jnp.concatenate(picked, 0), jnp.ones((128, 128), LOW)).astype(CODE)
+    senders = []
+    for aa in range(a_frame):
+        chosen = jnp.where(found[aa * 128 : aa * 128 + 128] == up_places, one, zero)
+        ohu[aa] = chosen
+        senders.append(mm(chosen, fx[2 * aa : 2 * aa + 4].reshape(128, 256)).astype(LOW))
+        su[aa] = senders[aa]
+    up_pre = mm(jnp.concatenate(senders, 0), halved(weights[3]))
     pools = []
     for aa in range(a_frame):
-        vec = uv[aa]
-        picked = (up_mask.reshape(16, 8, 128) * vec[None]).reshape(128, 128).astype(LOW)
-        chosen = jnp.where(mm(picked, up_ones) == up_places, 1.0, 0.0).astype(LOW)
-        ohu[aa] = chosen
-        senders = mm(chosen, fx[2 * aa : 2 * aa + 4].reshape(128, 256)).astype(LOW)
-        su[aa] = senders
-        act, rise = silu_of(mm(senders, weight).reshape(8, 16, 256) + up_recv[aa][None])
+        act, rise = silu_of(up_pre[aa * 128 : aa * 128 + 128].reshape(8, 16, 256) + up_recv[aa][None])
         pools.append(jnp.sum(act, axis=0) * (1.0 / 8))
         uslope[aa] = rise.reshape(128, 256)
+    cot_w = mm_nt(cx[...].reshape(cx.shape[0] * 32, 256), weights[8])
     up_pool = jnp.concatenate(pools, 0).astype(LOW)
     coarse = (m2_flat + mm(up_pool, weights[5])).astype(LOW)
 
@@ -499,7 +501,6 @@
     parents = mm(spread[...], coarse).astype(LOW)
     fine_mid = fx[1 : 1 + c_frame].reshape(c_frame * 32, 256)
     act, rise = silu_of((mm(parents, weights[6]) + mm(fine_mid, weights[7])) * 0.5)
-    cot_w = mm_nt(cx[...].reshape(c_frame * 32, 256), weights[8])
     dd[0] = (cot_w * 0.5 * rise).astype(LOW).reshape(c_frame, 32, 256)
     dd[1] = act.astype(LOW).reshape(c_frame, 32, 256)
 
@@ -790,7 +791,7 @@
         pltpu.VMEM((frame, 24, 256), WIDE),
         pltpu.VMEM((frame, 16, 256), LOW),
         pltpu.VMEM((frame, 16, 256), LOW),
-        pltpu.VMEM((a_frame, 8, 128), WIDE),
+        pltpu.VMEM((a_frame, 16, 128), LOW),
         pltpu.VMEM((frame, 24, 256), WIDE),
         pltpu.VMEM((frame, 32, 256), LOW),
         pltpu.VMEM((c_frame, 32, 256), LOW),

time: 57.8 us -> 56.4 us (0.976)
  Pallas kernels: 17.1 us -> 15.8 us
    pallas_call x1, Pallas kernels: 7.3 us -> 5.95 us  [body(): pl.pallas_call(functools.partial(flat_main, dirs, n_lat), out_shape=[jax....]
where the time goes in v8:
time: 56.4 us; the launch traced here: 56.3 us
  waiting for transfers between devices  21.8 us (39%)
  starting transfers between devices  18 us (32%)
  Pallas kernels  15.8 us (28%)
  between operations  0.71 us (1%)
    ppermute x18, waiting for transfers between devices, permute(): lax.ppermute(values, axes, [(i, j) for i, j in pairs if j is not None])  21.8 us
    ppermute x18, starting transfers between devices, permute(): lax.ppermute(values, axes, [(i, j) for i, j in pairs if j is not None])  18 us
    pallas_call x1, Pallas kernels, body(): pl.pallas_call(functools.partial(flat_main, dirs, n_lat), out_shape=[jax....  5.95 us
    pallas_call x1, Pallas kernels, body(): pl.pallas_call(inner_kernel, out_shape=[jax.ShapeDtypeStruct((16, 2, 128,...  3.58 us
    pallas_call x1, Pallas kernels, body(): pl.pallas_call(back_kernel, out_shape=[jax.ShapeDtypeStruct(mesh1_state.s...  2.29 us
    pallas_call x2, Pallas kernels, body(): pl.pallas_call(functools.partial(spread_kernel, scale, own), out_shape=ja...  2.21 us
    pallas_call x1, Pallas kernels, body(): pl.pallas_call(functools.partial(pack_kernel, dirs, glon, m1lon), out_sha...  1.53 us
  transfers between devices with their start and end apart: 18, of which 11 were waited for; matrix products, arithmetic and copies ran while one was open for 0% of the time, Pallas kernels for 12%

profile of v8, /device:TPU:0, one launch (start us, length us, event | category | flops | bytes accessed | tf_op | source)
XLA Modules:
  0.0 56.3 jit_solution(6356051649870860016)
XLA Ops:
  0.6 1.5 %pack_halos.1 = (bf16[32,32,256]{2,1,0:T(8,128)(2,1)S(1)}, bf16[16,16,256]{2,1,0:T(8,128)(2,1)S(1)}, bf16[16,16,256]{2,1,0:T(8,128)(2,1)S(1)}, bf16[8,16,256]{2,...) custom-call(bf16[32,32,256]{2,1,0:T(8,128)(2,1)} %refs_0_.1, ...), custom_call_target="tpu_custom_call" | custom-call | tf_op jit(solution)/shard_map/pack_halos/pallas_call | solution.py:712
  2.2 0.5 collective-permute-start
  2.7 4.7 %collective-permute-start.1 = (bf16[416,256]{1,0:T(8,128)(2,1)S(1)}, bf16[416,256]{1,0:T(8,128)(2,1)S(1)}, u32[]{:S(2)}, u32[]{:S(2)}) collective-permute-start(bf16[416,256]{1,0:T(8,128)(2,1)S(1)} %get-tuple-element.49), channel_id=1, source_target_pairs={{0,13},{1,4},{2,15},{3,6},{4,1},{5,8},{6,3},{7,10},{8,5},{9,12},{1... | collective-permute-start | bytes 638984 | tf_op jit(solution)/shard_map/ppermute | solution.py:27
  7.4 1.5 %collective-permute-start.2 = (bf16[352,256]{1,0:T(8,128)(2,1)S(1)}, bf16[352,256]{1,0:T(8,128)(2,1)S(1)}, u32[]{:S(2)}, u32[]{:S(2)}) collective-permute-start(bf16[352,256]{1,0:T(8,128)(2,1)S(1)} %get-tuple-element.50), channel_id=1, source_target_pairs={{0,2},{1,3},{2,0},{3,1},{4,6},{5,7},{6,4},{7,5},{8,10},{9,11},{10,... | collective-permute-start | bytes 540680 | tf_op jit(solution)/shard_map/ppermute | solution.py:27
  8.9 1.6 %collective-permute-start.4 = (bf16[112,256]{1,0:T(8,128)(2,1)S(1)}, bf16[112,256]{1,0:T(8,128)(2,1)S(1)}, u32[]{:S(2)}, u32[]{:S(2)}) collective-permute-start(bf16[112,256]{1,0:T(8,128)(2,1)S(1)} %get-tuple-element.52), channel_id=1, source_target_pairs={{0,15},{1,6},{2,13},{3,4},{4,3},{5,10},{6,1},{7,8},{8,7},{9,14},{1... | collective-permute-start | bytes 172040 | tf_op jit(solution)/shard_map/ppermute | solution.py:27
  10.5 3.6 %inner_rows.1 = (bf16[16,2,128,256]{3,2,1,0:T(8,128)(2,1)S(1)}, bf16[16,2,128,256]{3,2,1,0:T(8,128)(2,1)S(1)}, f32[16,16,256]{2,1,0:T(8,128)S(1)}, f32[16,16,256...) custom-call(bf16[32,32,256]{2,1,0:T(8,128)(2,1)S(1)} %get-tuple-elem, ...), custom_call_target="tpu_custom_call" | custom-call | flops 1000000000 | bytes 1000 | tf_op jit(solution)/shard_map/inner_rows/pallas_call | solution.py:730
  14.4 1.0 %collective-permute-done.4.refs_14_ = bf16[112,256]{1,0:T(8,128)(2,1)S(1)} collective-permute-done((bf16[112,256]{1,0:T(8,128)(2,1)S(1)}, bf16[112,256]{1,0:T(8,128)(2,1)S(1)}, u32[]{:S(2)}, u32[]{:S(2)}) %collective-permute-start.4) | collective-permute-done | bytes 57376 | tf_op jit(solution)/shard_map/ppermute | solution.py:27
  15.4 5.9 %sweep.1 = (bf16[16,16,256]{2,1,0:T(8,128)(2,1)}, f32[6,128,256]{2,1,0:T(8,128)S(1)}, bf16[6,128,256]{2,1,0:T(8,128)(2,1)S(1)}, f32[256,256]{1,0:T(8,128)S(1)}, ...) custom-call(bf16[32,32,256]{2,1,0:T(8,128)(2,1)S(1)} %get-tuple-elem, ...), custom_call_target="tpu_custom_call" | custom-call | tf_op jit(solution)/shard_map/sweep/pallas_call | solution.py:805
  21.3 2.3 %encoder_back.1 = (bf16[16,16,256]{2,1,0:T(8,128)(2,1)}, f32[3,128,256]{2,1,0:T(8,128)S(1)}, bf16[3,128,256]{2,1,0:T(8,128)(2,1)S(1)}) custom-call(bf16[16,16,256]{2,1,0:T(8,128)(2,1)S(1)} %get-tuple-element.39.m1.refs_1_, bf16[9,256,256]{2,1,0:T(8,128)(2,1)S(1)} %get-tuple-element.53.refs_15_.weights, f32[256,256]{1,0:T(8,128)S(1)} %get-tuple-element.55.fine_delta, ...), custom_call_target="tpu_custom_call" | custom-call | flops 3000000000 | bytes 8000000 | tf_op jit(solution)/shard_map/encoder_back/pallas_call | solution.py:827
  23.6 0.5 collective-permute-start.5
  24.1 1.1 %collective-permute-done.5.got_first = bf16[3,128,256]{2,1,0:T(8,128)(2,1)S(1)} collective-permute-done((bf16[3,128,256]{2,1,0:T(8,128)(2,1)S(1)}, bf16[3,128,256]{2,1,0:T(8,128)(2,1)S(1)}, u32[]{:S(2)}, u32[]{:S(2)}) %collective-permute-start.5) | collective-permute-done | bytes 196640 | tf_op jit(solution)/shard_map/ppermute | solution.py:27
  25.7 1.5 %collective-permute-start.8 = (bf16[9,32,256]{2,1,0:T(8,128)(2,1)S(1)}, bf16[9,32,256]{2,1,0:T(8,128)(2,1)S(1)}, u32[]{:S(2)}, u32[]{:S(2)}) collective-permute-start(bf16[9,32,256]{2,1,0:T(8,128)(2,1)S(1)} %get-tuple-element.71), channel_id=1, source_target_pairs={{0,2},{2,0},{4,6},{6,4},{8,10},{10,8},{12,14},{14,12},{1,3},{3,1},... | collective-permute-start | bytes 442376 | tf_op jit(solution)/shard_map/ppermute | solution.py:27
  27.2 1.6 %collective-permute-start.9 = (bf16[9,32,256]{2,1,0:T(8,128)(2,1)S(1)}, bf16[9,32,256]{2,1,0:T(8,128)(2,1)S(1)}, u32[]{:S(2)}, u32[]{:S(2)}) collective-permute-start(bf16[9,32,256]{2,1,0:T(8,128)(2,1)S(1)} %get-tuple-element.72), channel_id=1, source_target_pairs={{0,6},{2,4},{4,2},{6,0},{8,14},{10,12},{12,10},{14,8},{1,7},{3,5},... | collective-permute-start | bytes 442376 | tf_op jit(solution)/shard_map/ppermute | solution.py:27
  28.9 3.2 %collective-permute-done.7.refs_1_ = bf16[9,32,256]{2,1,0:T(8,128)(2,1)S(1)} collective-permute-done((bf16[9,32,256]{2,1,0:T(8,128)(2,1)S(1)}, bf16[9,32,256]{2,1,0:T(8,128)(2,1)S(1)}, u32[]{:S(2)}, u32[]{:S(2)}) %collective-permute-start.7) | collective-permute-done | bytes 147488 | tf_op jit(solution)/shard_map/ppermute | solution.py:27
  32.1 2.9 %collective-permute-done.9.refs_3_ = bf16[9,32,256]{2,1,0:T(8,128)(2,1)S(1)} collective-permute-done((bf16[9,32,256]{2,1,0:T(8,128)(2,1)S(1)}, bf16[9,32,256]{2,1,0:T(8,128)(2,1)S(1)}, u32[]{:S(2)}, u32[]{:S(2)}) %collective-permute-start.9) | collective-permute-done | bytes 147488 | tf_op jit(solution)/shard_map/ppermute | solution.py:27
  35.1 2.0 %collective-permute-start.10 = (bf16[9,32,256]{2,1,0:T(8,128)(2,1)S(1)}, bf16[9,32,256]{2,1,0:T(8,128)(2,1)S(1)}, u32[]{:S(2)}, u32[]{:S(2)}) collective-permute-start(bf16[9,32,256]{2,1,0:T(8,128)(2,1)S(1)} %block_sum.1.refs_0_), channel_id=1, source_target_pairs={{0,8},{2,10},{4,12},{6,14},{8,0},{10,2},{12,4},{14,6},{1,9},{3,11}... | collective-permute-start | bytes 442376 | tf_op jit(solution)/shard_map/ppermute | solution.py:27
  37.1 7.2 %collective-permute-done.10.refs_1_ = bf16[9,32,256]{2,1,0:T(8,128)(2,1)S(1)} collective-permute-done((bf16[9,32,256]{2,1,0:T(8,128)(2,1)S(1)}, bf16[9,32,256]{2,1,0:T(8,128)(2,1)S(1)}, u32[]{:S(2)}, u32[]{:S(2)}) %collective-permute-start.10) | collective-permute-done | bytes 147488 | tf_op jit(solution)/shard_map/ppermute | solution.py:27
  44.6 0.9 %collective-permute-start.14 = (bf16[9,32,256]{2,1,0:T(8,128)(2,1)S(1)}, bf16[9,32,256]{2,1,0:T(8,128)(2,1)S(1)}, u32[]{:S(2)}, u32[]{:S(2)}) collective-permute-start(bf16[9,32,256]{2,1,0:T(8,128)(2,1)S(1)} %pair_sum.1.refs_0_), channel_id=1, source_target_pairs={{0,2},{2,0},{4,6},{6,4},{8,10},{10,8},{12,14},{14,12},{1,3},{3,1},... | collective-permute-start | bytes 442376 | tf_op jit(solution)/shard_map/ppermute | solution.py:27
  45.5 2.3 %collective-permute-start.12 = (bf16[9,32,256]{2,1,0:T(8,128)(2,1)S(1)}, bf16[9,32,256]{2,1,0:T(8,128)(2,1)S(1)}, u32[]{:S(2)}, u32[]{:S(2)}) collective-permute-start(bf16[9,32,256]{2,1,0:T(8,128)(2,1)S(1)} %pair_sum.1.refs_0_), channel_id=1, source_target_pairs={{0,4},{2,6},{4,0},{6,2},{8,12},{10,14},{12,8},{14,10},{1,5},{3,7},... | collective-permute-start | bytes 442376 | tf_op jit(solution)/shard_map/ppermute | solution.py:27
  47.8 4.1 %collective-permute-done.16.refs_3_ = bf16[9,32,256]{2,1,0:T(8,128)(2,1)S(1)} collective-permute-done((bf16[9,32,256]{2,1,0:T(8,128)(2,1)S(1)}, bf16[9,32,256]{2,1,0:T(8,128)(2,1)S(1)}, u32[]{:S(2)}, u32[]{:S(2)}) %collective-permute-start.16) | collective-permute-done | bytes 147488 | tf_op jit(solution)/shard_map/ppermute | solution.py:27
  51.9 1.3 %collective-permute-done.14.refs_2_ = bf16[9,32,256]{2,1,0:T(8,128)(2,1)S(1)} collective-permute-done((bf16[9,32,256]{2,1,0:T(8,128)(2,1)S(1)}, bf16[9,32,256]{2,1,0:T(8,128)(2,1)S(1)}, u32[]{:S(2)}, u32[]{:S(2)}) %collective-permute-start.14) | collective-permute-done | bytes 147488 | tf_op jit(solution)/shard_map/ppermute | solution.py:27
  53.2 0.6 %collective-permute-done.12.refs_1_ = bf16[9,32,256]{2,1,0:T(8,128)(2,1)S(1)} collective-permute-done((bf16[9,32,256]{2,1,0:T(8,128)(2,1)S(1)}, bf16[9,32,256]{2,1,0:T(8,128)(2,1)S(1)}, u32[]{:S(2)}, u32[]{:S(2)}) %collective-permute-start.12) | collective-permute-done | bytes 147488 | tf_op jit(solution)/shard_map/ppermute | solution.py:27
  53.8 1.1 %spread_own.1.refs_4_ = f32[9,256,256]{2,1,0:T(8,128)} custom-call(bf16[9,32,256]{2,1,0:T(8,128)(2,1)S(1)} %pair_sum.1.refs_0_, bf16[9,32,256]{2,1,0:T(8,128)(2,1)S(1)} %collective-permute-done.12.refs_1_, bf16[9,32,256]{2,1,0:T(8,128)(2,1)S(1)} %collective-permute-done.14.refs_2_, bf16[9,32,256]{2,1,0:T(8,128)(2,1)S(1)} %collective-permute-done.16.refs_3_), custom_call_target="tpu_custom_call" | custom-call | tf_op jit(solution)/shard_map/spread_own/pallas_call | solution.py:848
  55.2 1.1 %spread_other.1 = f32[9,256,256]{2,1,0:T(8,128)} custom-call(bf16[9,32,256]{2,1,0:T(8,128)(2,1)S(1)} %collective-permute-done.11.refs_0_, bf16[9,32,256]{2,1,0:T(8,128)(2,1)S(1)} %collective-permute-done.13.refs_1_, bf16[9,32,256]{2,1,0:T(8,128)(2,1)S(1)} %collective-permute-done.15.refs_2_, ...), custom_call_target="tpu_custom_call", output_to_operand_aliasing={{}: (4, {})} | custom-call | tf_op jit(solution)/shard_map/spread_other/pallas_call | solution.py:848
  (21 shorter events, 1.5 us)
Async XLA Ops:
  2.2 13.2 %collective-permute-start = (bf16[416,256]{1,0:T(8,128)(2,1)S(1)}, bf16[416,256]{1,0:T(8,128)(2,1)S(1)}, u32[]{:S(2)}, u32[]{:S(2)}) collective-permute-start(bf16[416,256]{1,0:T(8,128)(2,1)S(1)} %get-tuple-element.48), channel_id=1, source_target_pairs={{0,1},{1,0},{2,3},{3,2},{4,5},{5,4},{6,7},{7,6},{8,9},{9,8},{10,11... | collective-permute-start | bytes 638984 | tf_op jit(solution)/shard_map/ppermute | solution.py:27
  2.7 12.7 %collective-permute-start.1 = (bf16[416,256]{1,0:T(8,128)(2,1)S(1)}, bf16[416,256]{1,0:T(8,128)(2,1)S(1)}, u32[]{:S(2)}, u32[]{:S(2)}) collective-permute-start(bf16[416,256]{1,0:T(8,128)(2,1)S(1)} %get-tuple-element.49), channel_id=1, source_target_pairs={{0,13},{1,4},{2,15},{3,6},{4,1},{5,8},{6,3},{7,10},{8,5},{9,12},{1... | collective-permute-start | bytes 638984 | tf_op jit(solution)/shard_map/ppermute | solution.py:27
  7.4 8.0 %collective-permute-start.2 = (bf16[352,256]{1,0:T(8,128)(2,1)S(1)}, bf16[352,256]{1,0:T(8,128)(2,1)S(1)}, u32[]{:S(2)}, u32[]{:S(2)}) collective-permute-start(bf16[352,256]{1,0:T(8,128)(2,1)S(1)} %get-tuple-element.50), channel_id=1, source_target_pairs={{0,2},{1,3},{2,0},{3,1},{4,6},{5,7},{6,4},{7,5},{8,10},{9,11},{10,... | collective-permute-start | bytes 540680 | tf_op jit(solution)/shard_map/ppermute | solution.py:27
  8.9 5.5 %collective-permute-start.3 = (bf16[112,256]{1,0:T(8,128)(2,1)S(1)}, bf16[112,256]{1,0:T(8,128)(2,1)S(1)}, u32[]{:S(2)}, u32[]{:S(2)}) collective-permute-start(bf16[112,256]{1,0:T(8,128)(2,1)S(1)} %get-tuple-element.51), channel_id=1, source_target_pairs={{0,3},{1,2},{2,1},{3,0},{4,7},{5,6},{6,5},{7,4},{8,11},{9,10},{10,... | collective-permute-start | bytes 172040 | tf_op jit(solution)/shard_map/ppermute | solution.py:27
  8.9 6.5 %collective-permute-start.4 = (bf16[112,256]{1,0:T(8,128)(2,1)S(1)}, bf16[112,256]{1,0:T(8,128)(2,1)S(1)}, u32[]{:S(2)}, u32[]{:S(2)}) collective-permute-start(bf16[112,256]{1,0:T(8,128)(2,1)S(1)} %get-tuple-element.52), channel_id=1, source_target_pairs={{0,15},{1,6},{2,13},{3,4},{4,3},{5,10},{6,1},{7,8},{8,7},{9,14},{1... | collective-permute-start | bytes 172040 | tf_op jit(solution)/shard_map/ppermute | solution.py:27
  21.3 3.9 %collective-permute-start.6 = (bf16[6,128,256]{2,1,0:T(8,128)(2,1)S(1)}, bf16[6,128,256]{2,1,0:T(8,128)(2,1)S(1)}, u32[]{:S(2)}, u32[]{:S(2)}) collective-permute-start(bf16[6,128,256]{2,1,0:T(8,128)(2,1)S(1)} %get-tuple-element.68), channel_id=1, source_target_pairs={{0,1},{1,0},{2,3},{3,2},{4,5},{5,4},{6,7},{7,6},{8,9},{9,8},{10,11... | collective-permute-start | bytes 1179656 | tf_op jit(solution)/shard_map/ppermute | solution.py:27
  23.6 1.6 %collective-permute-start.5 = (bf16[3,128,256]{2,1,0:T(8,128)(2,1)S(1)}, bf16[3,128,256]{2,1,0:T(8,128)(2,1)S(1)}, u32[]{:S(2)}, u32[]{:S(2)}) collective-permute-start(bf16[3,128,256]{2,1,0:T(8,128)(2,1)S(1)} %get-tuple-element.66), channel_id=1, source_target_pairs={{0,1},{1,0},{2,3},{3,2},{4,5},{5,4},{6,7},{7,6},{8,9},{9,8},{10,11... | collective-permute-start | bytes 589832 | tf_op jit(solution)/shard_map/ppermute | solution.py:27
  25.3 6.7 %collective-permute-start.7 = (bf16[9,32,256]{2,1,0:T(8,128)(2,1)S(1)}, bf16[9,32,256]{2,1,0:T(8,128)(2,1)S(1)}, u32[]{:S(2)}, u32[]{:S(2)}) collective-permute-start(bf16[9,32,256]{2,1,0:T(8,128)(2,1)S(1)} %get-tuple-element.70), channel_id=1, source_target_pairs={{0,4},{2,6},{4,0},{6,2},{8,12},{10,14},{12,8},{14,10},{1,5},{3,7},... | collective-permute-start | bytes 442376 | tf_op jit(solution)/shard_map/ppermute | solution.py:27
  25.7 6.4 %collective-permute-start.8 = (bf16[9,32,256]{2,1,0:T(8,128)(2,1)S(1)}, bf16[9,32,256]{2,1,0:T(8,128)(2,1)S(1)}, u32[]{:S(2)}, u32[]{:S(2)}) collective-permute-start(bf16[9,32,256]{2,1,0:T(8,128)(2,1)S(1)} %get-tuple-element.71), channel_id=1, source_target_pairs={{0,2},{2,0},{4,6},{6,4},{8,10},{10,8},{12,14},{14,12},{1,3},{3,1},... | collective-permute-start | bytes 442376 | tf_op jit(solution)/shard_map/ppermute | solution.py:27
  27.2 7.8 %collective-permute-start.9 = (bf16[9,32,256]{2,1,0:T(8,128)(2,1)S(1)}, bf16[9,32,256]{2,1,0:T(8,128)(2,1)S(1)}, u32[]{:S(2)}, u32[]{:S(2)}) collective-permute-start(bf16[9,32,256]{2,1,0:T(8,128)(2,1)S(1)} %get-tuple-element.72), channel_id=1, source_target_pairs={{0,6},{2,4},{4,2},{6,0},{8,14},{10,12},{12,10},{14,8},{1,7},{3,5},... | collective-permute-start | bytes 442376 | tf_op jit(solution)/shard_map/ppermute | solution.py:27
  35.1 9.2 %collective-permute-start.10 = (bf16[9,32,256]{2,1,0:T(8,128)(2,1)S(1)}, bf16[9,32,256]{2,1,0:T(8,128)(2,1)S(1)}, u32[]{:S(2)}, u32[]{:S(2)}) collective-permute-start(bf16[9,32,256]{2,1,0:T(8,128)(2,1)S(1)} %block_sum.1.refs_0_), channel_id=1, source_target_pairs={{0,8},{2,10},{4,12},{6,14},{8,0},{10,2},{12,4},{14,6},{1,9},{3,11}... | collective-permute-start | bytes 442376 | tf_op jit(solution)/shard_map/ppermute | solution.py:27
  44.3 7.6 %collective-permute-start.16 = (bf16[9,32,256]{2,1,0:T(8,128)(2,1)S(1)}, bf16[9,32,256]{2,1,0:T(8,128)(2,1)S(1)}, u32[]{:S(2)}, u32[]{:S(2)}) collective-permute-start(bf16[9,32,256]{2,1,0:T(8,128)(2,1)S(1)} %pair_sum.1.refs_0_), channel_id=1, source_target_pairs={{0,6},{2,4},{4,2},{6,0},{8,14},{10,12},{12,10},{14,8},{1,7},{3,5},... | collective-permute-start | bytes 442376 | tf_op jit(solution)/shard_map/ppermute | solution.py:27
  44.6 8.6 %collective-permute-start.14 = (bf16[9,32,256]{2,1,0:T(8,128)(2,1)S(1)}, bf16[9,32,256]{2,1,0:T(8,128)(2,1)S(1)}, u32[]{:S(2)}, u32[]{:S(2)}) collective-permute-start(bf16[9,32,256]{2,1,0:T(8,128)(2,1)S(1)} %pair_sum.1.refs_0_), channel_id=1, source_target_pairs={{0,2},{2,0},{4,6},{6,4},{8,10},{10,8},{12,14},{14,12},{1,3},{3,1},... | collective-permute-start | bytes 442376 | tf_op jit(solution)/shard_map/ppermute | solution.py:27
  45.5 8.2 %collective-permute-start.12 = (bf16[9,32,256]{2,1,0:T(8,128)(2,1)S(1)}, bf16[9,32,256]{2,1,0:T(8,128)(2,1)S(1)}, u32[]{:S(2)}, u32[]{:S(2)}) collective-permute-start(bf16[9,32,256]{2,1,0:T(8,128)(2,1)S(1)} %pair_sum.1.refs_0_), channel_id=1, source_target_pairs={{0,4},{2,6},{4,0},{6,2},{8,12},{10,14},{12,8},{14,10},{1,5},{3,7},... | collective-permute-start | bytes 442376 | tf_op jit(solution)/shard_map/ppermute | solution.py:27
  47.8 7.1 %collective-permute-start.11 = (bf16[9,32,256]{2,1,0:T(8,128)(2,1)S(1)}, bf16[9,32,256]{2,1,0:T(8,128)(2,1)S(1)}, u32[]{:S(2)}, u32[]{:S(2)}) collective-permute-start(bf16[9,32,256]{2,1,0:T(8,128)(2,1)S(1)} %pair_sum.1.refs_0_), channel_id=1, source_target_pairs={{0,1},{1,0},{2,3},{3,2},{4,5},{5,4},{6,7},{7,6},{8,9},{9,8},{10,11... | collective-permute-start | bytes 442376 | tf_op jit(solution)/shard_map/ppermute | solution.py:27
  51.9 3.0 %collective-permute-start.17 = (bf16[9,32,256]{2,1,0:T(8,128)(2,1)S(1)}, bf16[9,32,256]{2,1,0:T(8,128)(2,1)S(1)}, u32[]{:S(2)}, u32[]{:S(2)}) collective-permute-start(bf16[9,32,256]{2,1,0:T(8,128)(2,1)S(1)} %collective-permute-done.16.refs_3_), channel_id=1, source_target_pairs={{0,1},{1,0},{2,3},{3,2},{4,5},{5,4},{6,7},{7,6},{8,9},{9,8},{10,11... | collective-permute-start | bytes 442376 | tf_op jit(solution)/shard_map/ppermute | solution.py:27
  53.2 1.7 %collective-permute-start.15 = (bf16[9,32,256]{2,1,0:T(8,128)(2,1)S(1)}, bf16[9,32,256]{2,1,0:T(8,128)(2,1)S(1)}, u32[]{:S(2)}, u32[]{:S(2)}) collective-permute-start(bf16[9,32,256]{2,1,0:T(8,128)(2,1)S(1)} %collective-permute-done.14.refs_2_), channel_id=1, source_target_pairs={{0,1},{1,0},{2,3},{3,2},{4,5},{5,4},{6,7},{7,6},{8,9},{9,8},{10,11... | collective-permute-start | bytes 442376 | tf_op jit(solution)/shard_map/ppermute | solution.py:27
  53.8 1.4 %collective-permute-start.13 = (bf16[9,32,256]{2,1,0:T(8,128)(2,1)S(1)}, bf16[9,32,256]{2,1,0:T(8,128)(2,1)S(1)}, u32[]{:S(2)}, u32[]{:S(2)}) collective-permute-start(bf16[9,32,256]{2,1,0:T(8,128)(2,1)S(1)} %collective-permute-done.12.refs_1_), channel_id=1, source_target_pairs={{0,1},{1,0},{2,3},{3,2},{4,5},{5,4},{6,7},{7,6},{8,9},{9,8},{10,11... | collective-permute-start | bytes 442376 | tf_op jit(solution)/shard_map/ppermute | solution.py:27

commit v9 on v8

--- a/solution.py
+++ b/solution.py
@@ -112,9 +112,9 @@
     copies = [
         pltpu.make_async_copy(a, b, sems.at[i]) for i, (a, b) in enumerate(zip(far, (grid, m1, cot, m2, edges, ups)))
     ]
-    for copy in copies:
+    for copy in copies[::-1]:
         copy.start()
-    for copy in copies[::-1]:
+    for copy in copies[4:]:
         copy.wait()
     rep = lax.axis_index("rep")
     lat = lax.axis_index("lat")
@@ -129,6 +129,8 @@
     codes[0:16, :] = own_k.astype(LOW)
     codes[16:32, :] = sent_k.astype(LOW)
     codes[32:48, :] = jnp.concatenate([up_k, jnp.zeros_like(up_k)], 0).astype(LOW)
+    for copy in copies[:4]:
+        copy.wait()
     m2w = m2[...].astype(WIDE)
     m2_half = jnp.where(rep == 0, m2w[:, 0:8], m2w[:, 8:16])
     row8 = iota((8, 256), 0)
@@ -318,11 +320,12 @@
 
     def own_grid(step, carry):
         r = step * 8
-        r8 = pl.multiple_of(step * 64, 64)
+        r8 = step * 64
         put_grid(g_own + r, grid[pl.ds(r, 8)], sides[0][pl.ds(r8, 64), :], sides[1][pl.ds(r8, 64), :])
         return carry
 
-    lax.fori_loop(0, 4, own_grid, 0)
+    for step in range(4):
+        own_grid(step, 0)
 
     def put_fine(sib, out, n, mid):
         left, right = left_right(sib.astype(WIDE), out.astype(WIDE))

time: 56.4 us -> 56.4 us (level)
  no operation moved by 1% of the time
where the time goes in v9:
time: 56.4 us; the launch traced here: 56.2 us
  waiting for transfers between devices  21.8 us (39%)
  starting transfers between devices  18 us (32%)
  Pallas kernels  15.7 us (28%)
  between operations  0.71 us (1%)
    ppermute x18, waiting for transfers between devices, permute(): lax.ppermute(values, axes, [(i, j) for i, j in pairs if j is not None])  21.8 us
    ppermute x18, starting transfers between devices, permute(): lax.ppermute(values, axes, [(i, j) for i, j in pairs if j is not None])  18 us
    pallas_call x1, Pallas kernels, body(): pl.pallas_call(functools.partial(flat_main, dirs, n_lat), out_shape=[jax....  5.94 us
    pallas_call x1, Pallas kernels, body(): pl.pallas_call(inner_kernel, out_shape=[jax.ShapeDtypeStruct((16, 2, 128,...  3.57 us
    pallas_call x1, Pallas kernels, body(): pl.pallas_call(back_kernel, out_shape=[jax.ShapeDtypeStruct(mesh1_state.s...  2.29 us
    pallas_call x2, Pallas kernels, body(): pl.pallas_call(functools.partial(spread_kernel, scale, own), out_shape=ja...  2.21 us
    pallas_call x1, Pallas kernels, body(): pl.pallas_call(functools.partial(pack_kernel, dirs, glon, m1lon), out_sha...  1.47 us
  transfers between devices with their start and end apart: 18, of which 11 were waited for; matrix products, arithmetic and copies ran while one was open for 0% of the time, Pallas kernels for 12%

profile of v9, /device:TPU:0, one launch (start us, length us, event | category | flops | bytes accessed | tf_op | source)
XLA Modules:
  0.0 56.2 jit_solution(1846125957053032450)
XLA Ops:
  0.6 1.5 %pack_halos.1 = (bf16[32,32,256]{2,1,0:T(8,128)(2,1)S(1)}, bf16[16,16,256]{2,1,0:T(8,128)(2,1)S(1)}, bf16[16,16,256]{2,1,0:T(8,128)(2,1)S(1)}, bf16[8,16,256]{2,...) custom-call(bf16[32,32,256]{2,1,0:T(8,128)(2,1)} %refs_0_.1, ...), custom_call_target="tpu_custom_call" | custom-call | tf_op jit(solution)/shard_map/pack_halos/pallas_call | solution.py:715
  2.1 0.5 collective-permute-start
  2.6 4.7 %collective-permute-start.1 = (bf16[416,256]{1,0:T(8,128)(2,1)S(1)}, bf16[416,256]{1,0:T(8,128)(2,1)S(1)}, u32[]{:S(2)}, u32[]{:S(2)}) collective-permute-start(bf16[416,256]{1,0:T(8,128)(2,1)S(1)} %get-tuple-element.49), channel_id=1, source_target_pairs={{0,13},{1,4},{2,15},{3,6},{4,1},{5,8},{6,3},{7,10},{8,5},{9,12},{1... | collective-permute-start | bytes 638984 | tf_op jit(solution)/shard_map/ppermute | solution.py:27
  7.3 1.5 %collective-permute-start.2 = (bf16[352,256]{1,0:T(8,128)(2,1)S(1)}, bf16[352,256]{1,0:T(8,128)(2,1)S(1)}, u32[]{:S(2)}, u32[]{:S(2)}) collective-permute-start(bf16[352,256]{1,0:T(8,128)(2,1)S(1)} %get-tuple-element.50), channel_id=1, source_target_pairs={{0,2},{1,3},{2,0},{3,1},{4,6},{5,7},{6,4},{7,5},{8,10},{9,11},{10,... | collective-permute-start | bytes 540680 | tf_op jit(solution)/shard_map/ppermute | solution.py:27
  8.8 1.6 %collective-permute-start.4 = (bf16[112,256]{1,0:T(8,128)(2,1)S(1)}, bf16[112,256]{1,0:T(8,128)(2,1)S(1)}, u32[]{:S(2)}, u32[]{:S(2)}) collective-permute-start(bf16[112,256]{1,0:T(8,128)(2,1)S(1)} %get-tuple-element.52), channel_id=1, source_target_pairs={{0,15},{1,6},{2,13},{3,4},{4,3},{5,10},{6,1},{7,8},{8,7},{9,14},{1... | collective-permute-start | bytes 172040 | tf_op jit(solution)/shard_map/ppermute | solution.py:27
  10.5 3.6 %inner_rows.1 = (bf16[16,2,128,256]{3,2,1,0:T(8,128)(2,1)S(1)}, bf16[16,2,128,256]{3,2,1,0:T(8,128)(2,1)S(1)}, f32[16,16,256]{2,1,0:T(8,128)S(1)}, f32[16,16,256...) custom-call(bf16[32,32,256]{2,1,0:T(8,128)(2,1)S(1)} %get-tuple-elem, ...), custom_call_target="tpu_custom_call" | custom-call | flops 1000000000 | bytes 1000 | tf_op jit(solution)/shard_map/inner_rows/pallas_call | solution.py:733
  14.3 1.0 %collective-permute-done.4.refs_14_ = bf16[112,256]{1,0:T(8,128)(2,1)S(1)} collective-permute-done((bf16[112,256]{1,0:T(8,128)(2,1)S(1)}, bf16[112,256]{1,0:T(8,128)(2,1)S(1)}, u32[]{:S(2)}, u32[]{:S(2)}) %collective-permute-start.4) | collective-permute-done | bytes 57376 | tf_op jit(solution)/shard_map/ppermute | solution.py:27
  15.3 5.9 %sweep.1 = (bf16[16,16,256]{2,1,0:T(8,128)(2,1)}, f32[6,128,256]{2,1,0:T(8,128)S(1)}, bf16[6,128,256]{2,1,0:T(8,128)(2,1)S(1)}, f32[256,256]{1,0:T(8,128)S(1)}, ...) custom-call(bf16[32,32,256]{2,1,0:T(8,128)(2,1)S(1)} %get-tuple-elem, ...), custom_call_target="tpu_custom_call" | custom-call | tf_op jit(solution)/shard_map/sweep/pallas_call | solution.py:808
  21.3 2.3 %encoder_back.1 = (bf16[16,16,256]{2,1,0:T(8,128)(2,1)}, f32[3,128,256]{2,1,0:T(8,128)S(1)}, bf16[3,128,256]{2,1,0:T(8,128)(2,1)S(1)}) custom-call(bf16[16,16,256]{2,1,0:T(8,128)(2,1)S(1)} %get-tuple-element.39.m1.refs_1_, bf16[9,256,256]{2,1,0:T(8,128)(2,1)S(1)} %get-tuple-element.53.refs_15_.weights, f32[256,256]{1,0:T(8,128)S(1)} %get-tuple-element.55.fine_delta, ...), custom_call_target="tpu_custom_call" | custom-call | flops 3000000000 | bytes 8000000 | tf_op jit(solution)/shard_map/encoder_back/pallas_call | solution.py:830
  23.6 0.5 collective-permute-start.5
  24.1 1.1 %collective-permute-done.5.got_first = bf16[3,128,256]{2,1,0:T(8,128)(2,1)S(1)} collective-permute-done((bf16[3,128,256]{2,1,0:T(8,128)(2,1)S(1)}, bf16[3,128,256]{2,1,0:T(8,128)(2,1)S(1)}, u32[]{:S(2)}, u32[]{:S(2)}) %collective-permute-start.5) | collective-permute-done | bytes 196640 | tf_op jit(solution)/shard_map/ppermute | solution.py:27
  25.7 1.5 %collective-permute-start.8 = (bf16[9,32,256]{2,1,0:T(8,128)(2,1)S(1)}, bf16[9,32,256]{2,1,0:T(8,128)(2,1)S(1)}, u32[]{:S(2)}, u32[]{:S(2)}) collective-permute-start(bf16[9,32,256]{2,1,0:T(8,128)(2,1)S(1)} %get-tuple-element.71), channel_id=1, source_target_pairs={{0,2},{2,0},{4,6},{6,4},{8,10},{10,8},{12,14},{14,12},{1,3},{3,1},... | collective-permute-start | bytes 442376 | tf_op jit(solution)/shard_map/ppermute | solution.py:27
  27.2 1.6 %collective-permute-start.9 = (bf16[9,32,256]{2,1,0:T(8,128)(2,1)S(1)}, bf16[9,32,256]{2,1,0:T(8,128)(2,1)S(1)}, u32[]{:S(2)}, u32[]{:S(2)}) collective-permute-start(bf16[9,32,256]{2,1,0:T(8,128)(2,1)S(1)} %get-tuple-element.72), channel_id=1, source_target_pairs={{0,6},{2,4},{4,2},{6,0},{8,14},{10,12},{12,10},{14,8},{1,7},{3,5},... | collective-permute-start | bytes 442376 | tf_op jit(solution)/shard_map/ppermute | solution.py:27
  28.8 3.2 %collective-permute-done.7.refs_1_ = bf16[9,32,256]{2,1,0:T(8,128)(2,1)S(1)} collective-permute-done((bf16[9,32,256]{2,1,0:T(8,128)(2,1)S(1)}, bf16[9,32,256]{2,1,0:T(8,128)(2,1)S(1)}, u32[]{:S(2)}, u32[]{:S(2)}) %collective-permute-start.7) | collective-permute-done | bytes 147488 | tf_op jit(solution)/shard_map/ppermute | solution.py:27
  32.0 2.9 %collective-permute-done.9.refs_3_ = bf16[9,32,256]{2,1,0:T(8,128)(2,1)S(1)} collective-permute-done((bf16[9,32,256]{2,1,0:T(8,128)(2,1)S(1)}, bf16[9,32,256]{2,1,0:T(8,128)(2,1)S(1)}, u32[]{:S(2)}, u32[]{:S(2)}) %collective-permute-start.9) | collective-permute-done | bytes 147488 | tf_op jit(solution)/shard_map/ppermute | solution.py:27
  35.0 2.0 %collective-permute-start.10 = (bf16[9,32,256]{2,1,0:T(8,128)(2,1)S(1)}, bf16[9,32,256]{2,1,0:T(8,128)(2,1)S(1)}, u32[]{:S(2)}, u32[]{:S(2)}) collective-permute-start(bf16[9,32,256]{2,1,0:T(8,128)(2,1)S(1)} %block_sum.1.refs_0_), channel_id=1, source_target_pairs={{0,8},{2,10},{4,12},{6,14},{8,0},{10,2},{12,4},{14,6},{1,9},{3,11}... | collective-permute-start | bytes 442376 | tf_op jit(solution)/shard_map/ppermute | solution.py:27
  37.0 7.2 %collective-permute-done.10.refs_1_ = bf16[9,32,256]{2,1,0:T(8,128)(2,1)S(1)} collective-permute-done((bf16[9,32,256]{2,1,0:T(8,128)(2,1)S(1)}, bf16[9,32,256]{2,1,0:T(8,128)(2,1)S(1)}, u32[]{:S(2)}, u32[]{:S(2)}) %collective-permute-start.10) | collective-permute-done | bytes 147488 | tf_op jit(solution)/shard_map/ppermute | solution.py:27
  44.5 0.9 %collective-permute-start.14 = (bf16[9,32,256]{2,1,0:T(8,128)(2,1)S(1)}, bf16[9,32,256]{2,1,0:T(8,128)(2,1)S(1)}, u32[]{:S(2)}, u32[]{:S(2)}) collective-permute-start(bf16[9,32,256]{2,1,0:T(8,128)(2,1)S(1)} %pair_sum.1.refs_0_), channel_id=1, source_target_pairs={{0,2},{2,0},{4,6},{6,4},{8,10},{10,8},{12,14},{14,12},{1,3},{3,1},... | collective-permute-start | bytes 442376 | tf_op jit(solution)/shard_map/ppermute | solution.py:27
  45.5 2.3 %collective-permute-start.12 = (bf16[9,32,256]{2,1,0:T(8,128)(2,1)S(1)}, bf16[9,32,256]{2,1,0:T(8,128)(2,1)S(1)}, u32[]{:S(2)}, u32[]{:S(2)}) collective-permute-start(bf16[9,32,256]{2,1,0:T(8,128)(2,1)S(1)} %pair_sum.1.refs_0_), channel_id=1, source_target_pairs={{0,4},{2,6},{4,0},{6,2},{8,12},{10,14},{12,8},{14,10},{1,5},{3,7},... | collective-permute-start | bytes 442376 | tf_op jit(solution)/shard_map/ppermute | solution.py:27
  47.8 4.1 %collective-permute-done.16.refs_3_ = bf16[9,32,256]{2,1,0:T(8,128)(2,1)S(1)} collective-permute-done((bf16[9,32,256]{2,1,0:T(8,128)(2,1)S(1)}, bf16[9,32,256]{2,1,0:T(8,128)(2,1)S(1)}, u32[]{:S(2)}, u32[]{:S(2)}) %collective-permute-start.16) | collective-permute-done | bytes 147488 | tf_op jit(solution)/shard_map/ppermute | solution.py:27
  51.9 1.3 %collective-permute-done.14.refs_2_ = bf16[9,32,256]{2,1,0:T(8,128)(2,1)S(1)} collective-permute-done((bf16[9,32,256]{2,1,0:T(8,128)(2,1)S(1)}, bf16[9,32,256]{2,1,0:T(8,128)(2,1)S(1)}, u32[]{:S(2)}, u32[]{:S(2)}) %collective-permute-start.14) | collective-permute-done | bytes 147488 | tf_op jit(solution)/shard_map/ppermute | solution.py:27
  53.2 0.6 %collective-permute-done.12.refs_1_ = bf16[9,32,256]{2,1,0:T(8,128)(2,1)S(1)} collective-permute-done((bf16[9,32,256]{2,1,0:T(8,128)(2,1)S(1)}, bf16[9,32,256]{2,1,0:T(8,128)(2,1)S(1)}, u32[]{:S(2)}, u32[]{:S(2)}) %collective-permute-start.12) | collective-permute-done | bytes 147488 | tf_op jit(solution)/shard_map/ppermute | solution.py:27
  53.7 1.1 %spread_own.1.refs_4_ = f32[9,256,256]{2,1,0:T(8,128)} custom-call(bf16[9,32,256]{2,1,0:T(8,128)(2,1)S(1)} %pair_sum.1.refs_0_, bf16[9,32,256]{2,1,0:T(8,128)(2,1)S(1)} %collective-permute-done.12.refs_1_, bf16[9,32,256]{2,1,0:T(8,128)(2,1)S(1)} %collective-permute-done.14.refs_2_, bf16[9,32,256]{2,1,0:T(8,128)(2,1)S(1)} %collective-permute-done.16.refs_3_), custom_call_target="tpu_custom_call" | custom-call | tf_op jit(solution)/shard_map/spread_own/pallas_call | solution.py:851
  55.1 1.1 %spread_other.1 = f32[9,256,256]{2,1,0:T(8,128)} custom-call(bf16[9,32,256]{2,1,0:T(8,128)(2,1)S(1)} %collective-permute-done.11.refs_0_, bf16[9,32,256]{2,1,0:T(8,128)(2,1)S(1)} %collective-permute-done.13.refs_1_, bf16[9,32,256]{2,1,0:T(8,128)(2,1)S(1)} %collective-permute-done.15.refs_2_, ...), custom_call_target="tpu_custom_call", output_to_operand_aliasing={{}: (4, {})} | custom-call | tf_op jit(solution)/shard_map/spread_other/pallas_call | solution.py:851
  (21 shorter events, 1.5 us)
Async XLA Ops:
  2.1 13.2 %collective-permute-start = (bf16[416,256]{1,0:T(8,128)(2,1)S(1)}, bf16[416,256]{1,0:T(8,128)(2,1)S(1)}, u32[]{:S(2)}, u32[]{:S(2)}) collective-permute-start(bf16[416,256]{1,0:T(8,128)(2,1)S(1)} %get-tuple-element.48), channel_id=1, source_target_pairs={{0,1},{1,0},{2,3},{3,2},{4,5},{5,4},{6,7},{7,6},{8,9},{9,8},{10,11... | collective-permute-start | bytes 638984 | tf_op jit(solution)/shard_map/ppermute | solution.py:27
  2.6 12.7 %collective-permute-start.1 = (bf16[416,256]{1,0:T(8,128)(2,1)S(1)}, bf16[416,256]{1,0:T(8,128)(2,1)S(1)}, u32[]{:S(2)}, u32[]{:S(2)}) collective-permute-start(bf16[416,256]{1,0:T(8,128)(2,1)S(1)} %get-tuple-element.49), channel_id=1, source_target_pairs={{0,13},{1,4},{2,15},{3,6},{4,1},{5,8},{6,3},{7,10},{8,5},{9,12},{1... | collective-permute-start | bytes 638984 | tf_op jit(solution)/shard_map/ppermute | solution.py:27
  7.3 8.0 %collective-permute-start.2 = (bf16[352,256]{1,0:T(8,128)(2,1)S(1)}, bf16[352,256]{1,0:T(8,128)(2,1)S(1)}, u32[]{:S(2)}, u32[]{:S(2)}) collective-permute-start(bf16[352,256]{1,0:T(8,128)(2,1)S(1)} %get-tuple-element.50), channel_id=1, source_target_pairs={{0,2},{1,3},{2,0},{3,1},{4,6},{5,7},{6,4},{7,5},{8,10},{9,11},{10,... | collective-permute-start | bytes 540680 | tf_op jit(solution)/shard_map/ppermute | solution.py:27
  8.8 5.5 %collective-permute-start.3 = (bf16[112,256]{1,0:T(8,128)(2,1)S(1)}, bf16[112,256]{1,0:T(8,128)(2,1)S(1)}, u32[]{:S(2)}, u32[]{:S(2)}) collective-permute-start(bf16[112,256]{1,0:T(8,128)(2,1)S(1)} %get-tuple-element.51), channel_id=1, source_target_pairs={{0,3},{1,2},{2,1},{3,0},{4,7},{5,6},{6,5},{7,4},{8,11},{9,10},{10,... | collective-permute-start | bytes 172040 | tf_op jit(solution)/shard_map/ppermute | solution.py:27
  8.8 6.5 %collective-permute-start.4 = (bf16[112,256]{1,0:T(8,128)(2,1)S(1)}, bf16[112,256]{1,0:T(8,128)(2,1)S(1)}, u32[]{:S(2)}, u32[]{:S(2)}) collective-permute-start(bf16[112,256]{1,0:T(8,128)(2,1)S(1)} %get-tuple-element.52), channel_id=1, source_target_pairs={{0,15},{1,6},{2,13},{3,4},{4,3},{5,10},{6,1},{7,8},{8,7},{9,14},{1... | collective-permute-start | bytes 172040 | tf_op jit(solution)/shard_map/ppermute | solution.py:27
  21.3 3.9 %collective-permute-start.6 = (bf16[6,128,256]{2,1,0:T(8,128)(2,1)S(1)}, bf16[6,128,256]{2,1,0:T(8,128)(2,1)S(1)}, u32[]{:S(2)}, u32[]{:S(2)}) collective-permute-start(bf16[6,128,256]{2,1,0:T(8,128)(2,1)S(1)} %get-tuple-element.68), channel_id=1, source_target_pairs={{0,1},{1,0},{2,3},{3,2},{4,5},{5,4},{6,7},{7,6},{8,9},{9,8},{10,11... | collective-permute-start | bytes 1179656 | tf_op jit(solution)/shard_map/ppermute | solution.py:27
  23.6 1.6 %collective-permute-start.5 = (bf16[3,128,256]{2,1,0:T(8,128)(2,1)S(1)}, bf16[3,128,256]{2,1,0:T(8,128)(2,1)S(1)}, u32[]{:S(2)}, u32[]{:S(2)}) collective-permute-start(bf16[3,128,256]{2,1,0:T(8,128)(2,1)S(1)} %get-tuple-element.66), channel_id=1, source_target_pairs={{0,1},{1,0},{2,3},{3,2},{4,5},{5,4},{6,7},{7,6},{8,9},{9,8},{10,11... | collective-permute-start | bytes 589832 | tf_op jit(solution)/shard_map/ppermute | solution.py:27
  25.2 6.7 %collective-permute-start.7 = (bf16[9,32,256]{2,1,0:T(8,128)(2,1)S(1)}, bf16[9,32,256]{2,1,0:T(8,128)(2,1)S(1)}, u32[]{:S(2)}, u32[]{:S(2)}) collective-permute-start(bf16[9,32,256]{2,1,0:T(8,128)(2,1)S(1)} %get-tuple-element.70), channel_id=1, source_target_pairs={{0,4},{2,6},{4,0},{6,2},{8,12},{10,14},{12,8},{14,10},{1,5},{3,7},... | collective-permute-start | bytes 442376 | tf_op jit(solution)/shard_map/ppermute | solution.py:27
  25.7 6.4 %collective-permute-start.8 = (bf16[9,32,256]{2,1,0:T(8,128)(2,1)S(1)}, bf16[9,32,256]{2,1,0:T(8,128)(2,1)S(1)}, u32[]{:S(2)}, u32[]{:S(2)}) collective-permute-start(bf16[9,32,256]{2,1,0:T(8,128)(2,1)S(1)} %get-tuple-element.71), channel_id=1, source_target_pairs={{0,2},{2,0},{4,6},{6,4},{8,10},{10,8},{12,14},{14,12},{1,3},{3,1},... | collective-permute-start | bytes 442376 | tf_op jit(solution)/shard_map/ppermute | solution.py:27
  27.2 7.8 %collective-permute-start.9 = (bf16[9,32,256]{2,1,0:T(8,128)(2,1)S(1)}, bf16[9,32,256]{2,1,0:T(8,128)(2,1)S(1)}, u32[]{:S(2)}, u32[]{:S(2)}) collective-permute-start(bf16[9,32,256]{2,1,0:T(8,128)(2,1)S(1)} %get-tuple-element.72), channel_id=1, source_target_pairs={{0,6},{2,4},{4,2},{6,0},{8,14},{10,12},{12,10},{14,8},{1,7},{3,5},... | collective-permute-start | bytes 442376 | tf_op jit(solution)/shard_map/ppermute | solution.py:27
  35.0 9.2 %collective-permute-start.10 = (bf16[9,32,256]{2,1,0:T(8,128)(2,1)S(1)}, bf16[9,32,256]{2,1,0:T(8,128)(2,1)S(1)}, u32[]{:S(2)}, u32[]{:S(2)}) collective-permute-start(bf16[9,32,256]{2,1,0:T(8,128)(2,1)S(1)} %block_sum.1.refs_0_), channel_id=1, source_target_pairs={{0,8},{2,10},{4,12},{6,14},{8,0},{10,2},{12,4},{14,6},{1,9},{3,11}... | collective-permute-start | bytes 442376 | tf_op jit(solution)/shard_map/ppermute | solution.py:27
  44.2 7.6 %collective-permute-start.16 = (bf16[9,32,256]{2,1,0:T(8,128)(2,1)S(1)}, bf16[9,32,256]{2,1,0:T(8,128)(2,1)S(1)}, u32[]{:S(2)}, u32[]{:S(2)}) collective-permute-start(bf16[9,32,256]{2,1,0:T(8,128)(2,1)S(1)} %pair_sum.1.refs_0_), channel_id=1, source_target_pairs={{0,6},{2,4},{4,2},{6,0},{8,14},{10,12},{12,10},{14,8},{1,7},{3,5},... | collective-permute-start | bytes 442376 | tf_op jit(solution)/shard_map/ppermute | solution.py:27
  44.5 8.6 %collective-permute-start.14 = (bf16[9,32,256]{2,1,0:T(8,128)(2,1)S(1)}, bf16[9,32,256]{2,1,0:T(8,128)(2,1)S(1)}, u32[]{:S(2)}, u32[]{:S(2)}) collective-permute-start(bf16[9,32,256]{2,1,0:T(8,128)(2,1)S(1)} %pair_sum.1.refs_0_), channel_id=1, source_target_pairs={{0,2},{2,0},{4,6},{6,4},{8,10},{10,8},{12,14},{14,12},{1,3},{3,1},... | collective-permute-start | bytes 442376 | tf_op jit(solution)/shard_map/ppermute | solution.py:27
  45.5 8.2 %collective-permute-start.12 = (bf16[9,32,256]{2,1,0:T(8,128)(2,1)S(1)}, bf16[9,32,256]{2,1,0:T(8,128)(2,1)S(1)}, u32[]{:S(2)}, u32[]{:S(2)}) collective-permute-start(bf16[9,32,256]{2,1,0:T(8,128)(2,1)S(1)} %pair_sum.1.refs_0_), channel_id=1, source_target_pairs={{0,4},{2,6},{4,0},{6,2},{8,12},{10,14},{12,8},{14,10},{1,5},{3,7},... | collective-permute-start | bytes 442376 | tf_op jit(solution)/shard_map/ppermute | solution.py:27
  47.8 7.1 %collective-permute-start.11 = (bf16[9,32,256]{2,1,0:T(8,128)(2,1)S(1)}, bf16[9,32,256]{2,1,0:T(8,128)(2,1)S(1)}, u32[]{:S(2)}, u32[]{:S(2)}) collective-permute-start(bf16[9,32,256]{2,1,0:T(8,128)(2,1)S(1)} %pair_sum.1.refs_0_), channel_id=1, source_target_pairs={{0,1},{1,0},{2,3},{3,2},{4,5},{5,4},{6,7},{7,6},{8,9},{9,8},{10,11... | collective-permute-start | bytes 442376 | tf_op jit(solution)/shard_map/ppermute | solution.py:27
  51.9 3.0 %collective-permute-start.17 = (bf16[9,32,256]{2,1,0:T(8,128)(2,1)S(1)}, bf16[9,32,256]{2,1,0:T(8,128)(2,1)S(1)}, u32[]{:S(2)}, u32[]{:S(2)}) collective-permute-start(bf16[9,32,256]{2,1,0:T(8,128)(2,1)S(1)} %collective-permute-done.16.refs_3_), channel_id=1, source_target_pairs={{0,1},{1,0},{2,3},{3,2},{4,5},{5,4},{6,7},{7,6},{8,9},{9,8},{10,11... | collective-permute-start | bytes 442376 | tf_op jit(solution)/shard_map/ppermute | solution.py:27
  53.1 1.7 %collective-permute-start.15 = (bf16[9,32,256]{2,1,0:T(8,128)(2,1)S(1)}, bf16[9,32,256]{2,1,0:T(8,128)(2,1)S(1)}, u32[]{:S(2)}, u32[]{:S(2)}) collective-permute-start(bf16[9,32,256]{2,1,0:T(8,128)(2,1)S(1)} %collective-permute-done.14.refs_2_), channel_id=1, source_target_pairs={{0,1},{1,0},{2,3},{3,2},{4,5},{5,4},{6,7},{7,6},{8,9},{9,8},{10,11... | collective-permute-start | bytes 442376 | tf_op jit(solution)/shard_map/ppermute | solution.py:27
  53.7 1.4 %collective-permute-start.13 = (bf16[9,32,256]{2,1,0:T(8,128)(2,1)S(1)}, bf16[9,32,256]{2,1,0:T(8,128)(2,1)S(1)}, u32[]{:S(2)}, u32[]{:S(2)}) collective-permute-start(bf16[9,32,256]{2,1,0:T(8,128)(2,1)S(1)} %collective-permute-done.12.refs_1_), channel_id=1, source_target_pairs={{0,1},{1,0},{2,3},{3,2},{4,5},{5,4},{6,7},{7,6},{8,9},{9,8},{10,11... | collective-permute-start | bytes 442376 | tf_op jit(solution)/shard_map/ppermute | solution.py:27
